TPU v7x, 512 devices: a whole 4x8x8 slice. The times are simulated.
512 devices in a mesh: section: 16 (over x, y_lo, core), ctx: 32 (over z, y_hi).
Axes of the slice: x: 4, y: 8 (y_hi: 4, y_lo: 2; y = y_hi * 2 + y_lo), z: 8, core: 2. Of those that a mesh axis runs over, the one named last changes fastest.
Arguments:
- queries: bfloat16 [16, 4096, 4096], P('section', 'ctx')
- key_values: bfloat16 [16, 4096, 2, 512], P('section', 'ctx')
- token_pos: int32 [4096], P('ctx'), may hold values from 0 to 4095, as said below
- layer_of_section: int32 [16], replicated, may hold values from 0 to 15, each once
Outputs:
- attended: bfloat16 [16, 4096, 4096], P('section', 'ctx')
Inputs may be any that keep to these rules, and one draw needn't show every extreme that they name: `token_pos`: each aligned block of 64 entries holds 64 consecutive positions rising by one; all entries together are each position of 0 to 4095 once.
All inputs are finite; a program needn't handle non-finite values.
Results may differ from a plain program's by a relative error of at most 0.0065.
Values may be sent and summed in bfloat16 or wider, within the bound.
No kernel may reach another device: no remote copies, remote signals or barrier semaphores. Data moves between devices by JAX's collectives and lax.ppermute only.
A program may use at most 64 MiB of HBM per device.

v0:
```python
import jax
import jax.numpy as jnp
from jax import lax
from jax.sharding import PartitionSpec as P

H = 32
KVH = 4
HD = 128
WARM = 2


masked_score = -1e30


def spread(value, axis, source):
    kept = jnp.where(lax.axis_index(axis) == source, value, 0).astype(value.dtype)
    return lax.psum(kept, axis)


def per_device(queries, key_values, token_pos, layer_of_section):
    layers = layer_of_section.shape[0]
    tok_rows = token_pos.shape[0]
    head_dim = HD
    kv_heads = KVH
    group_size = H // KVH
    score_scale = HD ** (-0.5)
    section_id = lax.axis_index("section")
    layer_ids = jnp.arange(layers, dtype=jnp.int32)
    layer_id = jnp.sum(jnp.where(layer_ids == section_id, layer_of_section, 0))
    top_section = jnp.sum(jnp.where(layer_of_section == layers - 1, layer_ids, 0))
    own_rows = key_values[0]
    top_rows = spread(own_rows, "section", top_section)
    source = jnp.where(layer_id < WARM, own_rows, top_rows)
    all_pos = lax.all_gather(token_pos, "ctx", axis=0, tiled=True)
    query_groups = queries[0].reshape(tok_rows, kv_heads, group_size, head_dim)
    latest = jnp.max(token_pos)
    start_state = (
        jnp.full((tok_rows, kv_heads, group_size), masked_score, jnp.float32),
        jnp.zeros((tok_rows, kv_heads, group_size), jnp.float32),
        jnp.zeros((tok_rows, kv_heads, group_size, head_dim), jnp.float32),
    )
    shard_rows = lax.all_gather(source, "ctx", axis=0, tiled=True)
    row_count = shard_rows.shape[0]
    block_rows = 512
    kv_blocks = shard_rows.reshape(row_count // block_rows, block_rows, 2, kv_heads, head_dim)
    pos_blocks = all_pos.reshape(row_count // block_rows, block_rows)

    def absorb(state_in, block_args):
        kv_block, block_pos = block_args

        def update(running):
            running_max, running_sum, running_acc = running
            scores = (
                jnp.einsum(
                    "qkgd,ckd->qkgc",
                    query_groups,
                    kv_block[:, 0],
                    preferred_element_type=jnp.float32,
                )
                * score_scale
            )
            visible = (block_pos[None, :] <= token_pos[:, None])[:, None, None, :]
            scores = jnp.where(visible, scores, masked_score)
            new_max = jnp.maximum(running_max, jnp.max(scores, axis=-1))
            weights = jnp.where(visible, jnp.exp(scores - new_max[..., None]), 0.0)
            factor = jnp.exp(running_max - new_max)
            new_sum = running_sum * factor + jnp.sum(weights, axis=-1)
            new_acc = running_acc * factor[..., None] + jnp.einsum(
                "qkgc,ckd->qkgd",
                weights.astype(jnp.bfloat16),
                kv_block[:, 1],
                preferred_element_type=jnp.float32,
            )
            return (new_max, new_sum, new_acc)

        return (
            lax.cond(jnp.min(block_pos) <= latest, update, lambda running: running, state_in),
            None,
        )

    state_out, _ = lax.scan(absorb, start_state, (kv_blocks, pos_blocks))
    running_max, running_sum, running_acc = state_out
    result = (running_acc / running_sum[..., None]).astype(jnp.bfloat16)
    return result.reshape(1, tok_rows, H * head_dim)


def solution(mesh):
    in_specs = (P("section", "ctx", None), P("section", "ctx", None, None), P("ctx"), P())
    out_specs = P("section", "ctx", None)
    return jax.shard_map(
        per_device, mesh=mesh, in_specs=in_specs, out_specs=out_specs, check_vma=False
    )
```

profile of v0, /device:TPU:1, one launch (start us, length us, event | category | flops | bytes accessed | tf_op | source)
XLA Modules:
  0.0 399.8 jit_solution(14780418470908281921)
XLA Ops:
  11.1 131.5 %all-reduce.2.cloned.1.call-done = bf16[128,2,512]{2,1,0:T(2,128)(2,1)} async-done(((bf16[128,2,512]{2,1,0:T(2,128)(2,1)}), bf16[128,2,512]{2,1,0:T(2,128)(2,1)}) %all-reduce.2.cloned.1.call-update) | async-done | bytes 262160 | tf_op jit(solution)/shard_map/psum | solution.py:17
  144.6 68.2 %all-gather = s32[32,1,128]{2,1,0:T(1,128)S(1)} all-gather(s32[1,1,128]{2,1,0:T(1,128)} %bitcast.42), channel_id=1, replica_groups=mesh['section'=16,'ctx'=32] {'ctx'}, dimensions={0}, use_global_device_ids=true | all-gather | bytes 16896 | tf_op jit(solution)/shard_map/all_gather | solution.py:34
  217.5 67.7 %all-gather.3.cloned.1.call-done = bf16[4096,2,512]{2,1,0:T(2,128)(2,1)} async-done(((bf16[128,2,512]{2,1,0:T(2,128)(2,1)}), bf16[4096,2,512]{2,1,0:T(2,128)(2,1)}) %all-gather.3.cloned.1.call-update) | async-done | bytes 8388624 | tf_op jit(solution)/shard_map/all_gather | solution.py:42
  285.3 14.1 %reshape.45 = bf16[8,512,2,4,128]{4,3,2,1,0:T(4,128)(2,1)} reshape(bf16[4096,2,512]{2,1,0:T(2,128)(2,1)} %all-gather.3.cloned.1.call-done) | data formatting | bytes 16777216 | tf_op jit(solution)/shard_map/reshape | solution.py:45
  299.4 8.9 %copy.16 = bf16[8,512,2,4,128]{4,1,3,2,0:T(8,128)(2,1)} copy(bf16[8,512,2,4,128]{4,3,2,1,0:T(4,128)(2,1)} %reshape.45) | data formatting | bytes 16777216 | tf_op jit(solution)/shard_map/while | solution.py:81
  308.5 81.7 %while.14 = (s32[]{:T(128)}, f32[128,4,8]{0,2,1:T(8,128)S(1)}, f32[128,4,8]{0,2,1:T(8,128)S(1)}, f32[128,4,8,128]{3,0,2,1:T(8,128)S(1)}, s32[8,512]{1,0:T(8,128)...) while((s32[]{:T(128)}, f32[128,4,8]{0,2,1:T(8,128)S(1)}, ...), condition=%wide.region_10.11_spmd, body=%wide.region_4.10_spmd.sunk | while | flops 1102127616 | bytes 34085624 | solution.py:81
  310.4 8.3 %conditional.2 = ((f32[128,4,8]{0,2,1:T(8,128)S(1)}, f32[128,4,8]{0,2,1:T(8,128)S(1)}, f32[128,4,8,128]{3,0,2,1:T(8,128)S(1)})) conditional(s32[]{:T(128)} %convert_element_type.19, (f32[128,4,8]{0,2,1:T(8,128)S(1)}, f32[128,4,8]{0,2,1:T(8,128)S(1)}, f32[128,4,8,128]{3,0,2,1:T(8,128)S(1)}) %tuple.37, (s32[1,512]{1,0:T(1,128)S(1)}, s32[128]{0:T(128)S(1)}, ...), branch_computations={%region_6.6_spmd, %region_7.9_spmd} | conditional | flops 1102127104 | bytes 34081316 | solution.py:77
  315.3 3.4 bitcast_add_fusion
  320.6 8.3 %conditional.2 = ((f32[128,4,8]{0,2,1:T(8,128)S(1)}, f32[128,4,8]{0,2,1:T(8,128)S(1)}, f32[128,4,8,128]{3,0,2,1:T(8,128)S(1)})) conditional(s32[]{:T(128)} %convert_element_type.19, (f32[128,4,8]{0,2,1:T(8,128)S(1)}, f32[128,4,8]{0,2,1:T(8,128)S(1)}, f32[128,4,8,128]{3,0,2,1:T(8,128)S(1)}) %tuple.37, (s32[1,512]{1,0:T(1,128)S(1)}, s32[128]{0:T(128)S(1)}, ...), branch_computations={%region_6.6_spmd, %region_7.9_spmd} | conditional | flops 1102127104 | bytes 34081316 | solution.py:77
  325.5 3.4 bitcast_add_fusion
  330.8 8.3 %conditional.2 = ((f32[128,4,8]{0,2,1:T(8,128)S(1)}, f32[128,4,8]{0,2,1:T(8,128)S(1)}, f32[128,4,8,128]{3,0,2,1:T(8,128)S(1)})) conditional(s32[]{:T(128)} %convert_element_type.19, (f32[128,4,8]{0,2,1:T(8,128)S(1)}, f32[128,4,8]{0,2,1:T(8,128)S(1)}, f32[128,4,8,128]{3,0,2,1:T(8,128)S(1)}) %tuple.37, (s32[1,512]{1,0:T(1,128)S(1)}, s32[128]{0:T(128)S(1)}, ...), branch_computations={%region_6.6_spmd, %region_7.9_spmd} | conditional | flops 1102127104 | bytes 34081316 | solution.py:77
  335.8 3.4 bitcast_add_fusion
  341.1 8.3 %conditional.2 = ((f32[128,4,8]{0,2,1:T(8,128)S(1)}, f32[128,4,8]{0,2,1:T(8,128)S(1)}, f32[128,4,8,128]{3,0,2,1:T(8,128)S(1)})) conditional(s32[]{:T(128)} %convert_element_type.19, (f32[128,4,8]{0,2,1:T(8,128)S(1)}, f32[128,4,8]{0,2,1:T(8,128)S(1)}, f32[128,4,8,128]{3,0,2,1:T(8,128)S(1)}) %tuple.37, (s32[1,512]{1,0:T(1,128)S(1)}, s32[128]{0:T(128)S(1)}, ...), branch_computations={%region_6.6_spmd, %region_7.9_spmd} | conditional | flops 1102127104 | bytes 34081316 | solution.py:77
  346.0 3.4 bitcast_add_fusion
  351.3 8.3 %conditional.2 = ((f32[128,4,8]{0,2,1:T(8,128)S(1)}, f32[128,4,8]{0,2,1:T(8,128)S(1)}, f32[128,4,8,128]{3,0,2,1:T(8,128)S(1)})) conditional(s32[]{:T(128)} %convert_element_type.19, (f32[128,4,8]{0,2,1:T(8,128)S(1)}, f32[128,4,8]{0,2,1:T(8,128)S(1)}, f32[128,4,8,128]{3,0,2,1:T(8,128)S(1)}) %tuple.37, (s32[1,512]{1,0:T(1,128)S(1)}, s32[128]{0:T(128)S(1)}, ...), branch_computations={%region_6.6_spmd, %region_7.9_spmd} | conditional | flops 1102127104 | bytes 34081316 | solution.py:77
  356.2 3.4 bitcast_add_fusion
  361.5 8.3 %conditional.2 = ((f32[128,4,8]{0,2,1:T(8,128)S(1)}, f32[128,4,8]{0,2,1:T(8,128)S(1)}, f32[128,4,8,128]{3,0,2,1:T(8,128)S(1)})) conditional(s32[]{:T(128)} %convert_element_type.19, (f32[128,4,8]{0,2,1:T(8,128)S(1)}, f32[128,4,8]{0,2,1:T(8,128)S(1)}, f32[128,4,8,128]{3,0,2,1:T(8,128)S(1)}) %tuple.37, (s32[1,512]{1,0:T(1,128)S(1)}, s32[128]{0:T(128)S(1)}, ...), branch_computations={%region_6.6_spmd, %region_7.9_spmd} | conditional | flops 1102127104 | bytes 34081316 | solution.py:77
  364.3 2.1 fusion.2
  366.4 3.4 bitcast_add_fusion
  371.7 8.3 %conditional.2 = ((f32[128,4,8]{0,2,1:T(8,128)S(1)}, f32[128,4,8]{0,2,1:T(8,128)S(1)}, f32[128,4,8,128]{3,0,2,1:T(8,128)S(1)})) conditional(s32[]{:T(128)} %convert_element_type.19, (f32[128,4,8]{0,2,1:T(8,128)S(1)}, f32[128,4,8]{0,2,1:T(8,128)S(1)}, f32[128,4,8,128]{3,0,2,1:T(8,128)S(1)}) %tuple.37, (s32[1,512]{1,0:T(1,128)S(1)}, s32[128]{0:T(128)S(1)}, ...), branch_computations={%region_6.6_spmd, %region_7.9_spmd} | conditional | flops 1102127104 | bytes 34081316 | solution.py:77
  374.5 2.1 fusion.2
  376.6 3.4 bitcast_add_fusion
  381.9 8.3 %conditional.2 = ((f32[128,4,8]{0,2,1:T(8,128)S(1)}, f32[128,4,8]{0,2,1:T(8,128)S(1)}, f32[128,4,8,128]{3,0,2,1:T(8,128)S(1)})) conditional(s32[]{:T(128)} %convert_element_type.19, (f32[128,4,8]{0,2,1:T(8,128)S(1)}, f32[128,4,8]{0,2,1:T(8,128)S(1)}, f32[128,4,8,128]{3,0,2,1:T(8,128)S(1)}) %tuple.37, (s32[1,512]{1,0:T(1,128)S(1)}, s32[128]{0:T(128)S(1)}, ...), branch_computations={%region_6.6_spmd, %region_7.9_spmd} | conditional | flops 1102127104 | bytes 34081316 | solution.py:77
  386.8 3.4 bitcast_add_fusion
  (83 shorter events, 52.7 us)
Async XLA Ops:
  6.5 136.1 %all-reduce.2.cloned.1.call-start = ((), (), s32[]{:S(2)}) async-start(), calls=%async_computation | async-start | bytes 524288 | tf_op jit(solution)/shard_map/psum | solution.py:17
  10.4 274.8 %all-gather.3.cloned.1.call-start = ((), (), s32[]{:S(2)}) async-start(), calls=%async_computation.1 | async-start | bytes 8650752 | tf_op jit(solution)/shard_map/all_gather | solution.py:42
  299.4 9.2 %copy-start = (s32[128]{0:T(128)S(1)}, s32[128]{0:T(128)}, u32[]{:S(2)}) copy-start(s32[128]{0:T(128)} %param.10) | copy-start | bytes 1540
Sparse Core Ops, SparseCore 0:
  10.6 132.0 all-reduce.1
  146.3 138.9 all-gather.2
where the time goes:
time: 401 us; the launch traced here: 400 us
  waiting for transfers between devices  199 us (50%)
  blocking collectives  68.2 us (17%)
  local copies, waits for them, and re-layouts  38.4 us (10%)
  matrix products  37.6 us (9%)
  other arithmetic  31.1 us (8%)
  between operations  14.8 us (4%)
  loops' own time  10.5 us (3%)
    psum x1, waiting for transfers between devices, spread(): return lax.psum(kept, axis)  132 us
    all_gather x1, blocking collectives, per_device(): all_pos = lax.all_gather(token_pos, 'ctx', axis=0, tiled=True)  68.2 us
    all_gather x1, waiting for transfers between devices, per_device(): shard_rows = lax.all_gather(source, 'ctx', axis=0, tiled=True)  67.7 us
    dot_general x8, matrix products, update(): jnp.einsum('qkgc,ckd->qkgd', weights.astype(jnp.bfloat16), kv_block[:, 1]...  27.2 us
    reduce_sum x8, other arithmetic, update(): new_sum = running_sum * factor + jnp.sum(weights, axis=-1)  16.9 us
    reshape x1, local copies, waits for them, and re-layouts, per_device(): shard_rows.reshape(row_count // block_rows, block_rows, 2, kv_heads, head...  14.1 us
    squeeze x8, local copies, waits for them, and re-layouts, per_device(): state_out, _ = lax.scan(absorb, start_state, (kv_blocks, pos_blocks))  10.4 us
    dot_general x8, matrix products, update(): jnp.einsum('qkgd,ckd->qkgc', query_groups, kv_block[:, 0], preferred_elem...  10.4 us
  transfers between devices with their start and end apart: 2, of which 2 were waited for; matrix products, arithmetic and copies ran while one was open for 1% of the time, Pallas kernels for 0%

commit v1 on v0

v1 whole, which is shorter than its diff:
```python
import functools

import jax
import jax.numpy as jnp
from jax import lax
from jax.experimental import pallas as pl
from jax.experimental.pallas import tpu as pltpu
from jax.sharding import Mesh, PartitionSpec as P

H = 32
KVH = 4
HD = 128
GROUP = 8
BLOCK = 64
WARM = 2
ROWS = 128
POS_ROWS = 16
SHARD = 2 * KVH * ROWS + POS_ROWS
MASKED = -1e30
SCALE = 1.4426950408889634 / HD**0.5


def attend_body(shards, first, last, *refs):
    it = iter(refs)
    q_ref, pos_ref = next(it), next(it)
    keys, values, caps = [], [], []
    lane = (lax.broadcasted_iota(jnp.int32, (1, ROWS), 1) % BLOCK).astype(jnp.float32)
    for n in shards:
        k_ref, v_ref, p_ref = next(it), next(it), next(it)
        for i in range(n):
            keys.append(k_ref[i])
            values.append(v_ref[i])
            key_pos = p_ref[i][0:1, :].astype(jnp.float32) * BLOCK + lane
            caps.append(jnp.where(key_pos <= pos_ref[...], jnp.inf, MASKED))
    k = jnp.concatenate(keys, axis=0)
    count = k.shape[0]
    v = jnp.concatenate(values, axis=0)
    v = jnp.concatenate([v, jnp.ones((count, HD), jnp.bfloat16)], axis=1)
    cap = jnp.concatenate(caps, axis=1).astype(jnp.float32)
    if not first:
        m_in, l_in, a_in = next(it), next(it), next(it)
    outs = list(it)
    for g in range(GROUP):
        cols = slice(g * HD, (g + 1) * HD)
        s = lax.dot_general(
            q_ref[:, cols], k, (((1,), (1,)), ((), ())), preferred_element_type=jnp.float32
        )
        s = jnp.minimum(s, cap)
        top = jnp.max(s, axis=1, keepdims=True)
        if first:
            m = jnp.broadcast_to(top, (ROWS, HD))
        else:
            m_old = m_in[:, cols]
            m = jnp.maximum(m_old, top)
        wide = jnp.concatenate([m] * (count // HD), axis=1)
        w = jnp.exp2((s - wide) * SCALE).astype(jnp.bfloat16)
        o = lax.dot_general(
            w, v, (((1,), (0,)), ((), ())), preferred_element_type=jnp.float32
        )
        acc, den = o[:, :HD], o[:, HD:]
        if not first:
            f = jnp.exp2((m_old - m) * SCALE)
            acc = acc + f * a_in[:, cols]
            den = den + f * l_in[:, cols]
        if last:
            outs[0][:, cols] = (acc / den).astype(jnp.bfloat16)
        else:
            outs[0][:, cols] = m
            outs[1][:, cols] = den
            outs[2][:, cols] = acc


def attend(q, pos, blocks, state, last):
    shards = tuple(b.shape[0] for b in blocks)
    wide = pl.BlockSpec((ROWS, GROUP * HD), lambda h: (0, h))
    in_specs = [wide, pl.BlockSpec((ROWS, 1), lambda h: (0, 0))]
    args = [q, pos]
    for b in blocks:
        n = b.shape[0]
        in_specs += [
            pl.BlockSpec((n, ROWS, HD), lambda h: (0, h, 0)),
            pl.BlockSpec((n, ROWS, HD), lambda h: (0, KVH + h, 0)),
            pl.BlockSpec((n, POS_ROWS, HD), lambda h: (0, 2 * KVH * ROWS // POS_ROWS, 0)),
        ]
        args += [b, b, b]
    if state is not None:
        in_specs += [wide] * 3
        args += list(state)
    kept = jax.ShapeDtypeStruct((ROWS, H * HD), jnp.float32)
    done = jax.ShapeDtypeStruct((ROWS, H * HD), jnp.bfloat16)
    count = sum(shards) * ROWS
    return pl.pallas_call(
        functools.partial(attend_body, shards, state is None, last),
        grid=(KVH,),
        in_specs=in_specs,
        out_specs=wide if last else [wide] * 3,
        out_shape=done if last else [kept] * 3,
        compiler_params=pltpu.CompilerParams(vmem_limit_bytes=40 << 20),
        cost_estimate=pl.CostEstimate(
            flops=4 * ROWS * H * count * HD,
            bytes_accessed=8 << 20,
            transcendentals=ROWS * H * count,
        ),
        name="attend",
    )(*args)


def turn(value, axis, size, shift):
    return lax.ppermute(value, axis, [(i, (i + shift) % size) for i in range(size)])


def per_device(sizes, queries, key_values, token_pos, layer_of_section):
    nx, nyl, nz, nyh = sizes["x"], sizes["yl"], sizes["z"], sizes["yh"]
    layers = layer_of_section.shape[0]
    section = lax.axis_index(("x", "yl", "core"))
    ids = jnp.arange(layers, dtype=jnp.int32)
    layer = jnp.sum(jnp.where(ids == section, layer_of_section, 0))
    own = key_values[0].reshape(ROWS, 2 * KVH, HD).transpose(1, 0, 2).reshape(2 * KVH * ROWS, HD)
    top = jnp.where(layer == layers - 1, own, 0).astype(jnp.bfloat16)
    top = top + turn(top, "core", 2, 1)
    top = top + turn(top, "yl", nyl, 1)
    parts = [turn(top, "x", nx, shift) for shift in range(1, nx)]
    for part in parts:
        top = top + part
    rows = jnp.where(layer < WARM, own, top)
    block_id = jnp.broadcast_to((token_pos // BLOCK).astype(jnp.bfloat16)[None, :], (POS_ROWS, ROWS))
    shard = jnp.concatenate([rows, block_id], axis=0)
    line = jnp.stack([shard] + [turn(shard, "yh", nyh, shift) for shift in range(1, nyh)])
    q = queries[0]
    pos = token_pos.astype(jnp.float32)[:, None]
    up, down = turn(line, "z", nz, 1), turn(line, "z", nz, -1)
    state = attend(q, pos, [line], None, False)
    for _ in range(nz // 2 - 2):
        nup, ndown = turn(up, "z", nz, 1), turn(down, "z", nz, -1)
        state = attend(q, pos, [up, down], state, False)
        up, down = nup, ndown
    half = nyh // 2
    last_up, last_down = turn(up[:half], "z", nz, 1), turn(down[half:], "z", nz, -1)
    state = attend(q, pos, [up, down], state, False)
    out = attend(q, pos, [last_up, last_down], state, True)
    return out[None]


def solution(mesh):
    sizes = {"x": 4, "yl": 2, "core": 2, "z": 8, "yh": 4}
    fine = Mesh(mesh.devices.reshape(tuple(sizes.values())), tuple(sizes))
    section, ctx = ("x", "yl", "core"), ("z", "yh")
    in_specs = (P(section, ctx, None), P(section, ctx, None, None), P(ctx), P())
    return jax.shard_map(
        functools.partial(per_device, sizes),
        mesh=fine,
        in_specs=in_specs,
        out_specs=P(section, ctx, None),
        check_vma=False,
    )
```

time: 401 us -> 207 us (0.52)
  the two profiles are of different devices: /device:TPU:1 before, /device:TPU:2 now
where the time goes in v1:
time: 207 us; the launch traced here: 206 us
  waiting for transfers between devices  91.7 us (44%)
  starting transfers between devices  65 us (31%)
  Pallas kernels  38.5 us (19%)
  local copies, waits for them, and re-layouts  8.36 us (4%)
    ppermute x16, waiting for transfers between devices, turn(): lax.ppermute(value, axis, [(i, (i + shift) % size) for i in range(size)])  91.7 us
    ppermute x16, starting transfers between devices, turn(): lax.ppermute(value, axis, [(i, (i + shift) % size) for i in range(size)])  65 us
    pallas_call x5, Pallas kernels, attend(): pl.pallas_call(functools.partial(attend_body, shards, state is None, last...  38.5 us
    unnamed x20, local copies, waits for them, and re-layouts  5.96 us
  transfers between devices with their start and end apart: 16, of which 11 were waited for; matrix products, arithmetic and copies ran while one was open for 1% of the time, Pallas kernels for 16%

profile of v1, /device:TPU:2, one launch (start us, length us, event | category | flops | bytes accessed | tf_op | source)
XLA Modules:
  0.0 206.3 jit_solution(16770228722107631039)
XLA Ops:
  2.5 1.9 collective-permute-start
  6.0 3.5 %collective-permute-start.1 = (bf16[1024,128]{1,0:T(8,128)(2,1)S(1)}, bf16[1024,128]{1,0:T(8,128)(2,1)S(1)}, u32[]{:S(2)}, u32[]{:S(2)}) collective-permute-start(bf16[1024,128]{1,0:T(8,128)(2,1)S(1)} %fusion.3), channel_id=1, source_target_pairs={{0,64},{64,0},{1,65},{65,1},{2,66},{66,2},{3,67},{67,3},{4,68},{68... | collective-permute-start | bytes 786440 | tf_op jit(solution)/shard_map/ppermute | solution.py:109
  9.5 6.7 %collective-permute-done.1 = bf16[1024,128]{1,0:T(8,128)(2,1)S(1)} collective-permute-done((bf16[1024,128]{1,0:T(8,128)(2,1)S(1)}, bf16[1024,128]{1,0:T(8,128)(2,1)S(1)}, u32[]{:S(2)}, u32[]{:S(2)}) %collective-permute-start.1) | collective-permute-done | bytes 262176 | tf_op jit(solution)/shard_map/ppermute | solution.py:109
  16.4 3.4 %collective-permute-start.2 = (bf16[1024,128]{1,0:T(8,128)(2,1)S(1)}, bf16[1024,128]{1,0:T(8,128)(2,1)S(1)}, u32[]{:S(2)}, u32[]{:S(2)}) collective-permute-start(bf16[1024,128]{1,0:T(8,128)(2,1)S(1)} %add.25), channel_id=1, source_target_pairs={{0,128},{128,256},{256,384},{384,0},{1,129},{129,257},{257,385},{3... | collective-permute-start | bytes 786440 | tf_op jit(solution)/shard_map/ppermute | solution.py:109
  19.8 8.4 %collective-permute-start.3 = (bf16[1024,128]{1,0:T(8,128)(2,1)S(1)}, bf16[1024,128]{1,0:T(8,128)(2,1)S(1)}, u32[]{:S(2)}, u32[]{:S(2)}) collective-permute-start(bf16[1024,128]{1,0:T(8,128)(2,1)S(1)} %add.25), channel_id=1, source_target_pairs={{0,256},{128,384},{256,0},{384,128},{1,257},{129,385},{257,1},{385... | collective-permute-start | bytes 786440 | tf_op jit(solution)/shard_map/ppermute | solution.py:109
  31.4 4.0 %collective-permute-done.3 = bf16[1024,128]{1,0:T(8,128)(2,1)S(1)} collective-permute-done((bf16[1024,128]{1,0:T(8,128)(2,1)S(1)}, bf16[1024,128]{1,0:T(8,128)(2,1)S(1)}, u32[]{:S(2)}, u32[]{:S(2)}) %collective-permute-start.3) | collective-permute-done | bytes 262176 | tf_op jit(solution)/shard_map/ppermute | solution.py:109
  35.4 3.9 %collective-permute-done.4 = bf16[1024,128]{1,0:T(8,128)(2,1)S(1)} collective-permute-done((bf16[1024,128]{1,0:T(8,128)(2,1)S(1)}, bf16[1024,128]{1,0:T(8,128)(2,1)S(1)}, u32[]{:S(2)}, u32[]{:S(2)}) %collective-permute-start.4) | collective-permute-done | bytes 262176 | tf_op jit(solution)/shard_map/ppermute | solution.py:109
  41.3 5.3 %collective-permute-start.6 = (bf16[1040,128]{1,0:T(8,128)(2,1)S(1)}, bf16[1040,128]{1,0:T(8,128)(2,1)S(1)}, u32[]{:S(2)}, u32[]{:S(2)}) collective-permute-start(bf16[1040,128]{1,0:T(8,128)(2,1)S(1)} %get-tuple-element.30), channel_id=1, source_target_pairs={{0,2},{1,3},{2,0},{3,1},{4,6},{5,7},{6,4},{7,5},{8,10},{9,11},{10,... | collective-permute-start | bytes 798728 | tf_op jit(solution)/shard_map/ppermute | solution.py:109
  46.6 5.3 %collective-permute-start.7 = (bf16[1040,128]{1,0:T(8,128)(2,1)S(1)}, bf16[1040,128]{1,0:T(8,128)(2,1)S(1)}, u32[]{:S(2)}, u32[]{:S(2)}) collective-permute-start(bf16[1040,128]{1,0:T(8,128)(2,1)S(1)} %get-tuple-element.30), channel_id=1, source_target_pairs={{0,3},{1,0},{2,1},{3,2},{4,7},{5,4},{6,5},{7,6},{8,11},{9,8},{10,9... | collective-permute-start | bytes 798728 | tf_op jit(solution)/shard_map/ppermute | solution.py:109
  51.9 11.4 %collective-permute-done.5 = bf16[1040,128]{1,0:T(8,128)(2,1)S(1)} collective-permute-done((bf16[1040,128]{1,0:T(8,128)(2,1)S(1)}, bf16[1040,128]{1,0:T(8,128)(2,1)S(1)}, u32[]{:S(2)}, u32[]{:S(2)}) %collective-permute-start.5) | collective-permute-done | bytes 266272 | tf_op jit(solution)/shard_map/ppermute | solution.py:109
  63.3 9.1 %collective-permute-done.7 = bf16[1040,128]{1,0:T(8,128)(2,1)S(1)} collective-permute-done((bf16[1040,128]{1,0:T(8,128)(2,1)S(1)}, bf16[1040,128]{1,0:T(8,128)(2,1)S(1)}, u32[]{:S(2)}, u32[]{:S(2)}) %collective-permute-start.7) | collective-permute-done | bytes 266272 | tf_op jit(solution)/shard_map/ppermute | solution.py:109
  72.5 2.7 %collective-permute-start.8 = (bf16[4,1040,128]{2,1,0:T(8,128)(2,1)S(1)}, bf16[4,1040,128]{2,1,0:T(8,128)(2,1)S(1)}, u32[]{:S(2)}, u32[]{:S(2)}) collective-permute-start(bf16[4,1040,128]{2,1,0:T(8,128)(2,1)S(1)} %pad_maximum_fusion.refs_2_.refs_3_.refs_4_), channel_id=1, source_target_pairs={{0,4},{4,8},{8,12},{12,16},{16,20},{20,24},{24,28},{28,0},{1,5},{5... | collective-permute-start | bytes 3194888 | tf_op jit(solution)/shard_map/ppermute | solution.py:109
  75.2 8.6 %collective-permute-start.12 = (bf16[4,1040,128]{2,1,0:T(8,128)(2,1)S(1)}, bf16[4,1040,128]{2,1,0:T(8,128)(2,1)S(1)}, u32[]{:S(2)}, u32[]{:S(2)}) collective-permute-start(bf16[4,1040,128]{2,1,0:T(8,128)(2,1)S(1)} %pad_maximum_fusion.refs_2_.refs_3_.refs_4_), channel_id=1, source_target_pairs={{0,28},{4,0},{8,4},{12,8},{16,12},{20,16},{24,20},{28,24},{1,29},{... | collective-permute-start | bytes 3194888 | tf_op jit(solution)/shard_map/ppermute | solution.py:109
  83.8 21.7 %collective-permute-done.8.refs_2_.refs_3_.refs_4_ = bf16[4,1040,128]{2,1,0:T(8,128)(2,1)S(1)} collective-permute-done((bf16[4,1040,128]{2,1,0:T(8,128)(2,1)S(1)}, bf16[4,1040,128]{2,1,0:T(8,128)(2,1)S(1)}, u32[]{:S(2)}, u32[]{:S(2)}) %collective-permute-start.8) | collective-permute-done | bytes 1064992 | tf_op jit(solution)/shard_map/ppermute | solution.py:109
  108.5 5.1 %collective-permute-start.13 = (bf16[4,1040,128]{2,1,0:T(8,128)(2,1)S(1)}, bf16[4,1040,128]{2,1,0:T(8,128)(2,1)}, u32[]{:S(2)}, u32[]{:S(2)}) collective-permute-start(bf16[4,1040,128]{2,1,0:T(8,128)(2,1)S(1)} %collective-permute-done.12.refs_5_.refs_6_.refs_7_), channel_id=1, source_target_pairs={{0,28},{4,0},{8,4},{12,8},{16,12},{20,16},{24,20},{28,24},{1,29},{... | collective-permute-start | bytes 3194888 | tf_op jit(solution)/shard_map/ppermute | solution.py:109
  114.6 19.1 %collective-permute-done.9.refs_2_.refs_3_.refs_4_ = bf16[4,1040,128]{2,1,0:T(8,128)(2,1)} collective-permute-done((bf16[4,1040,128]{2,1,0:T(8,128)(2,1)S(1)}, bf16[4,1040,128]{2,1,0:T(8,128)(2,1)}, u32[]{:S(2)}, u32[]{:S(2)}) %collective-permute-start.9) | collective-permute-done | bytes 1064992 | tf_op jit(solution)/shard_map/ppermute | solution.py:109
  135.7 5.7 %collective-permute-start.14 = (bf16[4,1040,128]{2,1,0:T(8,128)(2,1)}, bf16[4,1040,128]{2,1,0:T(8,128)(2,1)}, u32[]{:S(2)}, u32[]{:S(2)}) collective-permute-start(bf16[4,1040,128]{2,1,0:T(8,128)(2,1)} %collective-permute-done.13.refs_5_.refs_6_.refs_7_), channel_id=1, source_target_pairs={{0,28},{4,0},{8,4},{12,8},{16,12},{20,16},{24,20},{28,24},{1,29},{... | collective-permute-start | bytes 3194888 | tf_op jit(solution)/shard_map/ppermute | solution.py:109
  141.6 4.6 %attend.5 = (f32[128,4096]{1,0:T(8,128)S(1)}, f32[128,4096]{1,0:T(8,128)S(1)}, f32[128,4096]{1,0:T(8,128)S(1)}) custom-call(bf16[128,4096]{1,0:T(8,128)(2,1)S(1)} %bitcast.16, f32[128,1]{1,0:T(8,128)S(1)} %copy.10.refs_1_, bf16[4,1040,128]{2,1,0:T(8,128)(2,1)S(1)} %pad_maximum_fusion.refs_2_.refs_3_.refs_4_, ...), custom_call_target="tpu_custom_call" | custom-call | flops 1073741824 | bytes 8388608 | tf_op jit(solution)/shard_map/attend/pallas_call | solution.py:92
  147.5 13.4 %collective-permute-done.10.refs_2_.refs_3_.refs_4_ = bf16[4,1040,128]{2,1,0:T(8,128)(2,1)S(1)} collective-permute-done((bf16[4,1040,128]{2,1,0:T(8,128)(2,1)}, bf16[4,1040,128]{2,1,0:T(8,128)(2,1)S(1)}, u32[]{:S(2)}, u32[]{:S(2)}) %collective-permute-start.10) | collective-permute-done | bytes 1064992 | tf_op jit(solution)/shard_map/ppermute | solution.py:109
  164.0 5.6 %collective-permute-start.15 = (bf16[2,1040,128]{2,1,0:T(8,128)(2,1)S(1)}, bf16[2,1040,128]{2,1,0:T(8,128)(2,1)S(1)}, u32[]{:S(2)}, u32[]{:S(2)}) collective-permute-start(bf16[2,1040,128]{2,1,0:T(8,128)(2,1)S(1)} %slice.9), channel_id=1, source_target_pairs={{0,28},{4,0},{8,4},{12,8},{16,12},{20,16},{24,20},{28,24},{1,29},{... | collective-permute-start | bytes 1597448 | tf_op jit(solution)/shard_map/ppermute | solution.py:109
  169.7 9.4 %attend.6 = (f32[128,4096]{1,0:T(8,128)S(1)}, f32[128,4096]{1,0:T(8,128)S(1)}, f32[128,4096]{1,0:T(8,128)S(1)}) custom-call(bf16[128,4096]{1,0:T(8,128)(2,1)S(1)} %bitcast.17, f32[128,1]{1,0:T(8,128)S(1)} %copy.10.refs_1_, bf16[4,1040,128]{2,1,0:T(8,128)(2,1)S(1)} %copy-done.2, bf16[4,1040,128]{2,1,0:T(8,128)(2,1)S(1)} %copy-done.2, ...), custom_call_target="tpu_custom_call" | custom-call | flops 2147483648 | bytes 8388608 | tf_op jit(solution)/shard_map/attend/pallas_call | solution.py:92
  180.5 9.3 %attend.7 = (f32[128,4096]{1,0:T(8,128)S(1)}, f32[128,4096]{1,0:T(8,128)S(1)}, f32[128,4096]{1,0:T(8,128)S(1)}) custom-call(bf16[128,4096]{1,0:T(8,128)(2,1)S(1)} %bitcast.18, f32[128,1]{1,0:T(8,128)S(1)} %copy.10.refs_1_, bf16[4,1040,128]{2,1,0:T(8,128)(2,1)} %collective-permute-done.9.refs_2_.refs_3_.refs_4_, ...), custom_call_target="tpu_custom_call" | custom-call | flops 2147483648 | bytes 8388608 | tf_op jit(solution)/shard_map/attend/pallas_call | solution.py:92
  191.1 9.3 %attend.8 = (f32[128,4096]{1,0:T(8,128)S(1)}, f32[128,4096]{1,0:T(8,128)S(1)}, f32[128,4096]{1,0:T(8,128)S(1)}) custom-call(bf16[128,4096]{1,0:T(8,128)(2,1)S(1)} %bitcast.19, f32[128,1]{1,0:T(8,128)S(1)} %copy.10.refs_1_, bf16[4,1040,128]{2,1,0:T(8,128)(2,1)S(1)} %collective-permute-done.10.refs_2_.refs_3_.refs_4_, ...), custom_call_target="tpu_custom_call" | custom-call | flops 2147483648 | bytes 8388608 | tf_op jit(solution)/shard_map/attend/pallas_call | solution.py:92
  200.4 5.8 %attend.9 = bf16[128,4096]{1,0:T(8,128)(2,1)} custom-call(bf16[128,4096]{1,0:T(8,128)(2,1)S(1)} %bitcast.20, f32[128,1]{1,0:T(8,128)S(1)} %copy.10.refs_1_, bf16[2,1040,128]{2,1,0:T(8,128)(2,1)S(1)} %collective-permute-done.11.refs_2_.refs_3_.refs_4_, bf16[2,1040,128]{2,1,0:T(8,128)(2,1)S(1)} %collective-permute-done.11.refs_2_.refs_3_.refs_4_, ...), custom_call_target="tpu_custom_call" | custom-call | flops 1073741824 | bytes 8388608 | tf_op jit(solution)/shard_map/attend/pallas_call | solution.py:92
  (47 shorter events, 21.3 us)
Async XLA Ops:
  0.0 1.2 copy-start.8
  1.2 29.6 %copy-start.9 = (s32[128]{0:T(128)S(1)}, s32[128]{0:T(128)}, u32[]{:S(2)}) copy-start(s32[128]{0:T(128)} %param.6) | copy-start | bytes 1540
  2.5 3.4 %collective-permute-start = (bf16[1024,128]{1,0:T(8,128)(2,1)S(1)}, bf16[1024,128]{1,0:T(8,128)(2,1)S(1)}, u32[]{:S(2)}, u32[]{:S(2)}) collective-permute-start(bf16[1024,128]{1,0:T(8,128)(2,1)S(1)} %bitcast_select_fusion.1), channel_id=1, source_target_pairs={{0,32},{32,0},{1,33},{33,1},{2,34},{34,2},{3,35},{35,3},{4,36},{36... | collective-permute-start | bytes 786440 | tf_op jit(solution)/shard_map/ppermute | solution.py:109
  6.0 10.2 %collective-permute-start.1 = (bf16[1024,128]{1,0:T(8,128)(2,1)S(1)}, bf16[1024,128]{1,0:T(8,128)(2,1)S(1)}, u32[]{:S(2)}, u32[]{:S(2)}) collective-permute-start(bf16[1024,128]{1,0:T(8,128)(2,1)S(1)} %fusion.3), channel_id=1, source_target_pairs={{0,64},{64,0},{1,65},{65,1},{2,66},{66,2},{3,67},{67,3},{4,68},{68... | collective-permute-start | bytes 786440 | tf_op jit(solution)/shard_map/ppermute | solution.py:109
  16.4 15.0 %collective-permute-start.2 = (bf16[1024,128]{1,0:T(8,128)(2,1)S(1)}, bf16[1024,128]{1,0:T(8,128)(2,1)S(1)}, u32[]{:S(2)}, u32[]{:S(2)}) collective-permute-start(bf16[1024,128]{1,0:T(8,128)(2,1)S(1)} %add.25), channel_id=1, source_target_pairs={{0,128},{128,256},{256,384},{384,0},{1,129},{129,257},{257,385},{3... | collective-permute-start | bytes 786440 | tf_op jit(solution)/shard_map/ppermute | solution.py:109
  19.8 15.6 %collective-permute-start.3 = (bf16[1024,128]{1,0:T(8,128)(2,1)S(1)}, bf16[1024,128]{1,0:T(8,128)(2,1)S(1)}, u32[]{:S(2)}, u32[]{:S(2)}) collective-permute-start(bf16[1024,128]{1,0:T(8,128)(2,1)S(1)} %add.25), channel_id=1, source_target_pairs={{0,256},{128,384},{256,0},{384,128},{1,257},{129,385},{257,1},{385... | collective-permute-start | bytes 786440 | tf_op jit(solution)/shard_map/ppermute | solution.py:109
  28.2 11.1 %collective-permute-start.4 = (bf16[1024,128]{1,0:T(8,128)(2,1)S(1)}, bf16[1024,128]{1,0:T(8,128)(2,1)S(1)}, u32[]{:S(2)}, u32[]{:S(2)}) collective-permute-start(bf16[1024,128]{1,0:T(8,128)(2,1)S(1)} %add.25), channel_id=1, source_target_pairs={{0,384},{128,0},{256,128},{384,256},{1,385},{129,1},{257,129},{385... | collective-permute-start | bytes 786440 | tf_op jit(solution)/shard_map/ppermute | solution.py:109
  39.4 23.9 %collective-permute-start.5 = (bf16[1040,128]{1,0:T(8,128)(2,1)S(1)}, bf16[1040,128]{1,0:T(8,128)(2,1)S(1)}, u32[]{:S(2)}, u32[]{:S(2)}) collective-permute-start(bf16[1040,128]{1,0:T(8,128)(2,1)S(1)} %get-tuple-element.30), channel_id=1, source_target_pairs={{0,1},{1,2},{2,3},{3,0},{4,5},{5,6},{6,7},{7,4},{8,9},{9,10},{10,1... | collective-permute-start | bytes 798728 | tf_op jit(solution)/shard_map/ppermute | solution.py:109
  41.3 21.9 %collective-permute-start.6 = (bf16[1040,128]{1,0:T(8,128)(2,1)S(1)}, bf16[1040,128]{1,0:T(8,128)(2,1)S(1)}, u32[]{:S(2)}, u32[]{:S(2)}) collective-permute-start(bf16[1040,128]{1,0:T(8,128)(2,1)S(1)} %get-tuple-element.30), channel_id=1, source_target_pairs={{0,2},{1,3},{2,0},{3,1},{4,6},{5,7},{6,4},{7,5},{8,10},{9,11},{10,... | collective-permute-start | bytes 798728 | tf_op jit(solution)/shard_map/ppermute | solution.py:109
  46.6 25.8 %collective-permute-start.7 = (bf16[1040,128]{1,0:T(8,128)(2,1)S(1)}, bf16[1040,128]{1,0:T(8,128)(2,1)S(1)}, u32[]{:S(2)}, u32[]{:S(2)}) collective-permute-start(bf16[1040,128]{1,0:T(8,128)(2,1)S(1)} %get-tuple-element.30), channel_id=1, source_target_pairs={{0,3},{1,0},{2,1},{3,2},{4,7},{5,4},{6,5},{7,6},{8,11},{9,8},{10,9... | collective-permute-start | bytes 798728 | tf_op jit(solution)/shard_map/ppermute | solution.py:109
  72.4 69.2 %copy-start = (bf16[1,128,4096]{2,1,0:T(8,128)(2,1)S(1)}, bf16[1,128,4096]{2,1,0:T(8,128)(2,1)}, u32[]{:S(2)}) copy-start(bf16[1,128,4096]{2,1,0:T(8,128)(2,1)} %param.4) | copy-start | bytes 3145732
  72.5 33.0 %collective-permute-start.8 = (bf16[4,1040,128]{2,1,0:T(8,128)(2,1)S(1)}, bf16[4,1040,128]{2,1,0:T(8,128)(2,1)S(1)}, u32[]{:S(2)}, u32[]{:S(2)}) collective-permute-start(bf16[4,1040,128]{2,1,0:T(8,128)(2,1)S(1)} %pad_maximum_fusion.refs_2_.refs_3_.refs_4_), channel_id=1, source_target_pairs={{0,4},{4,8},{8,12},{12,16},{16,20},{20,24},{24,28},{28,0},{1,5},{5... | collective-permute-start | bytes 3194888 | tf_op jit(solution)/shard_map/ppermute | solution.py:109
  75.2 33.3 %collective-permute-start.12 = (bf16[4,1040,128]{2,1,0:T(8,128)(2,1)S(1)}, bf16[4,1040,128]{2,1,0:T(8,128)(2,1)S(1)}, u32[]{:S(2)}, u32[]{:S(2)}) collective-permute-start(bf16[4,1040,128]{2,1,0:T(8,128)(2,1)S(1)} %pad_maximum_fusion.refs_2_.refs_3_.refs_4_), channel_id=1, source_target_pairs={{0,28},{4,0},{8,4},{12,8},{16,12},{20,16},{24,20},{28,24},{1,29},{... | collective-permute-start | bytes 3194888 | tf_op jit(solution)/shard_map/ppermute | solution.py:109
  105.6 28.1 %collective-permute-start.9 = (bf16[4,1040,128]{2,1,0:T(8,128)(2,1)S(1)}, bf16[4,1040,128]{2,1,0:T(8,128)(2,1)}, u32[]{:S(2)}, u32[]{:S(2)}) collective-permute-start(bf16[4,1040,128]{2,1,0:T(8,128)(2,1)S(1)} %collective-permute-done.8.refs_2_.refs_3_.refs_4_), channel_id=1, source_target_pairs={{0,4},{4,8},{8,12},{12,16},{16,20},{20,24},{24,28},{28,0},{1,5},{5... | collective-permute-start | bytes 3194888 | tf_op jit(solution)/shard_map/ppermute | solution.py:109
  108.5 27.3 %collective-permute-start.13 = (bf16[4,1040,128]{2,1,0:T(8,128)(2,1)S(1)}, bf16[4,1040,128]{2,1,0:T(8,128)(2,1)}, u32[]{:S(2)}, u32[]{:S(2)}) collective-permute-start(bf16[4,1040,128]{2,1,0:T(8,128)(2,1)S(1)} %collective-permute-done.12.refs_5_.refs_6_.refs_7_), channel_id=1, source_target_pairs={{0,28},{4,0},{8,4},{12,8},{16,12},{20,16},{24,20},{28,24},{1,29},{... | collective-permute-start | bytes 3194888 | tf_op jit(solution)/shard_map/ppermute | solution.py:109
  133.7 27.3 %collective-permute-start.10 = (bf16[4,1040,128]{2,1,0:T(8,128)(2,1)}, bf16[4,1040,128]{2,1,0:T(8,128)(2,1)S(1)}, u32[]{:S(2)}, u32[]{:S(2)}) collective-permute-start(bf16[4,1040,128]{2,1,0:T(8,128)(2,1)} %collective-permute-done.9.refs_2_.refs_3_.refs_4_), channel_id=1, source_target_pairs={{0,4},{4,8},{8,12},{12,16},{16,20},{20,24},{24,28},{28,0},{1,5},{5... | collective-permute-start | bytes 3194888 | tf_op jit(solution)/shard_map/ppermute | solution.py:109
  135.7 27.2 %collective-permute-start.14 = (bf16[4,1040,128]{2,1,0:T(8,128)(2,1)}, bf16[4,1040,128]{2,1,0:T(8,128)(2,1)}, u32[]{:S(2)}, u32[]{:S(2)}) collective-permute-start(bf16[4,1040,128]{2,1,0:T(8,128)(2,1)} %collective-permute-done.13.refs_5_.refs_6_.refs_7_), channel_id=1, source_target_pairs={{0,28},{4,0},{8,4},{12,8},{16,12},{20,16},{24,20},{28,24},{1,29},{... | collective-permute-start | bytes 3194888 | tf_op jit(solution)/shard_map/ppermute | solution.py:109
  146.2 1.3 copy-start.5
  147.5 22.1 %copy-start.2 = (bf16[4,1040,128]{2,1,0:T(8,128)(2,1)S(1)}, bf16[4,1040,128]{2,1,0:T(8,128)(2,1)}, u32[]{:S(2)}) copy-start(bf16[4,1040,128]{2,1,0:T(8,128)(2,1)} %copy-done.1) | copy-start | bytes 3194884
  147.5 22.1 %copy-start.4 = (bf16[4,1040,128]{2,1,0:T(8,128)(2,1)S(1)}, bf16[4,1040,128]{2,1,0:T(8,128)(2,1)}, u32[]{:S(2)}) copy-start(bf16[4,1040,128]{2,1,0:T(8,128)(2,1)} %copy-done.3) | copy-start | bytes 3194884
  161.0 39.4 %collective-permute-start.11 = (bf16[2,1040,128]{2,1,0:T(8,128)(2,1)S(1)}, bf16[2,1040,128]{2,1,0:T(8,128)(2,1)S(1)}, u32[]{:S(2)}, u32[]{:S(2)}) collective-permute-start(bf16[2,1040,128]{2,1,0:T(8,128)(2,1)S(1)} %slice.8), channel_id=1, source_target_pairs={{0,4},{4,8},{8,12},{12,16},{16,20},{20,24},{24,28},{28,0},{1,5},{5... | collective-permute-start | bytes 1597448 | tf_op jit(solution)/shard_map/ppermute | solution.py:109
  164.0 36.4 %collective-permute-start.15 = (bf16[2,1040,128]{2,1,0:T(8,128)(2,1)S(1)}, bf16[2,1040,128]{2,1,0:T(8,128)(2,1)S(1)}, u32[]{:S(2)}, u32[]{:S(2)}) collective-permute-start(bf16[2,1040,128]{2,1,0:T(8,128)(2,1)S(1)} %slice.9), channel_id=1, source_target_pairs={{0,28},{4,0},{8,4},{12,8},{16,12},{20,16},{24,20},{28,24},{1,29},{... | collective-permute-start | bytes 1597448 | tf_op jit(solution)/shard_map/ppermute | solution.py:109
  179.1 1.3 copy-start.6
  189.7 1.3 copy-start.7
  (2 other events, 2.0 us)

commit v2 on v1

--- a/solution.py
+++ b/solution.py
@@ -15,7 +15,6 @@
 WARM = 2
 ROWS = 128
 POS_ROWS = 16
-SHARD = 2 * KVH * ROWS + POS_ROWS
 MASKED = -1e30
 SCALE = 1.4426950408889634 / HD**0.5
 
@@ -70,36 +69,39 @@
             outs[2][:, cols] = acc
 
 
-def attend(q, pos, blocks, state, last):
+def attend(q, pos, blocks, heads, offset, state, last):
     shards = tuple(b.shape[0] for b in blocks)
     wide = pl.BlockSpec((ROWS, GROUP * HD), lambda h: (0, h))
-    in_specs = [wide, pl.BlockSpec((ROWS, 1), lambda h: (0, 0))]
+    in_specs = [
+        pl.BlockSpec((ROWS, GROUP * HD), lambda h: (0, offset + h)),
+        pl.BlockSpec((ROWS, 1), lambda h: (0, 0)),
+    ]
     args = [q, pos]
     for b in blocks:
         n = b.shape[0]
         in_specs += [
             pl.BlockSpec((n, ROWS, HD), lambda h: (0, h, 0)),
-            pl.BlockSpec((n, ROWS, HD), lambda h: (0, KVH + h, 0)),
-            pl.BlockSpec((n, POS_ROWS, HD), lambda h: (0, 2 * KVH * ROWS // POS_ROWS, 0)),
+            pl.BlockSpec((n, ROWS, HD), lambda h: (0, heads + h, 0)),
+            pl.BlockSpec((n, POS_ROWS, HD), lambda h: (0, 2 * heads * ROWS // POS_ROWS, 0)),
         ]
         args += [b, b, b]
     if state is not None:
         in_specs += [wide] * 3
         args += list(state)
-    kept = jax.ShapeDtypeStruct((ROWS, H * HD), jnp.float32)
-    done = jax.ShapeDtypeStruct((ROWS, H * HD), jnp.bfloat16)
+    kept = jax.ShapeDtypeStruct((ROWS, heads * GROUP * HD), jnp.float32)
+    done = jax.ShapeDtypeStruct((ROWS, heads * GROUP * HD), jnp.bfloat16)
     count = sum(shards) * ROWS
     return pl.pallas_call(
         functools.partial(attend_body, shards, state is None, last),
-        grid=(KVH,),
+        grid=(heads,),
         in_specs=in_specs,
         out_specs=wide if last else [wide] * 3,
         out_shape=done if last else [kept] * 3,
         compiler_params=pltpu.CompilerParams(vmem_limit_bytes=40 << 20),
         cost_estimate=pl.CostEstimate(
-            flops=4 * ROWS * H * count * HD,
+            flops=4 * ROWS * heads * GROUP * count * HD,
             bytes_accessed=8 << 20,
-            transcendentals=ROWS * H * count,
+            transcendentals=ROWS * heads * GROUP * count,
         ),
         name="attend",
     )(*args)
@@ -109,36 +111,50 @@
     return lax.ppermute(value, axis, [(i, (i + shift) % size) for i in range(size)])
 
 
+def with_ids(rows, token_pos):
+    ids = (token_pos // BLOCK).astype(jnp.bfloat16)[None, :]
+    return jnp.concatenate([rows, jnp.broadcast_to(ids, (POS_ROWS, ROWS))], axis=0)
+
+
 def per_device(sizes, queries, key_values, token_pos, layer_of_section):
-    nx, nyl, nz, nyh = sizes["x"], sizes["yl"], sizes["z"], sizes["yh"]
+    nz, nyh = sizes["z"], sizes["yh"]
+    axes = ("x", "yl", "core")
     layers = layer_of_section.shape[0]
-    section = lax.axis_index(("x", "yl", "core"))
+    section = lax.axis_index(axes)
     ids = jnp.arange(layers, dtype=jnp.int32)
     layer = jnp.sum(jnp.where(ids == section, layer_of_section, 0))
-    own = key_values[0].reshape(ROWS, 2 * KVH, HD).transpose(1, 0, 2).reshape(2 * KVH * ROWS, HD)
-    top = jnp.where(layer == layers - 1, own, 0).astype(jnp.bfloat16)
-    top = top + turn(top, "core", 2, 1)
-    top = top + turn(top, "yl", nyl, 1)
-    parts = [turn(top, "x", nx, shift) for shift in range(1, nx)]
-    for part in parts:
-        top = top + part
-    rows = jnp.where(layer < WARM, own, top)
-    block_id = jnp.broadcast_to((token_pos // BLOCK).astype(jnp.bfloat16)[None, :], (POS_ROWS, ROWS))
-    shard = jnp.concatenate([rows, block_id], axis=0)
-    line = jnp.stack([shard] + [turn(shard, "yh", nyh, shift) for shift in range(1, nyh)])
+    top_section = jnp.sum(jnp.where(layer_of_section == layers - 1, ids, 0))
+    own = key_values[0].reshape(ROWS, 2, KVH, HD).transpose(2, 1, 0, 3)
+    pieces = own.reshape(layers, 2 * KVH * ROWS // layers, HD)
+    piece = lax.dynamic_index_in_dim(lax.all_to_all(pieces, axes, 0, 0), top_section, 0, True)
+    top = lax.all_to_all(jnp.broadcast_to(piece, pieces.shape), axes, 0, 0)
+    rows = jnp.where(layer < WARM, own, top.reshape(own.shape))
+    side = KVH - 1
+    ring_rows = rows[:side].transpose(1, 0, 2, 3).reshape(2 * side * ROWS, HD)
+    side_rows = rows[side:].transpose(1, 0, 2, 3).reshape(2 * (KVH - side) * ROWS, HD)
     q = queries[0]
     pos = token_pos.astype(jnp.float32)[:, None]
-    up, down = turn(line, "z", nz, 1), turn(line, "z", nz, -1)
-    state = attend(q, pos, [line], None, False)
-    for _ in range(nz // 2 - 2):
-        nup, ndown = turn(up, "z", nz, 1), turn(down, "z", nz, -1)
-        state = attend(q, pos, [up, down], state, False)
-        up, down = nup, ndown
+    beside = lax.all_gather(with_ids(side_rows, token_pos), ("z", "yh"), axis=0)
+    shard = with_ids(ring_rows, token_pos)
+    line = jnp.stack([shard] + [turn(shard, "yh", nyh, shift) for shift in range(1, nyh)])
+
+    def part(blocks, state, last=False):
+        return attend(q, pos, blocks, side, 0, state, last)
+
+    held, state = [line], None
+    up = down = line
+    for _ in range(nz // 2 - 1):
+        up, down = turn(up, "z", nz, 1), turn(down, "z", nz, -1)
+        state = part(held, state)
+        up, down, state = lax.optimization_barrier((up, down, state))
+        held = [up, down]
     half = nyh // 2
     last_up, last_down = turn(up[:half], "z", nz, 1), turn(down[half:], "z", nz, -1)
-    state = attend(q, pos, [up, down], state, False)
-    out = attend(q, pos, [last_up, last_down], state, True)
-    return out[None]
+    state = part(held, state)
+    side_out = attend(q, pos, [beside], KVH - side, side, None, True)
+    last_up, last_down, state, side_out = lax.optimization_barrier((last_up, last_down, state, side_out))
+    out = part([last_up, last_down], state, True)
+    return jnp.concatenate([out, side_out], axis=1)[None]
 
 
 def solution(mesh):

time: 207 us -> 191 us (0.923)
  the two profiles are of different devices: /device:TPU:2 before, /device:TPU:1 now
where the time goes in v2:
time: 191 us; the launch traced here: 188 us
  waiting for transfers between devices  69.6 us (36%)
  starting transfers between devices  56.5 us (30%)
  Pallas kernels  33.5 us (18%)
  between operations  16.1 us (8%)
  local copies, waits for them, and re-layouts  10.1 us (5%)
  other arithmetic  2.51 us (1%)
    ppermute x11, waiting for transfers between devices, turn(): lax.ppermute(value, axis, [(i, (i + shift) % size) for i in range(size)])  58.4 us
    ppermute x11, starting transfers between devices, turn(): lax.ppermute(value, axis, [(i, (i + shift) % size) for i in range(size)])  41.9 us
    pallas_call x6, Pallas kernels, attend(): pl.pallas_call(functools.partial(attend_body, shards, state is None, last...  33.5 us
    all_to_all x1, starting transfers between devices, per_device(): lax.all_to_all(pieces, axes, 0, 0)  10.2 us
    all_to_all x1, waiting for transfers between devices, per_device(): top = lax.all_to_all(jnp.broadcast_to(piece, pieces.shape), axes, 0, 0)  6.52 us
    unnamed x21, local copies, waits for them, and re-layouts  6.32 us
    all_to_all x1, waiting for transfers between devices, per_device(): lax.all_to_all(pieces, axes, 0, 0)  4.72 us
    all_to_all x1, starting transfers between devices, per_device(): top = lax.all_to_all(jnp.broadcast_to(piece, pieces.shape), axes, 0, 0)  4.33 us
  transfers between devices with their start and end apart: 14, of which 11 were waited for; matrix products, arithmetic and copies ran while one was open for 1% of the time, Pallas kernels for 16%

profile of v2, /device:TPU:1, one launch (start us, length us, event | category | flops | bytes accessed | tf_op | source)
XLA Modules:
  0.0 188.4 jit_solution(11663610856850269352)
XLA Ops:
  8.6 10.2 %all-to-all-start = ((bf16[16,64,128]{2,1,0:T(8,128)(2,1)}), bf16[16,64,128]{2,1,0:T(8,128)(2,1)S(1)}, u32[]{:S(2)}, u32[]{:S(2)}) async-start(bf16[16,64,128]{2,1,0:T(8,128)(2,1)} %bitcast.5), calls=%async_computation | async-start | bytes 524288 | tf_op jit(solution)/shard_map/all_to_all | solution.py:129
  21.3 4.7 %all-to-all-done = bf16[16,64,128]{2,1,0:T(8,128)(2,1)S(1)} async-done(((bf16[16,64,128]{2,1,0:T(8,128)(2,1)}), bf16[16,64,128]{2,1,0:T(8,128)(2,1)S(1)}, u32[]{:S(2)}, u32[]{:S(2)}) %all-to-all-start) | async-done | bytes 262176 | tf_op jit(solution)/shard_map/all_to_all | solution.py:129
  26.8 4.3 %all-to-all-start.1 = ((bf16[16,64,128]{2,1,0:T(8,128)(2,1)}), bf16[16,64,128]{2,1,0:T(8,128)(2,1)S(1)}, u32[]{:S(2)}, u32[]{:S(2)}) async-start(bf16[16,64,128]{2,1,0:T(8,128)(2,1)} %broadcast_in_dim.31), calls=%async_computation.1 | async-start | bytes 524288 | tf_op jit(solution)/shard_map/all_to_all | solution.py:130
  31.8 6.5 %all-to-all-done.1 = bf16[16,64,128]{2,1,0:T(8,128)(2,1)S(1)} async-done(((bf16[16,64,128]{2,1,0:T(8,128)(2,1)}), bf16[16,64,128]{2,1,0:T(8,128)(2,1)S(1)}, u32[]{:S(2)}, u32[]{:S(2)}) %all-to-all-start.1) | async-done | bytes 262176 | tf_op jit(solution)/shard_map/all_to_all | solution.py:130
  39.6 3.2 %collective-permute-start.1 = (bf16[784,128]{1,0:T(8,128)(2,1)S(1)}, bf16[784,128]{1,0:T(8,128)(2,1)S(1)}, u32[]{:S(2)}, u32[]{:S(2)}) collective-permute-start(bf16[784,128]{1,0:T(8,128)(2,1)S(1)} %get-tuple-element.74), channel_id=1, source_target_pairs={{0,2},{1,3},{2,0},{3,1},{4,6},{5,7},{6,4},{7,5},{8,10},{9,11},{10,... | collective-permute-start | bytes 602120 | tf_op jit(solution)/shard_map/ppermute | solution.py:111
  42.8 2.4 %collective-permute-start = (bf16[784,128]{1,0:T(8,128)(2,1)S(1)}, bf16[784,128]{1,0:T(8,128)(2,1)S(1)}, u32[]{:S(2)}, u32[]{:S(2)}) collective-permute-start(bf16[784,128]{1,0:T(8,128)(2,1)S(1)} %get-tuple-element.74), channel_id=1, source_target_pairs={{0,1},{1,2},{2,3},{3,0},{4,5},{5,6},{6,7},{7,4},{8,9},{9,10},{10,1... | collective-permute-start | bytes 602120 | tf_op jit(solution)/shard_map/ppermute | solution.py:111
  45.2 5.0 %collective-permute-start.2 = (bf16[784,128]{1,0:T(8,128)(2,1)S(1)}, bf16[784,128]{1,0:T(8,128)(2,1)S(1)}, u32[]{:S(2)}, u32[]{:S(2)}) collective-permute-start(bf16[784,128]{1,0:T(8,128)(2,1)S(1)} %get-tuple-element.74), channel_id=1, source_target_pairs={{0,3},{1,0},{2,1},{3,2},{4,7},{5,4},{6,5},{7,6},{8,11},{9,8},{10,9... | collective-permute-start | bytes 602120 | tf_op jit(solution)/shard_map/ppermute | solution.py:111
  50.2 5.7 %collective-permute-done.1 = bf16[784,128]{1,0:T(8,128)(2,1)S(1)} collective-permute-done((bf16[784,128]{1,0:T(8,128)(2,1)S(1)}, bf16[784,128]{1,0:T(8,128)(2,1)S(1)}, u32[]{:S(2)}, u32[]{:S(2)}) %collective-permute-start.1) | collective-permute-done | bytes 200736 | tf_op jit(solution)/shard_map/ppermute | solution.py:111
  57.1 8.7 %collective-permute-done.2 = bf16[784,128]{1,0:T(8,128)(2,1)S(1)} collective-permute-done((bf16[784,128]{1,0:T(8,128)(2,1)S(1)}, bf16[784,128]{1,0:T(8,128)(2,1)S(1)}, u32[]{:S(2)}, u32[]{:S(2)}) %collective-permute-start.2) | collective-permute-done | bytes 200736 | tf_op jit(solution)/shard_map/ppermute | solution.py:111
  66.0 8.4 %collective-permute-start.4 = (bf16[4,784,128]{2,1,0:T(8,128)(2,1)S(1)}, bf16[4,784,128]{2,1,0:T(8,128)(2,1)S(1)}, u32[]{:S(2)}, u32[]{:S(2)}) collective-permute-start(bf16[4,784,128]{2,1,0:T(8,128)(2,1)S(1)} %pad_maximum_fusion.refs_2_.refs_3_.refs_4_), channel_id=1, source_target_pairs={{0,28},{4,0},{8,4},{12,8},{16,12},{20,16},{24,20},{28,24},{1,29},{... | collective-permute-start | bytes 2408456 | tf_op jit(solution)/shard_map/ppermute | solution.py:111
  74.3 1.9 %collective-permute-start.3 = (bf16[4,784,128]{2,1,0:T(8,128)(2,1)S(1)}, bf16[4,784,128]{2,1,0:T(8,128)(2,1)S(1)}, u32[]{:S(2)}, u32[]{:S(2)}) collective-permute-start(bf16[4,784,128]{2,1,0:T(8,128)(2,1)S(1)} %pad_maximum_fusion.refs_2_.refs_3_.refs_4_), channel_id=1, source_target_pairs={{0,4},{4,8},{8,12},{12,16},{16,20},{20,24},{24,28},{28,0},{1,5},{5... | collective-permute-start | bytes 2408456 | tf_op jit(solution)/shard_map/ppermute | solution.py:111
  76.4 3.5 %attend.6 = (f32[128,3072]{1,0:T(8,128)S(1)}, f32[128,3072]{1,0:T(8,128)S(1)}, f32[128,3072]{1,0:T(8,128)S(1)}) custom-call(bf16[128,4096]{1,0:T(8,128)(2,1)S(1)} %bitcast.22, f32[128,1]{1,0:T(8,128)S(1)} %copy.39.refs_1_, bf16[4,784,128]{2,1,0:T(8,128)(2,1)S(1)} %pad_maximum_fusion.refs_2_.refs_3_.refs_4_, ...), custom_call_target="tpu_custom_call" | custom-call | flops 805306368 | bytes 8388608 | tf_op jit(solution)/shard_map/attend/pallas_call | solution.py:94
  79.9 12.2 %collective-permute-done.4.refs_5_.refs_6_.refs_7_ = bf16[4,784,128]{2,1,0:T(8,128)(2,1)S(1)} collective-permute-done((bf16[4,784,128]{2,1,0:T(8,128)(2,1)S(1)}, bf16[4,784,128]{2,1,0:T(8,128)(2,1)S(1)}, u32[]{:S(2)}, u32[]{:S(2)}) %collective-permute-start.4) | collective-permute-done | bytes 802848 | tf_op jit(solution)/shard_map/ppermute | solution.py:111
  92.1 4.8 %collective-permute-done.3.refs_2_.refs_3_.refs_4_ = bf16[4,784,128]{2,1,0:T(8,128)(2,1)S(1)} collective-permute-done((bf16[4,784,128]{2,1,0:T(8,128)(2,1)S(1)}, bf16[4,784,128]{2,1,0:T(8,128)(2,1)S(1)}, u32[]{:S(2)}, u32[]{:S(2)}) %collective-permute-start.3) | collective-permute-done | bytes 802848 | tf_op jit(solution)/shard_map/ppermute | solution.py:111
  98.7 4.6 %collective-permute-start.6 = (bf16[4,784,128]{2,1,0:T(8,128)(2,1)S(1)}, bf16[4,784,128]{2,1,0:T(8,128)(2,1)S(1)}, u32[]{:S(2)}, u32[]{:S(2)}) collective-permute-start(bf16[4,784,128]{2,1,0:T(8,128)(2,1)S(1)} %collective-permute-done.4.refs_5_.refs_6_.refs_7_), channel_id=1, source_target_pairs={{0,28},{4,0},{8,4},{12,8},{16,12},{20,16},{24,20},{28,24},{1,29},{... | collective-permute-start | bytes 2408456 | tf_op jit(solution)/shard_map/ppermute | solution.py:111
  103.3 6.6 %attend.7 = (f32[128,3072]{1,0:T(8,128)S(1)}, f32[128,3072]{1,0:T(8,128)S(1)}, f32[128,3072]{1,0:T(8,128)S(1)}) custom-call(bf16[128,4096]{1,0:T(8,128)(2,1)S(1)} %bitcast.23, f32[128,1]{1,0:T(8,128)S(1)} %copy.39.refs_1_, bf16[4,784,128]{2,1,0:T(8,128)(2,1)S(1)} %collective-permute-done.3.refs_2_.refs_3_.refs_4_, ...), custom_call_target="tpu_custom_call" | custom-call | flops 1610612736 | bytes 8388608 | tf_op jit(solution)/shard_map/attend/pallas_call | solution.py:94
  110.0 16.6 %collective-permute-done.5.refs_2_.refs_3_.refs_4_ = bf16[4,784,128]{2,1,0:T(8,128)(2,1)S(1)} collective-permute-done((bf16[4,784,128]{2,1,0:T(8,128)(2,1)S(1)}, bf16[4,784,128]{2,1,0:T(8,128)(2,1)S(1)}, u32[]{:S(2)}, u32[]{:S(2)}) %collective-permute-start.5) | collective-permute-done | bytes 802848 | tf_op jit(solution)/shard_map/ppermute | solution.py:111
  129.1 5.2 %collective-permute-start.8 = (bf16[4,784,128]{2,1,0:T(8,128)(2,1)S(1)}, bf16[4,784,128]{2,1,0:T(8,128)(2,1)S(1)}, u32[]{:S(2)}, u32[]{:S(2)}) collective-permute-start(bf16[4,784,128]{2,1,0:T(8,128)(2,1)S(1)} %collective-permute-done.6.refs_5_.refs_6_.refs_7_), channel_id=1, source_target_pairs={{0,28},{4,0},{8,4},{12,8},{16,12},{20,16},{24,20},{28,24},{1,29},{... | collective-permute-start | bytes 2408456 | tf_op jit(solution)/shard_map/ppermute | solution.py:111
  134.4 6.6 %attend.8 = (f32[128,3072]{1,0:T(8,128)S(1)}, f32[128,3072]{1,0:T(8,128)S(1)}, f32[128,3072]{1,0:T(8,128)S(1)}) custom-call(bf16[128,4096]{1,0:T(8,128)(2,1)S(1)} %bitcast.24, f32[128,1]{1,0:T(8,128)S(1)} %copy.39.refs_1_, bf16[4,784,128]{2,1,0:T(8,128)(2,1)S(1)} %collective-permute-done.5.refs_2_.refs_3_.refs_4_, ...), custom_call_target="tpu_custom_call" | custom-call | flops 1610612736 | bytes 8388608 | tf_op jit(solution)/shard_map/attend/pallas_call | solution.py:94
  141.0 7.6 %collective-permute-done.7.refs_2_.refs_3_.refs_4_ = bf16[4,784,128]{2,1,0:T(8,128)(2,1)S(1)} collective-permute-done((bf16[4,784,128]{2,1,0:T(8,128)(2,1)S(1)}, bf16[4,784,128]{2,1,0:T(8,128)(2,1)S(1)}, u32[]{:S(2)}, u32[]{:S(2)}) %collective-permute-start.7) | collective-permute-done | bytes 802848 | tf_op jit(solution)/shard_map/ppermute | solution.py:111
  153.0 5.5 %collective-permute-start.10 = (bf16[2,784,128]{2,1,0:T(8,128)(2,1)}, bf16[2,784,128]{2,1,0:T(8,128)(2,1)S(1)}, u32[]{:S(2)}, u32[]{:S(2)}) collective-permute-start(bf16[2,784,128]{2,1,0:T(8,128)(2,1)} %slice.14), channel_id=1, source_target_pairs={{0,28},{4,0},{8,4},{12,8},{16,12},{20,16},{24,20},{28,24},{1,29},{... | collective-permute-start | bytes 1204232 | tf_op jit(solution)/shard_map/ppermute | solution.py:111
  158.5 6.6 %attend.9 = (f32[128,3072]{1,0:T(8,128)S(1)}, f32[128,3072]{1,0:T(8,128)S(1)}, f32[128,3072]{1,0:T(8,128)S(1)}) custom-call(bf16[128,4096]{1,0:T(8,128)(2,1)S(1)} %bitcast.25, f32[128,1]{1,0:T(8,128)S(1)} %copy.39.refs_1_, bf16[4,784,128]{2,1,0:T(8,128)(2,1)S(1)} %collective-permute-done.7.refs_2_.refs_3_.refs_4_, ...), custom_call_target="tpu_custom_call" | custom-call | flops 1610612736 | bytes 8388608 | tf_op jit(solution)/shard_map/attend/pallas_call | solution.py:94
  170.3 6.2 %attend.10 = bf16[128,1024]{1,0:T(8,128)(2,1)S(1)} custom-call(bf16[128,4096]{1,0:T(8,128)(2,1)S(1)} %bitcast.26, f32[128,1]{1,0:T(8,128)S(1)} %copy.39.refs_1_, bf16[32,272,128]{2,1,0:T(8,128)(2,1)S(1)} %bitcast.28, bf16[32,272,128]{2,1,0:T(8,128)(2,1)S(1)} %bitcast.29, bf16[32,272,128]{2,1,0:T(8,128)(2,1)S(1)} %bitcast.30), custom_call_target="tpu_custom_call" | custom-call | flops 2147483648 | bytes 8388608 | tf_op jit(solution)/shard_map/attend/pallas_call | solution.py:94
  176.6 3.9 %attend.11 = bf16[128,3072]{1,0:T(8,128)(2,1)S(1)} custom-call(bf16[128,4096]{1,0:T(8,128)(2,1)S(1)} %bitcast.27, f32[128,1]{1,0:T(8,128)S(1)} %copy.39.refs_1_, bf16[2,784,128]{2,1,0:T(8,128)(2,1)S(1)} %collective-permute-done.9.refs_2_.refs_3_.refs_4_, bf16[2,784,128]{2,1,0:T(8,128)(2,1)S(1)} %collective-permute-done.9.refs_2_.refs_3_.refs_4_, ...), custom_call_target="tpu_custom_call" | custom-call | flops 805306368 | bytes 8388608 | tf_op jit(solution)/shard_map/attend/pallas_call | solution.py:94
  (51 shorter events, 21.0 us)
Async XLA Ops:
  6.5 12.2 %copy-start.8 = (s32[16]{0:T(128)S(1)}, s32[16]{0:T(128)}, u32[]{:S(2)}) copy-start(s32[16]{0:T(128)} %param.7) | copy-start | bytes 196
  6.5 25.2 %copy-start.9 = (s32[128]{0:T(128)S(1)}, s32[128]{0:T(128)}, u32[]{:S(2)}) copy-start(s32[128]{0:T(128)} %param.6) | copy-start | bytes 1540
  8.6 17.4 %all-to-all-start = ((bf16[16,64,128]{2,1,0:T(8,128)(2,1)}), bf16[16,64,128]{2,1,0:T(8,128)(2,1)S(1)}, u32[]{:S(2)}, u32[]{:S(2)}) async-start(bf16[16,64,128]{2,1,0:T(8,128)(2,1)} %bitcast.5), calls=%async_computation | async-start | bytes 524288 | tf_op jit(solution)/shard_map/all_to_all | solution.py:129
  26.8 11.6 %all-to-all-start.1 = ((bf16[16,64,128]{2,1,0:T(8,128)(2,1)}), bf16[16,64,128]{2,1,0:T(8,128)(2,1)S(1)}, u32[]{:S(2)}, u32[]{:S(2)}) async-start(bf16[16,64,128]{2,1,0:T(8,128)(2,1)} %broadcast_in_dim.31), calls=%async_computation.1 | async-start | bytes 524288 | tf_op jit(solution)/shard_map/all_to_all | solution.py:130
  31.1 137.6 %all-gather.3.cloned.1.call-start = ((), (), s32[]{:S(2)}) async-start(), calls=%async_computation.2 | async-start | bytes 2297856 | tf_op jit(solution)/shard_map/all_gather | solution.py:137
  39.3 37.1 %copy-start = (bf16[1,128,4096]{2,1,0:T(8,128)(2,1)S(1)}, bf16[1,128,4096]{2,1,0:T(8,128)(2,1)}, u32[]{:S(2)}) copy-start(bf16[1,128,4096]{2,1,0:T(8,128)(2,1)} %param.4) | copy-start | bytes 3145732
  39.6 16.4 %collective-permute-start.1 = (bf16[784,128]{1,0:T(8,128)(2,1)S(1)}, bf16[784,128]{1,0:T(8,128)(2,1)S(1)}, u32[]{:S(2)}, u32[]{:S(2)}) collective-permute-start(bf16[784,128]{1,0:T(8,128)(2,1)S(1)} %get-tuple-element.74), channel_id=1, source_target_pairs={{0,2},{1,3},{2,0},{3,1},{4,6},{5,7},{6,4},{7,5},{8,10},{9,11},{10,... | collective-permute-start | bytes 602120 | tf_op jit(solution)/shard_map/ppermute | solution.py:111
  42.8 14.3 %collective-permute-start = (bf16[784,128]{1,0:T(8,128)(2,1)S(1)}, bf16[784,128]{1,0:T(8,128)(2,1)S(1)}, u32[]{:S(2)}, u32[]{:S(2)}) collective-permute-start(bf16[784,128]{1,0:T(8,128)(2,1)S(1)} %get-tuple-element.74), channel_id=1, source_target_pairs={{0,1},{1,2},{2,3},{3,0},{4,5},{5,6},{6,7},{7,4},{8,9},{9,10},{10,1... | collective-permute-start | bytes 602120 | tf_op jit(solution)/shard_map/ppermute | solution.py:111
  45.2 20.6 %collective-permute-start.2 = (bf16[784,128]{1,0:T(8,128)(2,1)S(1)}, bf16[784,128]{1,0:T(8,128)(2,1)S(1)}, u32[]{:S(2)}, u32[]{:S(2)}) collective-permute-start(bf16[784,128]{1,0:T(8,128)(2,1)S(1)} %get-tuple-element.74), channel_id=1, source_target_pairs={{0,3},{1,0},{2,1},{3,2},{4,7},{5,4},{6,5},{7,6},{8,11},{9,8},{10,9... | collective-permute-start | bytes 602120 | tf_op jit(solution)/shard_map/ppermute | solution.py:111
  66.0 26.1 %collective-permute-start.4 = (bf16[4,784,128]{2,1,0:T(8,128)(2,1)S(1)}, bf16[4,784,128]{2,1,0:T(8,128)(2,1)S(1)}, u32[]{:S(2)}, u32[]{:S(2)}) collective-permute-start(bf16[4,784,128]{2,1,0:T(8,128)(2,1)S(1)} %pad_maximum_fusion.refs_2_.refs_3_.refs_4_), channel_id=1, source_target_pairs={{0,28},{4,0},{8,4},{12,8},{16,12},{20,16},{24,20},{28,24},{1,29},{... | collective-permute-start | bytes 2408456 | tf_op jit(solution)/shard_map/ppermute | solution.py:111
  74.3 22.5 %collective-permute-start.3 = (bf16[4,784,128]{2,1,0:T(8,128)(2,1)S(1)}, bf16[4,784,128]{2,1,0:T(8,128)(2,1)S(1)}, u32[]{:S(2)}, u32[]{:S(2)}) collective-permute-start(bf16[4,784,128]{2,1,0:T(8,128)(2,1)S(1)} %pad_maximum_fusion.refs_2_.refs_3_.refs_4_), channel_id=1, source_target_pairs={{0,4},{4,8},{8,12},{12,16},{16,20},{20,24},{24,28},{28,0},{1,5},{5... | collective-permute-start | bytes 2408456 | tf_op jit(solution)/shard_map/ppermute | solution.py:111
  96.8 29.8 %collective-permute-start.5 = (bf16[4,784,128]{2,1,0:T(8,128)(2,1)S(1)}, bf16[4,784,128]{2,1,0:T(8,128)(2,1)S(1)}, u32[]{:S(2)}, u32[]{:S(2)}) collective-permute-start(bf16[4,784,128]{2,1,0:T(8,128)(2,1)S(1)} %collective-permute-done.3.refs_2_.refs_3_.refs_4_), channel_id=1, source_target_pairs={{0,4},{4,8},{8,12},{12,16},{16,20},{20,24},{24,28},{28,0},{1,5},{5... | collective-permute-start | bytes 2408456 | tf_op jit(solution)/shard_map/ppermute | solution.py:111
  98.7 28.5 %collective-permute-start.6 = (bf16[4,784,128]{2,1,0:T(8,128)(2,1)S(1)}, bf16[4,784,128]{2,1,0:T(8,128)(2,1)S(1)}, u32[]{:S(2)}, u32[]{:S(2)}) collective-permute-start(bf16[4,784,128]{2,1,0:T(8,128)(2,1)S(1)} %collective-permute-done.4.refs_5_.refs_6_.refs_7_), channel_id=1, source_target_pairs={{0,28},{4,0},{8,4},{12,8},{16,12},{20,16},{24,20},{28,24},{1,29},{... | collective-permute-start | bytes 2408456 | tf_op jit(solution)/shard_map/ppermute | solution.py:111
  127.2 21.4 %collective-permute-start.7 = (bf16[4,784,128]{2,1,0:T(8,128)(2,1)S(1)}, bf16[4,784,128]{2,1,0:T(8,128)(2,1)S(1)}, u32[]{:S(2)}, u32[]{:S(2)}) collective-permute-start(bf16[4,784,128]{2,1,0:T(8,128)(2,1)S(1)} %collective-permute-done.5.refs_2_.refs_3_.refs_4_), channel_id=1, source_target_pairs={{0,4},{4,8},{8,12},{12,16},{16,20},{20,24},{24,28},{28,0},{1,5},{5... | collective-permute-start | bytes 2408456 | tf_op jit(solution)/shard_map/ppermute | solution.py:111
  129.1 20.4 %collective-permute-start.8 = (bf16[4,784,128]{2,1,0:T(8,128)(2,1)S(1)}, bf16[4,784,128]{2,1,0:T(8,128)(2,1)S(1)}, u32[]{:S(2)}, u32[]{:S(2)}) collective-permute-start(bf16[4,784,128]{2,1,0:T(8,128)(2,1)S(1)} %collective-permute-done.6.refs_5_.refs_6_.refs_7_), channel_id=1, source_target_pairs={{0,28},{4,0},{8,4},{12,8},{16,12},{20,16},{24,20},{28,24},{1,29},{... | collective-permute-start | bytes 2408456 | tf_op jit(solution)/shard_map/ppermute | solution.py:111
  151.1 25.5 %collective-permute-start.9 = (bf16[2,784,128]{2,1,0:T(8,128)(2,1)}, bf16[2,784,128]{2,1,0:T(8,128)(2,1)S(1)}, u32[]{:S(2)}, u32[]{:S(2)}) collective-permute-start(bf16[2,784,128]{2,1,0:T(8,128)(2,1)} %slice.13), channel_id=1, source_target_pairs={{0,4},{4,8},{8,12},{12,16},{16,20},{20,24},{24,28},{28,0},{1,5},{5... | collective-permute-start | bytes 1204232 | tf_op jit(solution)/shard_map/ppermute | solution.py:111
  153.0 23.6 %collective-permute-start.10 = (bf16[2,784,128]{2,1,0:T(8,128)(2,1)}, bf16[2,784,128]{2,1,0:T(8,128)(2,1)S(1)}, u32[]{:S(2)}, u32[]{:S(2)}) collective-permute-start(bf16[2,784,128]{2,1,0:T(8,128)(2,1)} %slice.14), channel_id=1, source_target_pairs={{0,28},{4,0},{8,4},{12,8},{16,12},{20,16},{24,20},{28,24},{1,29},{... | collective-permute-start | bytes 1204232 | tf_op jit(solution)/shard_map/ppermute | solution.py:111
  165.1 1.1 copy-start.2
  166.3 1.2 copy-start.4
  167.5 1.2 copy-start.6
  168.6 1.6 copy-start.1
  170.3 6.3 %copy-start.3 = (f32[128,3072]{1,0:T(8,128)S(1)}, f32[128,3072]{1,0:T(8,128)}, u32[]{:S(2)}) copy-start(f32[128,3072]{1,0:T(8,128)} %copy-done.2) | copy-start | bytes 4718596
  170.3 6.3 %copy-start.5 = (f32[128,3072]{1,0:T(8,128)S(1)}, f32[128,3072]{1,0:T(8,128)}, u32[]{:S(2)}) copy-start(f32[128,3072]{1,0:T(8,128)} %copy-done.4) | copy-start | bytes 4718596
  170.3 6.3 %copy-start.7 = (f32[128,3072]{1,0:T(8,128)S(1)}, f32[128,3072]{1,0:T(8,128)}, u32[]{:S(2)}) copy-start(f32[128,3072]{1,0:T(8,128)} %copy-done.6) | copy-start | bytes 4718596
Sparse Core Ops, SparseCore 0:
  39.5 87.5 all-gather.2

commit v3 on v2

v3 whole, which is shorter than its diff:
```python
import functools

import jax
import jax.numpy as jnp
from jax import lax
from jax.experimental import pallas as pl
from jax.experimental.pallas import tpu as pltpu
from jax.sharding import Mesh, PartitionSpec as P

H = 32
KVH = 4
HD = 128
BLOCK = 64
WARM = 2
LAYERS = 16
ROWS = 128
HEADS = H // LAYERS
WIDE = HEADS * HD
POS_ROWS = 16
MASKED = -1e30
SCALE = 1.4426950408889634 / HD**0.5
SECTION = ("x", "yl", "core")


def attend_body(shards, first, last, *refs):
    it = iter(refs)
    next(it)
    q_ref, pos_ref = next(it), next(it)
    blocks = [(next(it), next(it), next(it)) for _ in shards]
    if not first:
        m_in, l_in, a_in = next(it), next(it), next(it)
    outs = [next(it)] if last else [next(it), next(it), next(it)]
    k, v, cap = it
    step = pl.program_id(0)
    count = k.shape[0]

    @pl.when(step == 0)
    def _():
        lane = (lax.broadcasted_iota(jnp.int32, (1, ROWS), 1) % BLOCK).astype(jnp.float32)
        v[:, HD:] = jnp.ones((count, HD), jnp.bfloat16)
        at = 0
        for n, (_, _, p_ref) in zip(shards, blocks):
            for i in range(n):
                key_pos = p_ref[i][0:1, :].astype(jnp.float32) * BLOCK + lane
                cap[:, at : at + ROWS] = jnp.where(key_pos <= pos_ref[...], jnp.inf, MASKED)
                at += ROWS

    @pl.when((step == 0) | (step == WARM))
    def _():
        at = 0
        for n, (k_ref, v_ref, _) in zip(shards, blocks):
            for i in range(n):
                k[at : at + ROWS, :] = k_ref[i]
                v[at : at + ROWS, :HD] = v_ref[i]
                at += ROWS

    for g in range(HEADS):
        cols = slice(g * HD, (g + 1) * HD)
        s = lax.dot_general(
            q_ref[:, cols], k[...], (((1,), (1,)), ((), ())), preferred_element_type=jnp.float32
        )
        s = jnp.minimum(s, cap[...])
        top = jnp.max(s, axis=1, keepdims=True)
        if first:
            m = jnp.broadcast_to(top, (ROWS, HD))
        else:
            m_old = m_in[:, cols]
            m = jnp.maximum(m_old, top)
        wide = jnp.concatenate([m] * (count // HD), axis=1)
        w = jnp.exp2((s - wide) * SCALE).astype(jnp.bfloat16)
        o = lax.dot_general(
            w, v[...], (((1,), (0,)), ((), ())), preferred_element_type=jnp.float32
        )
        acc, den = o[:, :HD], o[:, HD:]
        if not first:
            f = jnp.exp2((m_old - m) * SCALE)
            acc = acc + f * a_in[:, cols]
            den = den + f * l_in[:, cols]
        if last:
            outs[0][:, cols] = (acc / den).astype(jnp.bfloat16)
        else:
            outs[0][:, cols] = m
            outs[1][:, cols] = den
            outs[2][:, cols] = acc


def attend(order, q, pos, blocks, state, last):
    shards = tuple(b.shape[0] for b in blocks)
    count = sum(shards) * ROWS
    picked = pl.BlockSpec((None, ROWS, WIDE), lambda i, order: (order[i], 0, 0))
    kept = pl.BlockSpec((None, ROWS, WIDE), lambda i, order: (i, 0, 0))
    in_specs = [picked, pl.BlockSpec((ROWS, 1), lambda i, order: (0, 0))]
    args = [q, pos]
    for b in blocks:
        n = b.shape[0]
        in_specs += [
            pl.BlockSpec((n, ROWS, HD), lambda i, order: (0, jnp.where(i < WARM, 2, 0), 0)),
            pl.BlockSpec((n, ROWS, HD), lambda i, order: (0, jnp.where(i < WARM, 3, 1), 0)),
            pl.BlockSpec((n, POS_ROWS, HD), lambda i, order: (0, 4 * ROWS // POS_ROWS, 0)),
        ]
        args += [b, b, b]
    if state is not None:
        in_specs += [kept] * 3
        args += list(state)
    held = jax.ShapeDtypeStruct((LAYERS, ROWS, WIDE), jnp.float32)
    done = jax.ShapeDtypeStruct((LAYERS + 1, ROWS, WIDE), jnp.bfloat16)
    return pl.pallas_call(
        functools.partial(attend_body, shards, state is None, last),
        grid_spec=pltpu.PrefetchScalarGridSpec(
            num_scalar_prefetch=1,
            grid=(LAYERS,),
            in_specs=in_specs,
            out_specs=picked if last else [kept] * 3,
            scratch_shapes=[
                pltpu.VMEM((count, HD), jnp.bfloat16),
                pltpu.VMEM((count, 2 * HD), jnp.bfloat16),
                pltpu.VMEM((ROWS, count), jnp.float32),
            ],
        ),
        out_shape=done if last else [held] * 3,
        compiler_params=pltpu.CompilerParams(vmem_limit_bytes=40 << 20),
        cost_estimate=pl.CostEstimate(
            flops=4 * ROWS * H * count * HD,
            bytes_accessed=8 << 20,
            transcendentals=ROWS * H * count,
        ),
        name="attend",
    )(order, *args)


def turn(value, axis, size, shift):
    return lax.ppermute(value, axis, [(i, (i + shift) % size) for i in range(size)])


def pick(slabs, index):
    return lax.dynamic_index_in_dim(slabs, index, 0, keepdims=False)


def per_device(sizes, queries, key_values, token_pos, layer_of_section):
    nz, nyh = sizes["z"], sizes["yh"]
    core = lax.axis_index("core")
    ids = jnp.arange(LAYERS, dtype=jnp.int32)
    holder = jnp.sum(jnp.where(layer_of_section[None, :] == ids[:, None], ids[None, :], 0), axis=1)
    warm, other_warm = pick(holder, core), pick(holder, 1 - core)
    heads = key_values[0].reshape(ROWS, 2, KVH, HD).transpose(2, 1, 0, 3)
    pieces = jnp.broadcast_to(
        heads.reshape(KVH, 1, 2 * ROWS, HD), (KVH, LAYERS // KVH, 2 * ROWS, HD)
    ).reshape(LAYERS, 2 * ROWS, HD)
    pieces = lax.all_to_all(pieces, SECTION, 0, 0)
    block_ids = jnp.broadcast_to((token_pos // BLOCK).astype(jnp.bfloat16)[None, :], (POS_ROWS, ROWS))
    shard = jnp.concatenate([pick(pieces, holder[LAYERS - 1]), pick(pieces, warm), block_ids], axis=0)
    q = queries[0].reshape(ROWS, LAYERS, WIDE).transpose(1, 0, 2)
    q, shard = lax.optimization_barrier((q, shard))
    q = lax.all_to_all(q, SECTION, 0, 0)
    q = jnp.concatenate([q, turn(pick(q, other_warm), "core", 2, 1)[None]], axis=0)
    order = jnp.concatenate([jnp.stack([warm, LAYERS]), holder[WARM:]]).astype(jnp.int32)
    pos = token_pos.astype(jnp.float32)[:, None]
    line = jnp.stack([shard] + [turn(shard, "yh", nyh, shift) for shift in range(1, nyh)])

    def part(blocks, state, last=False):
        return attend(order, q, pos, blocks, state, last)

    held, state = [line], None
    up = down = line
    for _ in range(nz // 2 - 1):
        up, down = turn(up, "z", nz, 1), turn(down, "z", nz, -1)
        state = part(held, state)
        up, down, state = lax.optimization_barrier((up, down, state))
        held = [up, down]
    half = nyh // 2
    last_up, last_down = turn(up[:half], "z", nz, 1), turn(down[half:], "z", nz, -1)
    state = part(held, state)
    last_up, last_down, state = lax.optimization_barrier((last_up, last_down, state))
    out = part([last_up, last_down], state, True)
    back = turn(out[LAYERS], "core", 2, 1)
    out = jnp.where(ids[:, None, None] == other_warm, back[None], out[:LAYERS])
    out = lax.all_to_all(out, SECTION, 0, 0)
    return out.transpose(1, 0, 2).reshape(1, ROWS, H * HD)


def solution(mesh):
    sizes = {"x": 4, "yl": 2, "core": 2, "z": 8, "yh": 4}
    fine = Mesh(mesh.devices.reshape(tuple(sizes.values())), tuple(sizes))
    ctx = ("z", "yh")
    in_specs = (P(SECTION, ctx, None), P(SECTION, ctx, None, None), P(ctx), P())
    return jax.shard_map(
        functools.partial(per_device, sizes),
        mesh=fine,
        in_specs=in_specs,
        out_specs=P(SECTION, ctx, None),
        check_vma=False,
    )
```

time: 191 us -> 198 us (1.037)
  waiting for transfers between devices: 69.6 us -> 24.2 us
  Pallas kernels: 33.5 us -> 67.9 us
  blocking collectives: 0 us -> 22.5 us
  between operations: 16.1 us -> 5.98 us
  starting transfers between devices: 56.5 us -> 62.6 us
    ppermute x11 -> x13, waiting for transfers between devices: 58.4 us -> 14.9 us  [turn(): lax.ppermute(value, axis, [(i, (i + shift) % size) for i in range(size)])]
    pallas_call x6 -> x5, Pallas kernels: 33.5 us -> 67.9 us  [attend(): pl.pallas_call(functools.partial(attend_body, shards, state is None, last...]
    all_to_all x0 -> x1, blocking collectives: none -> 22.5 us  [per_device(): out = lax.all_to_all(out, SECTION, 0, 0)]
    ppermute x11 -> x13, starting transfers between devices: 41.9 us -> 48 us  [turn(): lax.ppermute(value, axis, [(i, (i + shift) % size) for i in range(size)])]
    unnamed x21 -> x14, local copies, waits for them, and re-layouts: 6.32 us -> 5.8 us
  transfers between devices with their start and end apart: 14 -> 15, of which waited for: 11 -> 5; matrix products, arithmetic and copies ran while one was open for 1% -> 2% of each run, Pallas kernels for 16% -> 29%
where the time goes in v3:
time: 198 us; the launch traced here: 196 us
  Pallas kernels  67.9 us (34%)
  starting transfers between devices  62.6 us (32%)
  waiting for transfers between devices  24.2 us (12%)
  blocking collectives  22.5 us (11%)
  local copies, waits for them, and re-layouts  11.4 us (6%)
  between operations  5.98 us (3%)
    pallas_call x5, Pallas kernels, attend(): pl.pallas_call(functools.partial(attend_body, shards, state is None, last...  67.9 us
    ppermute x13, starting transfers between devices, turn(): lax.ppermute(value, axis, [(i, (i + shift) % size) for i in range(size)])  48 us
    all_to_all x1, blocking collectives, per_device(): out = lax.all_to_all(out, SECTION, 0, 0)  22.5 us
    ppermute x13, waiting for transfers between devices, turn(): lax.ppermute(value, axis, [(i, (i + shift) % size) for i in range(size)])  14.9 us
    all_to_all x1, starting transfers between devices, per_device(): pieces = lax.all_to_all(pieces, SECTION, 0, 0)  10.3 us
    all_to_all x1, waiting for transfers between devices, per_device(): pieces = lax.all_to_all(pieces, SECTION, 0, 0)  9.32 us
    unnamed x14, local copies, waits for them, and re-layouts  5.8 us
    all_to_all x1, starting transfers between devices, per_device(): q = lax.all_to_all(q, SECTION, 0, 0)  4.33 us
  transfers between devices with their start and end apart: 15, of which 5 were waited for; matrix products, arithmetic and copies ran while one was open for 2% of the time, Pallas kernels for 29%

profile of v3, /device:TPU:1, one launch (start us, length us, event | category | flops | bytes accessed | tf_op | source)
XLA Modules:
  0.0 196.3 jit_solution(2914413504043551683)
XLA Ops:
  2.6 10.3 %all-to-all-start = ((bf16[16,256,128]{2,1,0:T(8,128)(2,1)}), bf16[16,256,128]{2,1,0:T(8,128)(2,1)S(1)}, u32[]{:S(2)}, u32[]{:S(2)}) async-start(bf16[16,256,128]{2,1,0:T(8,128)(2,1)} %bitcast.6), calls=%async_computation | async-start | bytes 2097152 | tf_op jit(solution)/shard_map/all_to_all | solution.py:149
  19.5 9.3 %all-to-all-done = bf16[16,256,128]{2,1,0:T(8,128)(2,1)S(1)} async-done(((bf16[16,256,128]{2,1,0:T(8,128)(2,1)}), bf16[16,256,128]{2,1,0:T(8,128)(2,1)S(1)}, u32[]{:S(2)}, u32[]{:S(2)}) %all-to-all-start) | async-done | bytes 1048608 | tf_op jit(solution)/shard_map/all_to_all | solution.py:149
  28.9 4.3 %all-to-all-start.1 = ((bf16[16,128,256]{2,1,0:T(8,128)(2,1)}), bf16[16,128,256]{2,1,0:T(8,128)(2,1)S(1)}, u32[]{:S(2)}, u32[]{:S(2)}) async-start(bf16[16,128,256]{2,1,0:T(8,128)(2,1)} %bitcast.2), calls=%async_computation.1 | async-start | bytes 2097152 | tf_op jit(solution)/shard_map/all_to_all | solution.py:154
  33.2 1.9 collective-permute-start.3
  35.1 3.9 %collective-permute-start.2 = (bf16[528,128]{1,0:T(8,128)(2,1)S(1)}, bf16[528,128]{1,0:T(8,128)(2,1)S(1)}, u32[]{:S(2)}, u32[]{:S(2)}) collective-permute-start(bf16[528,128]{1,0:T(8,128)(2,1)S(1)} %pad_maximum_fusion.2), channel_id=1, source_target_pairs={{0,2},{1,3},{2,0},{3,1},{4,6},{5,7},{6,4},{7,5},{8,10},{9,11},{10,... | collective-permute-start | bytes 405512 | tf_op jit(solution)/shard_map/ppermute | solution.py:132
  39.0 3.3 %collective-permute-start.1 = (bf16[528,128]{1,0:T(8,128)(2,1)S(1)}, bf16[528,128]{1,0:T(8,128)(2,1)S(1)}, u32[]{:S(2)}, u32[]{:S(2)}) collective-permute-start(bf16[528,128]{1,0:T(8,128)(2,1)S(1)} %pad_maximum_fusion.2), channel_id=1, source_target_pairs={{0,1},{1,2},{2,3},{3,0},{4,5},{5,6},{6,7},{7,4},{8,9},{9,10},{10,1... | collective-permute-start | bytes 405512 | tf_op jit(solution)/shard_map/ppermute | solution.py:132
  42.4 13.0 %collective-permute-done.2 = bf16[528,128]{1,0:T(8,128)(2,1)S(1)} collective-permute-done((bf16[528,128]{1,0:T(8,128)(2,1)S(1)}, bf16[528,128]{1,0:T(8,128)(2,1)S(1)}, u32[]{:S(2)}, u32[]{:S(2)}) %collective-permute-start.2) | collective-permute-done | bytes 135200 | tf_op jit(solution)/shard_map/ppermute | solution.py:132
  55.4 1.4 collective-permute-done.1
  56.9 10.6 %collective-permute-start.5 = (bf16[4,528,128]{2,1,0:T(8,128)(2,1)S(1)}, bf16[4,528,128]{2,1,0:T(8,128)(2,1)S(1)}, u32[]{:S(2)}, u32[]{:S(2)}) collective-permute-start(bf16[4,528,128]{2,1,0:T(8,128)(2,1)S(1)} %pad_maximum_fusion.1.refs_3_.refs_4_.refs_5_), channel_id=1, source_target_pairs={{0,28},{4,0},{8,4},{12,8},{16,12},{20,16},{24,20},{28,24},{1,29},{... | collective-permute-start | bytes 1622024 | tf_op jit(solution)/shard_map/ppermute | solution.py:132
  67.5 1.9 collective-permute-start.4
  71.5 2.9 %collective-permute-start = (bf16[128,256]{1,0:T(8,128)(2,1)S(1)}, bf16[128,256]{1,0:T(8,128)(2,1)S(1)}, u32[]{:S(2)}, u32[]{:S(2)}) collective-permute-start(bf16[128,256]{1,0:T(8,128)(2,1)S(1)} %dynamic-slice_bitcast_fusion), channel_id=1, source_target_pairs={{0,32},{32,0},{1,33},{33,1},{2,34},{34,2},{3,35},{35,3},{4,36},{36... | collective-permute-start | bytes 196616 | tf_op jit(solution)/shard_map/ppermute | solution.py:132
  75.4 9.9 %attend.5 = (f32[16,128,256]{2,1,0:T(8,128)S(1)}, f32[16,128,256]{2,1,0:T(8,128)S(1)}, f32[16,128,256]{2,1,0:T(8,128)S(1)}) custom-call(s32[16]{0:T(128)S(1)} %pad_add_fusion.refs_0_, bf16[17,128,256]{2,1,0:T(8,128)(2,1)S(1)} %pad_maximum_fusion.refs_1_, f32[128,1]{1,0:T(8,128)S(1)} %copy.38.refs_2_, ...), custom_call_target="tpu_custom_call" | custom-call | flops 1073741824 | bytes 8388608 | tf_op jit(solution)/shard_map/attend/pallas_call | solution.py:107
  86.6 1.9 collective-permute-start.6
  88.5 4.9 %collective-permute-start.7 = (bf16[4,528,128]{2,1,0:T(8,128)(2,1)S(1)}, bf16[4,528,128]{2,1,0:T(8,128)(2,1)S(1)}, u32[]{:S(2)}, u32[]{:S(2)}) collective-permute-start(bf16[4,528,128]{2,1,0:T(8,128)(2,1)S(1)} %collective-permute-done.5.refs_6_.refs_7_.refs_8_), channel_id=1, source_target_pairs={{0,28},{4,0},{8,4},{12,8},{16,12},{20,16},{24,20},{28,24},{1,29},{... | collective-permute-start | bytes 1622024 | tf_op jit(solution)/shard_map/ppermute | solution.py:132
  93.4 15.8 %attend.6 = (f32[16,128,256]{2,1,0:T(8,128)S(1)}, f32[16,128,256]{2,1,0:T(8,128)S(1)}, f32[16,128,256]{2,1,0:T(8,128)S(1)}) custom-call(s32[16]{0:T(128)S(1)} %pad_add_fusion.refs_0_, bf16[17,128,256]{2,1,0:T(8,128)(2,1)S(1)} %pad_maximum_fusion.refs_1_, f32[128,1]{1,0:T(8,128)S(1)} %copy.38.refs_2_, ...), custom_call_target="tpu_custom_call" | custom-call | flops 2147483648 | bytes 8388608 | tf_op jit(solution)/shard_map/attend/pallas_call | solution.py:107
  110.5 1.9 collective-permute-start.8
  112.4 4.6 %collective-permute-start.9 = (bf16[4,528,128]{2,1,0:T(8,128)(2,1)S(1)}, bf16[4,528,128]{2,1,0:T(8,128)(2,1)S(1)}, u32[]{:S(2)}, u32[]{:S(2)}) collective-permute-start(bf16[4,528,128]{2,1,0:T(8,128)(2,1)S(1)} %collective-permute-done.7.refs_6_.refs_7_.refs_8_), channel_id=1, source_target_pairs={{0,28},{4,0},{8,4},{12,8},{16,12},{20,16},{24,20},{28,24},{1,29},{... | collective-permute-start | bytes 1622024 | tf_op jit(solution)/shard_map/ppermute | solution.py:132
  117.0 15.8 %attend.7 = (f32[16,128,256]{2,1,0:T(8,128)S(1)}, f32[16,128,256]{2,1,0:T(8,128)S(1)}, f32[16,128,256]{2,1,0:T(8,128)S(1)}) custom-call(s32[16]{0:T(128)S(1)} %pad_add_fusion.refs_0_, bf16[17,128,256]{2,1,0:T(8,128)(2,1)S(1)} %pad_maximum_fusion.refs_1_, f32[128,1]{1,0:T(8,128)S(1)} %copy.38.refs_2_, ...), custom_call_target="tpu_custom_call" | custom-call | flops 2147483648 | bytes 8388608 | tf_op jit(solution)/shard_map/attend/pallas_call | solution.py:107
  134.2 1.9 collective-permute-start.10
  136.1 4.6 %collective-permute-start.11 = (bf16[2,528,128]{2,1,0:T(8,128)(2,1)S(1)}, bf16[2,528,128]{2,1,0:T(8,128)(2,1)S(1)}, u32[]{:S(2)}, u32[]{:S(2)}) collective-permute-start(bf16[2,528,128]{2,1,0:T(8,128)(2,1)S(1)} %slice.21), channel_id=1, source_target_pairs={{0,28},{4,0},{8,4},{12,8},{16,12},{20,16},{24,20},{28,24},{1,29},{... | collective-permute-start | bytes 811016 | tf_op jit(solution)/shard_map/ppermute | solution.py:132
  140.7 15.8 %attend.8 = (f32[16,128,256]{2,1,0:T(8,128)S(1)}, f32[16,128,256]{2,1,0:T(8,128)S(1)}, f32[16,128,256]{2,1,0:T(8,128)S(1)}) custom-call(s32[16]{0:T(128)S(1)} %pad_add_fusion.refs_0_, bf16[17,128,256]{2,1,0:T(8,128)(2,1)S(1)} %pad_maximum_fusion.refs_1_, f32[128,1]{1,0:T(8,128)S(1)} %copy.38.refs_2_, ...), custom_call_target="tpu_custom_call" | custom-call | flops 2147483648 | bytes 8388608 | tf_op jit(solution)/shard_map/attend/pallas_call | solution.py:107
  156.5 10.6 %attend.9 = bf16[17,128,256]{2,1,0:T(8,128)(2,1)S(1)} custom-call(s32[16]{0:T(128)S(1)} %pad_add_fusion.refs_0_, bf16[17,128,256]{2,1,0:T(8,128)(2,1)S(1)} %pad_maximum_fusion.refs_1_, f32[128,1]{1,0:T(8,128)S(1)} %copy.38.refs_2_, bf16[2,528,128]{2,1,0:T(8,128)(2,1)S(1)} %collective-permute-done.10.refs_3_.refs_4_.refs_5_, ...), custom_call_target="tpu_custom_call" | custom-call | flops 1073741824 | bytes 8388608 | tf_op jit(solution)/shard_map/attend/pallas_call | solution.py:107
  167.2 3.7 %collective-permute-start.12 = (bf16[128,256]{1,0:T(8,128)(2,1)S(1)}, bf16[128,256]{1,0:T(8,128)(2,1)S(1)}, u32[]{:S(2)}, u32[]{:S(2)}) collective-permute-start(bf16[128,256]{1,0:T(8,128)(2,1)S(1)} %slice_bitcast_fusion), channel_id=1, source_target_pairs={{0,32},{32,0},{1,33},{33,1},{2,34},{34,2},{3,35},{35,3},{4,36},{36... | collective-permute-start | bytes 196616 | tf_op jit(solution)/shard_map/ppermute | solution.py:132
  171.9 22.5 %all_to_all.15 = bf16[16,128,256]{2,1,0:T(8,128)(2,1)S(1)} all-to-all(bf16[16,128,256]{2,1,0:T(8,128)(2,1)S(1)} %slice_select_fusion), channel_id=1, replica_groups=mesh['x'=4,'yl'=2,'core'=2,'z'=8,'yh'=4] {'x','yl','core'}, dimensions={0} | all-to-all | bytes 2097152 | tf_op jit(solution)/shard_map/all_to_all | solution.py:177
  (48 shorter events, 13.6 us)
Async XLA Ops:
  1.2 11.8 %copy-start.4 = (s32[16]{0:T(128)S(1)}, s32[16]{0:T(128)}, u32[]{:S(2)}) copy-start(s32[16]{0:T(128)} %param.7) | copy-start | bytes 196
  1.2 15.0 %copy-start.3 = (bf16[1,128,4096]{2,1,0:T(8,128)(2,1)S(1)}, bf16[1,128,4096]{2,1,0:T(8,128)(2,1)}, u32[]{:S(2)}) copy-start(bf16[1,128,4096]{2,1,0:T(8,128)(2,1)} %param.4) | copy-start | bytes 3145732
  2.6 26.2 %all-to-all-start = ((bf16[16,256,128]{2,1,0:T(8,128)(2,1)}), bf16[16,256,128]{2,1,0:T(8,128)(2,1)S(1)}, u32[]{:S(2)}, u32[]{:S(2)}) async-start(bf16[16,256,128]{2,1,0:T(8,128)(2,1)} %bitcast.6), calls=%async_computation | async-start | bytes 2097152 | tf_op jit(solution)/shard_map/all_to_all | solution.py:149
  16.2 3.3 %copy-start.5 = (s32[128]{0:T(128)S(1)}, s32[128]{0:T(128)}, u32[]{:S(2)}) copy-start(s32[128]{0:T(128)} %param.6) | copy-start | bytes 1540
  28.9 42.6 %all-to-all-start.1 = ((bf16[16,128,256]{2,1,0:T(8,128)(2,1)}), bf16[16,128,256]{2,1,0:T(8,128)(2,1)S(1)}, u32[]{:S(2)}, u32[]{:S(2)}) async-start(bf16[16,128,256]{2,1,0:T(8,128)(2,1)} %bitcast.2), calls=%async_computation.1 | async-start | bytes 2097152 | tf_op jit(solution)/shard_map/all_to_all | solution.py:154
  33.2 9.2 %collective-permute-start.3 = (bf16[528,128]{1,0:T(8,128)(2,1)S(1)}, bf16[528,128]{1,0:T(8,128)(2,1)S(1)}, u32[]{:S(2)}, u32[]{:S(2)}) collective-permute-start(bf16[528,128]{1,0:T(8,128)(2,1)S(1)} %pad_maximum_fusion.2), channel_id=1, source_target_pairs={{0,3},{1,0},{2,1},{3,2},{4,7},{5,4},{6,5},{7,6},{8,11},{9,8},{10,9... | collective-permute-start | bytes 405512 | tf_op jit(solution)/shard_map/ppermute | solution.py:132
  35.1 20.3 %collective-permute-start.2 = (bf16[528,128]{1,0:T(8,128)(2,1)S(1)}, bf16[528,128]{1,0:T(8,128)(2,1)S(1)}, u32[]{:S(2)}, u32[]{:S(2)}) collective-permute-start(bf16[528,128]{1,0:T(8,128)(2,1)S(1)} %pad_maximum_fusion.2), channel_id=1, source_target_pairs={{0,2},{1,3},{2,0},{3,1},{4,6},{5,7},{6,4},{7,5},{8,10},{9,11},{10,... | collective-permute-start | bytes 405512 | tf_op jit(solution)/shard_map/ppermute | solution.py:132
  39.0 17.8 %collective-permute-start.1 = (bf16[528,128]{1,0:T(8,128)(2,1)S(1)}, bf16[528,128]{1,0:T(8,128)(2,1)S(1)}, u32[]{:S(2)}, u32[]{:S(2)}) collective-permute-start(bf16[528,128]{1,0:T(8,128)(2,1)S(1)} %pad_maximum_fusion.2), channel_id=1, source_target_pairs={{0,1},{1,2},{2,3},{3,0},{4,5},{5,6},{6,7},{7,4},{8,9},{9,10},{10,1... | collective-permute-start | bytes 405512 | tf_op jit(solution)/shard_map/ppermute | solution.py:132
  56.9 29.7 %collective-permute-start.5 = (bf16[4,528,128]{2,1,0:T(8,128)(2,1)S(1)}, bf16[4,528,128]{2,1,0:T(8,128)(2,1)S(1)}, u32[]{:S(2)}, u32[]{:S(2)}) collective-permute-start(bf16[4,528,128]{2,1,0:T(8,128)(2,1)S(1)} %pad_maximum_fusion.1.refs_3_.refs_4_.refs_5_), channel_id=1, source_target_pairs={{0,28},{4,0},{8,4},{12,8},{16,12},{20,16},{24,20},{28,24},{1,29},{... | collective-permute-start | bytes 1622024 | tf_op jit(solution)/shard_map/ppermute | solution.py:132
  67.5 19.1 %collective-permute-start.4 = (bf16[4,528,128]{2,1,0:T(8,128)(2,1)S(1)}, bf16[4,528,128]{2,1,0:T(8,128)(2,1)S(1)}, u32[]{:S(2)}, u32[]{:S(2)}) collective-permute-start(bf16[4,528,128]{2,1,0:T(8,128)(2,1)S(1)} %pad_maximum_fusion.1.refs_3_.refs_4_.refs_5_), channel_id=1, source_target_pairs={{0,4},{4,8},{8,12},{12,16},{16,20},{20,24},{24,28},{28,0},{1,5},{5... | collective-permute-start | bytes 1622024 | tf_op jit(solution)/shard_map/ppermute | solution.py:132
  71.5 3.8 %collective-permute-start = (bf16[128,256]{1,0:T(8,128)(2,1)S(1)}, bf16[128,256]{1,0:T(8,128)(2,1)S(1)}, u32[]{:S(2)}, u32[]{:S(2)}) collective-permute-start(bf16[128,256]{1,0:T(8,128)(2,1)S(1)} %dynamic-slice_bitcast_fusion), channel_id=1, source_target_pairs={{0,32},{32,0},{1,33},{33,1},{2,34},{34,2},{3,35},{35,3},{4,36},{36... | collective-permute-start | bytes 196616 | tf_op jit(solution)/shard_map/ppermute | solution.py:132
  85.3 1.3 copy-start.2
  86.6 23.9 %collective-permute-start.6 = (bf16[4,528,128]{2,1,0:T(8,128)(2,1)S(1)}, bf16[4,528,128]{2,1,0:T(8,128)(2,1)S(1)}, u32[]{:S(2)}, u32[]{:S(2)}) collective-permute-start(bf16[4,528,128]{2,1,0:T(8,128)(2,1)S(1)} %collective-permute-done.4.refs_3_.refs_4_.refs_5_), channel_id=1, source_target_pairs={{0,4},{4,8},{8,12},{12,16},{16,20},{20,24},{24,28},{28,0},{1,5},{5... | collective-permute-start | bytes 1622024 | tf_op jit(solution)/shard_map/ppermute | solution.py:132
  88.5 22.0 %collective-permute-start.7 = (bf16[4,528,128]{2,1,0:T(8,128)(2,1)S(1)}, bf16[4,528,128]{2,1,0:T(8,128)(2,1)S(1)}, u32[]{:S(2)}, u32[]{:S(2)}) collective-permute-start(bf16[4,528,128]{2,1,0:T(8,128)(2,1)S(1)} %collective-permute-done.5.refs_6_.refs_7_.refs_8_), channel_id=1, source_target_pairs={{0,28},{4,0},{8,4},{12,8},{16,12},{20,16},{24,20},{28,24},{1,29},{... | collective-permute-start | bytes 1622024 | tf_op jit(solution)/shard_map/ppermute | solution.py:132
  109.2 1.3 copy-start.1
  110.5 23.6 %collective-permute-start.8 = (bf16[4,528,128]{2,1,0:T(8,128)(2,1)S(1)}, bf16[4,528,128]{2,1,0:T(8,128)(2,1)S(1)}, u32[]{:S(2)}, u32[]{:S(2)}) collective-permute-start(bf16[4,528,128]{2,1,0:T(8,128)(2,1)S(1)} %collective-permute-done.6.refs_3_.refs_4_.refs_5_), channel_id=1, source_target_pairs={{0,4},{4,8},{8,12},{12,16},{16,20},{20,24},{24,28},{28,0},{1,5},{5... | collective-permute-start | bytes 1622024 | tf_op jit(solution)/shard_map/ppermute | solution.py:132
  112.4 21.7 %collective-permute-start.9 = (bf16[4,528,128]{2,1,0:T(8,128)(2,1)S(1)}, bf16[4,528,128]{2,1,0:T(8,128)(2,1)S(1)}, u32[]{:S(2)}, u32[]{:S(2)}) collective-permute-start(bf16[4,528,128]{2,1,0:T(8,128)(2,1)S(1)} %collective-permute-done.7.refs_6_.refs_7_.refs_8_), channel_id=1, source_target_pairs={{0,28},{4,0},{8,4},{12,8},{16,12},{20,16},{24,20},{28,24},{1,29},{... | collective-permute-start | bytes 1622024 | tf_op jit(solution)/shard_map/ppermute | solution.py:132
  132.8 1.3 copy-start
  134.2 22.3 %collective-permute-start.10 = (bf16[2,528,128]{2,1,0:T(8,128)(2,1)S(1)}, bf16[2,528,128]{2,1,0:T(8,128)(2,1)S(1)}, u32[]{:S(2)}, u32[]{:S(2)}) collective-permute-start(bf16[2,528,128]{2,1,0:T(8,128)(2,1)S(1)} %slice.20), channel_id=1, source_target_pairs={{0,4},{4,8},{8,12},{12,16},{16,20},{20,24},{24,28},{28,0},{1,5},{5... | collective-permute-start | bytes 811016 | tf_op jit(solution)/shard_map/ppermute | solution.py:132
  136.1 20.4 %collective-permute-start.11 = (bf16[2,528,128]{2,1,0:T(8,128)(2,1)S(1)}, bf16[2,528,128]{2,1,0:T(8,128)(2,1)S(1)}, u32[]{:S(2)}, u32[]{:S(2)}) collective-permute-start(bf16[2,528,128]{2,1,0:T(8,128)(2,1)S(1)} %slice.21), channel_id=1, source_target_pairs={{0,28},{4,0},{8,4},{12,8},{16,12},{20,16},{24,20},{28,24},{1,29},{... | collective-permute-start | bytes 811016 | tf_op jit(solution)/shard_map/ppermute | solution.py:132
  167.2 4.5 %collective-permute-start.12 = (bf16[128,256]{1,0:T(8,128)(2,1)S(1)}, bf16[128,256]{1,0:T(8,128)(2,1)S(1)}, u32[]{:S(2)}, u32[]{:S(2)}) collective-permute-start(bf16[128,256]{1,0:T(8,128)(2,1)S(1)} %slice_bitcast_fusion), channel_id=1, source_target_pairs={{0,32},{32,0},{1,33},{33,1},{2,34},{34,2},{3,35},{35,3},{4,36},{36... | collective-permute-start | bytes 196616 | tf_op jit(solution)/shard_map/ppermute | solution.py:132

commit v4 on v3

v4 whole, which is shorter than its diff:
```python
import functools

import jax
import jax.numpy as jnp
from jax import lax
from jax.experimental import pallas as pl
from jax.experimental.pallas import tpu as pltpu
from jax.sharding import Mesh, PartitionSpec as P

H = 32
KVH = 4
HD = 128
BLOCK = 64
WARM = 2
LAYERS = 16
ROWS = 128
HEADS = H // LAYERS
WIDE = HEADS * HD
SLABS = 8
POS_ROWS = 16
MASKED = -1e30
SCALE = 1.4426950408889634 / HD**0.5
SECTION = ("x", "yl", "core")


def attend_body(shards, first, last, *refs):
    it = iter(refs)
    warm_ref, q_ref, pos_ref = next(it), next(it), next(it)
    blocks = [next(it) for _ in shards]
    if not first:
        m_in, l_in, a_in = next(it), next(it), next(it)
    outs = [next(it)] if last else [next(it), next(it), next(it)]
    k, v, cap = it
    step = pl.program_id(0)
    count = k.shape[1]

    @pl.when(step == 0)
    def _():
        row = lax.broadcasted_iota(jnp.int32, (BLOCK, ROWS), 0).astype(jnp.float32)
        at = 0
        for n, ref in zip(shards, blocks):
            for i in range(n):
                for source in range(2):
                    base = source * 2 * ROWS
                    k[source, at : at + ROWS, :] = ref[i, base : base + ROWS]
                    v[source, :HD, at : at + ROWS] = ref[i, base + ROWS : base + 2 * ROWS]
                ids = ref[i, 4 * ROWS : 4 * ROWS + POS_ROWS].astype(jnp.float32)
                for part in range(ROWS // BLOCK):
                    key_pos = ids[0:1, part * BLOCK : part * BLOCK + 1] * BLOCK + row
                    rows = slice(at + part * BLOCK, at + (part + 1) * BLOCK)
                    cap[rows, :] = jnp.where(key_pos <= pos_ref[...], jnp.inf, MASKED)
                at += ROWS
        for source in range(2):
            v[source, HD:, :] = jnp.ones((POS_ROWS, count), jnp.bfloat16)

    def scores(j):
        q = jnp.concatenate([q_ref[j][:, h * HD : (h + 1) * HD] for h in range(HEADS)], axis=0)
        source = warm_ref[step * SLABS + j]
        return lax.dot_general(
            k[source], q, (((1,), (1,)), ((), ())), preferred_element_type=jnp.float32
        )

    def absorb(j, s):
        s = jnp.minimum(s, jnp.concatenate([cap[...]] * HEADS, axis=1))
        m = jnp.max(s, axis=0, keepdims=True)
        if not first:
            m_old = m_in[j, 0:1, :]
            m = jnp.maximum(m_old, m)
        w = jnp.exp2((s - m) * SCALE).astype(jnp.bfloat16)
        o = lax.dot_general(
            v[warm_ref[step * SLABS + j]],
            w,
            (((1,), (0,)), ((), ())),
            preferred_element_type=jnp.float32,
        )
        acc, den = o[:HD], o[HD : HD + 8]
        if not first:
            f = jnp.exp2((m_old - m) * SCALE)
            acc = acc + f * a_in[j]
            den = den + f * l_in[j]
        if last:
            done = acc / den[0:1]
            for h in range(HEADS):
                cols = slice(h * HD, (h + 1) * HD)
                outs[0][j, :, cols] = done[:, cols].T.astype(jnp.bfloat16)
        else:
            outs[0][j] = jnp.broadcast_to(m, den.shape)
            outs[1][j] = den
            outs[2][j] = acc

    s = scores(0)
    for j in range(SLABS):
        ahead = scores(j + 1) if j + 1 < SLABS else None
        absorb(j, s)
        s = ahead


def attend(warm, q, pos, blocks, state, last):
    shards = tuple(b.shape[0] for b in blocks)
    count = sum(shards) * ROWS
    slab = pl.BlockSpec((SLABS, ROWS, WIDE), lambda i, warm: (i, 0, 0))
    small = pl.BlockSpec((SLABS, 8, WIDE), lambda i, warm: (i, 0, 0))
    in_specs = [slab, pl.BlockSpec((1, ROWS), lambda i, warm: (0, 0))]
    in_specs += [pl.BlockSpec(b.shape, lambda i, warm: (0, 0, 0)) for b in blocks]
    args = [q, pos, *blocks]
    if state is not None:
        in_specs += [small, small, slab]
        args += list(state)
    one = jax.ShapeDtypeStruct((LAYERS, 8, WIDE), jnp.float32)
    acc = jax.ShapeDtypeStruct((LAYERS, HD, WIDE), jnp.float32)
    done = jax.ShapeDtypeStruct((LAYERS, ROWS, WIDE), jnp.bfloat16)
    return pl.pallas_call(
        functools.partial(attend_body, shards, state is None, last),
        grid_spec=pltpu.PrefetchScalarGridSpec(
            num_scalar_prefetch=1,
            grid=(LAYERS // SLABS,),
            in_specs=in_specs,
            out_specs=slab if last else [small, small, slab],
            scratch_shapes=[
                pltpu.VMEM((2, count, HD), jnp.bfloat16),
                pltpu.VMEM((2, HD + POS_ROWS, count), jnp.bfloat16),
                pltpu.VMEM((count, ROWS), jnp.float32),
            ],
        ),
        out_shape=done if last else [one, one, acc],
        compiler_params=pltpu.CompilerParams(vmem_limit_bytes=48 << 20),
        cost_estimate=pl.CostEstimate(
            flops=4 * ROWS * H * count * HD,
            bytes_accessed=8 << 20,
            transcendentals=ROWS * H * count,
        ),
        name="attend",
    )(warm, *args)


def turn(value, axis, size, shift):
    return lax.ppermute(value, axis, [(i, (i + shift) % size) for i in range(size)])


def pick(slabs, index):
    return lax.dynamic_index_in_dim(slabs, index, 0, keepdims=False)


def swap(slabs, index):
    other = turn(pick(slabs, index), "core", 2, 1)
    return lax.dynamic_update_index_in_dim(slabs, other, index, 0)


def per_device(sizes, queries, key_values, token_pos, layer_of_section):
    nz, nyh = sizes["z"], sizes["yh"]
    core = lax.axis_index("core")
    ids = jnp.arange(LAYERS, dtype=jnp.int32)
    holder = jnp.sum(jnp.where(layer_of_section[None, :] == ids[:, None], ids[None, :], 0), axis=1)
    warm, other_warm = pick(holder, core), pick(holder, 1 - core)
    kv = key_values[0].reshape(ROWS, 2, KVH, HD)
    heads = jnp.stack([kv[:, 0].transpose(1, 0, 2), kv[:, 1].transpose(1, 2, 0)], axis=1)
    pieces = jnp.broadcast_to(
        heads.reshape(KVH, 1, 2 * ROWS, HD), (KVH, LAYERS // KVH, 2 * ROWS, HD)
    ).reshape(LAYERS, 2 * ROWS, HD)
    pieces = lax.all_to_all(pieces, SECTION, 0, 0)
    block_ids = jnp.broadcast_to((token_pos // BLOCK).astype(jnp.bfloat16)[None, :], (POS_ROWS, ROWS))
    shard = jnp.concatenate([pick(pieces, holder[LAYERS - 1]), pick(pieces, warm), block_ids], axis=0)
    line = jnp.stack([shard] + [turn(shard, "yh", nyh, shift) for shift in range(1, nyh)])
    q = queries[0].reshape(ROWS, LAYERS, WIDE).transpose(1, 0, 2)
    q, line = lax.optimization_barrier((q, line))
    up, down = turn(line, "z", nz, 1), turn(line, "z", nz, -1)
    q = lax.all_to_all(q, SECTION, 0, 0)
    q = swap(q, other_warm)
    use_warm = ((ids == warm) | (ids == other_warm)).astype(jnp.int32)
    pos = token_pos.astype(jnp.float32)[None, :]

    def part(blocks, state, last=False):
        return attend(use_warm, q, pos, blocks, state, last)

    up, down, q = lax.optimization_barrier((up, down, q))
    held, state = [line, up, down], None
    for _ in range(nz // 2 - 2):
        up, down = turn(up, "z", nz, 1), turn(down, "z", nz, -1)
        state = part(held, state)
        up, down, state = lax.optimization_barrier((up, down, state))
        held = [up, down]
    half = nyh // 2
    last_up, last_down = turn(up[:half], "z", nz, 1), turn(down[half:], "z", nz, -1)
    state = part(held, state)
    last_up, last_down, state = lax.optimization_barrier((last_up, last_down, state))
    out = swap(part([last_up, last_down], state, True), other_warm)
    out = lax.all_to_all(out, SECTION, 0, 0)
    return out.transpose(1, 0, 2).reshape(1, ROWS, H * HD)


def solution(mesh):
    sizes = {"x": 4, "yl": 2, "core": 2, "z": 8, "yh": 4}
    fine = Mesh(mesh.devices.reshape(tuple(sizes.values())), tuple(sizes))
    ctx = ("z", "yh")
    in_specs = (P(SECTION, ctx, None), P(SECTION, ctx, None, None), P(ctx), P())
    return jax.shard_map(
        functools.partial(per_device, sizes),
        mesh=fine,
        in_specs=in_specs,
        out_specs=P(SECTION, ctx, None),
        check_vma=False,
    )
```

time: 198 us -> 161 us (0.81)
  Pallas kernels: 67.9 us -> 30 us
  waiting for transfers between devices: 24.2 us -> 28.4 us
    pallas_call x5 -> x4, Pallas kernels: 67.9 us -> 30 us  [attend(): pl.pallas_call(functools.partial(attend_body, shards, state is None, last...]
    all_to_all x1, waiting for transfers between devices: 0.01 us -> 3.36 us  [per_device(): q = lax.all_to_all(q, SECTION, 0, 0)]
    unnamed x14 -> x12, local copies, waits for them, and re-layouts: 5.8 us -> 4.48 us
  transfers between devices with their start and end apart: 15 -> 15, of which waited for: 5 -> 9; matrix products, arithmetic and copies ran while one was open for 2% -> 3% of each run, Pallas kernels for 29% -> 16%
where the time goes in v4:
time: 161 us; the launch traced here: 160 us
  starting transfers between devices  63.5 us (39%)
  Pallas kernels  30 us (19%)
  waiting for transfers between devices  28.4 us (18%)
  blocking collectives  20.8 us (13%)
  local copies, waits for them, and re-layouts  9.84 us (6%)
  between operations  6.3 us (4%)
    ppermute x13, starting transfers between devices, turn(): lax.ppermute(value, axis, [(i, (i + shift) % size) for i in range(size)])  49.2 us
    pallas_call x4, Pallas kernels, attend(): pl.pallas_call(functools.partial(attend_body, shards, state is None, last...  30 us
    all_to_all x1, blocking collectives, per_device(): out = lax.all_to_all(out, SECTION, 0, 0)  20.8 us
    ppermute x13, waiting for transfers between devices, turn(): lax.ppermute(value, axis, [(i, (i + shift) % size) for i in range(size)])  13.8 us
    all_to_all x1, waiting for transfers between devices, per_device(): pieces = lax.all_to_all(pieces, SECTION, 0, 0)  11.2 us
    all_to_all x1, starting transfers between devices, per_device(): pieces = lax.all_to_all(pieces, SECTION, 0, 0)  10.3 us
    unnamed x12, local copies, waits for them, and re-layouts  4.48 us
    all_to_all x1, starting transfers between devices, per_device(): q = lax.all_to_all(q, SECTION, 0, 0)  3.95 us
  transfers between devices with their start and end apart: 15, of which 9 were waited for; matrix products, arithmetic and copies ran while one was open for 3% of the time, Pallas kernels for 16%

profile of v4, /device:TPU:1, one launch (start us, length us, event | category | flops | bytes accessed | tf_op | source)
XLA Modules:
  0.0 160.3 jit_solution(13997276973240031672)
XLA Ops:
  2.6 10.3 %all-to-all-start = ((bf16[16,256,128]{2,1,0:T(8,128)(2,1)}), bf16[16,256,128]{2,1,0:T(8,128)(2,1)S(1)}, u32[]{:S(2)}, u32[]{:S(2)}) async-start(bf16[16,256,128]{2,1,0:T(8,128)(2,1)} %bitcast.12), calls=%async_computation | async-start | bytes 2097152 | tf_op jit(solution)/shard_map/all_to_all | solution.py:160
  17.6 11.2 %all-to-all-done = bf16[16,256,128]{2,1,0:T(8,128)(2,1)S(1)} async-done(((bf16[16,256,128]{2,1,0:T(8,128)(2,1)}), bf16[16,256,128]{2,1,0:T(8,128)(2,1)S(1)}, u32[]{:S(2)}, u32[]{:S(2)}) %all-to-all-start) | async-done | bytes 1048608 | tf_op jit(solution)/shard_map/all_to_all | solution.py:160
  28.9 3.0 %collective-permute-start.1 = (bf16[528,128]{1,0:T(8,128)(2,1)S(1)}, bf16[528,128]{1,0:T(8,128)(2,1)S(1)}, u32[]{:S(2)}, u32[]{:S(2)}) collective-permute-start(bf16[528,128]{1,0:T(8,128)(2,1)S(1)} %get-tuple-element.68), channel_id=1, source_target_pairs={{0,2},{1,3},{2,0},{3,1},{4,6},{5,7},{6,4},{7,5},{8,10},{9,11},{10,... | collective-permute-start | bytes 405512 | tf_op jit(solution)/shard_map/ppermute | solution.py:137
  31.8 2.4 %collective-permute-start = (bf16[528,128]{1,0:T(8,128)(2,1)S(1)}, bf16[528,128]{1,0:T(8,128)(2,1)S(1)}, u32[]{:S(2)}, u32[]{:S(2)}) collective-permute-start(bf16[528,128]{1,0:T(8,128)(2,1)S(1)} %get-tuple-element.68), channel_id=1, source_target_pairs={{0,1},{1,2},{2,3},{3,0},{4,5},{5,6},{6,7},{7,4},{8,9},{9,10},{10,1... | collective-permute-start | bytes 405512 | tf_op jit(solution)/shard_map/ppermute | solution.py:137
  34.3 5.0 %collective-permute-start.2 = (bf16[528,128]{1,0:T(8,128)(2,1)S(1)}, bf16[528,128]{1,0:T(8,128)(2,1)S(1)}, u32[]{:S(2)}, u32[]{:S(2)}) collective-permute-start(bf16[528,128]{1,0:T(8,128)(2,1)S(1)} %get-tuple-element.68), channel_id=1, source_target_pairs={{0,3},{1,0},{2,1},{3,2},{4,7},{5,4},{6,5},{7,6},{8,11},{9,8},{10,9... | collective-permute-start | bytes 405512 | tf_op jit(solution)/shard_map/ppermute | solution.py:137
  43.2 4.7 %collective-permute-done.2 = bf16[528,128]{1,0:T(8,128)(2,1)S(1)} collective-permute-done((bf16[528,128]{1,0:T(8,128)(2,1)S(1)}, bf16[528,128]{1,0:T(8,128)(2,1)S(1)}, u32[]{:S(2)}, u32[]{:S(2)}) %collective-permute-start.2) | collective-permute-done | bytes 135200 | tf_op jit(solution)/shard_map/ppermute | solution.py:137
  48.0 3.9 %all-to-all-start.1 = ((bf16[16,128,256]{2,1,0:T(8,128)(2,1)}), bf16[16,128,256]{2,1,0:T(8,128)(2,1)S(1)}, u32[]{:S(2)}, u32[]{:S(2)}) async-start(bf16[16,128,256]{2,1,0:T(8,128)(2,1)} %bitcast.3), calls=%async_computation.1 | async-start | bytes 2097152 | tf_op jit(solution)/shard_map/all_to_all | solution.py:167
  51.9 8.6 %collective-permute-start.4 = (bf16[4,528,128]{2,1,0:T(8,128)(2,1)S(1)}, bf16[4,528,128]{2,1,0:T(8,128)(2,1)S(1)}, u32[]{:S(2)}, u32[]{:S(2)}) collective-permute-start(bf16[4,528,128]{2,1,0:T(8,128)(2,1)S(1)} %pad_maximum_fusion.refs_3_), channel_id=1, source_target_pairs={{0,28},{4,0},{8,4},{12,8},{16,12},{20,16},{24,20},{28,24},{1,29},{... | collective-permute-start | bytes 1622024 | tf_op jit(solution)/shard_map/ppermute | solution.py:137
  60.5 1.9 %collective-permute-start.3 = (bf16[4,528,128]{2,1,0:T(8,128)(2,1)S(1)}, bf16[4,528,128]{2,1,0:T(8,128)(2,1)S(1)}, u32[]{:S(2)}, u32[]{:S(2)}) collective-permute-start(bf16[4,528,128]{2,1,0:T(8,128)(2,1)S(1)} %pad_maximum_fusion.refs_3_), channel_id=1, source_target_pairs={{0,4},{4,8},{8,12},{12,16},{16,20},{20,24},{24,28},{28,0},{1,5},{5... | collective-permute-start | bytes 1622024 | tf_op jit(solution)/shard_map/ppermute | solution.py:137
  64.5 3.4 %all-to-all-done.1 = bf16[16,128,256]{2,1,0:T(8,128)(2,1)S(1)} async-done(((bf16[16,128,256]{2,1,0:T(8,128)(2,1)}), bf16[16,128,256]{2,1,0:T(8,128)(2,1)S(1)}, u32[]{:S(2)}, u32[]{:S(2)}) %all-to-all-start.1) | async-done | bytes 1048608 | tf_op jit(solution)/shard_map/all_to_all | solution.py:167
  67.8 2.8 %collective-permute-start.5 = (bf16[128,256]{1,0:T(8,128)(2,1)S(1)}, bf16[128,256]{1,0:T(8,128)(2,1)S(1)}, u32[]{:S(2)}, u32[]{:S(2)}) collective-permute-start(bf16[128,256]{1,0:T(8,128)(2,1)S(1)} %dynamic-slice_bitcast_fusion.1), channel_id=1, source_target_pairs={{0,32},{32,0},{1,33},{33,1},{2,34},{34,2},{3,35},{35,3},{4,36},{36... | collective-permute-start | bytes 196616 | tf_op jit(solution)/shard_map/ppermute | solution.py:137
  71.9 5.0 %collective-permute-done.3.refs_4_ = bf16[4,528,128]{2,1,0:T(8,128)(2,1)S(1)} collective-permute-done((bf16[4,528,128]{2,1,0:T(8,128)(2,1)S(1)}, bf16[4,528,128]{2,1,0:T(8,128)(2,1)S(1)}, u32[]{:S(2)}, u32[]{:S(2)}) %collective-permute-start.3) | collective-permute-done | bytes 540704 | tf_op jit(solution)/shard_map/ppermute | solution.py:137
  76.9 1.9 %collective-permute-start.6 = (bf16[4,528,128]{2,1,0:T(8,128)(2,1)S(1)}, bf16[4,528,128]{2,1,0:T(8,128)(2,1)S(1)}, u32[]{:S(2)}, u32[]{:S(2)}) collective-permute-start(bf16[4,528,128]{2,1,0:T(8,128)(2,1)S(1)} %collective-permute-done.3.refs_4_), channel_id=1, source_target_pairs={{0,4},{4,8},{8,12},{12,16},{16,20},{20,24},{24,28},{28,0},{1,5},{5... | collective-permute-start | bytes 1622024 | tf_op jit(solution)/shard_map/ppermute | solution.py:137
  78.8 4.6 %collective-permute-start.7 = (bf16[4,528,128]{2,1,0:T(8,128)(2,1)S(1)}, bf16[4,528,128]{2,1,0:T(8,128)(2,1)S(1)}, u32[]{:S(2)}, u32[]{:S(2)}) collective-permute-start(bf16[4,528,128]{2,1,0:T(8,128)(2,1)S(1)} %collective-permute-done.4.refs_5_), channel_id=1, source_target_pairs={{0,28},{4,0},{8,4},{12,8},{16,12},{20,16},{24,20},{28,24},{1,29},{... | collective-permute-start | bytes 1622024 | tf_op jit(solution)/shard_map/ppermute | solution.py:137
  84.7 9.1 %attend.4 = (f32[16,8,256]{2,1,0:T(8,128)S(1)}, f32[16,8,256]{2,1,0:T(8,128)S(1)}, f32[16,128,256]{2,1,0:T(8,128)S(1)}) custom-call(s32[16]{0:T(128)S(1)} %or_convert_fusion.refs_0_, bf16[16,128,256]{2,1,0:T(8,128)(2,1)S(1)} %bitcast_dynamic-update-slice_fusion.1.refs_1_, f32[1,128]{1,0:T(1,128)S(1)} %get-tuple-element.69.refs_2_, ...), custom_call_target="tpu_custom_call" | custom-call | flops 3221225472 | bytes 8388608 | tf_op jit(solution)/shard_map/attend/pallas_call | solution.py:112
  95.2 1.9 %collective-permute-start.8 = (bf16[4,528,128]{2,1,0:T(8,128)(2,1)S(1)}, bf16[4,528,128]{2,1,0:T(8,128)(2,1)S(1)}, u32[]{:S(2)}, u32[]{:S(2)}) collective-permute-start(bf16[4,528,128]{2,1,0:T(8,128)(2,1)S(1)} %collective-permute-done.6.refs_3_), channel_id=1, source_target_pairs={{0,4},{4,8},{8,12},{12,16},{16,20},{20,24},{24,28},{28,0},{1,5},{5... | collective-permute-start | bytes 1622024 | tf_op jit(solution)/shard_map/ppermute | solution.py:137
  97.1 4.6 %collective-permute-start.9 = (bf16[4,528,128]{2,1,0:T(8,128)(2,1)S(1)}, bf16[4,528,128]{2,1,0:T(8,128)(2,1)S(1)}, u32[]{:S(2)}, u32[]{:S(2)}) collective-permute-start(bf16[4,528,128]{2,1,0:T(8,128)(2,1)S(1)} %collective-permute-done.7.refs_4_), channel_id=1, source_target_pairs={{0,28},{4,0},{8,4},{12,8},{16,12},{20,16},{24,20},{28,24},{1,29},{... | collective-permute-start | bytes 1622024 | tf_op jit(solution)/shard_map/ppermute | solution.py:137
  101.7 8.1 %attend.5 = (f32[16,8,256]{2,1,0:T(8,128)S(1)}, f32[16,8,256]{2,1,0:T(8,128)S(1)}, f32[16,128,256]{2,1,0:T(8,128)S(1)}) custom-call(s32[16]{0:T(128)S(1)} %or_convert_fusion.refs_0_, bf16[16,128,256]{2,1,0:T(8,128)(2,1)S(1)} %bitcast_dynamic-update-slice_fusion.1.refs_1_, f32[1,128]{1,0:T(1,128)S(1)} %get-tuple-element.69.refs_2_, ...), custom_call_target="tpu_custom_call" | custom-call | flops 2147483648 | bytes 8388608 | tf_op jit(solution)/shard_map/attend/pallas_call | solution.py:112
  111.2 2.5 %collective-permute-start.10 = (bf16[2,528,128]{2,1,0:T(8,128)(2,1)S(1)}, bf16[2,528,128]{2,1,0:T(8,128)(2,1)S(1)}, u32[]{:S(2)}, u32[]{:S(2)}) collective-permute-start(bf16[2,528,128]{2,1,0:T(8,128)(2,1)S(1)} %slice.18), channel_id=1, source_target_pairs={{0,4},{4,8},{8,12},{12,16},{16,20},{20,24},{24,28},{28,0},{1,5},{5... | collective-permute-start | bytes 811016 | tf_op jit(solution)/shard_map/ppermute | solution.py:137
  113.8 4.8 %collective-permute-start.11 = (bf16[2,528,128]{2,1,0:T(8,128)(2,1)S(1)}, bf16[2,528,128]{2,1,0:T(8,128)(2,1)S(1)}, u32[]{:S(2)}, u32[]{:S(2)}) collective-permute-start(bf16[2,528,128]{2,1,0:T(8,128)(2,1)S(1)} %slice.19), channel_id=1, source_target_pairs={{0,28},{4,0},{8,4},{12,8},{16,12},{20,16},{24,20},{28,24},{1,29},{... | collective-permute-start | bytes 811016 | tf_op jit(solution)/shard_map/ppermute | solution.py:137
  118.5 8.1 %attend.6 = (f32[16,8,256]{2,1,0:T(8,128)S(1)}, f32[16,8,256]{2,1,0:T(8,128)S(1)}, f32[16,128,256]{2,1,0:T(8,128)S(1)}) custom-call(s32[16]{0:T(128)S(1)} %or_convert_fusion.refs_0_, bf16[16,128,256]{2,1,0:T(8,128)(2,1)S(1)} %bitcast_dynamic-update-slice_fusion.1.refs_1_, f32[1,128]{1,0:T(1,128)S(1)} %get-tuple-element.69.refs_2_, ...), custom_call_target="tpu_custom_call" | custom-call | flops 2147483648 | bytes 8388608 | tf_op jit(solution)/shard_map/attend/pallas_call | solution.py:112
  126.7 4.6 %attend.7 = bf16[16,128,256]{2,1,0:T(8,128)(2,1)S(1)} custom-call(s32[16]{0:T(128)S(1)} %or_convert_fusion.refs_0_, bf16[16,128,256]{2,1,0:T(8,128)(2,1)S(1)} %bitcast_dynamic-update-slice_fusion.1.refs_1_, f32[1,128]{1,0:T(1,128)S(1)} %get-tuple-element.69.refs_2_, bf16[2,528,128]{2,1,0:T(8,128)(2,1)S(1)} %collective-permute-done.10.refs_3_, ...), custom_call_target="tpu_custom_call" | custom-call | flops 1073741824 | bytes 8388608 | tf_op jit(solution)/shard_map/attend/pallas_call | solution.py:112
  131.3 5.3 %collective-permute-start.12 = (bf16[128,256]{1,0:T(8,128)(2,1)S(1)}, bf16[128,256]{1,0:T(8,128)(2,1)S(1)}, u32[]{:S(2)}, u32[]{:S(2)}) collective-permute-start(bf16[128,256]{1,0:T(8,128)(2,1)S(1)} %dynamic-slice_bitcast_fusion), channel_id=1, source_target_pairs={{0,32},{32,0},{1,33},{33,1},{2,34},{34,2},{3,35},{35,3},{4,36},{36... | collective-permute-start | bytes 196616 | tf_op jit(solution)/shard_map/ppermute | solution.py:137
  137.5 20.8 %all_to_all.15 = bf16[16,128,256]{2,1,0:T(8,128)(2,1)S(1)} all-to-all(bf16[16,128,256]{2,1,0:T(8,128)(2,1)S(1)} %bitcast_dynamic-update-slice_fusion), channel_id=1, replica_groups=mesh['x'=4,'yl'=2,'core'=2,'z'=8,'yh'=4] {'x','yl','core'}, dimensions={0} | all-to-all | bytes 2097152 | tf_op jit(solution)/shard_map/all_to_all | solution.py:187
  (44 shorter events, 15.5 us)
Async XLA Ops:
  1.2 11.7 %copy-start.3 = (s32[16]{0:T(128)S(1)}, s32[16]{0:T(128)}, u32[]{:S(2)}) copy-start(s32[16]{0:T(128)} %param.7) | copy-start | bytes 196
  1.2 16.4 %copy-start.4 = (s32[128]{0:T(128)S(1)}, s32[128]{0:T(128)}, u32[]{:S(2)}) copy-start(s32[128]{0:T(128)} %param.6) | copy-start | bytes 1540
  1.4 37.9 %copy-start.2 = (bf16[1,128,4096]{2,1,0:T(8,128)(2,1)S(1)}, bf16[1,128,4096]{2,1,0:T(8,128)(2,1)}, u32[]{:S(2)}) copy-start(bf16[1,128,4096]{2,1,0:T(8,128)(2,1)} %param.4) | copy-start | bytes 3145732
  2.6 26.2 %all-to-all-start = ((bf16[16,256,128]{2,1,0:T(8,128)(2,1)}), bf16[16,256,128]{2,1,0:T(8,128)(2,1)S(1)}, u32[]{:S(2)}, u32[]{:S(2)}) async-start(bf16[16,256,128]{2,1,0:T(8,128)(2,1)} %bitcast.12), calls=%async_computation | async-start | bytes 2097152 | tf_op jit(solution)/shard_map/all_to_all | solution.py:160
  28.9 13.1 %collective-permute-start.1 = (bf16[528,128]{1,0:T(8,128)(2,1)S(1)}, bf16[528,128]{1,0:T(8,128)(2,1)S(1)}, u32[]{:S(2)}, u32[]{:S(2)}) collective-permute-start(bf16[528,128]{1,0:T(8,128)(2,1)S(1)} %get-tuple-element.68), channel_id=1, source_target_pairs={{0,2},{1,3},{2,0},{3,1},{4,6},{5,7},{6,4},{7,5},{8,10},{9,11},{10,... | collective-permute-start | bytes 405512 | tf_op jit(solution)/shard_map/ppermute | solution.py:137
  31.8 11.3 %collective-permute-start = (bf16[528,128]{1,0:T(8,128)(2,1)S(1)}, bf16[528,128]{1,0:T(8,128)(2,1)S(1)}, u32[]{:S(2)}, u32[]{:S(2)}) collective-permute-start(bf16[528,128]{1,0:T(8,128)(2,1)S(1)} %get-tuple-element.68), channel_id=1, source_target_pairs={{0,1},{1,2},{2,3},{3,0},{4,5},{5,6},{6,7},{7,4},{8,9},{9,10},{10,1... | collective-permute-start | bytes 405512 | tf_op jit(solution)/shard_map/ppermute | solution.py:137
  34.3 13.6 %collective-permute-start.2 = (bf16[528,128]{1,0:T(8,128)(2,1)S(1)}, bf16[528,128]{1,0:T(8,128)(2,1)S(1)}, u32[]{:S(2)}, u32[]{:S(2)}) collective-permute-start(bf16[528,128]{1,0:T(8,128)(2,1)S(1)} %get-tuple-element.68), channel_id=1, source_target_pairs={{0,3},{1,0},{2,1},{3,2},{4,7},{5,4},{6,5},{7,6},{8,11},{9,8},{10,9... | collective-permute-start | bytes 405512 | tf_op jit(solution)/shard_map/ppermute | solution.py:137
  48.0 19.9 %all-to-all-start.1 = ((bf16[16,128,256]{2,1,0:T(8,128)(2,1)}), bf16[16,128,256]{2,1,0:T(8,128)(2,1)S(1)}, u32[]{:S(2)}, u32[]{:S(2)}) async-start(bf16[16,128,256]{2,1,0:T(8,128)(2,1)} %bitcast.3), calls=%async_computation.1 | async-start | bytes 2097152 | tf_op jit(solution)/shard_map/all_to_all | solution.py:167
  51.9 20.0 %collective-permute-start.4 = (bf16[4,528,128]{2,1,0:T(8,128)(2,1)S(1)}, bf16[4,528,128]{2,1,0:T(8,128)(2,1)S(1)}, u32[]{:S(2)}, u32[]{:S(2)}) collective-permute-start(bf16[4,528,128]{2,1,0:T(8,128)(2,1)S(1)} %pad_maximum_fusion.refs_3_), channel_id=1, source_target_pairs={{0,28},{4,0},{8,4},{12,8},{16,12},{20,16},{24,20},{28,24},{1,29},{... | collective-permute-start | bytes 1622024 | tf_op jit(solution)/shard_map/ppermute | solution.py:137
  60.5 16.4 %collective-permute-start.3 = (bf16[4,528,128]{2,1,0:T(8,128)(2,1)S(1)}, bf16[4,528,128]{2,1,0:T(8,128)(2,1)S(1)}, u32[]{:S(2)}, u32[]{:S(2)}) collective-permute-start(bf16[4,528,128]{2,1,0:T(8,128)(2,1)S(1)} %pad_maximum_fusion.refs_3_), channel_id=1, source_target_pairs={{0,4},{4,8},{8,12},{12,16},{16,20},{20,24},{24,28},{28,0},{1,5},{5... | collective-permute-start | bytes 1622024 | tf_op jit(solution)/shard_map/ppermute | solution.py:137
  67.8 3.7 %collective-permute-start.5 = (bf16[128,256]{1,0:T(8,128)(2,1)S(1)}, bf16[128,256]{1,0:T(8,128)(2,1)S(1)}, u32[]{:S(2)}, u32[]{:S(2)}) collective-permute-start(bf16[128,256]{1,0:T(8,128)(2,1)S(1)} %dynamic-slice_bitcast_fusion.1), channel_id=1, source_target_pairs={{0,32},{32,0},{1,33},{33,1},{2,34},{34,2},{3,35},{35,3},{4,36},{36... | collective-permute-start | bytes 196616 | tf_op jit(solution)/shard_map/ppermute | solution.py:137
  76.9 18.3 %collective-permute-start.6 = (bf16[4,528,128]{2,1,0:T(8,128)(2,1)S(1)}, bf16[4,528,128]{2,1,0:T(8,128)(2,1)S(1)}, u32[]{:S(2)}, u32[]{:S(2)}) collective-permute-start(bf16[4,528,128]{2,1,0:T(8,128)(2,1)S(1)} %collective-permute-done.3.refs_4_), channel_id=1, source_target_pairs={{0,4},{4,8},{8,12},{12,16},{16,20},{20,24},{24,28},{28,0},{1,5},{5... | collective-permute-start | bytes 1622024 | tf_op jit(solution)/shard_map/ppermute | solution.py:137
  78.8 16.4 %collective-permute-start.7 = (bf16[4,528,128]{2,1,0:T(8,128)(2,1)S(1)}, bf16[4,528,128]{2,1,0:T(8,128)(2,1)S(1)}, u32[]{:S(2)}, u32[]{:S(2)}) collective-permute-start(bf16[4,528,128]{2,1,0:T(8,128)(2,1)S(1)} %collective-permute-done.4.refs_5_), channel_id=1, source_target_pairs={{0,28},{4,0},{8,4},{12,8},{16,12},{20,16},{24,20},{28,24},{1,29},{... | collective-permute-start | bytes 1622024 | tf_op jit(solution)/shard_map/ppermute | solution.py:137
  93.9 1.3 copy-start.1
  95.2 16.0 %collective-permute-start.8 = (bf16[4,528,128]{2,1,0:T(8,128)(2,1)S(1)}, bf16[4,528,128]{2,1,0:T(8,128)(2,1)S(1)}, u32[]{:S(2)}, u32[]{:S(2)}) collective-permute-start(bf16[4,528,128]{2,1,0:T(8,128)(2,1)S(1)} %collective-permute-done.6.refs_3_), channel_id=1, source_target_pairs={{0,4},{4,8},{8,12},{12,16},{16,20},{20,24},{24,28},{28,0},{1,5},{5... | collective-permute-start | bytes 1622024 | tf_op jit(solution)/shard_map/ppermute | solution.py:137
  97.1 14.0 %collective-permute-start.9 = (bf16[4,528,128]{2,1,0:T(8,128)(2,1)S(1)}, bf16[4,528,128]{2,1,0:T(8,128)(2,1)S(1)}, u32[]{:S(2)}, u32[]{:S(2)}) collective-permute-start(bf16[4,528,128]{2,1,0:T(8,128)(2,1)S(1)} %collective-permute-done.7.refs_4_), channel_id=1, source_target_pairs={{0,28},{4,0},{8,4},{12,8},{16,12},{20,16},{24,20},{28,24},{1,29},{... | collective-permute-start | bytes 1622024 | tf_op jit(solution)/shard_map/ppermute | solution.py:137
  109.8 1.3 copy-start
  111.2 15.4 %collective-permute-start.10 = (bf16[2,528,128]{2,1,0:T(8,128)(2,1)S(1)}, bf16[2,528,128]{2,1,0:T(8,128)(2,1)S(1)}, u32[]{:S(2)}, u32[]{:S(2)}) collective-permute-start(bf16[2,528,128]{2,1,0:T(8,128)(2,1)S(1)} %slice.18), channel_id=1, source_target_pairs={{0,4},{4,8},{8,12},{12,16},{16,20},{20,24},{24,28},{28,0},{1,5},{5... | collective-permute-start | bytes 811016 | tf_op jit(solution)/shard_map/ppermute | solution.py:137
  113.8 12.9 %collective-permute-start.11 = (bf16[2,528,128]{2,1,0:T(8,128)(2,1)S(1)}, bf16[2,528,128]{2,1,0:T(8,128)(2,1)S(1)}, u32[]{:S(2)}, u32[]{:S(2)}) collective-permute-start(bf16[2,528,128]{2,1,0:T(8,128)(2,1)S(1)} %slice.19), channel_id=1, source_target_pairs={{0,28},{4,0},{8,4},{12,8},{16,12},{20,16},{24,20},{28,24},{1,29},{... | collective-permute-start | bytes 811016 | tf_op jit(solution)/shard_map/ppermute | solution.py:137
  131.3 6.2 %collective-permute-start.12 = (bf16[128,256]{1,0:T(8,128)(2,1)S(1)}, bf16[128,256]{1,0:T(8,128)(2,1)S(1)}, u32[]{:S(2)}, u32[]{:S(2)}) collective-permute-start(bf16[128,256]{1,0:T(8,128)(2,1)S(1)} %dynamic-slice_bitcast_fusion), channel_id=1, source_target_pairs={{0,32},{32,0},{1,33},{33,1},{2,34},{34,2},{3,35},{35,3},{4,36},{36... | collective-permute-start | bytes 196616 | tf_op jit(solution)/shard_map/ppermute | solution.py:137

commit v5 on v4

--- a/solution.py
+++ b/solution.py
@@ -31,33 +31,28 @@
         m_in, l_in, a_in = next(it), next(it), next(it)
     outs = [next(it)] if last else [next(it), next(it), next(it)]
     k, v, cap = it
-    step = pl.program_id(0)
     count = k.shape[1]
-
-    @pl.when(step == 0)
-    def _():
-        row = lax.broadcasted_iota(jnp.int32, (BLOCK, ROWS), 0).astype(jnp.float32)
-        at = 0
-        for n, ref in zip(shards, blocks):
-            for i in range(n):
-                for source in range(2):
-                    base = source * 2 * ROWS
-                    k[source, at : at + ROWS, :] = ref[i, base : base + ROWS]
-                    v[source, :HD, at : at + ROWS] = ref[i, base + ROWS : base + 2 * ROWS]
-                ids = ref[i, 4 * ROWS : 4 * ROWS + POS_ROWS].astype(jnp.float32)
-                for part in range(ROWS // BLOCK):
-                    key_pos = ids[0:1, part * BLOCK : part * BLOCK + 1] * BLOCK + row
-                    rows = slice(at + part * BLOCK, at + (part + 1) * BLOCK)
-                    cap[rows, :] = jnp.where(key_pos <= pos_ref[...], jnp.inf, MASKED)
-                at += ROWS
-        for source in range(2):
-            v[source, HD:, :] = jnp.ones((POS_ROWS, count), jnp.bfloat16)
+    row = lax.broadcasted_iota(jnp.int32, (BLOCK, ROWS), 0).astype(jnp.float32)
+    at = 0
+    for n, ref in zip(shards, blocks):
+        for i in range(n):
+            for source in range(2):
+                base = source * 2 * ROWS
+                k[source, at : at + ROWS, :] = ref[i, base : base + ROWS]
+                v[source, :HD, at : at + ROWS] = ref[i, base + ROWS : base + 2 * ROWS]
+            ids = ref[i, 4 * ROWS : 4 * ROWS + POS_ROWS].astype(jnp.float32)
+            for part in range(ROWS // BLOCK):
+                key_pos = ids[0:1, part * BLOCK : part * BLOCK + 1] * BLOCK + row
+                rows = slice(at + part * BLOCK, at + (part + 1) * BLOCK)
+                cap[rows, :] = jnp.where(key_pos <= pos_ref[...], jnp.inf, MASKED)
+            at += ROWS
+    for source in range(2):
+        v[source, HD:, :] = jnp.ones((POS_ROWS, count), jnp.bfloat16)
 
     def scores(j):
-        q = jnp.concatenate([q_ref[j][:, h * HD : (h + 1) * HD] for h in range(HEADS)], axis=0)
-        source = warm_ref[step * SLABS + j]
+        q = jnp.concatenate([q_ref[j, :, h * HD : (h + 1) * HD] for h in range(HEADS)], axis=0)
         return lax.dot_general(
-            k[source], q, (((1,), (1,)), ((), ())), preferred_element_type=jnp.float32
+            k[warm_ref[j]], q, (((1,), (1,)), ((), ())), preferred_element_type=jnp.float32
         )
 
     def absorb(j, s):
@@ -68,10 +63,7 @@
             m = jnp.maximum(m_old, m)
         w = jnp.exp2((s - m) * SCALE).astype(jnp.bfloat16)
         o = lax.dot_general(
-            v[warm_ref[step * SLABS + j]],
-            w,
-            (((1,), (0,)), ((), ())),
-            preferred_element_type=jnp.float32,
+            v[warm_ref[j]], w, (((1,), (0,)), ((), ())), preferred_element_type=jnp.float32
         )
         acc, den = o[:HD], o[HD : HD + 8]
         if not first:
@@ -88,49 +80,48 @@
             outs[1][j] = den
             outs[2][j] = acc
 
-    s = scores(0)
-    for j in range(SLABS):
-        ahead = scores(j + 1) if j + 1 < SLABS else None
-        absorb(j, s)
-        s = ahead
+    @pl.loop(0, LAYERS // SLABS)
+    def _(step):
+        base = step * SLABS
+        s = scores(base)
+        for j in range(SLABS):
+            ahead = scores(base + j + 1) if j + 1 < SLABS else None
+            absorb(base + j, s)
+            s = ahead
 
 
 def attend(warm, q, pos, blocks, state, last):
     shards = tuple(b.shape[0] for b in blocks)
     count = sum(shards) * ROWS
-    slab = pl.BlockSpec((SLABS, ROWS, WIDE), lambda i, warm: (i, 0, 0))
-    small = pl.BlockSpec((SLABS, 8, WIDE), lambda i, warm: (i, 0, 0))
-    in_specs = [slab, pl.BlockSpec((1, ROWS), lambda i, warm: (0, 0))]
-    in_specs += [pl.BlockSpec(b.shape, lambda i, warm: (0, 0, 0)) for b in blocks]
-    args = [q, pos, *blocks]
+    args = [warm, q, pos, *blocks]
+    aliases = {}
     if state is not None:
-        in_specs += [small, small, slab]
+        if not last:
+            aliases = {len(args) + i: i for i in range(len(state))}
         args += list(state)
+    whole = pl.BlockSpec(memory_space=pltpu.VMEM)
     one = jax.ShapeDtypeStruct((LAYERS, 8, WIDE), jnp.float32)
     acc = jax.ShapeDtypeStruct((LAYERS, HD, WIDE), jnp.float32)
     done = jax.ShapeDtypeStruct((LAYERS, ROWS, WIDE), jnp.bfloat16)
     return pl.pallas_call(
         functools.partial(attend_body, shards, state is None, last),
-        grid_spec=pltpu.PrefetchScalarGridSpec(
-            num_scalar_prefetch=1,
-            grid=(LAYERS // SLABS,),
-            in_specs=in_specs,
-            out_specs=slab if last else [small, small, slab],
-            scratch_shapes=[
-                pltpu.VMEM((2, count, HD), jnp.bfloat16),
-                pltpu.VMEM((2, HD + POS_ROWS, count), jnp.bfloat16),
-                pltpu.VMEM((count, ROWS), jnp.float32),
-            ],
-        ),
+        in_specs=[pl.BlockSpec(memory_space=pltpu.SMEM)] + [whole] * (len(args) - 1),
+        out_specs=whole if last else [whole] * 3,
         out_shape=done if last else [one, one, acc],
-        compiler_params=pltpu.CompilerParams(vmem_limit_bytes=48 << 20),
+        scratch_shapes=[
+            pltpu.VMEM((2, count, HD), jnp.bfloat16),
+            pltpu.VMEM((2, HD + POS_ROWS, count), jnp.bfloat16),
+            pltpu.VMEM((count, ROWS), jnp.float32),
+        ],
+        input_output_aliases=aliases,
+        compiler_params=pltpu.CompilerParams(vmem_limit_bytes=24 << 20),
         cost_estimate=pl.CostEstimate(
             flops=4 * ROWS * H * count * HD,
             bytes_accessed=8 << 20,
             transcendentals=ROWS * H * count,
         ),
         name="attend",
-    )(warm, *args)
+    )(*args)
 
 
 def turn(value, axis, size, shift):
@@ -172,8 +163,9 @@
     def part(blocks, state, last=False):
         return attend(use_warm, q, pos, blocks, state, last)
 
-    up, down, q = lax.optimization_barrier((up, down, q))
-    held, state = [line, up, down], None
+    state = part([line], None)
+    up, down, state = lax.optimization_barrier((up, down, state))
+    held = [up, down]
     for _ in range(nz // 2 - 2):
         up, down = turn(up, "z", nz, 1), turn(down, "z", nz, -1)
         state = part(held, state)

time: 161 us -> 161 us (level)
  waiting for transfers between devices: 28.4 us -> 33.1 us
  local copies, waits for them, and re-layouts: 9.84 us -> 7.2 us
  blocking collectives: 20.8 us -> 18.3 us
    ppermute x13, waiting for transfers between devices: 13.8 us -> 18.4 us  [turn(): lax.ppermute(value, axis, [(i, (i + shift) % size) for i in range(size)])]
    unnamed x12 -> x8, local copies, waits for them, and re-layouts: 4.48 us -> 1.83 us
    all_to_all x1, blocking collectives: 20.8 us -> 18.3 us  [per_device(): out = lax.all_to_all(out, SECTION, 0, 0)]
    pallas_call x4 -> x5, Pallas kernels: 30 us -> 29.7 us  [attend(): pl.pallas_call(functools.partial(attend_body, shards, state is None, last...]
  transfers between devices with their start and end apart: 15 -> 15, of which waited for: 9 -> 11; matrix products, arithmetic and copies ran while one was open for 3% -> 3% of each run, Pallas kernels for 16% -> 16%
where the time goes in v5:
time: 161 us
  starting transfers between devices  64.6 us (40%)
  waiting for transfers between devices  33.1 us (21%)
  Pallas kernels  29.7 us (18%)
  blocking collectives  18.3 us (11%)
  local copies, waits for them, and re-layouts  7.2 us (4%)
  between operations  6.12 us (4%)
  other arithmetic  1.61 us (1%)
    ppermute x13, starting transfers between devices, turn(): lax.ppermute(value, axis, [(i, (i + shift) % size) for i in range(size)])  50.3 us
    pallas_call x5, Pallas kernels, attend(): pl.pallas_call(functools.partial(attend_body, shards, state is None, last...  29.7 us
    ppermute x13, waiting for transfers between devices, turn(): lax.ppermute(value, axis, [(i, (i + shift) % size) for i in range(size)])  18.4 us
    all_to_all x1, blocking collectives, per_device(): out = lax.all_to_all(out, SECTION, 0, 0)  18.3 us
    all_to_all x1, waiting for transfers between devices, per_device(): pieces = lax.all_to_all(pieces, SECTION, 0, 0)  11.3 us
    all_to_all x1, starting transfers between devices, per_device(): pieces = lax.all_to_all(pieces, SECTION, 0, 0)  10.3 us
    all_to_all x1, starting transfers between devices, per_device(): q = lax.all_to_all(q, SECTION, 0, 0)  3.95 us
    all_to_all x1, waiting for transfers between devices, per_device(): q = lax.all_to_all(q, SECTION, 0, 0)  3.38 us
  transfers between devices with their start and end apart: 15, of which 11 were waited for; matrix products, arithmetic and copies ran while one was open for 3% of the time, Pallas kernels for 16%

profile of v5, /device:TPU:1, one launch (start us, length us, event | category | flops | bytes accessed | tf_op | source)
XLA Modules:
  0.0 160.5 jit_solution(4223898339491279026)
XLA Ops:
  2.6 10.3 %all-to-all-start = ((bf16[16,256,128]{2,1,0:T(8,128)(2,1)}), bf16[16,256,128]{2,1,0:T(8,128)(2,1)S(1)}, u32[]{:S(2)}, u32[]{:S(2)}) async-start(bf16[16,256,128]{2,1,0:T(8,128)(2,1)} %bitcast.12), calls=%async_computation | async-start | bytes 2097152 | tf_op jit(solution)/shard_map/all_to_all | solution.py:151
  17.5 11.3 %all-to-all-done = bf16[16,256,128]{2,1,0:T(8,128)(2,1)S(1)} async-done(((bf16[16,256,128]{2,1,0:T(8,128)(2,1)}), bf16[16,256,128]{2,1,0:T(8,128)(2,1)S(1)}, u32[]{:S(2)}, u32[]{:S(2)}) %all-to-all-start) | async-done | bytes 1048608 | tf_op jit(solution)/shard_map/all_to_all | solution.py:151
  28.9 3.0 %collective-permute-start.1 = (bf16[528,128]{1,0:T(8,128)(2,1)S(1)}, bf16[528,128]{1,0:T(8,128)(2,1)S(1)}, u32[]{:S(2)}, u32[]{:S(2)}) collective-permute-start(bf16[528,128]{1,0:T(8,128)(2,1)S(1)} %get-tuple-element.78), channel_id=1, source_target_pairs={{0,2},{1,3},{2,0},{3,1},{4,6},{5,7},{6,4},{7,5},{8,10},{9,11},{10,... | collective-permute-start | bytes 405512 | tf_op jit(solution)/shard_map/ppermute | solution.py:128
  31.8 2.4 %collective-permute-start = (bf16[528,128]{1,0:T(8,128)(2,1)S(1)}, bf16[528,128]{1,0:T(8,128)(2,1)S(1)}, u32[]{:S(2)}, u32[]{:S(2)}) collective-permute-start(bf16[528,128]{1,0:T(8,128)(2,1)S(1)} %get-tuple-element.78), channel_id=1, source_target_pairs={{0,1},{1,2},{2,3},{3,0},{4,5},{5,6},{6,7},{7,4},{8,9},{9,10},{10,1... | collective-permute-start | bytes 405512 | tf_op jit(solution)/shard_map/ppermute | solution.py:128
  34.3 5.0 %collective-permute-start.2 = (bf16[528,128]{1,0:T(8,128)(2,1)S(1)}, bf16[528,128]{1,0:T(8,128)(2,1)S(1)}, u32[]{:S(2)}, u32[]{:S(2)}) collective-permute-start(bf16[528,128]{1,0:T(8,128)(2,1)S(1)} %get-tuple-element.78), channel_id=1, source_target_pairs={{0,3},{1,0},{2,1},{3,2},{4,7},{5,4},{6,5},{7,6},{8,11},{9,8},{10,9... | collective-permute-start | bytes 405512 | tf_op jit(solution)/shard_map/ppermute | solution.py:128
  43.2 4.7 %collective-permute-done.2 = bf16[528,128]{1,0:T(8,128)(2,1)S(1)} collective-permute-done((bf16[528,128]{1,0:T(8,128)(2,1)S(1)}, bf16[528,128]{1,0:T(8,128)(2,1)S(1)}, u32[]{:S(2)}, u32[]{:S(2)}) %collective-permute-start.2) | collective-permute-done | bytes 135200 | tf_op jit(solution)/shard_map/ppermute | solution.py:128
  48.0 3.9 %all-to-all-start.1 = ((bf16[16,128,256]{2,1,0:T(8,128)(2,1)}), bf16[16,128,256]{2,1,0:T(8,128)(2,1)S(1)}, u32[]{:S(2)}, u32[]{:S(2)}) async-start(bf16[16,128,256]{2,1,0:T(8,128)(2,1)} %bitcast.3), calls=%async_computation.1 | async-start | bytes 2097152 | tf_op jit(solution)/shard_map/all_to_all | solution.py:158
  53.9 8.6 %collective-permute-start.5 = (bf16[4,528,128]{2,1,0:T(8,128)(2,1)S(1)}, bf16[4,528,128]{2,1,0:T(8,128)(2,1)S(1)}, u32[]{:S(2)}, u32[]{:S(2)}) collective-permute-start(bf16[4,528,128]{2,1,0:T(8,128)(2,1)S(1)} %pad_maximum_fusion.refs_3_), channel_id=1, source_target_pairs={{0,28},{4,0},{8,4},{12,8},{16,12},{20,16},{24,20},{28,24},{1,29},{... | collective-permute-start | bytes 1622024 | tf_op jit(solution)/shard_map/ppermute | solution.py:128
  64.4 3.4 %all-to-all-done.1 = bf16[16,128,256]{2,1,0:T(8,128)(2,1)S(1)} async-done(((bf16[16,128,256]{2,1,0:T(8,128)(2,1)}), bf16[16,128,256]{2,1,0:T(8,128)(2,1)S(1)}, u32[]{:S(2)}, u32[]{:S(2)}) %all-to-all-start.1) | async-done | bytes 1048608 | tf_op jit(solution)/shard_map/all_to_all | solution.py:158
  67.8 2.8 %collective-permute-start.3 = (bf16[128,256]{1,0:T(8,128)(2,1)S(1)}, bf16[128,256]{1,0:T(8,128)(2,1)S(1)}, u32[]{:S(2)}, u32[]{:S(2)}) collective-permute-start(bf16[128,256]{1,0:T(8,128)(2,1)S(1)} %dynamic-slice_bitcast_fusion.1), channel_id=1, source_target_pairs={{0,32},{32,0},{1,33},{33,1},{2,34},{34,2},{3,35},{35,3},{4,36},{36... | collective-permute-start | bytes 196616 | tf_op jit(solution)/shard_map/ppermute | solution.py:128
  72.0 4.4 %attend.5 = (f32[16,8,256]{2,1,0:T(8,128)S(1)}, f32[16,8,256]{2,1,0:T(8,128)S(1)}, f32[16,128,256]{2,1,0:T(8,128)S(1)}) custom-call(s32[16]{0:T(128)S(1)} %or_convert_fusion.refs_0_, bf16[16,128,256]{2,1,0:T(8,128)(2,1)S(1)} %bitcast_dynamic-update-slice_fusion.1.refs_1_, f32[1,128]{1,0:T(1,128)S(1)} %get-tuple-element.79.refs_2_, ...), custom_call_target="tpu_custom_call" | custom-call | flops 1073741824 | bytes 8388608 | tf_op jit(solution)/shard_map/attend/pallas_call | solution.py:106
  76.4 2.5 %collective-permute-done.4.refs_3_ = bf16[4,528,128]{2,1,0:T(8,128)(2,1)S(1)} collective-permute-done((bf16[4,528,128]{2,1,0:T(8,128)(2,1)S(1)}, bf16[4,528,128]{2,1,0:T(8,128)(2,1)S(1)}, u32[]{:S(2)}, u32[]{:S(2)}) %collective-permute-start.4) | collective-permute-done | bytes 540704 | tf_op jit(solution)/shard_map/ppermute | solution.py:128
  80.9 6.0 %collective-permute-start.7 = (bf16[4,528,128]{2,1,0:T(8,128)(2,1)S(1)}, bf16[4,528,128]{2,1,0:T(8,128)(2,1)S(1)}, u32[]{:S(2)}, u32[]{:S(2)}) collective-permute-start(bf16[4,528,128]{2,1,0:T(8,128)(2,1)S(1)} %collective-permute-done.5.refs_4_), channel_id=1, source_target_pairs={{0,28},{4,0},{8,4},{12,8},{16,12},{20,16},{24,20},{28,24},{1,29},{... | collective-permute-start | bytes 1622024 | tf_op jit(solution)/shard_map/ppermute | solution.py:128
  86.9 6.9 %attend.6 = (f32[16,8,256]{2,1,0:T(8,128)S(1)}, f32[16,8,256]{2,1,0:T(8,128)S(1)}, f32[16,128,256]{2,1,0:T(8,128)S(1)}) custom-call(s32[16]{0:T(128)S(1)} %or_convert_fusion.refs_0_, bf16[16,128,256]{2,1,0:T(8,128)(2,1)S(1)} %bitcast_dynamic-update-slice_fusion.1.refs_1_, ...), custom_call_target="tpu_custom_call", output_to_operand_aliasing={{0}: (5, {}), {1}: (6, {}), {2}: (7, {})} | custom-call | flops 2147483648 | bytes 8388608 | tf_op jit(solution)/shard_map/attend/pallas_call | solution.py:106
  93.9 3.7 %collective-permute-done.6.refs_3_ = bf16[4,528,128]{2,1,0:T(8,128)(2,1)S(1)} collective-permute-done((bf16[4,528,128]{2,1,0:T(8,128)(2,1)S(1)}, bf16[4,528,128]{2,1,0:T(8,128)(2,1)S(1)}, u32[]{:S(2)}, u32[]{:S(2)}) %collective-permute-start.6) | collective-permute-done | bytes 540704 | tf_op jit(solution)/shard_map/ppermute | solution.py:128
  100.4 5.3 %collective-permute-start.9 = (bf16[4,528,128]{2,1,0:T(8,128)(2,1)S(1)}, bf16[4,528,128]{2,1,0:T(8,128)(2,1)S(1)}, u32[]{:S(2)}, u32[]{:S(2)}) collective-permute-start(bf16[4,528,128]{2,1,0:T(8,128)(2,1)S(1)} %collective-permute-done.7.refs_4_), channel_id=1, source_target_pairs={{0,28},{4,0},{8,4},{12,8},{16,12},{20,16},{24,20},{28,24},{1,29},{... | collective-permute-start | bytes 1622024 | tf_op jit(solution)/shard_map/ppermute | solution.py:128
  105.7 6.9 %attend.7 = (f32[16,8,256]{2,1,0:T(8,128)S(1)}, f32[16,8,256]{2,1,0:T(8,128)S(1)}, f32[16,128,256]{2,1,0:T(8,128)S(1)}) custom-call(s32[16]{0:T(128)S(1)} %or_convert_fusion.refs_0_, bf16[16,128,256]{2,1,0:T(8,128)(2,1)S(1)} %bitcast_dynamic-update-slice_fusion.1.refs_1_, ...), custom_call_target="tpu_custom_call", output_to_operand_aliasing={{0}: (5, {}), {1}: (6, {}), {2}: (7, {})} | custom-call | flops 2147483648 | bytes 8388608 | tf_op jit(solution)/shard_map/attend/pallas_call | solution.py:106
  112.6 2.8 %collective-permute-done.8.refs_3_ = bf16[4,528,128]{2,1,0:T(8,128)(2,1)S(1)} collective-permute-done((bf16[4,528,128]{2,1,0:T(8,128)(2,1)S(1)}, bf16[4,528,128]{2,1,0:T(8,128)(2,1)S(1)}, u32[]{:S(2)}, u32[]{:S(2)}) %collective-permute-start.8) | collective-permute-done | bytes 540704 | tf_op jit(solution)/shard_map/ppermute | solution.py:128
  116.3 3.2 %collective-permute-start.10 = (bf16[2,528,128]{2,1,0:T(8,128)(2,1)S(1)}, bf16[2,528,128]{2,1,0:T(8,128)(2,1)S(1)}, u32[]{:S(2)}, u32[]{:S(2)}) collective-permute-start(bf16[2,528,128]{2,1,0:T(8,128)(2,1)S(1)} %slice.18), channel_id=1, source_target_pairs={{0,4},{4,8},{8,12},{12,16},{16,20},{20,24},{24,28},{28,0},{1,5},{5... | collective-permute-start | bytes 811016 | tf_op jit(solution)/shard_map/ppermute | solution.py:128
  119.5 4.3 %collective-permute-start.11 = (bf16[2,528,128]{2,1,0:T(8,128)(2,1)S(1)}, bf16[2,528,128]{2,1,0:T(8,128)(2,1)S(1)}, u32[]{:S(2)}, u32[]{:S(2)}) collective-permute-start(bf16[2,528,128]{2,1,0:T(8,128)(2,1)S(1)} %slice.19), channel_id=1, source_target_pairs={{0,28},{4,0},{8,4},{12,8},{16,12},{20,16},{24,20},{28,24},{1,29},{... | collective-permute-start | bytes 811016 | tf_op jit(solution)/shard_map/ppermute | solution.py:128
  123.8 6.9 %attend.8 = (f32[16,8,256]{2,1,0:T(8,128)S(1)}, f32[16,8,256]{2,1,0:T(8,128)S(1)}, f32[16,128,256]{2,1,0:T(8,128)S(1)}) custom-call(s32[16]{0:T(128)S(1)} %or_convert_fusion.refs_0_, bf16[16,128,256]{2,1,0:T(8,128)(2,1)S(1)} %bitcast_dynamic-update-slice_fusion.1.refs_1_, ...), custom_call_target="tpu_custom_call", output_to_operand_aliasing={{0}: (5, {}), {1}: (6, {}), {2}: (7, {})} | custom-call | flops 2147483648 | bytes 8388608 | tf_op jit(solution)/shard_map/attend/pallas_call | solution.py:106
  130.7 4.6 %attend.9 = bf16[16,128,256]{2,1,0:T(8,128)(2,1)S(1)} custom-call(s32[16]{0:T(128)S(1)} %or_convert_fusion.refs_0_, bf16[16,128,256]{2,1,0:T(8,128)(2,1)S(1)} %bitcast_dynamic-update-slice_fusion.1.refs_1_, f32[1,128]{1,0:T(1,128)S(1)} %get-tuple-element.79.refs_2_, bf16[2,528,128]{2,1,0:T(8,128)(2,1)S(1)} %collective-permute-done.10.refs_3_, ...), custom_call_target="tpu_custom_call" | custom-call | flops 1073741824 | bytes 8388608 | tf_op jit(solution)/shard_map/attend/pallas_call | solution.py:106
  135.3 4.1 %collective-permute-start.12 = (bf16[128,256]{1,0:T(8,128)(2,1)S(1)}, bf16[128,256]{1,0:T(8,128)(2,1)S(1)}, u32[]{:S(2)}, u32[]{:S(2)}) collective-permute-start(bf16[128,256]{1,0:T(8,128)(2,1)S(1)} %dynamic-slice_bitcast_fusion), channel_id=1, source_target_pairs={{0,32},{32,0},{1,33},{33,1},{2,34},{34,2},{3,35},{35,3},{4,36},{36... | collective-permute-start | bytes 196616 | tf_op jit(solution)/shard_map/ppermute | solution.py:128
  140.3 18.3 %all_to_all.15 = bf16[16,128,256]{2,1,0:T(8,128)(2,1)S(1)} all-to-all(bf16[16,128,256]{2,1,0:T(8,128)(2,1)S(1)} %bitcast_dynamic-update-slice_fusion), channel_id=1, replica_groups=mesh['x'=4,'yl'=2,'core'=2,'z'=8,'yh'=4] {'x','yl','core'}, dimensions={0} | all-to-all | bytes 2097152 | tf_op jit(solution)/shard_map/all_to_all | solution.py:179
  (41 shorter events, 19.2 us)
Async XLA Ops:
  1.2 11.7 %copy-start.1 = (s32[16]{0:T(128)S(1)}, s32[16]{0:T(128)}, u32[]{:S(2)}) copy-start(s32[16]{0:T(128)} %param.7) | copy-start | bytes 196
  1.2 16.3 %copy-start.2 = (s32[128]{0:T(128)S(1)}, s32[128]{0:T(128)}, u32[]{:S(2)}) copy-start(s32[128]{0:T(128)} %param.6) | copy-start | bytes 1540
  1.4 37.9 %copy-start = (bf16[1,128,4096]{2,1,0:T(8,128)(2,1)S(1)}, bf16[1,128,4096]{2,1,0:T(8,128)(2,1)}, u32[]{:S(2)}) copy-start(bf16[1,128,4096]{2,1,0:T(8,128)(2,1)} %param.4) | copy-start | bytes 3145732
  2.6 26.2 %all-to-all-start = ((bf16[16,256,128]{2,1,0:T(8,128)(2,1)}), bf16[16,256,128]{2,1,0:T(8,128)(2,1)S(1)}, u32[]{:S(2)}, u32[]{:S(2)}) async-start(bf16[16,256,128]{2,1,0:T(8,128)(2,1)} %bitcast.12), calls=%async_computation | async-start | bytes 2097152 | tf_op jit(solution)/shard_map/all_to_all | solution.py:151
  28.9 13.1 %collective-permute-start.1 = (bf16[528,128]{1,0:T(8,128)(2,1)S(1)}, bf16[528,128]{1,0:T(8,128)(2,1)S(1)}, u32[]{:S(2)}, u32[]{:S(2)}) collective-permute-start(bf16[528,128]{1,0:T(8,128)(2,1)S(1)} %get-tuple-element.78), channel_id=1, source_target_pairs={{0,2},{1,3},{2,0},{3,1},{4,6},{5,7},{6,4},{7,5},{8,10},{9,11},{10,... | collective-permute-start | bytes 405512 | tf_op jit(solution)/shard_map/ppermute | solution.py:128
  31.8 11.3 %collective-permute-start = (bf16[528,128]{1,0:T(8,128)(2,1)S(1)}, bf16[528,128]{1,0:T(8,128)(2,1)S(1)}, u32[]{:S(2)}, u32[]{:S(2)}) collective-permute-start(bf16[528,128]{1,0:T(8,128)(2,1)S(1)} %get-tuple-element.78), channel_id=1, source_target_pairs={{0,1},{1,2},{2,3},{3,0},{4,5},{5,6},{6,7},{7,4},{8,9},{9,10},{10,1... | collective-permute-start | bytes 405512 | tf_op jit(solution)/shard_map/ppermute | solution.py:128
  34.3 13.6 %collective-permute-start.2 = (bf16[528,128]{1,0:T(8,128)(2,1)S(1)}, bf16[528,128]{1,0:T(8,128)(2,1)S(1)}, u32[]{:S(2)}, u32[]{:S(2)}) collective-permute-start(bf16[528,128]{1,0:T(8,128)(2,1)S(1)} %get-tuple-element.78), channel_id=1, source_target_pairs={{0,3},{1,0},{2,1},{3,2},{4,7},{5,4},{6,5},{7,6},{8,11},{9,8},{10,9... | collective-permute-start | bytes 405512 | tf_op jit(solution)/shard_map/ppermute | solution.py:128
  48.0 19.9 %all-to-all-start.1 = ((bf16[16,128,256]{2,1,0:T(8,128)(2,1)}), bf16[16,128,256]{2,1,0:T(8,128)(2,1)S(1)}, u32[]{:S(2)}, u32[]{:S(2)}) async-start(bf16[16,128,256]{2,1,0:T(8,128)(2,1)} %bitcast.3), calls=%async_computation.1 | async-start | bytes 2097152 | tf_op jit(solution)/shard_map/all_to_all | solution.py:158
  53.9 22.5 %collective-permute-start.5 = (bf16[4,528,128]{2,1,0:T(8,128)(2,1)S(1)}, bf16[4,528,128]{2,1,0:T(8,128)(2,1)S(1)}, u32[]{:S(2)}, u32[]{:S(2)}) collective-permute-start(bf16[4,528,128]{2,1,0:T(8,128)(2,1)S(1)} %pad_maximum_fusion.refs_3_), channel_id=1, source_target_pairs={{0,28},{4,0},{8,4},{12,8},{16,12},{20,16},{24,20},{28,24},{1,29},{... | collective-permute-start | bytes 1622024 | tf_op jit(solution)/shard_map/ppermute | solution.py:128
  62.5 16.5 %collective-permute-start.4 = (bf16[4,528,128]{2,1,0:T(8,128)(2,1)S(1)}, bf16[4,528,128]{2,1,0:T(8,128)(2,1)S(1)}, u32[]{:S(2)}, u32[]{:S(2)}) collective-permute-start(bf16[4,528,128]{2,1,0:T(8,128)(2,1)S(1)} %pad_maximum_fusion.refs_3_), channel_id=1, source_target_pairs={{0,4},{4,8},{8,12},{12,16},{16,20},{20,24},{24,28},{28,0},{1,5},{5... | collective-permute-start | bytes 1622024 | tf_op jit(solution)/shard_map/ppermute | solution.py:128
  67.8 4.1 %collective-permute-start.3 = (bf16[128,256]{1,0:T(8,128)(2,1)S(1)}, bf16[128,256]{1,0:T(8,128)(2,1)S(1)}, u32[]{:S(2)}, u32[]{:S(2)}) collective-permute-start(bf16[128,256]{1,0:T(8,128)(2,1)S(1)} %dynamic-slice_bitcast_fusion.1), channel_id=1, source_target_pairs={{0,32},{32,0},{1,33},{33,1},{2,34},{34,2},{3,35},{35,3},{4,36},{36... | collective-permute-start | bytes 196616 | tf_op jit(solution)/shard_map/ppermute | solution.py:128
  79.0 18.5 %collective-permute-start.6 = (bf16[4,528,128]{2,1,0:T(8,128)(2,1)S(1)}, bf16[4,528,128]{2,1,0:T(8,128)(2,1)S(1)}, u32[]{:S(2)}, u32[]{:S(2)}) collective-permute-start(bf16[4,528,128]{2,1,0:T(8,128)(2,1)S(1)} %collective-permute-done.4.refs_3_), channel_id=1, source_target_pairs={{0,4},{4,8},{8,12},{12,16},{16,20},{20,24},{24,28},{28,0},{1,5},{5... | collective-permute-start | bytes 1622024 | tf_op jit(solution)/shard_map/ppermute | solution.py:128
  80.9 17.6 %collective-permute-start.7 = (bf16[4,528,128]{2,1,0:T(8,128)(2,1)S(1)}, bf16[4,528,128]{2,1,0:T(8,128)(2,1)S(1)}, u32[]{:S(2)}, u32[]{:S(2)}) collective-permute-start(bf16[4,528,128]{2,1,0:T(8,128)(2,1)S(1)} %collective-permute-done.5.refs_4_), channel_id=1, source_target_pairs={{0,28},{4,0},{8,4},{12,8},{16,12},{20,16},{24,20},{28,24},{1,29},{... | collective-permute-start | bytes 1622024 | tf_op jit(solution)/shard_map/ppermute | solution.py:128
  98.5 17.0 %collective-permute-start.8 = (bf16[4,528,128]{2,1,0:T(8,128)(2,1)S(1)}, bf16[4,528,128]{2,1,0:T(8,128)(2,1)S(1)}, u32[]{:S(2)}, u32[]{:S(2)}) collective-permute-start(bf16[4,528,128]{2,1,0:T(8,128)(2,1)S(1)} %collective-permute-done.6.refs_3_), channel_id=1, source_target_pairs={{0,4},{4,8},{8,12},{12,16},{16,20},{20,24},{24,28},{28,0},{1,5},{5... | collective-permute-start | bytes 1622024 | tf_op jit(solution)/shard_map/ppermute | solution.py:128
  100.4 15.9 %collective-permute-start.9 = (bf16[4,528,128]{2,1,0:T(8,128)(2,1)S(1)}, bf16[4,528,128]{2,1,0:T(8,128)(2,1)S(1)}, u32[]{:S(2)}, u32[]{:S(2)}) collective-permute-start(bf16[4,528,128]{2,1,0:T(8,128)(2,1)S(1)} %collective-permute-done.7.refs_4_), channel_id=1, source_target_pairs={{0,28},{4,0},{8,4},{12,8},{16,12},{20,16},{24,20},{28,24},{1,29},{... | collective-permute-start | bytes 1622024 | tf_op jit(solution)/shard_map/ppermute | solution.py:128
  116.3 14.4 %collective-permute-start.10 = (bf16[2,528,128]{2,1,0:T(8,128)(2,1)S(1)}, bf16[2,528,128]{2,1,0:T(8,128)(2,1)S(1)}, u32[]{:S(2)}, u32[]{:S(2)}) collective-permute-start(bf16[2,528,128]{2,1,0:T(8,128)(2,1)S(1)} %slice.18), channel_id=1, source_target_pairs={{0,4},{4,8},{8,12},{12,16},{16,20},{20,24},{24,28},{28,0},{1,5},{5... | collective-permute-start | bytes 811016 | tf_op jit(solution)/shard_map/ppermute | solution.py:128
  119.5 11.2 %collective-permute-start.11 = (bf16[2,528,128]{2,1,0:T(8,128)(2,1)S(1)}, bf16[2,528,128]{2,1,0:T(8,128)(2,1)S(1)}, u32[]{:S(2)}, u32[]{:S(2)}) collective-permute-start(bf16[2,528,128]{2,1,0:T(8,128)(2,1)S(1)} %slice.19), channel_id=1, source_target_pairs={{0,28},{4,0},{8,4},{12,8},{16,12},{20,16},{24,20},{28,24},{1,29},{... | collective-permute-start | bytes 811016 | tf_op jit(solution)/shard_map/ppermute | solution.py:128
  135.3 4.9 %collective-permute-start.12 = (bf16[128,256]{1,0:T(8,128)(2,1)S(1)}, bf16[128,256]{1,0:T(8,128)(2,1)S(1)}, u32[]{:S(2)}, u32[]{:S(2)}) collective-permute-start(bf16[128,256]{1,0:T(8,128)(2,1)S(1)} %dynamic-slice_bitcast_fusion), channel_id=1, source_target_pairs={{0,32},{32,0},{1,33},{33,1},{2,34},{34,2},{3,35},{35,3},{4,36},{36... | collective-permute-start | bytes 196616 | tf_op jit(solution)/shard_map/ppermute | solution.py:128

commit v6 on v5

--- a/solution.py
+++ b/solution.py
@@ -18,6 +18,9 @@
 WIDE = HEADS * HD
 SLABS = 8
 POS_ROWS = 16
+PART = 2 * ROWS
+LINE_ROWS = 3 * PART + 2 * POS_ROWS
+HANDED_ROWS = 2 * PART + POS_ROWS
 MASKED = -1e30
 SCALE = 1.4426950408889634 / HD**0.5
 SECTION = ("x", "yl", "core")
@@ -25,7 +28,7 @@
 
 def attend_body(shards, first, last, *refs):
     it = iter(refs)
-    warm_ref, q_ref, pos_ref = next(it), next(it), next(it)
+    info, q_ref, pos_ref = next(it), next(it), next(it)
     blocks = [next(it) for _ in shards]
     if not first:
         m_in, l_in, a_in = next(it), next(it), next(it)
@@ -35,12 +38,13 @@
     row = lax.broadcasted_iota(jnp.int32, (BLOCK, ROWS), 0).astype(jnp.float32)
     at = 0
     for n, ref in zip(shards, blocks):
+        place = LAYERS + (0 if ref.shape[1] == LINE_ROWS else 3)
+        starts = [pl.multiple_of(info[place + i], POS_ROWS) for i in range(3)]
         for i in range(n):
             for source in range(2):
-                base = source * 2 * ROWS
-                k[source, at : at + ROWS, :] = ref[i, base : base + ROWS]
-                v[source, :HD, at : at + ROWS] = ref[i, base + ROWS : base + 2 * ROWS]
-            ids = ref[i, 4 * ROWS : 4 * ROWS + POS_ROWS].astype(jnp.float32)
+                k[source, at : at + ROWS, :] = ref[i, pl.ds(starts[source], ROWS), :]
+                v[source, :HD, at : at + ROWS] = ref[i, pl.ds(starts[source] + ROWS, ROWS), :]
+            ids = ref[i, pl.ds(starts[2], POS_ROWS), :].astype(jnp.float32)
             for part in range(ROWS // BLOCK):
                 key_pos = ids[0:1, part * BLOCK : part * BLOCK + 1] * BLOCK + row
                 rows = slice(at + part * BLOCK, at + (part + 1) * BLOCK)
@@ -52,7 +56,7 @@
     def scores(j):
         q = jnp.concatenate([q_ref[j, :, h * HD : (h + 1) * HD] for h in range(HEADS)], axis=0)
         return lax.dot_general(
-            k[warm_ref[j]], q, (((1,), (1,)), ((), ())), preferred_element_type=jnp.float32
+            k[info[j]], q, (((1,), (1,)), ((), ())), preferred_element_type=jnp.float32
         )
 
     def absorb(j, s):
@@ -63,7 +67,7 @@
             m = jnp.maximum(m_old, m)
         w = jnp.exp2((s - m) * SCALE).astype(jnp.bfloat16)
         o = lax.dot_general(
-            v[warm_ref[j]], w, (((1,), (0,)), ((), ())), preferred_element_type=jnp.float32
+            v[info[j]], w, (((1,), (0,)), ((), ())), preferred_element_type=jnp.float32
         )
         acc, den = o[:HD], o[HD : HD + 8]
         if not first:
@@ -90,10 +94,10 @@
             s = ahead
 
 
-def attend(warm, q, pos, blocks, state, last):
+def attend(info, q, pos, blocks, state, last):
     shards = tuple(b.shape[0] for b in blocks)
     count = sum(shards) * ROWS
-    args = [warm, q, pos, *blocks]
+    args = [info, q, pos, *blocks]
     aliases = {}
     if state is not None:
         if not last:
@@ -128,6 +132,56 @@
     return lax.ppermute(value, axis, [(i, (i + shift) % size) for i in range(size)])
 
 
+def packed(kv):
+    def body(kv_ref, out_ref):
+        for h in range(KVH):
+            k = kv_ref[:, h * HD : (h + 1) * HD]
+            v = kv_ref[:, (KVH + h) * HD : (KVH + h + 1) * HD].T
+            for yl in range(LAYERS // KVH // 2):
+                out_ref[h * 4 + yl * 2] = k
+                out_ref[h * 4 + yl * 2 + 1] = v
+
+    return pl.pallas_call(
+        body,
+        in_specs=[pl.BlockSpec(memory_space=pltpu.VMEM)],
+        out_specs=pl.BlockSpec(memory_space=pltpu.VMEM),
+        out_shape=jax.ShapeDtypeStruct((LAYERS, ROWS, HD), jnp.bfloat16),
+        name="pack",
+    )(kv)
+
+
+def joined(core, mine, theirs):
+    def body(core_ref, mine_ref, theirs_ref, out_ref):
+        def fill(k_ref, v_ref):
+            for i in range(mine.shape[0]):
+                for s in range(3):
+                    rows = slice(s * ROWS, (s + 1) * ROWS)
+                    at = POS_ROWS + s * PART
+                    out_ref[i, at : at + ROWS] = k_ref[i, rows]
+                    out_ref[i, at + ROWS : at + PART] = v_ref[i, rows]
+
+        for i in range(mine.shape[0]):
+            out_ref[i, :POS_ROWS] = mine_ref[i, 3 * ROWS :]
+            out_ref[i, LINE_ROWS - POS_ROWS :] = mine_ref[i, 3 * ROWS :]
+
+        @pl.when(core_ref[0] == 0)
+        def _():
+            fill(mine_ref, theirs_ref)
+
+        @pl.when(core_ref[0] != 0)
+        def _():
+            fill(theirs_ref, mine_ref)
+
+    whole = pl.BlockSpec(memory_space=pltpu.VMEM)
+    return pl.pallas_call(
+        body,
+        in_specs=[pl.BlockSpec(memory_space=pltpu.SMEM), whole, whole],
+        out_specs=whole,
+        out_shape=jax.ShapeDtypeStruct((mine.shape[0], LINE_ROWS, HD), jnp.bfloat16),
+        name="join",
+    )(core.astype(jnp.int32).reshape(1), mine, theirs)
+
+
 def pick(slabs, index):
     return lax.dynamic_index_in_dim(slabs, index, 0, keepdims=False)
 
@@ -143,39 +197,53 @@
     ids = jnp.arange(LAYERS, dtype=jnp.int32)
     holder = jnp.sum(jnp.where(layer_of_section[None, :] == ids[:, None], ids[None, :], 0), axis=1)
     warm, other_warm = pick(holder, core), pick(holder, 1 - core)
-    kv = key_values[0].reshape(ROWS, 2, KVH, HD)
-    heads = jnp.stack([kv[:, 0].transpose(1, 0, 2), kv[:, 1].transpose(1, 2, 0)], axis=1)
-    pieces = jnp.broadcast_to(
-        heads.reshape(KVH, 1, 2 * ROWS, HD), (KVH, LAYERS // KVH, 2 * ROWS, HD)
-    ).reshape(LAYERS, 2 * ROWS, HD)
+    pieces = packed(key_values[0].reshape(ROWS, 2 * KVH * HD))
     pieces = lax.all_to_all(pieces, SECTION, 0, 0)
     block_ids = jnp.broadcast_to((token_pos // BLOCK).astype(jnp.bfloat16)[None, :], (POS_ROWS, ROWS))
-    shard = jnp.concatenate([pick(pieces, holder[LAYERS - 1]), pick(pieces, warm), block_ids], axis=0)
-    line = jnp.stack([shard] + [turn(shard, "yh", nyh, shift) for shift in range(1, nyh)])
-    q = queries[0].reshape(ROWS, LAYERS, WIDE).transpose(1, 0, 2)
-    q, line = lax.optimization_barrier((q, line))
-    up, down = turn(line, "z", nz, 1), turn(line, "z", nz, -1)
+    wanted = [holder[0], holder[LAYERS - 1], holder[1]]
+    shard = jnp.concatenate([pick(pieces, index) for index in wanted] + [block_ids], axis=0)
+    mine = jnp.stack([shard] + [turn(shard, "yh", nyh, shift) for shift in range(1, nyh)])
+    theirs = turn(mine, "core", 2, 1)
+    line = joined(core, mine, theirs)
+    q, line = lax.optimization_barrier((queries[0], line))
+    q = q.reshape(ROWS, LAYERS, WIDE).transpose(1, 0, 2)
+
+    pairs = [(z, (z + 1) % nz) for z in range(nz)] + [(nz + z, nz + (z - 1) % nz) for z in range(nz)]
+
+    def onward(value):
+        return lax.ppermute(value, ("core", "z"), pairs)
+
+    def handed(value):
+        start = (1 - core) * (PART + POS_ROWS)
+        return turn(lax.dynamic_slice_in_dim(value, start, HANDED_ROWS, axis=1), "core", 2, 1)
+
+    arrived = onward(line)
     q = lax.all_to_all(q, SECTION, 0, 0)
     q = swap(q, other_warm)
     use_warm = ((ids == warm) | (ids == other_warm)).astype(jnp.int32)
+    top_row = POS_ROWS + PART
+    whole_rows = [top_row, POS_ROWS + 2 * PART * core, 0]
+    handed_rows = [(1 - core) * top_row, (1 - core) * POS_ROWS + core * PART, core * 2 * PART]
+    info = jnp.concatenate([use_warm, jnp.stack(whole_rows + handed_rows).astype(jnp.int32)])
     pos = token_pos.astype(jnp.float32)[None, :]
 
     def part(blocks, state, last=False):
-        return attend(use_warm, q, pos, blocks, state, last)
-
-    state = part([line], None)
-    up, down, state = lax.optimization_barrier((up, down, state))
-    held = [up, down]
-    for _ in range(nz // 2 - 2):
-        up, down = turn(up, "z", nz, 1), turn(down, "z", nz, -1)
+        return attend(info, q, pos, blocks, state, last)
+
+    held, state = [line], None
+    half = nyh // 2
+    for step in range(nz // 2 - 1):
+        if step < nz // 2 - 2:
+            coming = onward(arrived)
+        else:
+            coming = onward(lax.dynamic_slice_in_dim(arrived, core * half, half, axis=0))
+        passed = handed(arrived)
         state = part(held, state)
-        up, down, state = lax.optimization_barrier((up, down, state))
-        held = [up, down]
-    half = nyh // 2
-    last_up, last_down = turn(up[:half], "z", nz, 1), turn(down[half:], "z", nz, -1)
+        held = [arrived, passed]
+        arrived, held, state = lax.optimization_barrier((coming, held, state))
+    passed = handed(arrived)
     state = part(held, state)
-    last_up, last_down, state = lax.optimization_barrier((last_up, last_down, state))
-    out = swap(part([last_up, last_down], state, True), other_warm)
+    out = swap(part([arrived, passed], state, True), other_warm)
     out = lax.all_to_all(out, SECTION, 0, 0)
     return out.transpose(1, 0, 2).reshape(1, ROWS, H * HD)
 

time: 161 us -> 165 us (1.025)
  waiting for transfers between devices: 33.1 us -> 19.5 us
  local copies, waits for them, and re-layouts: 7.2 us -> 16.1 us
  Pallas kernels: 29.7 us -> 35.6 us
  blocking collectives: 18.3 us -> 21 us
  starting transfers between devices: 64.6 us -> 62.5 us
  between operations: 6.12 us -> 7.79 us
    ppermute x13 -> x10, starting transfers between devices: 50.3 us -> 28.1 us  [turn(): lax.ppermute(value, axis, [(i, (i + shift) % size) for i in range(size)])]
    ppermute x0 -> x4, starting transfers between devices: none -> 20.4 us  [onward(): return lax.ppermute(value, ('core', 'z'), pairs)]
    ppermute x13 -> x10, waiting for transfers between devices: 18.4 us -> 6.71 us  [turn(): lax.ppermute(value, axis, [(i, (i + shift) % size) for i in range(size)])]
    ppermute x0 -> x4, waiting for transfers between devices: none -> 9.27 us  [onward(): return lax.ppermute(value, ('core', 'z'), pairs)]
    all_to_all x1, waiting for transfers between devices: 11.3 us -> 3.54 us  [per_device(): pieces = lax.all_to_all(pieces, SECTION, 0, 0)]
    unnamed x8 -> x24, local copies, waits for them, and re-layouts: 1.83 us -> 7.09 us
    dynamic_slice x0 -> x5, local copies, waits for them, and re-layouts: none -> 4.9 us  [the longest x4 3.87 us: handed(): lax.dynamic_slice_in_dim(value, start, HANDED_ROWS, axis=1)]
    pallas_call x0 -> x2, Pallas kernels: none -> 3.94 us  [the longest x1 2.11 us: joined(): pl.pallas_call(body, in_specs=[pl.BlockSpec(memory_space=pltpu.SMEM), who...]
  transfers between devices with their start and end apart: 15 -> 16, of which waited for: 11 -> 6; matrix products, arithmetic and copies ran while one was open for 3% -> 4% of each run, Pallas kernels for 16% -> 17%
where the time goes in v6:
time: 165 us; the launch traced here: 164 us
  starting transfers between devices  62.5 us (38%)
  Pallas kernels  35.6 us (22%)
  blocking collectives  21 us (13%)
  waiting for transfers between devices  19.5 us (12%)
  local copies, waits for them, and re-layouts  16.1 us (10%)
  between operations  7.79 us (5%)
    pallas_call x5, Pallas kernels, attend(): pl.pallas_call(functools.partial(attend_body, shards, state is None, last...  31.7 us
    ppermute x10, starting transfers between devices, turn(): lax.ppermute(value, axis, [(i, (i + shift) % size) for i in range(size)])  28.1 us
    all_to_all x1, blocking collectives, per_device(): out = lax.all_to_all(out, SECTION, 0, 0)  21 us
    ppermute x4, starting transfers between devices, onward(): return lax.ppermute(value, ('core', 'z'), pairs)  20.4 us
    all_to_all x1, starting transfers between devices, per_device(): pieces = lax.all_to_all(pieces, SECTION, 0, 0)  10.2 us
    ppermute x4, waiting for transfers between devices, onward(): return lax.ppermute(value, ('core', 'z'), pairs)  9.27 us
    unnamed x24, local copies, waits for them, and re-layouts  7.09 us
    ppermute x10, waiting for transfers between devices, turn(): lax.ppermute(value, axis, [(i, (i + shift) % size) for i in range(size)])  6.71 us
  transfers between devices with their start and end apart: 16, of which 6 were waited for; matrix products, arithmetic and copies ran while one was open for 4% of the time, Pallas kernels for 17%

profile of v6, /device:TPU:1, one launch (start us, length us, event | category | flops | bytes accessed | tf_op | source)
XLA Modules:
  0.0 164.1 jit_solution(14852060897781120274)
XLA Ops:
  3.6 10.2 %all-to-all-start = ((bf16[16,128,128]{2,1,0:T(8,128)(2,1)}), bf16[16,128,128]{2,1,0:T(8,128)(2,1)S(1)}, u32[]{:S(2)}, u32[]{:S(2)}) async-start(bf16[16,128,128]{2,1,0:T(8,128)(2,1)} %pack.1), calls=%async_computation | async-start | bytes 1048576 | tf_op jit(solution)/shard_map/all_to_all | solution.py:201
  20.2 3.5 %all-to-all-done = bf16[16,128,128]{2,1,0:T(8,128)(2,1)S(1)} async-done(((bf16[16,128,128]{2,1,0:T(8,128)(2,1)}), bf16[16,128,128]{2,1,0:T(8,128)(2,1)S(1)}, u32[]{:S(2)}, u32[]{:S(2)}) %all-to-all-start) | async-done | bytes 524320 | tf_op jit(solution)/shard_map/all_to_all | solution.py:201
  23.8 3.1 %collective-permute-start.1 = (bf16[400,128]{1,0:T(8,128)(2,1)S(1)}, bf16[400,128]{1,0:T(8,128)(2,1)S(1)}, u32[]{:S(2)}, u32[]{:S(2)}) collective-permute-start(bf16[400,128]{1,0:T(8,128)(2,1)S(1)} %get-tuple-element.73), channel_id=1, source_target_pairs={{0,2},{1,3},{2,0},{3,1},{4,6},{5,7},{6,4},{7,5},{8,10},{9,11},{10,... | collective-permute-start | bytes 307208 | tf_op jit(solution)/shard_map/ppermute | solution.py:132
  26.8 2.4 %collective-permute-start = (bf16[400,128]{1,0:T(8,128)(2,1)S(1)}, bf16[400,128]{1,0:T(8,128)(2,1)S(1)}, u32[]{:S(2)}, u32[]{:S(2)}) collective-permute-start(bf16[400,128]{1,0:T(8,128)(2,1)S(1)} %get-tuple-element.73), channel_id=1, source_target_pairs={{0,1},{1,2},{2,3},{3,0},{4,5},{5,6},{6,7},{7,4},{8,9},{9,10},{10,1... | collective-permute-start | bytes 307208 | tf_op jit(solution)/shard_map/ppermute | solution.py:132
  29.3 5.0 %collective-permute-start.2 = (bf16[400,128]{1,0:T(8,128)(2,1)S(1)}, bf16[400,128]{1,0:T(8,128)(2,1)S(1)}, u32[]{:S(2)}, u32[]{:S(2)}) collective-permute-start(bf16[400,128]{1,0:T(8,128)(2,1)S(1)} %get-tuple-element.73), channel_id=1, source_target_pairs={{0,3},{1,0},{2,1},{3,2},{4,7},{5,4},{6,5},{7,6},{8,11},{9,8},{10,9... | collective-permute-start | bytes 307208 | tf_op jit(solution)/shard_map/ppermute | solution.py:132
  35.2 4.3 %collective-permute-done.2 = bf16[400,128]{1,0:T(8,128)(2,1)S(1)} collective-permute-done((bf16[400,128]{1,0:T(8,128)(2,1)S(1)}, bf16[400,128]{1,0:T(8,128)(2,1)S(1)}, u32[]{:S(2)}, u32[]{:S(2)}) %collective-permute-start.2) | collective-permute-done | bytes 102432 | tf_op jit(solution)/shard_map/ppermute | solution.py:132
  39.5 3.7 %collective-permute-start.3 = (bf16[4,400,128]{2,1,0:T(8,128)(2,1)S(1)}, bf16[4,400,128]{2,1,0:T(8,128)(2,1)S(1)}, u32[]{:S(2)}, u32[]{:S(2)}) collective-permute-start(bf16[4,400,128]{2,1,0:T(8,128)(2,1)S(1)} %pad_maximum_fusion.mine_ref), channel_id=1, source_target_pairs={{0,32},{32,0},{1,33},{33,1},{2,34},{34,2},{3,35},{35,3},{4,36},{36... | collective-permute-start | bytes 1228808 | tf_op jit(solution)/shard_map/ppermute | solution.py:132
  45.3 2.1 %join.1.refs_3_ = bf16[4,800,128]{2,1,0:T(8,128)(2,1)} custom-call(s32[1]{0:T(128)} %bitcast.7.core_ref, bf16[4,400,128]{2,1,0:T(8,128)(2,1)} %copy-done.6, bf16[4,400,128]{2,1,0:T(8,128)(2,1)} %copy-done.8), custom_call_target="tpu_custom_call" | custom-call | tf_op jit(solution)/shard_map/join/pallas_call | solution.py:176
  48.7 3.8 %all-to-all-start.1 = ((bf16[16,128,256]{2,1,0:T(8,128)(2,1)}), bf16[16,128,256]{2,1,0:T(8,128)(2,1)S(1)}, u32[]{:S(2)}, u32[]{:S(2)}) async-start(bf16[16,128,256]{2,1,0:T(8,128)(2,1)} %bitcast.19), calls=%async_computation.1 | async-start | bytes 2097152 | tf_op jit(solution)/shard_map/all_to_all | solution.py:221
  52.6 9.7 %collective-permute-start.5 = (bf16[4,800,128]{2,1,0:T(8,128)(2,1)S(1)}, bf16[4,800,128]{2,1,0:T(8,128)(2,1)}, u32[]{:S(2)}, u32[]{:S(2)}) collective-permute-start(bf16[4,800,128]{2,1,0:T(8,128)(2,1)S(1)} %copy-done.2), channel_id=1, source_target_pairs={{0,4},{4,8},{8,12},{12,16},{16,20},{20,24},{24,28},{28,0},{32,60},... | collective-permute-start | bytes 2457608 | tf_op jit(solution)/shard_map/ppermute | solution.py:214
  62.2 9.3 %collective-permute-done.5.refs_3_ = bf16[4,800,128]{2,1,0:T(8,128)(2,1)} collective-permute-done((bf16[4,800,128]{2,1,0:T(8,128)(2,1)S(1)}, bf16[4,800,128]{2,1,0:T(8,128)(2,1)}, u32[]{:S(2)}, u32[]{:S(2)}) %collective-permute-start.5) | collective-permute-done | bytes 819232 | tf_op jit(solution)/shard_map/ppermute | solution.py:214
  71.5 5.1 %collective-permute-start.6 = (bf16[4,800,128]{2,1,0:T(8,128)(2,1)}, bf16[4,800,128]{2,1,0:T(8,128)(2,1)}, u32[]{:S(2)}, u32[]{:S(2)}) collective-permute-start(bf16[4,800,128]{2,1,0:T(8,128)(2,1)} %collective-permute-done.5.refs_3_), channel_id=1, source_target_pairs={{0,4},{4,8},{8,12},{12,16},{16,20},{20,24},{24,28},{28,0},{32,60},... | collective-permute-start | bytes 2457608 | tf_op jit(solution)/shard_map/ppermute | solution.py:214
  82.4 2.4 %collective-permute-start.4 = (bf16[128,256]{1,0:T(8,128)(2,1)S(1)}, bf16[128,256]{1,0:T(8,128)(2,1)S(1)}, u32[]{:S(2)}, u32[]{:S(2)}) collective-permute-start(bf16[128,256]{1,0:T(8,128)(2,1)S(1)} %dynamic-slice_bitcast_fusion.1), channel_id=1, source_target_pairs={{0,32},{32,0},{1,33},{33,1},{2,34},{34,2},{3,35},{35,3},{4,36},{36... | collective-permute-start | bytes 196616 | tf_op jit(solution)/shard_map/ppermute | solution.py:132
  87.4 4.4 %attend.5 = (f32[16,8,256]{2,1,0:T(8,128)S(1)}, f32[16,8,256]{2,1,0:T(8,128)S(1)}, f32[16,128,256]{2,1,0:T(8,128)S(1)}) custom-call(s32[22]{0:T(128)S(1)} %concatenate.6.refs_0_, bf16[16,128,256]{2,1,0:T(8,128)(2,1)S(1)} %bitcast_dynamic-update-slice_fusion.1.refs_1_, f32[1,128]{1,0:T(1,128)S(1)} %get-tuple-element.74.refs_2_, bf16[4,800,128]{2,1,0:T(8,128)(2,1)S(1)} %copy-done.3), custom_call_target="tpu_custom_call" | custom-call | flops 1073741824 | bytes 8388608 | tf_op jit(solution)/shard_map/attend/pallas_call | solution.py:110
  91.8 2.8 %collective-permute-start.8 = (bf16[4,800,128]{2,1,0:T(8,128)(2,1)}, bf16[4,800,128]{2,1,0:T(8,128)(2,1)S(1)}, u32[]{:S(2)}, u32[]{:S(2)}) collective-permute-start(bf16[4,800,128]{2,1,0:T(8,128)(2,1)} %collective-permute-done.6.refs_3_), channel_id=1, source_target_pairs={{0,4},{4,8},{8,12},{12,16},{16,20},{20,24},{24,28},{28,0},{32,60},... | collective-permute-start | bytes 2457608 | tf_op jit(solution)/shard_map/ppermute | solution.py:214
  97.6 7.7 %attend.6 = (f32[16,8,256]{2,1,0:T(8,128)S(1)}, f32[16,8,256]{2,1,0:T(8,128)S(1)}, f32[16,128,256]{2,1,0:T(8,128)S(1)}) custom-call(s32[22]{0:T(128)S(1)} %concatenate.6.refs_0_, bf16[16,128,256]{2,1,0:T(8,128)(2,1)S(1)} %bitcast_dynamic-update-slice_fusion.1.refs_1_, ...), custom_call_target="tpu_custom_call", output_to_operand_aliasing={{0}: (5, {}), {1}: (6, {}), {2}: (7, {})} | custom-call | flops 2147483648 | bytes 8388608 | tf_op jit(solution)/shard_map/attend/pallas_call | solution.py:110
  107.9 3.2 %collective-permute-start.11 = (bf16[4,528,128]{2,1,0:T(8,128)(2,1)}, bf16[4,528,128]{2,1,0:T(8,128)(2,1)}, u32[]{:S(2)}, u32[]{:S(2)}) collective-permute-start(bf16[4,528,128]{2,1,0:T(8,128)(2,1)} %constant_dynamic-slice_fusion.1), channel_id=1, source_target_pairs={{0,32},{32,0},{1,33},{33,1},{2,34},{34,2},{3,35},{35,3},{4,36},{36... | collective-permute-start | bytes 1622024 | tf_op jit(solution)/shard_map/ppermute | solution.py:132
  112.2 2.8 %collective-permute-start.10 = (bf16[2,800,128]{2,1,0:T(8,128)(2,1)S(1)}, bf16[2,800,128]{2,1,0:T(8,128)(2,1)S(1)}, u32[]{:S(2)}, u32[]{:S(2)}) collective-permute-start(bf16[2,800,128]{2,1,0:T(8,128)(2,1)S(1)} %constant_dynamic-slice_fusion.2), channel_id=1, source_target_pairs={{0,4},{4,8},{8,12},{12,16},{16,20},{20,24},{24,28},{28,0},{32,60},... | collective-permute-start | bytes 1228808 | tf_op jit(solution)/shard_map/ppermute | solution.py:214
  116.0 7.5 %attend.7 = (f32[16,8,256]{2,1,0:T(8,128)S(1)}, f32[16,8,256]{2,1,0:T(8,128)S(1)}, f32[16,128,256]{2,1,0:T(8,128)S(1)}) custom-call(s32[22]{0:T(128)S(1)} %concatenate.6.refs_0_, bf16[16,128,256]{2,1,0:T(8,128)(2,1)S(1)} %bitcast_dynamic-update-slice_fusion.1.refs_1_, ...), custom_call_target="tpu_custom_call", output_to_operand_aliasing={{0}: (5, {}), {1}: (6, {}), {2}: (7, {})} | custom-call | flops 2147483648 | bytes 8388608 | tf_op jit(solution)/shard_map/attend/pallas_call | solution.py:110
  123.6 2.1 %collective-permute-start.12 = (bf16[2,528,128]{2,1,0:T(8,128)(2,1)S(1)}, bf16[2,528,128]{2,1,0:T(8,128)(2,1)S(1)}, u32[]{:S(2)}, u32[]{:S(2)}) collective-permute-start(bf16[2,528,128]{2,1,0:T(8,128)(2,1)S(1)} %constant_dynamic-slice_fusion), channel_id=1, source_target_pairs={{0,32},{32,0},{1,33},{33,1},{2,34},{34,2},{3,35},{35,3},{4,36},{36... | collective-permute-start | bytes 811016 | tf_op jit(solution)/shard_map/ppermute | solution.py:132
  125.7 7.4 %attend.8 = (f32[16,8,256]{2,1,0:T(8,128)S(1)}, f32[16,8,256]{2,1,0:T(8,128)S(1)}, f32[16,128,256]{2,1,0:T(8,128)S(1)}) custom-call(s32[22]{0:T(128)S(1)} %concatenate.6.refs_0_, bf16[16,128,256]{2,1,0:T(8,128)(2,1)S(1)} %bitcast_dynamic-update-slice_fusion.1.refs_1_, ...), custom_call_target="tpu_custom_call", output_to_operand_aliasing={{0}: (5, {}), {1}: (6, {}), {2}: (7, {})} | custom-call | flops 2147483648 | bytes 8388608 | tf_op jit(solution)/shard_map/attend/pallas_call | solution.py:110
  133.2 4.6 %attend.9 = bf16[16,128,256]{2,1,0:T(8,128)(2,1)S(1)} custom-call(s32[22]{0:T(128)S(1)} %concatenate.6.refs_0_, bf16[16,128,256]{2,1,0:T(8,128)(2,1)S(1)} %bitcast_dynamic-update-slice_fusion.1.refs_1_, f32[1,128]{1,0:T(1,128)S(1)} %get-tuple-element.74.refs_2_, bf16[2,800,128]{2,1,0:T(8,128)(2,1)S(1)} %collective-permute-done.10.refs_3_, ...), custom_call_target="tpu_custom_call" | custom-call | flops 1073741824 | bytes 8388608 | tf_op jit(solution)/shard_map/attend/pallas_call | solution.py:110
  137.8 2.4 %collective-permute-start.13 = (bf16[128,256]{1,0:T(8,128)(2,1)S(1)}, bf16[128,256]{1,0:T(8,128)(2,1)S(1)}, u32[]{:S(2)}, u32[]{:S(2)}) collective-permute-start(bf16[128,256]{1,0:T(8,128)(2,1)S(1)} %dynamic-slice_bitcast_fusion), channel_id=1, source_target_pairs={{0,32},{32,0},{1,33},{33,1},{2,34},{34,2},{3,35},{35,3},{4,36},{36... | collective-permute-start | bytes 196616 | tf_op jit(solution)/shard_map/ppermute | solution.py:132
  141.1 21.0 %all_to_all.15 = bf16[16,128,256]{2,1,0:T(8,128)(2,1)S(1)} all-to-all(bf16[16,128,256]{2,1,0:T(8,128)(2,1)S(1)} %bitcast_dynamic-update-slice_fusion), channel_id=1, replica_groups=mesh['x'=4,'yl'=2,'core'=2,'z'=8,'yh'=4] {'x','yl','core'}, dimensions={0} | all-to-all | bytes 2097152 | tf_op jit(solution)/shard_map/all_to_all | solution.py:247
  (61 shorter events, 25.7 us)
Async XLA Ops:
  0.0 13.9 %copy-start.9 = (s32[16]{0:T(128)S(1)}, s32[16]{0:T(128)}, u32[]{:S(2)}) copy-start(s32[16]{0:T(128)} %param.7) | copy-start | bytes 196
  0.0 20.2 %copy-start.10 = (s32[128]{0:T(128)S(1)}, s32[128]{0:T(128)}, u32[]{:S(2)}) copy-start(s32[128]{0:T(128)} %param.6) | copy-start | bytes 1540
  0.0 43.2 %copy-start.7 = (bf16[1,128,4096]{2,1,0:T(8,128)(2,1)S(1)}, bf16[1,128,4096]{2,1,0:T(8,128)(2,1)}, u32[]{:S(2)}) copy-start(bf16[1,128,4096]{2,1,0:T(8,128)(2,1)} %param.4) | copy-start | bytes 3145732
  3.6 20.1 %all-to-all-start = ((bf16[16,128,128]{2,1,0:T(8,128)(2,1)}), bf16[16,128,128]{2,1,0:T(8,128)(2,1)S(1)}, u32[]{:S(2)}, u32[]{:S(2)}) async-start(bf16[16,128,128]{2,1,0:T(8,128)(2,1)} %pack.1), calls=%async_computation | async-start | bytes 1048576 | tf_op jit(solution)/shard_map/all_to_all | solution.py:201
  23.8 10.5 %collective-permute-start.1 = (bf16[400,128]{1,0:T(8,128)(2,1)S(1)}, bf16[400,128]{1,0:T(8,128)(2,1)S(1)}, u32[]{:S(2)}, u32[]{:S(2)}) collective-permute-start(bf16[400,128]{1,0:T(8,128)(2,1)S(1)} %get-tuple-element.73), channel_id=1, source_target_pairs={{0,2},{1,3},{2,0},{3,1},{4,6},{5,7},{6,4},{7,5},{8,10},{9,11},{10,... | collective-permute-start | bytes 307208 | tf_op jit(solution)/shard_map/ppermute | solution.py:132
  26.8 8.3 %collective-permute-start = (bf16[400,128]{1,0:T(8,128)(2,1)S(1)}, bf16[400,128]{1,0:T(8,128)(2,1)S(1)}, u32[]{:S(2)}, u32[]{:S(2)}) collective-permute-start(bf16[400,128]{1,0:T(8,128)(2,1)S(1)} %get-tuple-element.73), channel_id=1, source_target_pairs={{0,1},{1,2},{2,3},{3,0},{4,5},{5,6},{6,7},{7,4},{8,9},{9,10},{10,1... | collective-permute-start | bytes 307208 | tf_op jit(solution)/shard_map/ppermute | solution.py:132
  29.3 10.2 %collective-permute-start.2 = (bf16[400,128]{1,0:T(8,128)(2,1)S(1)}, bf16[400,128]{1,0:T(8,128)(2,1)S(1)}, u32[]{:S(2)}, u32[]{:S(2)}) collective-permute-start(bf16[400,128]{1,0:T(8,128)(2,1)S(1)} %get-tuple-element.73), channel_id=1, source_target_pairs={{0,3},{1,0},{2,1},{3,2},{4,7},{5,4},{6,5},{7,6},{8,11},{9,8},{10,9... | collective-permute-start | bytes 307208 | tf_op jit(solution)/shard_map/ppermute | solution.py:132
  39.5 5.1 %copy-start.6 = (bf16[4,400,128]{2,1,0:T(8,128)(2,1)}, bf16[4,400,128]{2,1,0:T(8,128)(2,1)S(1)}, u32[]{:S(2)}) copy-start(bf16[4,400,128]{2,1,0:T(8,128)(2,1)S(1)} %pad_maximum_fusion.mine_ref) | copy-start | bytes 1228804
  39.5 5.1 %collective-permute-start.3 = (bf16[4,400,128]{2,1,0:T(8,128)(2,1)S(1)}, bf16[4,400,128]{2,1,0:T(8,128)(2,1)S(1)}, u32[]{:S(2)}, u32[]{:S(2)}) collective-permute-start(bf16[4,400,128]{2,1,0:T(8,128)(2,1)S(1)} %pad_maximum_fusion.mine_ref), channel_id=1, source_target_pairs={{0,32},{32,0},{1,33},{33,1},{2,34},{34,2},{3,35},{35,3},{4,36},{36... | collective-permute-start | bytes 1228808 | tf_op jit(solution)/shard_map/ppermute | solution.py:132
  47.4 5.1 %copy-start.2 = (bf16[4,800,128]{2,1,0:T(8,128)(2,1)S(1)}, bf16[4,800,128]{2,1,0:T(8,128)(2,1)}, u32[]{:S(2)}) copy-start(bf16[4,800,128]{2,1,0:T(8,128)(2,1)} %join.1.refs_3_) | copy-start | bytes 2457604
  48.7 33.6 %all-to-all-start.1 = ((bf16[16,128,256]{2,1,0:T(8,128)(2,1)}), bf16[16,128,256]{2,1,0:T(8,128)(2,1)S(1)}, u32[]{:S(2)}, u32[]{:S(2)}) async-start(bf16[16,128,256]{2,1,0:T(8,128)(2,1)} %bitcast.19), calls=%async_computation.1 | async-start | bytes 2097152 | tf_op jit(solution)/shard_map/all_to_all | solution.py:221
  52.6 18.9 %collective-permute-start.5 = (bf16[4,800,128]{2,1,0:T(8,128)(2,1)S(1)}, bf16[4,800,128]{2,1,0:T(8,128)(2,1)}, u32[]{:S(2)}, u32[]{:S(2)}) collective-permute-start(bf16[4,800,128]{2,1,0:T(8,128)(2,1)S(1)} %copy-done.2), channel_id=1, source_target_pairs={{0,4},{4,8},{8,12},{12,16},{16,20},{20,24},{24,28},{28,0},{32,60},... | collective-permute-start | bytes 2457608 | tf_op jit(solution)/shard_map/ppermute | solution.py:214
  71.5 20.3 %collective-permute-start.6 = (bf16[4,800,128]{2,1,0:T(8,128)(2,1)}, bf16[4,800,128]{2,1,0:T(8,128)(2,1)}, u32[]{:S(2)}, u32[]{:S(2)}) collective-permute-start(bf16[4,800,128]{2,1,0:T(8,128)(2,1)} %collective-permute-done.5.refs_3_), channel_id=1, source_target_pairs={{0,4},{4,8},{8,12},{12,16},{16,20},{20,24},{24,28},{28,0},{32,60},... | collective-permute-start | bytes 2457608 | tf_op jit(solution)/shard_map/ppermute | solution.py:214
  80.4 11.4 %collective-permute-start.7 = (bf16[4,528,128]{2,1,0:T(8,128)(2,1)}, bf16[4,528,128]{2,1,0:T(8,128)(2,1)}, u32[]{:S(2)}, u32[]{:S(2)}) collective-permute-start(bf16[4,528,128]{2,1,0:T(8,128)(2,1)} %constant_dynamic-slice_fusion.4), channel_id=1, source_target_pairs={{0,32},{32,0},{1,33},{33,1},{2,34},{34,2},{3,35},{35,3},{4,36},{36... | collective-permute-start | bytes 1622024 | tf_op jit(solution)/shard_map/ppermute | solution.py:132
  82.4 3.8 %collective-permute-start.4 = (bf16[128,256]{1,0:T(8,128)(2,1)S(1)}, bf16[128,256]{1,0:T(8,128)(2,1)S(1)}, u32[]{:S(2)}, u32[]{:S(2)}) collective-permute-start(bf16[128,256]{1,0:T(8,128)(2,1)S(1)} %dynamic-slice_bitcast_fusion.1), channel_id=1, source_target_pairs={{0,32},{32,0},{1,33},{33,1},{2,34},{34,2},{3,35},{35,3},{4,36},{36... | collective-permute-start | bytes 196616 | tf_op jit(solution)/shard_map/ppermute | solution.py:132
  86.2 1.1 copy-start.3
  91.8 14.3 %collective-permute-start.8 = (bf16[4,800,128]{2,1,0:T(8,128)(2,1)}, bf16[4,800,128]{2,1,0:T(8,128)(2,1)S(1)}, u32[]{:S(2)}, u32[]{:S(2)}) collective-permute-start(bf16[4,800,128]{2,1,0:T(8,128)(2,1)} %collective-permute-done.6.refs_3_), channel_id=1, source_target_pairs={{0,4},{4,8},{8,12},{12,16},{16,20},{20,24},{24,28},{28,0},{32,60},... | collective-permute-start | bytes 2457608 | tf_op jit(solution)/shard_map/ppermute | solution.py:214
  95.7 9.6 %collective-permute-start.9 = (bf16[4,528,128]{2,1,0:T(8,128)(2,1)S(1)}, bf16[4,528,128]{2,1,0:T(8,128)(2,1)S(1)}, u32[]{:S(2)}, u32[]{:S(2)}) collective-permute-start(bf16[4,528,128]{2,1,0:T(8,128)(2,1)S(1)} %constant_dynamic-slice_fusion.3), channel_id=1, source_target_pairs={{0,32},{32,0},{1,33},{33,1},{2,34},{34,2},{3,35},{35,3},{4,36},{36... | collective-permute-start | bytes 1622024 | tf_op jit(solution)/shard_map/ppermute | solution.py:132
  107.9 15.7 %collective-permute-start.11 = (bf16[4,528,128]{2,1,0:T(8,128)(2,1)}, bf16[4,528,128]{2,1,0:T(8,128)(2,1)}, u32[]{:S(2)}, u32[]{:S(2)}) collective-permute-start(bf16[4,528,128]{2,1,0:T(8,128)(2,1)} %constant_dynamic-slice_fusion.1), channel_id=1, source_target_pairs={{0,32},{32,0},{1,33},{33,1},{2,34},{34,2},{3,35},{35,3},{4,36},{36... | collective-permute-start | bytes 1622024 | tf_op jit(solution)/shard_map/ppermute | solution.py:132
  112.2 13.6 %copy-start.1 = (bf16[4,800,128]{2,1,0:T(8,128)(2,1)S(1)}, bf16[4,800,128]{2,1,0:T(8,128)(2,1)}, u32[]{:S(2)}) copy-start(bf16[4,800,128]{2,1,0:T(8,128)(2,1)} %copy-done) | copy-start | bytes 2457604
  112.2 11.4 %collective-permute-start.10 = (bf16[2,800,128]{2,1,0:T(8,128)(2,1)S(1)}, bf16[2,800,128]{2,1,0:T(8,128)(2,1)S(1)}, u32[]{:S(2)}, u32[]{:S(2)}) collective-permute-start(bf16[2,800,128]{2,1,0:T(8,128)(2,1)S(1)} %constant_dynamic-slice_fusion.2), channel_id=1, source_target_pairs={{0,4},{4,8},{8,12},{12,16},{16,20},{20,24},{24,28},{28,0},{32,60},... | collective-permute-start | bytes 1228808 | tf_op jit(solution)/shard_map/ppermute | solution.py:214
  115.0 1.0 copy-start.5
  123.6 9.6 %collective-permute-start.12 = (bf16[2,528,128]{2,1,0:T(8,128)(2,1)S(1)}, bf16[2,528,128]{2,1,0:T(8,128)(2,1)S(1)}, u32[]{:S(2)}, u32[]{:S(2)}) collective-permute-start(bf16[2,528,128]{2,1,0:T(8,128)(2,1)S(1)} %constant_dynamic-slice_fusion), channel_id=1, source_target_pairs={{0,32},{32,0},{1,33},{33,1},{2,34},{34,2},{3,35},{35,3},{4,36},{36... | collective-permute-start | bytes 811016 | tf_op jit(solution)/shard_map/ppermute | solution.py:132
  137.8 3.3 %collective-permute-start.13 = (bf16[128,256]{1,0:T(8,128)(2,1)S(1)}, bf16[128,256]{1,0:T(8,128)(2,1)S(1)}, u32[]{:S(2)}, u32[]{:S(2)}) collective-permute-start(bf16[128,256]{1,0:T(8,128)(2,1)S(1)} %dynamic-slice_bitcast_fusion), channel_id=1, source_target_pairs={{0,32},{32,0},{1,33},{33,1},{2,34},{34,2},{3,35},{35,3},{4,36},{36... | collective-permute-start | bytes 196616 | tf_op jit(solution)/shard_map/ppermute | solution.py:132
  (3 other events, 2.4 us)

commit v7 on v5

v7 whole, which is shorter than its diff:
```python
import functools

import jax
import jax.numpy as jnp
from jax import lax
from jax.experimental import pallas as pl
from jax.experimental.pallas import tpu as pltpu
from jax.sharding import Mesh, PartitionSpec as P

H = 32
KVH = 4
HD = 128
GROUP = H // KVH
BLOCK = 64
WARM = 2
LAYERS = 16
ROWS = 128
WIDE = 2 * HD
SLABS = GROUP * HD // WIDE
PART = 2 * ROWS
POS_ROWS = 16
RING = 3
MASKED = -1e30
SCALE = 1.4426950408889634 / HD**0.5
SECTION = ("x", "yl", "core")
VMEM = pl.BlockSpec(memory_space=pltpu.VMEM)


def attend_body(heads, offset, shards, first, last, extra, *refs):
    it = iter(refs)
    q_ref, pos_ref = next(it), next(it)
    blocks = [next(it) for _ in shards]
    if not first:
        m_in, l_in, a_in = next(it), next(it), next(it)
    if extra:
        extra_ref = next(it)
    outs = [next(it)] if last else [next(it), next(it), next(it)]
    k, v, cap = it
    count = k.shape[1]
    row = lax.broadcasted_iota(jnp.int32, (BLOCK, ROWS), 0).astype(jnp.float32)
    at = 0
    for n, ref in zip(shards, blocks):
        for i in range(n):
            for h in range(heads):
                base = h * PART
                k[h, at : at + ROWS, :] = ref[i, base : base + ROWS]
                v[h, :HD, at : at + ROWS] = ref[i, base + ROWS : base + PART]
            ids = ref[i, heads * PART :].astype(jnp.float32)
            for part in range(ROWS // BLOCK):
                key_pos = ids[0:1, part * BLOCK : part * BLOCK + 1] * BLOCK + row
                rows = slice(at + part * BLOCK, at + (part + 1) * BLOCK)
                cap[rows, :] = jnp.where(key_pos <= pos_ref[...], jnp.inf, MASKED)
            at += ROWS
    for h in range(heads):
        v[h, HD:, :] = jnp.ones((POS_ROWS, count), jnp.bfloat16)

    def scores(j):
        col = (offset * SLABS + j) * WIDE
        q = jnp.concatenate([q_ref[:, col : col + HD], q_ref[:, col + HD : col + WIDE]], axis=0)
        return lax.dot_general(
            k[j // SLABS], q, (((1,), (1,)), ((), ())), preferred_element_type=jnp.float32
        )

    def absorb(j, s):
        s = jnp.minimum(s, jnp.concatenate([cap[...]] * 2, axis=1))
        m = jnp.max(s, axis=0, keepdims=True)
        if not first:
            m_old = m_in[j, 0:1, :]
            m = jnp.maximum(m_old, m)
        w = jnp.exp2((s - m) * SCALE).astype(jnp.bfloat16)
        o = lax.dot_general(
            v[j // SLABS], w, (((1,), (0,)), ((), ())), preferred_element_type=jnp.float32
        )
        acc, den = o[:HD], o[HD : HD + 8]
        if not first:
            f = jnp.exp2((m_old - m) * SCALE)
            acc = acc + f * a_in[j]
            den = den + f * l_in[j]
        if last:
            done = acc / den[0:1]
            for h in range(2):
                cols = slice(j * WIDE + h * HD, j * WIDE + (h + 1) * HD)
                outs[0][:, cols] = done[:, h * HD : (h + 1) * HD].T.astype(jnp.bfloat16)
        else:
            outs[0][j] = jnp.broadcast_to(m, den.shape)
            outs[1][j] = den
            outs[2][j] = acc

    if extra:
        outs[0][:, heads * GROUP * HD :] = extra_ref[...]
    s = scores(0)
    for j in range(heads * SLABS):
        ahead = scores(j + 1) if j + 1 < heads * SLABS else None
        absorb(j, s)
        s = ahead


def attend(q, pos, heads, offset, blocks, state, last, extra=None):
    shards = tuple(b.shape[0] for b in blocks)
    count = sum(shards) * ROWS
    pairs = heads * SLABS
    args = [q, pos, *blocks]
    aliases = {}
    if state is not None:
        if not last:
            aliases = {len(args) + i: i for i in range(len(state))}
        args += list(state)
    if extra is not None:
        args.append(extra)
    one = jax.ShapeDtypeStruct((pairs, 8, WIDE), jnp.float32)
    acc = jax.ShapeDtypeStruct((pairs, HD, WIDE), jnp.float32)
    columns = pairs * WIDE + (0 if extra is None else extra.shape[1])
    done = jax.ShapeDtypeStruct((ROWS, columns), jnp.bfloat16)
    return pl.pallas_call(
        functools.partial(
            attend_body, heads, offset, shards, state is None, last, extra is not None
        ),
        in_specs=[VMEM] * len(args),
        out_specs=VMEM if last else [VMEM] * 3,
        out_shape=done if last else [one, one, acc],
        scratch_shapes=[
            pltpu.VMEM((heads, count, HD), jnp.bfloat16),
            pltpu.VMEM((heads, HD + POS_ROWS, count), jnp.bfloat16),
            pltpu.VMEM((count, ROWS), jnp.float32),
        ],
        input_output_aliases=aliases,
        compiler_params=pltpu.CompilerParams(vmem_limit_bytes=32 << 20),
        cost_estimate=pl.CostEstimate(
            flops=4 * ROWS * heads * GROUP * count * HD,
            bytes_accessed=8 << 20,
            transcendentals=ROWS * heads * GROUP * count,
        ),
        name="attend",
    )(*args)


def packed(kv):
    def body(kv_ref, out_ref):
        for h in range(KVH):
            at = h * PART
            out_ref[at : at + ROWS] = kv_ref[:, h * HD : (h + 1) * HD]
            out_ref[at + ROWS : at + PART] = kv_ref[:, (KVH + h) * HD : (KVH + h + 1) * HD].T

    return pl.pallas_call(
        body,
        in_specs=[VMEM],
        out_specs=VMEM,
        out_shape=jax.ShapeDtypeStruct((KVH * PART, HD), jnp.bfloat16),
        name="pack",
    )(kv)


def turn(value, axis, size, shift):
    return lax.ppermute(value, axis, [(i, (i + shift) % size) for i in range(size)])


def around(value, axis, size):
    return [turn(value, axis, size, shift) for shift in range(1, size)]


def per_device(sizes, queries, key_values, token_pos, layer_of_section):
    nz, nyh = sizes["z"], sizes["yh"]
    section = lax.axis_index(SECTION)
    ids = jnp.arange(LAYERS, dtype=jnp.int32)
    layer = jnp.sum(jnp.where(ids == section, layer_of_section, 0))
    top_section = jnp.sum(jnp.where(layer_of_section == LAYERS - 1, ids, 0))
    own = packed(key_values[0].reshape(ROWS, 2 * KVH * HD))
    pieces = own.reshape(LAYERS, KVH * PART // LAYERS, HD)
    piece = lax.dynamic_index_in_dim(lax.all_to_all(pieces, SECTION, 0, 0), top_section, 0, True)
    top = lax.all_to_all(jnp.broadcast_to(piece, pieces.shape), SECTION, 0, 0)
    rows = jnp.where(layer < WARM, own, top.reshape(own.shape))
    block_ids = jnp.broadcast_to((token_pos // BLOCK).astype(jnp.bfloat16)[None, :], (POS_ROWS, ROWS))
    shard = jnp.concatenate([rows[: RING * PART], block_ids], axis=0)
    beside = jnp.concatenate([rows[RING * PART :], block_ids], axis=0)
    q = queries[0]
    pos = token_pos.astype(jnp.float32)[None, :]

    def ring_part(blocks, state, last=False, extra=None):
        return attend(q, pos, RING, 0, blocks, state, last, extra)

    def side_part(blocks, state, last=False):
        return attend(q, pos, KVH - RING, RING, blocks, state, last)

    line = jnp.stack([shard] + around(shard, "yh", nyh))
    column = lax.all_to_all(jnp.broadcast_to(beside[None], (nz, *beside.shape)), "z", 0, 0)
    line, column = lax.optimization_barrier((line, column))
    half, side_half = nyh // 2, nz // 2
    up, down = turn(line, "z", nz, 1), turn(line, "z", nz, -1)
    side_up = turn(column, "yh", nyh, 1)
    state = ring_part([line], None)
    up, down, side_up, state = lax.optimization_barrier((up, down, side_up, state))

    held = [up, down]
    up, down = turn(up, "z", nz, 1), turn(down, "z", nz, -1)
    side_down = turn(column, "yh", nyh, -1)
    far_up = turn(side_up[:side_half], "yh", nyh, 1)
    state, side = ring_part(held, state), side_part([column, side_up], None)
    up, down, side_down, far_up, state, side = lax.optimization_barrier(
        (up, down, side_down, far_up, state, side)
    )

    held = [up, down]
    up, down = turn(up, "z", nz, 1), turn(down, "z", nz, -1)
    far_down = turn(side_down[side_half:], "yh", nyh, -1)
    state = ring_part(held, state)
    up, down, far_down, state = lax.optimization_barrier((up, down, far_down, state))

    last_up, last_down = turn(up[:half], "z", nz, 1), turn(down[half:], "z", nz, -1)
    state = ring_part([up, down], state)
    side_out = side_part([side_down, far_up, far_down], side, True)
    last_up, last_down, state, side_out = lax.optimization_barrier((last_up, last_down, state, side_out))
    out = ring_part([last_up, last_down], state, True, side_out)
    return out[None]


def solution(mesh):
    sizes = {"x": 4, "yl": 2, "core": 2, "z": 8, "yh": 4}
    fine = Mesh(mesh.devices.reshape(tuple(sizes.values())), tuple(sizes))
    ctx = ("z", "yh")
    in_specs = (P(SECTION, ctx, None), P(SECTION, ctx, None, None), P(ctx), P())
    return jax.shard_map(
        functools.partial(per_device, sizes),
        mesh=fine,
        in_specs=in_specs,
        out_specs=P(SECTION, ctx, None),
        check_vma=False,
    )
```

time: 161 us -> 178 us (1.11); the launches traced: 161 us -> 175 us
  waiting for transfers between devices: 33.1 us -> 63.5 us
  blocking collectives: 18.3 us -> 0 us
  starting transfers between devices: 64.6 us -> 75.5 us
  local copies, waits for them, and re-layouts: 7.2 us -> 3.48 us
  between operations: 6.12 us -> 2.87 us
    ppermute x13 -> x15, waiting for transfers between devices: 18.4 us -> 52.3 us  [turn(): lax.ppermute(value, axis, [(i, (i + shift) % size) for i in range(size)])]
    all_to_all x1 -> x0, blocking collectives: 18.3 us -> none  [per_device(): out = lax.all_to_all(out, SECTION, 0, 0)]
    all_to_all x2 -> x3, starting transfers between devices: 14.3 us -> 21.2 us  [the longest x1 10.3 us: per_device(): lax.all_to_all(pieces, SECTION, 0, 0)]
    ppermute x13 -> x15, starting transfers between devices: 50.3 us -> 54.2 us  [turn(): lax.ppermute(value, axis, [(i, (i + shift) % size) for i in range(size)])]
    all_to_all x2 -> x3, waiting for transfers between devices: 14.7 us -> 11.2 us  [the longest x1 6.56 us: per_device(): top = lax.all_to_all(jnp.broadcast_to(piece, pieces.shape), SECTION, 0, 0)]
    pallas_call x5 -> x8, Pallas kernels: 29.7 us -> 29.2 us  [the longest x7 27.5 us: attend(): pl.pallas_call(functools.partial(attend_body, heads, offset, shards, stat...]
  transfers between devices with their start and end apart: 15 -> 18, of which waited for: 11 -> 10; matrix products, arithmetic and copies ran while one was open for 3% -> 1% of each run, Pallas kernels for 16% -> 13%
where the time goes in v7:
time: 178 us; the launch traced here: 175 us
  starting transfers between devices  75.5 us (42%)
  waiting for transfers between devices  63.5 us (36%)
  Pallas kernels  29.2 us (16%)
  local copies, waits for them, and re-layouts  3.48 us (2%)
  between operations  2.87 us (2%)
    ppermute x15, starting transfers between devices, turn(): lax.ppermute(value, axis, [(i, (i + shift) % size) for i in range(size)])  54.2 us
    ppermute x15, waiting for transfers between devices, turn(): lax.ppermute(value, axis, [(i, (i + shift) % size) for i in range(size)])  52.3 us
    pallas_call x7, Pallas kernels, attend(): pl.pallas_call(functools.partial(attend_body, heads, offset, shards, stat...  27.5 us
    all_to_all x1, starting transfers between devices, per_device(): lax.all_to_all(pieces, SECTION, 0, 0)  10.3 us
    all_to_all x1, starting transfers between devices, per_device(): lax.all_to_all(jnp.broadcast_to(beside[None], (nz, *beside.shape)), 'z',...  6.59 us
    all_to_all x1, waiting for transfers between devices, per_device(): top = lax.all_to_all(jnp.broadcast_to(piece, pieces.shape), SECTION, 0, 0)  6.56 us
    all_to_all x1, waiting for transfers between devices, per_device(): lax.all_to_all(pieces, SECTION, 0, 0)  4.61 us
    all_to_all x1, starting transfers between devices, per_device(): top = lax.all_to_all(jnp.broadcast_to(piece, pieces.shape), SECTION, 0, 0)  4.33 us
  transfers between devices with their start and end apart: 18, of which 10 were waited for; matrix products, arithmetic and copies ran while one was open for 1% of the time, Pallas kernels for 13%

profile of v7, /device:TPU:1, one launch (start us, length us, event | category | flops | bytes accessed | tf_op | source)
XLA Modules:
  0.0 175.4 jit_solution(9232148017450629239)
XLA Ops:
  3.5 10.3 %all-to-all-start = ((bf16[16,64,128]{2,1,0:T(8,128)(2,1)}), bf16[16,64,128]{2,1,0:T(8,128)(2,1)S(1)}, u32[]{:S(2)}, u32[]{:S(2)}) async-start(bf16[16,64,128]{2,1,0:T(8,128)(2,1)} %bitcast.24), calls=%async_computation | async-start | bytes 524288 | tf_op jit(solution)/shard_map/all_to_all | solution.py:169
  16.4 4.6 %all-to-all-done = bf16[16,64,128]{2,1,0:T(8,128)(2,1)S(1)} async-done(((bf16[16,64,128]{2,1,0:T(8,128)(2,1)}), bf16[16,64,128]{2,1,0:T(8,128)(2,1)S(1)}, u32[]{:S(2)}, u32[]{:S(2)}) %all-to-all-start) | async-done | bytes 262176 | tf_op jit(solution)/shard_map/all_to_all | solution.py:169
  21.8 4.3 %all-to-all-start.1 = ((bf16[16,64,128]{2,1,0:T(8,128)(2,1)}), bf16[16,64,128]{2,1,0:T(8,128)(2,1)S(1)}, u32[]{:S(2)}, u32[]{:S(2)}) async-start(bf16[16,64,128]{2,1,0:T(8,128)(2,1)} %broadcast_in_dim.33), calls=%async_computation.1 | async-start | bytes 524288 | tf_op jit(solution)/shard_map/all_to_all | solution.py:170
  26.8 6.6 %all-to-all-done.1 = bf16[16,64,128]{2,1,0:T(8,128)(2,1)S(1)} async-done(((bf16[16,64,128]{2,1,0:T(8,128)(2,1)}), bf16[16,64,128]{2,1,0:T(8,128)(2,1)S(1)}, u32[]{:S(2)}, u32[]{:S(2)}) %all-to-all-start.1) | async-done | bytes 262176 | tf_op jit(solution)/shard_map/all_to_all | solution.py:170
  34.3 6.6 %all-to-all-start.2 = ((bf16[8,272,128]{2,1,0:T(8,128)(2,1)}), bf16[8,272,128]{2,1,0:T(8,128)(2,1)S(1)}, u32[]{:S(2)}, u32[]{:S(2)}) async-start(bf16[8,272,128]{2,1,0:T(8,128)(2,1)} %broadcast_in_dim.35), calls=%async_computation.2 | async-start | bytes 1114112 | tf_op jit(solution)/shard_map/all_to_all | solution.py:185
  41.0 4.3 %collective-permute-start = (bf16[784,128]{1,0:T(8,128)(2,1)S(1)}, bf16[784,128]{1,0:T(8,128)(2,1)S(1)}, u32[]{:S(2)}, u32[]{:S(2)}) collective-permute-start(bf16[784,128]{1,0:T(8,128)(2,1)S(1)} %get-tuple-element.98), channel_id=1, source_target_pairs={{0,1},{1,2},{2,3},{3,0},{4,5},{5,6},{6,7},{7,4},{8,9},{9,10},{10,1... | collective-permute-start | bytes 602120 | tf_op jit(solution)/shard_map/ppermute | solution.py:154
  45.3 4.8 %collective-permute-start.1 = (bf16[784,128]{1,0:T(8,128)(2,1)S(1)}, bf16[784,128]{1,0:T(8,128)(2,1)S(1)}, u32[]{:S(2)}, u32[]{:S(2)}) collective-permute-start(bf16[784,128]{1,0:T(8,128)(2,1)S(1)} %get-tuple-element.98), channel_id=1, source_target_pairs={{0,2},{1,3},{2,0},{3,1},{4,6},{5,7},{6,4},{7,5},{8,10},{9,11},{10,... | collective-permute-start | bytes 602120 | tf_op jit(solution)/shard_map/ppermute | solution.py:154
  50.1 5.0 %collective-permute-start.2 = (bf16[784,128]{1,0:T(8,128)(2,1)S(1)}, bf16[784,128]{1,0:T(8,128)(2,1)S(1)}, u32[]{:S(2)}, u32[]{:S(2)}) collective-permute-start(bf16[784,128]{1,0:T(8,128)(2,1)S(1)} %get-tuple-element.98), channel_id=1, source_target_pairs={{0,3},{1,0},{2,1},{3,2},{4,7},{5,4},{6,5},{7,6},{8,11},{9,8},{10,9... | collective-permute-start | bytes 602120 | tf_op jit(solution)/shard_map/ppermute | solution.py:154
  55.1 5.0 %collective-permute-done.1 = bf16[784,128]{1,0:T(8,128)(2,1)S(1)} collective-permute-done((bf16[784,128]{1,0:T(8,128)(2,1)S(1)}, bf16[784,128]{1,0:T(8,128)(2,1)S(1)}, u32[]{:S(2)}, u32[]{:S(2)}) %collective-permute-start.1) | collective-permute-done | bytes 200736 | tf_op jit(solution)/shard_map/ppermute | solution.py:154
  60.1 9.5 %collective-permute-done.2 = bf16[784,128]{1,0:T(8,128)(2,1)S(1)} collective-permute-done((bf16[784,128]{1,0:T(8,128)(2,1)S(1)}, bf16[784,128]{1,0:T(8,128)(2,1)S(1)}, u32[]{:S(2)}, u32[]{:S(2)}) %collective-permute-start.2) | collective-permute-done | bytes 200736 | tf_op jit(solution)/shard_map/ppermute | solution.py:154
  69.7 3.4 %collective-permute-start.3 = (bf16[4,784,128]{2,1,0:T(8,128)(2,1)S(1)}, bf16[4,784,128]{2,1,0:T(8,128)(2,1)S(1)}, u32[]{:S(2)}, u32[]{:S(2)}) collective-permute-start(bf16[4,784,128]{2,1,0:T(8,128)(2,1)S(1)} %pad_maximum_fusion.refs_2_), channel_id=1, source_target_pairs={{0,4},{4,8},{8,12},{12,16},{16,20},{20,24},{24,28},{28,0},{1,5},{5... | collective-permute-start | bytes 2408456 | tf_op jit(solution)/shard_map/ppermute | solution.py:154
  73.1 3.1 %collective-permute-start.4 = (bf16[4,784,128]{2,1,0:T(8,128)(2,1)S(1)}, bf16[4,784,128]{2,1,0:T(8,128)(2,1)S(1)}, u32[]{:S(2)}, u32[]{:S(2)}) collective-permute-start(bf16[4,784,128]{2,1,0:T(8,128)(2,1)S(1)} %pad_maximum_fusion.refs_2_), channel_id=1, source_target_pairs={{0,28},{4,0},{8,4},{12,8},{16,12},{20,16},{24,20},{28,24},{1,29},{... | collective-permute-start | bytes 2408456 | tf_op jit(solution)/shard_map/ppermute | solution.py:154
  76.3 4.2 %collective-permute-start.5 = (bf16[8,272,128]{2,1,0:T(8,128)(2,1)S(1)}, bf16[8,272,128]{2,1,0:T(8,128)(2,1)S(1)}, u32[]{:S(2)}, u32[]{:S(2)}) collective-permute-start(bf16[8,272,128]{2,1,0:T(8,128)(2,1)S(1)} %all-to-all-done.2.refs_2_), channel_id=1, source_target_pairs={{0,1},{1,2},{2,3},{3,0},{4,5},{5,6},{6,7},{7,4},{8,9},{9,10},{10,1... | collective-permute-start | bytes 1671176 | tf_op jit(solution)/shard_map/ppermute | solution.py:154
  83.3 19.7 %collective-permute-done.5.refs_3_ = bf16[8,272,128]{2,1,0:T(8,128)(2,1)S(1)} collective-permute-done((bf16[8,272,128]{2,1,0:T(8,128)(2,1)S(1)}, bf16[8,272,128]{2,1,0:T(8,128)(2,1)S(1)}, u32[]{:S(2)}, u32[]{:S(2)}) %collective-permute-start.5) | collective-permute-done | bytes 557088 | tf_op jit(solution)/shard_map/ppermute | solution.py:154
  105.2 4.3 %collective-permute-start.7 = (bf16[4,784,128]{2,1,0:T(8,128)(2,1)S(1)}, bf16[4,784,128]{2,1,0:T(8,128)(2,1)S(1)}, u32[]{:S(2)}, u32[]{:S(2)}) collective-permute-start(bf16[4,784,128]{2,1,0:T(8,128)(2,1)S(1)} %collective-permute-done.4.refs_3_), channel_id=1, source_target_pairs={{0,28},{4,0},{8,4},{12,8},{16,12},{20,16},{24,20},{28,24},{1,29},{... | collective-permute-start | bytes 2408456 | tf_op jit(solution)/shard_map/ppermute | solution.py:154
  112.4 3.5 %collective-permute-start.9 = (bf16[4,272,128]{2,1,0:T(8,128)(2,1)S(1)}, bf16[4,272,128]{2,1,0:T(8,128)(2,1)S(1)}, u32[]{:S(2)}, u32[]{:S(2)}) collective-permute-start(bf16[4,272,128]{2,1,0:T(8,128)(2,1)S(1)} %slice.20), channel_id=1, source_target_pairs={{0,1},{1,2},{2,3},{3,0},{4,5},{5,6},{6,7},{7,4},{8,9},{9,10},{10,1... | collective-permute-start | bytes 835592 | tf_op jit(solution)/shard_map/ppermute | solution.py:154
  118.8 4.9 %attend.8 = (f32[12,8,256]{2,1,0:T(8,128)S(1)}, f32[12,8,256]{2,1,0:T(8,128)S(1)}, f32[12,128,256]{2,1,0:T(8,128)S(1)}) custom-call(bf16[128,4096]{1,0:T(8,128)(2,1)S(1)} %bitcast.19, f32[1,128]{1,0:T(1,128)S(1)} %get-tuple-element.100.refs_1_, ...), custom_call_target="tpu_custom_call", output_to_operand_aliasing={{0}: (4, {}), {1}: (5, {}), {2}: (6, {})} | custom-call | flops 1610612736 | bytes 8388608 | tf_op jit(solution)/shard_map/attend/pallas_call | solution.py:114
  123.7 3.8 %collective-permute-done.8.refs_2_ = bf16[8,272,128]{2,1,0:T(8,128)(2,1)S(1)} collective-permute-done((bf16[8,272,128]{2,1,0:T(8,128)(2,1)S(1)}, bf16[8,272,128]{2,1,0:T(8,128)(2,1)S(1)}, u32[]{:S(2)}, u32[]{:S(2)}) %collective-permute-start.8) | collective-permute-done | bytes 557088 | tf_op jit(solution)/shard_map/ppermute | solution.py:154
  130.2 3.9 %collective-permute-start.11 = (bf16[4,784,128]{2,1,0:T(8,128)(2,1)S(1)}, bf16[4,784,128]{2,1,0:T(8,128)(2,1)S(1)}, u32[]{:S(2)}, u32[]{:S(2)}) collective-permute-start(bf16[4,784,128]{2,1,0:T(8,128)(2,1)S(1)} %collective-permute-done.7.refs_3_), channel_id=1, source_target_pairs={{0,28},{4,0},{8,4},{12,8},{16,12},{20,16},{24,20},{28,24},{1,29},{... | collective-permute-start | bytes 2408456 | tf_op jit(solution)/shard_map/ppermute | solution.py:154
  136.3 4.9 %attend.10 = (f32[12,8,256]{2,1,0:T(8,128)S(1)}, f32[12,8,256]{2,1,0:T(8,128)S(1)}, f32[12,128,256]{2,1,0:T(8,128)S(1)}) custom-call(bf16[128,4096]{1,0:T(8,128)(2,1)S(1)} %bitcast.20, f32[1,128]{1,0:T(1,128)S(1)} %get-tuple-element.100.refs_1_, ...), custom_call_target="tpu_custom_call", output_to_operand_aliasing={{0}: (4, {}), {1}: (5, {}), {2}: (6, {})} | custom-call | flops 1610612736 | bytes 8388608 | tf_op jit(solution)/shard_map/attend/pallas_call | solution.py:114
  143.3 10.9 %collective-permute-done.11.refs_3_ = bf16[4,784,128]{2,1,0:T(8,128)(2,1)S(1)} collective-permute-done((bf16[4,784,128]{2,1,0:T(8,128)(2,1)S(1)}, bf16[4,784,128]{2,1,0:T(8,128)(2,1)S(1)}, u32[]{:S(2)}, u32[]{:S(2)}) %collective-permute-start.11) | collective-permute-done | bytes 802848 | tf_op jit(solution)/shard_map/ppermute | solution.py:154
  154.2 5.7 %collective-permute-start.13 = (bf16[2,784,128]{2,1,0:T(8,128)(2,1)S(1)}, bf16[2,784,128]{2,1,0:T(8,128)(2,1)S(1)}, u32[]{:S(2)}, u32[]{:S(2)}) collective-permute-start(bf16[2,784,128]{2,1,0:T(8,128)(2,1)S(1)} %slice.22), channel_id=1, source_target_pairs={{0,4},{4,8},{8,12},{12,16},{16,20},{20,24},{24,28},{28,0},{1,5},{5... | collective-permute-start | bytes 1204232 | tf_op jit(solution)/shard_map/ppermute | solution.py:154
  165.2 4.9 %attend.11 = (f32[12,8,256]{2,1,0:T(8,128)S(1)}, f32[12,8,256]{2,1,0:T(8,128)S(1)}, f32[12,128,256]{2,1,0:T(8,128)S(1)}) custom-call(bf16[128,4096]{1,0:T(8,128)(2,1)S(1)} %bitcast.22, f32[1,128]{1,0:T(1,128)S(1)} %get-tuple-element.100.refs_1_, ...), custom_call_target="tpu_custom_call", output_to_operand_aliasing={{0}: (4, {}), {1}: (5, {}), {2}: (6, {})} | custom-call | flops 1610612736 | bytes 8388608 | tf_op jit(solution)/shard_map/attend/pallas_call | solution.py:114
  171.5 3.9 %attend.13 = bf16[128,4096]{1,0:T(8,128)(2,1)} custom-call(bf16[128,4096]{1,0:T(8,128)(2,1)S(1)} %bitcast.23, f32[1,128]{1,0:T(1,128)S(1)} %get-tuple-element.100.refs_1_, bf16[2,784,128]{2,1,0:T(8,128)(2,1)S(1)} %collective-permute-done.13.refs_2_, bf16[2,784,128]{2,1,0:T(8,128)(2,1)S(1)} %collective-permute-done.14.refs_3_, ...), custom_call_target="tpu_custom_call" | custom-call | flops 805306368 | bytes 8388608 | tf_op jit(solution)/shard_map/attend/pallas_call | solution.py:114
  (45 shorter events, 30.3 us)
Async XLA Ops:
  0.0 13.8 %copy-start.2 = (s32[16]{0:T(128)S(1)}, s32[16]{0:T(128)}, u32[]{:S(2)}) copy-start(s32[16]{0:T(128)} %param.7) | copy-start | bytes 196
  0.0 26.7 %copy-start.3 = (s32[128]{0:T(128)S(1)}, s32[128]{0:T(128)}, u32[]{:S(2)}) copy-start(s32[128]{0:T(128)} %param.6) | copy-start | bytes 1540
  3.5 29.9 %copy-start.1 = (bf16[1024,128]{1,0:T(8,128)(2,1)S(1)}, bf16[1024,128]{1,0:T(8,128)(2,1)}, u32[]{:S(2)}) copy-start(bf16[1024,128]{1,0:T(8,128)(2,1)} %pack.1) | copy-start | bytes 786436
  3.5 17.6 %all-to-all-start = ((bf16[16,64,128]{2,1,0:T(8,128)(2,1)}), bf16[16,64,128]{2,1,0:T(8,128)(2,1)S(1)}, u32[]{:S(2)}, u32[]{:S(2)}) async-start(bf16[16,64,128]{2,1,0:T(8,128)(2,1)} %bitcast.24), calls=%async_computation | async-start | bytes 524288 | tf_op jit(solution)/shard_map/all_to_all | solution.py:169
  21.8 11.6 %all-to-all-start.1 = ((bf16[16,64,128]{2,1,0:T(8,128)(2,1)}), bf16[16,64,128]{2,1,0:T(8,128)(2,1)S(1)}, u32[]{:S(2)}, u32[]{:S(2)}) async-start(bf16[16,64,128]{2,1,0:T(8,128)(2,1)} %broadcast_in_dim.33), calls=%async_computation.1 | async-start | bytes 524288 | tf_op jit(solution)/shard_map/all_to_all | solution.py:170
  34.3 35.4 %all-to-all-start.2 = ((bf16[8,272,128]{2,1,0:T(8,128)(2,1)}), bf16[8,272,128]{2,1,0:T(8,128)(2,1)S(1)}, u32[]{:S(2)}, u32[]{:S(2)}) async-start(bf16[8,272,128]{2,1,0:T(8,128)(2,1)} %broadcast_in_dim.35), calls=%async_computation.2 | async-start | bytes 1114112 | tf_op jit(solution)/shard_map/all_to_all | solution.py:185
  40.9 39.6 %copy-start = (bf16[1,128,4096]{2,1,0:T(8,128)(2,1)S(1)}, bf16[1,128,4096]{2,1,0:T(8,128)(2,1)}, u32[]{:S(2)}) copy-start(bf16[1,128,4096]{2,1,0:T(8,128)(2,1)} %param.4) | copy-start | bytes 3145732
  41.0 14.1 %collective-permute-start = (bf16[784,128]{1,0:T(8,128)(2,1)S(1)}, bf16[784,128]{1,0:T(8,128)(2,1)S(1)}, u32[]{:S(2)}, u32[]{:S(2)}) collective-permute-start(bf16[784,128]{1,0:T(8,128)(2,1)S(1)} %get-tuple-element.98), channel_id=1, source_target_pairs={{0,1},{1,2},{2,3},{3,0},{4,5},{5,6},{6,7},{7,4},{8,9},{9,10},{10,1... | collective-permute-start | bytes 602120 | tf_op jit(solution)/shard_map/ppermute | solution.py:154
  45.3 14.8 %collective-permute-start.1 = (bf16[784,128]{1,0:T(8,128)(2,1)S(1)}, bf16[784,128]{1,0:T(8,128)(2,1)S(1)}, u32[]{:S(2)}, u32[]{:S(2)}) collective-permute-start(bf16[784,128]{1,0:T(8,128)(2,1)S(1)} %get-tuple-element.98), channel_id=1, source_target_pairs={{0,2},{1,3},{2,0},{3,1},{4,6},{5,7},{6,4},{7,5},{8,10},{9,11},{10,... | collective-permute-start | bytes 602120 | tf_op jit(solution)/shard_map/ppermute | solution.py:154
  50.1 19.5 %collective-permute-start.2 = (bf16[784,128]{1,0:T(8,128)(2,1)S(1)}, bf16[784,128]{1,0:T(8,128)(2,1)S(1)}, u32[]{:S(2)}, u32[]{:S(2)}) collective-permute-start(bf16[784,128]{1,0:T(8,128)(2,1)S(1)} %get-tuple-element.98), channel_id=1, source_target_pairs={{0,3},{1,0},{2,1},{3,2},{4,7},{5,4},{6,5},{7,6},{8,11},{9,8},{10,9... | collective-permute-start | bytes 602120 | tf_op jit(solution)/shard_map/ppermute | solution.py:154
  69.7 33.3 %collective-permute-start.3 = (bf16[4,784,128]{2,1,0:T(8,128)(2,1)S(1)}, bf16[4,784,128]{2,1,0:T(8,128)(2,1)S(1)}, u32[]{:S(2)}, u32[]{:S(2)}) collective-permute-start(bf16[4,784,128]{2,1,0:T(8,128)(2,1)S(1)} %pad_maximum_fusion.refs_2_), channel_id=1, source_target_pairs={{0,4},{4,8},{8,12},{12,16},{16,20},{20,24},{24,28},{28,0},{1,5},{5... | collective-permute-start | bytes 2408456 | tf_op jit(solution)/shard_map/ppermute | solution.py:154
  73.1 29.9 %collective-permute-start.4 = (bf16[4,784,128]{2,1,0:T(8,128)(2,1)S(1)}, bf16[4,784,128]{2,1,0:T(8,128)(2,1)S(1)}, u32[]{:S(2)}, u32[]{:S(2)}) collective-permute-start(bf16[4,784,128]{2,1,0:T(8,128)(2,1)S(1)} %pad_maximum_fusion.refs_2_), channel_id=1, source_target_pairs={{0,28},{4,0},{8,4},{12,8},{16,12},{20,16},{24,20},{28,24},{1,29},{... | collective-permute-start | bytes 2408456 | tf_op jit(solution)/shard_map/ppermute | solution.py:154
  76.3 26.7 %collective-permute-start.5 = (bf16[8,272,128]{2,1,0:T(8,128)(2,1)S(1)}, bf16[8,272,128]{2,1,0:T(8,128)(2,1)S(1)}, u32[]{:S(2)}, u32[]{:S(2)}) collective-permute-start(bf16[8,272,128]{2,1,0:T(8,128)(2,1)S(1)} %all-to-all-done.2.refs_2_), channel_id=1, source_target_pairs={{0,1},{1,2},{2,3},{3,0},{4,5},{5,6},{6,7},{7,4},{8,9},{9,10},{10,1... | collective-permute-start | bytes 1671176 | tf_op jit(solution)/shard_map/ppermute | solution.py:154
  103.0 24.5 %collective-permute-start.6 = (bf16[4,784,128]{2,1,0:T(8,128)(2,1)S(1)}, bf16[4,784,128]{2,1,0:T(8,128)(2,1)S(1)}, u32[]{:S(2)}, u32[]{:S(2)}) collective-permute-start(bf16[4,784,128]{2,1,0:T(8,128)(2,1)S(1)} %collective-permute-done.3.refs_2_), channel_id=1, source_target_pairs={{0,4},{4,8},{8,12},{12,16},{16,20},{20,24},{24,28},{28,0},{1,5},{5... | collective-permute-start | bytes 2408456 | tf_op jit(solution)/shard_map/ppermute | solution.py:154
  105.2 22.4 %collective-permute-start.7 = (bf16[4,784,128]{2,1,0:T(8,128)(2,1)S(1)}, bf16[4,784,128]{2,1,0:T(8,128)(2,1)S(1)}, u32[]{:S(2)}, u32[]{:S(2)}) collective-permute-start(bf16[4,784,128]{2,1,0:T(8,128)(2,1)S(1)} %collective-permute-done.4.refs_3_), channel_id=1, source_target_pairs={{0,28},{4,0},{8,4},{12,8},{16,12},{20,16},{24,20},{28,24},{1,29},{... | collective-permute-start | bytes 2408456 | tf_op jit(solution)/shard_map/ppermute | solution.py:154
  109.5 18.0 %collective-permute-start.8 = (bf16[8,272,128]{2,1,0:T(8,128)(2,1)S(1)}, bf16[8,272,128]{2,1,0:T(8,128)(2,1)S(1)}, u32[]{:S(2)}, u32[]{:S(2)}) collective-permute-start(bf16[8,272,128]{2,1,0:T(8,128)(2,1)S(1)} %all-to-all-done.2.refs_2_), channel_id=1, source_target_pairs={{0,3},{1,0},{2,1},{3,2},{4,7},{5,4},{6,5},{7,6},{8,11},{9,8},{10,9... | collective-permute-start | bytes 1671176 | tf_op jit(solution)/shard_map/ppermute | solution.py:154
  112.4 15.1 %collective-permute-start.9 = (bf16[4,272,128]{2,1,0:T(8,128)(2,1)S(1)}, bf16[4,272,128]{2,1,0:T(8,128)(2,1)S(1)}, u32[]{:S(2)}, u32[]{:S(2)}) collective-permute-start(bf16[4,272,128]{2,1,0:T(8,128)(2,1)S(1)} %slice.20), channel_id=1, source_target_pairs={{0,1},{1,2},{2,3},{3,0},{4,5},{5,6},{6,7},{7,4},{8,9},{9,10},{10,1... | collective-permute-start | bytes 835592 | tf_op jit(solution)/shard_map/ppermute | solution.py:154
  127.5 15.7 %collective-permute-start.10 = (bf16[4,784,128]{2,1,0:T(8,128)(2,1)S(1)}, bf16[4,784,128]{2,1,0:T(8,128)(2,1)S(1)}, u32[]{:S(2)}, u32[]{:S(2)}) collective-permute-start(bf16[4,784,128]{2,1,0:T(8,128)(2,1)S(1)} %collective-permute-done.6.refs_2_), channel_id=1, source_target_pairs={{0,4},{4,8},{8,12},{12,16},{16,20},{20,24},{24,28},{28,0},{1,5},{5... | collective-permute-start | bytes 2408456 | tf_op jit(solution)/shard_map/ppermute | solution.py:154
  130.2 24.0 %collective-permute-start.11 = (bf16[4,784,128]{2,1,0:T(8,128)(2,1)S(1)}, bf16[4,784,128]{2,1,0:T(8,128)(2,1)S(1)}, u32[]{:S(2)}, u32[]{:S(2)}) collective-permute-start(bf16[4,784,128]{2,1,0:T(8,128)(2,1)S(1)} %collective-permute-done.7.refs_3_), channel_id=1, source_target_pairs={{0,28},{4,0},{8,4},{12,8},{16,12},{20,16},{24,20},{28,24},{1,29},{... | collective-permute-start | bytes 2408456 | tf_op jit(solution)/shard_map/ppermute | solution.py:154
  134.1 8.5 %collective-permute-start.12 = (bf16[4,272,128]{2,1,0:T(8,128)(2,1)S(1)}, bf16[4,272,128]{2,1,0:T(8,128)(2,1)S(1)}, u32[]{:S(2)}, u32[]{:S(2)}) collective-permute-start(bf16[4,272,128]{2,1,0:T(8,128)(2,1)S(1)} %slice.21), channel_id=1, source_target_pairs={{0,3},{1,0},{2,1},{3,2},{4,7},{5,4},{6,5},{7,6},{8,11},{9,8},{10,9... | collective-permute-start | bytes 835592 | tf_op jit(solution)/shard_map/ppermute | solution.py:154
  154.2 16.0 %collective-permute-start.13 = (bf16[2,784,128]{2,1,0:T(8,128)(2,1)S(1)}, bf16[2,784,128]{2,1,0:T(8,128)(2,1)S(1)}, u32[]{:S(2)}, u32[]{:S(2)}) collective-permute-start(bf16[2,784,128]{2,1,0:T(8,128)(2,1)S(1)} %slice.22), channel_id=1, source_target_pairs={{0,4},{4,8},{8,12},{12,16},{16,20},{20,24},{24,28},{28,0},{1,5},{5... | collective-permute-start | bytes 1204232 | tf_op jit(solution)/shard_map/ppermute | solution.py:154
  159.9 11.6 %collective-permute-start.14 = (bf16[2,784,128]{2,1,0:T(8,128)(2,1)S(1)}, bf16[2,784,128]{2,1,0:T(8,128)(2,1)S(1)}, u32[]{:S(2)}, u32[]{:S(2)}) collective-permute-start(bf16[2,784,128]{2,1,0:T(8,128)(2,1)S(1)} %slice.23), channel_id=1, source_target_pairs={{0,28},{4,0},{8,4},{12,8},{16,12},{20,16},{24,20},{28,24},{1,29},{... | collective-permute-start | bytes 1204232 | tf_op jit(solution)/shard_map/ppermute | solution.py:154

commit v8 on v6

--- a/solution.py
+++ b/solution.py
@@ -19,8 +19,7 @@
 SLABS = 8
 POS_ROWS = 16
 PART = 2 * ROWS
-LINE_ROWS = 3 * PART + 2 * POS_ROWS
-HANDED_ROWS = 2 * PART + POS_ROWS
+LINE_ROWS = 2 * PART + POS_ROWS
 MASKED = -1e30
 SCALE = 1.4426950408889634 / HD**0.5
 SECTION = ("x", "yl", "core")
@@ -28,7 +27,7 @@
 
 def attend_body(shards, first, last, *refs):
     it = iter(refs)
-    info, q_ref, pos_ref = next(it), next(it), next(it)
+    warm_ref, q_ref, pos_ref = next(it), next(it), next(it)
     blocks = [next(it) for _ in shards]
     if not first:
         m_in, l_in, a_in = next(it), next(it), next(it)
@@ -38,13 +37,12 @@
     row = lax.broadcasted_iota(jnp.int32, (BLOCK, ROWS), 0).astype(jnp.float32)
     at = 0
     for n, ref in zip(shards, blocks):
-        place = LAYERS + (0 if ref.shape[1] == LINE_ROWS else 3)
-        starts = [pl.multiple_of(info[place + i], POS_ROWS) for i in range(3)]
         for i in range(n):
             for source in range(2):
-                k[source, at : at + ROWS, :] = ref[i, pl.ds(starts[source], ROWS), :]
-                v[source, :HD, at : at + ROWS] = ref[i, pl.ds(starts[source] + ROWS, ROWS), :]
-            ids = ref[i, pl.ds(starts[2], POS_ROWS), :].astype(jnp.float32)
+                base = source * 2 * ROWS
+                k[source, at : at + ROWS, :] = ref[i, base : base + ROWS]
+                v[source, :HD, at : at + ROWS] = ref[i, base + ROWS : base + 2 * ROWS]
+            ids = ref[i, 4 * ROWS : 4 * ROWS + POS_ROWS].astype(jnp.float32)
             for part in range(ROWS // BLOCK):
                 key_pos = ids[0:1, part * BLOCK : part * BLOCK + 1] * BLOCK + row
                 rows = slice(at + part * BLOCK, at + (part + 1) * BLOCK)
@@ -56,7 +54,7 @@
     def scores(j):
         q = jnp.concatenate([q_ref[j, :, h * HD : (h + 1) * HD] for h in range(HEADS)], axis=0)
         return lax.dot_general(
-            k[info[j]], q, (((1,), (1,)), ((), ())), preferred_element_type=jnp.float32
+            k[warm_ref[j]], q, (((1,), (1,)), ((), ())), preferred_element_type=jnp.float32
         )
 
     def absorb(j, s):
@@ -67,7 +65,7 @@
             m = jnp.maximum(m_old, m)
         w = jnp.exp2((s - m) * SCALE).astype(jnp.bfloat16)
         o = lax.dot_general(
-            v[info[j]], w, (((1,), (0,)), ((), ())), preferred_element_type=jnp.float32
+            v[warm_ref[j]], w, (((1,), (0,)), ((), ())), preferred_element_type=jnp.float32
         )
         acc, den = o[:HD], o[HD : HD + 8]
         if not first:
@@ -94,10 +92,10 @@
             s = ahead
 
 
-def attend(info, q, pos, blocks, state, last):
+def attend(warm, q, pos, blocks, state, last):
     shards = tuple(b.shape[0] for b in blocks)
     count = sum(shards) * ROWS
-    args = [info, q, pos, *blocks]
+    args = [warm, q, pos, *blocks]
     aliases = {}
     if state is not None:
         if not last:
@@ -154,15 +152,14 @@
     def body(core_ref, mine_ref, theirs_ref, out_ref):
         def fill(k_ref, v_ref):
             for i in range(mine.shape[0]):
-                for s in range(3):
+                for s in range(2):
                     rows = slice(s * ROWS, (s + 1) * ROWS)
-                    at = POS_ROWS + s * PART
+                    at = s * PART
                     out_ref[i, at : at + ROWS] = k_ref[i, rows]
                     out_ref[i, at + ROWS : at + PART] = v_ref[i, rows]
 
         for i in range(mine.shape[0]):
-            out_ref[i, :POS_ROWS] = mine_ref[i, 3 * ROWS :]
-            out_ref[i, LINE_ROWS - POS_ROWS :] = mine_ref[i, 3 * ROWS :]
+            out_ref[i, 2 * PART :] = mine_ref[i, 2 * ROWS :]
 
         @pl.when(core_ref[0] == 0)
         def _():
@@ -187,20 +184,20 @@
 
 
 def swap(slabs, index):
-    other = turn(pick(slabs, index), "core", 2, 1)
+    other = turn(pick(slabs, index), "yl", 2, 1)
     return lax.dynamic_update_index_in_dim(slabs, other, index, 0)
 
 
 def per_device(sizes, queries, key_values, token_pos, layer_of_section):
     nz, nyh = sizes["z"], sizes["yh"]
-    core = lax.axis_index("core")
+    core, yl = lax.axis_index("core"), lax.axis_index("yl")
     ids = jnp.arange(LAYERS, dtype=jnp.int32)
     holder = jnp.sum(jnp.where(layer_of_section[None, :] == ids[:, None], ids[None, :], 0), axis=1)
-    warm, other_warm = pick(holder, core), pick(holder, 1 - core)
+    warm, other_warm = pick(holder, yl), pick(holder, 1 - yl)
     pieces = packed(key_values[0].reshape(ROWS, 2 * KVH * HD))
     pieces = lax.all_to_all(pieces, SECTION, 0, 0)
     block_ids = jnp.broadcast_to((token_pos // BLOCK).astype(jnp.bfloat16)[None, :], (POS_ROWS, ROWS))
-    wanted = [holder[0], holder[LAYERS - 1], holder[1]]
+    wanted = [holder[LAYERS - 1], warm]
     shard = jnp.concatenate([pick(pieces, index) for index in wanted] + [block_ids], axis=0)
     mine = jnp.stack([shard] + [turn(shard, "yh", nyh, shift) for shift in range(1, nyh)])
     theirs = turn(mine, "core", 2, 1)
@@ -214,21 +211,16 @@
         return lax.ppermute(value, ("core", "z"), pairs)
 
     def handed(value):
-        start = (1 - core) * (PART + POS_ROWS)
-        return turn(lax.dynamic_slice_in_dim(value, start, HANDED_ROWS, axis=1), "core", 2, 1)
+        return turn(value, "core", 2, 1)
 
     arrived = onward(line)
     q = lax.all_to_all(q, SECTION, 0, 0)
     q = swap(q, other_warm)
     use_warm = ((ids == warm) | (ids == other_warm)).astype(jnp.int32)
-    top_row = POS_ROWS + PART
-    whole_rows = [top_row, POS_ROWS + 2 * PART * core, 0]
-    handed_rows = [(1 - core) * top_row, (1 - core) * POS_ROWS + core * PART, core * 2 * PART]
-    info = jnp.concatenate([use_warm, jnp.stack(whole_rows + handed_rows).astype(jnp.int32)])
     pos = token_pos.astype(jnp.float32)[None, :]
 
     def part(blocks, state, last=False):
-        return attend(info, q, pos, blocks, state, last)
+        return attend(use_warm, q, pos, blocks, state, last)
 
     held, state = [line], None
     half = nyh // 2

time: 165 us -> 160 us (0.970)
  local copies, waits for them, and re-layouts: 16.1 us -> 11 us
  waiting for transfers between devices: 19.5 us -> 15.2 us
  starting transfers between devices: 62.5 us -> 66.5 us
  between operations: 7.79 us -> 6.03 us
    ppermute x4, waiting for transfers between devices: 9.27 us -> 4.4 us  [onward(): return lax.ppermute(value, ('core', 'z'), pairs)]
    ppermute x10, starting transfers between devices: 28.1 us -> 32.6 us  [turn(): lax.ppermute(value, axis, [(i, (i + shift) % size) for i in range(size)])]
    dynamic_slice x4 -> x0, local copies, waits for them, and re-layouts: 3.87 us -> none  [handed(): lax.dynamic_slice_in_dim(value, start, HANDED_ROWS, axis=1)]
    all_to_all x1, waiting for transfers between devices: 3.54 us -> 5.29 us  [per_device(): pieces = lax.all_to_all(pieces, SECTION, 0, 0)]
    unnamed x24 -> x20, local copies, waits for them, and re-layouts: 7.09 us -> 6.02 us
  transfers between devices with their start and end apart: 16 -> 16, of which waited for: 6 -> 7; matrix products, arithmetic and copies ran while one was open for 4% -> 2% of each run, Pallas kernels for 17% -> 18%
where the time goes in v8:
time: 160 us; the launch traced here: 159 us
  starting transfers between devices  66.5 us (42%)
  Pallas kernels  36.2 us (23%)
  blocking collectives  22.3 us (14%)
  waiting for transfers between devices  15.2 us (10%)
  local copies, waits for them, and re-layouts  11 us (7%)
  between operations  6.03 us (4%)
    ppermute x10, starting transfers between devices, turn(): lax.ppermute(value, axis, [(i, (i + shift) % size) for i in range(size)])  32.6 us
    pallas_call x5, Pallas kernels, attend(): pl.pallas_call(functools.partial(attend_body, shards, state is None, last...  32.5 us
    all_to_all x1, blocking collectives, per_device(): out = lax.all_to_all(out, SECTION, 0, 0)  22.3 us
    ppermute x4, starting transfers between devices, onward(): return lax.ppermute(value, ('core', 'z'), pairs)  19.8 us
    all_to_all x1, starting transfers between devices, per_device(): pieces = lax.all_to_all(pieces, SECTION, 0, 0)  10.2 us
    unnamed x20, local copies, waits for them, and re-layouts  6.02 us
    ppermute x10, waiting for transfers between devices, turn(): lax.ppermute(value, axis, [(i, (i + shift) % size) for i in range(size)])  5.48 us
    all_to_all x1, waiting for transfers between devices, per_device(): pieces = lax.all_to_all(pieces, SECTION, 0, 0)  5.29 us
  transfers between devices with their start and end apart: 16, of which 7 were waited for; matrix products, arithmetic and copies ran while one was open for 2% of the time, Pallas kernels for 18%

profile of v8, /device:TPU:1, one launch (start us, length us, event | category | flops | bytes accessed | tf_op | source)
XLA Modules:
  0.0 158.7 jit_solution(9873505731340971366)
XLA Ops:
  3.6 10.2 %all-to-all-start = ((bf16[16,128,128]{2,1,0:T(8,128)(2,1)}), bf16[16,128,128]{2,1,0:T(8,128)(2,1)S(1)}, u32[]{:S(2)}, u32[]{:S(2)}) async-start(bf16[16,128,128]{2,1,0:T(8,128)(2,1)} %pack.1), calls=%async_computation | async-start | bytes 1048576 | tf_op jit(solution)/shard_map/all_to_all | solution.py:198
  18.4 5.3 %all-to-all-done = bf16[16,128,128]{2,1,0:T(8,128)(2,1)S(1)} async-done(((bf16[16,128,128]{2,1,0:T(8,128)(2,1)}), bf16[16,128,128]{2,1,0:T(8,128)(2,1)S(1)}, u32[]{:S(2)}, u32[]{:S(2)}) %all-to-all-start) | async-done | bytes 524320 | tf_op jit(solution)/shard_map/all_to_all | solution.py:198
  23.8 3.1 %collective-permute-start.1 = (bf16[272,128]{1,0:T(8,128)(2,1)S(1)}, bf16[272,128]{1,0:T(8,128)(2,1)S(1)}, u32[]{:S(2)}, u32[]{:S(2)}) collective-permute-start(bf16[272,128]{1,0:T(8,128)(2,1)S(1)} %get-tuple-element.72), channel_id=1, source_target_pairs={{0,2},{1,3},{2,0},{3,1},{4,6},{5,7},{6,4},{7,5},{8,10},{9,11},{10,... | collective-permute-start | bytes 208904 | tf_op jit(solution)/shard_map/ppermute | solution.py:130
  26.8 2.4 %collective-permute-start = (bf16[272,128]{1,0:T(8,128)(2,1)S(1)}, bf16[272,128]{1,0:T(8,128)(2,1)S(1)}, u32[]{:S(2)}, u32[]{:S(2)}) collective-permute-start(bf16[272,128]{1,0:T(8,128)(2,1)S(1)} %get-tuple-element.72), channel_id=1, source_target_pairs={{0,1},{1,2},{2,3},{3,0},{4,5},{5,6},{6,7},{7,4},{8,9},{9,10},{10,1... | collective-permute-start | bytes 208904 | tf_op jit(solution)/shard_map/ppermute | solution.py:130
  29.3 5.0 %collective-permute-start.2 = (bf16[272,128]{1,0:T(8,128)(2,1)S(1)}, bf16[272,128]{1,0:T(8,128)(2,1)S(1)}, u32[]{:S(2)}, u32[]{:S(2)}) collective-permute-start(bf16[272,128]{1,0:T(8,128)(2,1)S(1)} %get-tuple-element.72), channel_id=1, source_target_pairs={{0,3},{1,0},{2,1},{3,2},{4,7},{5,4},{6,5},{7,6},{8,11},{9,8},{10,9... | collective-permute-start | bytes 208904 | tf_op jit(solution)/shard_map/ppermute | solution.py:130
  34.5 2.4 %collective-permute-done.2 = bf16[272,128]{1,0:T(8,128)(2,1)S(1)} collective-permute-done((bf16[272,128]{1,0:T(8,128)(2,1)S(1)}, bf16[272,128]{1,0:T(8,128)(2,1)S(1)}, u32[]{:S(2)}, u32[]{:S(2)}) %collective-permute-start.2) | collective-permute-done | bytes 69664 | tf_op jit(solution)/shard_map/ppermute | solution.py:130
  36.9 5.2 %collective-permute-start.3 = (bf16[4,272,128]{2,1,0:T(8,128)(2,1)S(1)}, bf16[4,272,128]{2,1,0:T(8,128)(2,1)S(1)}, u32[]{:S(2)}, u32[]{:S(2)}) collective-permute-start(bf16[4,272,128]{2,1,0:T(8,128)(2,1)S(1)} %pad_maximum_fusion.mine_ref), channel_id=1, source_target_pairs={{0,32},{32,0},{1,33},{33,1},{2,34},{34,2},{3,35},{35,3},{4,36},{36... | collective-permute-start | bytes 835592 | tf_op jit(solution)/shard_map/ppermute | solution.py:130
  47.2 3.8 %all-to-all-start.1 = ((bf16[16,128,256]{2,1,0:T(8,128)(2,1)}), bf16[16,128,256]{2,1,0:T(8,128)(2,1)S(1)}, u32[]{:S(2)}, u32[]{:S(2)}) async-start(bf16[16,128,256]{2,1,0:T(8,128)(2,1)} %bitcast.12), calls=%async_computation.1 | async-start | bytes 2097152 | tf_op jit(solution)/shard_map/all_to_all | solution.py:217
  51.0 9.6 %collective-permute-start.5 = (bf16[4,528,128]{2,1,0:T(8,128)(2,1)S(1)}, bf16[4,528,128]{2,1,0:T(8,128)(2,1)}, u32[]{:S(2)}, u32[]{:S(2)}) collective-permute-start(bf16[4,528,128]{2,1,0:T(8,128)(2,1)S(1)} %copy-done), channel_id=1, source_target_pairs={{0,4},{4,8},{8,12},{12,16},{16,20},{20,24},{24,28},{28,0},{32,60},... | collective-permute-start | bytes 1622024 | tf_op jit(solution)/shard_map/ppermute | solution.py:211
  62.5 4.4 %collective-permute-done.5.refs_3_ = bf16[4,528,128]{2,1,0:T(8,128)(2,1)} collective-permute-done((bf16[4,528,128]{2,1,0:T(8,128)(2,1)S(1)}, bf16[4,528,128]{2,1,0:T(8,128)(2,1)}, u32[]{:S(2)}, u32[]{:S(2)}) %collective-permute-start.5) | collective-permute-done | bytes 540704 | tf_op jit(solution)/shard_map/ppermute | solution.py:211
  66.9 3.5 %collective-permute-start.7 = (bf16[4,528,128]{2,1,0:T(8,128)(2,1)}, bf16[4,528,128]{2,1,0:T(8,128)(2,1)}, u32[]{:S(2)}, u32[]{:S(2)}) collective-permute-start(bf16[4,528,128]{2,1,0:T(8,128)(2,1)} %collective-permute-done.5.refs_3_), channel_id=1, source_target_pairs={{0,32},{32,0},{1,33},{33,1},{2,34},{34,2},{3,35},{35,3},{4,36},{36... | collective-permute-start | bytes 1622024 | tf_op jit(solution)/shard_map/ppermute | solution.py:130
  70.5 3.7 %collective-permute-start.6 = (bf16[4,528,128]{2,1,0:T(8,128)(2,1)}, bf16[4,528,128]{2,1,0:T(8,128)(2,1)}, u32[]{:S(2)}, u32[]{:S(2)}) collective-permute-start(bf16[4,528,128]{2,1,0:T(8,128)(2,1)} %collective-permute-done.5.refs_3_), channel_id=1, source_target_pairs={{0,4},{4,8},{8,12},{12,16},{16,20},{20,24},{24,28},{28,0},{32,60},... | collective-permute-start | bytes 1622024 | tf_op jit(solution)/shard_map/ppermute | solution.py:211
  74.2 3.4 %collective-permute-start.4 = (bf16[128,256]{1,0:T(8,128)(2,1)S(1)}, bf16[128,256]{1,0:T(8,128)(2,1)S(1)}, u32[]{:S(2)}, u32[]{:S(2)}) collective-permute-start(bf16[128,256]{1,0:T(8,128)(2,1)S(1)} %dynamic-slice_bitcast_fusion.1), channel_id=1, source_target_pairs={{0,64},{64,0},{1,65},{65,1},{2,66},{66,2},{3,67},{67,3},{4,68},{68... | collective-permute-start | bytes 196616 | tf_op jit(solution)/shard_map/ppermute | solution.py:130
  80.7 4.5 %attend.5 = (f32[16,8,256]{2,1,0:T(8,128)S(1)}, f32[16,8,256]{2,1,0:T(8,128)S(1)}, f32[16,128,256]{2,1,0:T(8,128)S(1)}) custom-call(s32[16]{0:T(128)S(1)} %or_convert_fusion.refs_0_, bf16[16,128,256]{2,1,0:T(8,128)(2,1)S(1)} %bitcast_dynamic-update-slice_fusion.1.refs_1_, f32[1,128]{1,0:T(1,128)S(1)} %get-tuple-element.73.refs_2_, ...), custom_call_target="tpu_custom_call" | custom-call | flops 1073741824 | bytes 8388608 | tf_op jit(solution)/shard_map/attend/pallas_call | solution.py:108
  87.1 3.9 %collective-permute-start.8 = (bf16[4,528,128]{2,1,0:T(8,128)(2,1)}, bf16[4,528,128]{2,1,0:T(8,128)(2,1)}, u32[]{:S(2)}, u32[]{:S(2)}) collective-permute-start(bf16[4,528,128]{2,1,0:T(8,128)(2,1)} %collective-permute-done.6.refs_3_), channel_id=1, source_target_pairs={{0,4},{4,8},{8,12},{12,16},{16,20},{20,24},{24,28},{28,0},{32,60},... | collective-permute-start | bytes 1622024 | tf_op jit(solution)/shard_map/ppermute | solution.py:211
  91.1 7.8 %attend.6 = (f32[16,8,256]{2,1,0:T(8,128)S(1)}, f32[16,8,256]{2,1,0:T(8,128)S(1)}, f32[16,128,256]{2,1,0:T(8,128)S(1)}) custom-call(s32[16]{0:T(128)S(1)} %or_convert_fusion.refs_0_, bf16[16,128,256]{2,1,0:T(8,128)(2,1)S(1)} %bitcast_dynamic-update-slice_fusion.1.refs_1_, ...), custom_call_target="tpu_custom_call", output_to_operand_aliasing={{0}: (5, {}), {1}: (6, {}), {2}: (7, {})} | custom-call | flops 2147483648 | bytes 8388608 | tf_op jit(solution)/shard_map/attend/pallas_call | solution.py:108
  99.7 2.6 %collective-permute-start.11 = (bf16[4,528,128]{2,1,0:T(8,128)(2,1)}, bf16[4,528,128]{2,1,0:T(8,128)(2,1)}, u32[]{:S(2)}, u32[]{:S(2)}) collective-permute-start(bf16[4,528,128]{2,1,0:T(8,128)(2,1)} %collective-permute-done.8.refs_3_), channel_id=1, source_target_pairs={{0,32},{32,0},{1,33},{33,1},{2,34},{34,2},{3,35},{35,3},{4,36},{36... | collective-permute-start | bytes 1622024 | tf_op jit(solution)/shard_map/ppermute | solution.py:130
  103.3 2.7 %collective-permute-start.10 = (bf16[2,528,128]{2,1,0:T(8,128)(2,1)S(1)}, bf16[2,528,128]{2,1,0:T(8,128)(2,1)S(1)}, u32[]{:S(2)}, u32[]{:S(2)}) collective-permute-start(bf16[2,528,128]{2,1,0:T(8,128)(2,1)S(1)} %constant_dynamic-slice_fusion), channel_id=1, source_target_pairs={{0,4},{4,8},{8,12},{12,16},{16,20},{20,24},{24,28},{28,0},{32,60},... | collective-permute-start | bytes 811016 | tf_op jit(solution)/shard_map/ppermute | solution.py:211
  107.0 7.7 %attend.7 = (f32[16,8,256]{2,1,0:T(8,128)S(1)}, f32[16,8,256]{2,1,0:T(8,128)S(1)}, f32[16,128,256]{2,1,0:T(8,128)S(1)}) custom-call(s32[16]{0:T(128)S(1)} %or_convert_fusion.refs_0_, bf16[16,128,256]{2,1,0:T(8,128)(2,1)S(1)} %bitcast_dynamic-update-slice_fusion.1.refs_1_, ...), custom_call_target="tpu_custom_call", output_to_operand_aliasing={{0}: (5, {}), {1}: (6, {}), {2}: (7, {})} | custom-call | flops 2147483648 | bytes 8388608 | tf_op jit(solution)/shard_map/attend/pallas_call | solution.py:108
  114.7 2.1 %collective-permute-start.12 = (bf16[2,528,128]{2,1,0:T(8,128)(2,1)S(1)}, bf16[2,528,128]{2,1,0:T(8,128)(2,1)S(1)}, u32[]{:S(2)}, u32[]{:S(2)}) collective-permute-start(bf16[2,528,128]{2,1,0:T(8,128)(2,1)S(1)} %collective-permute-done.10.refs_3_), channel_id=1, source_target_pairs={{0,32},{32,0},{1,33},{33,1},{2,34},{34,2},{3,35},{35,3},{4,36},{36... | collective-permute-start | bytes 811016 | tf_op jit(solution)/shard_map/ppermute | solution.py:130
  116.8 7.8 %attend.8 = (f32[16,8,256]{2,1,0:T(8,128)S(1)}, f32[16,8,256]{2,1,0:T(8,128)S(1)}, f32[16,128,256]{2,1,0:T(8,128)S(1)}) custom-call(s32[16]{0:T(128)S(1)} %or_convert_fusion.refs_0_, bf16[16,128,256]{2,1,0:T(8,128)(2,1)S(1)} %bitcast_dynamic-update-slice_fusion.1.refs_1_, ...), custom_call_target="tpu_custom_call", output_to_operand_aliasing={{0}: (5, {}), {1}: (6, {}), {2}: (7, {})} | custom-call | flops 2147483648 | bytes 8388608 | tf_op jit(solution)/shard_map/attend/pallas_call | solution.py:108
  124.7 4.7 %attend.9 = bf16[16,128,256]{2,1,0:T(8,128)(2,1)S(1)} custom-call(s32[16]{0:T(128)S(1)} %or_convert_fusion.refs_0_, bf16[16,128,256]{2,1,0:T(8,128)(2,1)S(1)} %bitcast_dynamic-update-slice_fusion.1.refs_1_, f32[1,128]{1,0:T(1,128)S(1)} %get-tuple-element.73.refs_2_, bf16[2,528,128]{2,1,0:T(8,128)(2,1)S(1)} %collective-permute-done.10.refs_3_, ...), custom_call_target="tpu_custom_call" | custom-call | flops 1073741824 | bytes 8388608 | tf_op jit(solution)/shard_map/attend/pallas_call | solution.py:108
  129.4 3.4 %collective-permute-start.13 = (bf16[128,256]{1,0:T(8,128)(2,1)S(1)}, bf16[128,256]{1,0:T(8,128)(2,1)S(1)}, u32[]{:S(2)}, u32[]{:S(2)}) collective-permute-start(bf16[128,256]{1,0:T(8,128)(2,1)S(1)} %dynamic-slice_bitcast_fusion), channel_id=1, source_target_pairs={{0,64},{64,0},{1,65},{65,1},{2,66},{66,2},{3,67},{67,3},{4,68},{68... | collective-permute-start | bytes 196616 | tf_op jit(solution)/shard_map/ppermute | solution.py:130
  134.4 22.3 %all_to_all.15 = bf16[16,128,256]{2,1,0:T(8,128)(2,1)S(1)} all-to-all(bf16[16,128,256]{2,1,0:T(8,128)(2,1)S(1)} %bitcast_dynamic-update-slice_fusion), channel_id=1, replica_groups=mesh['x'=4,'yl'=2,'core'=2,'z'=8,'yh'=4] {'x','yl','core'}, dimensions={0} | all-to-all | bytes 2097152 | tf_op jit(solution)/shard_map/all_to_all | solution.py:239
  (52 shorter events, 21.2 us)
Async XLA Ops:
  0.0 13.9 %copy-start.7 = (s32[16]{0:T(128)S(1)}, s32[16]{0:T(128)}, u32[]{:S(2)}) copy-start(s32[16]{0:T(128)} %param.7) | copy-start | bytes 196
  0.0 18.4 %copy-start.8 = (s32[128]{0:T(128)S(1)}, s32[128]{0:T(128)}, u32[]{:S(2)}) copy-start(s32[128]{0:T(128)} %param.6) | copy-start | bytes 1540
  0.0 42.2 %copy-start.5 = (bf16[1,128,4096]{2,1,0:T(8,128)(2,1)S(1)}, bf16[1,128,4096]{2,1,0:T(8,128)(2,1)}, u32[]{:S(2)}) copy-start(bf16[1,128,4096]{2,1,0:T(8,128)(2,1)} %param.4) | copy-start | bytes 3145732
  3.6 20.1 %all-to-all-start = ((bf16[16,128,128]{2,1,0:T(8,128)(2,1)}), bf16[16,128,128]{2,1,0:T(8,128)(2,1)S(1)}, u32[]{:S(2)}, u32[]{:S(2)}) async-start(bf16[16,128,128]{2,1,0:T(8,128)(2,1)} %pack.1), calls=%async_computation | async-start | bytes 1048576 | tf_op jit(solution)/shard_map/all_to_all | solution.py:198
  23.8 10.5 %collective-permute-start.1 = (bf16[272,128]{1,0:T(8,128)(2,1)S(1)}, bf16[272,128]{1,0:T(8,128)(2,1)S(1)}, u32[]{:S(2)}, u32[]{:S(2)}) collective-permute-start(bf16[272,128]{1,0:T(8,128)(2,1)S(1)} %get-tuple-element.72), channel_id=1, source_target_pairs={{0,2},{1,3},{2,0},{3,1},{4,6},{5,7},{6,4},{7,5},{8,10},{9,11},{10,... | collective-permute-start | bytes 208904 | tf_op jit(solution)/shard_map/ppermute | solution.py:130
  26.8 7.6 %collective-permute-start = (bf16[272,128]{1,0:T(8,128)(2,1)S(1)}, bf16[272,128]{1,0:T(8,128)(2,1)S(1)}, u32[]{:S(2)}, u32[]{:S(2)}) collective-permute-start(bf16[272,128]{1,0:T(8,128)(2,1)S(1)} %get-tuple-element.72), channel_id=1, source_target_pairs={{0,1},{1,2},{2,3},{3,0},{4,5},{5,6},{6,7},{7,4},{8,9},{9,10},{10,1... | collective-permute-start | bytes 208904 | tf_op jit(solution)/shard_map/ppermute | solution.py:130
  29.3 7.6 %collective-permute-start.2 = (bf16[272,128]{1,0:T(8,128)(2,1)S(1)}, bf16[272,128]{1,0:T(8,128)(2,1)S(1)}, u32[]{:S(2)}, u32[]{:S(2)}) collective-permute-start(bf16[272,128]{1,0:T(8,128)(2,1)S(1)} %get-tuple-element.72), channel_id=1, source_target_pairs={{0,3},{1,0},{2,1},{3,2},{4,7},{5,4},{6,5},{7,6},{8,11},{9,8},{10,9... | collective-permute-start | bytes 208904 | tf_op jit(solution)/shard_map/ppermute | solution.py:130
  36.9 6.4 %copy-start.4 = (bf16[4,272,128]{2,1,0:T(8,128)(2,1)}, bf16[4,272,128]{2,1,0:T(8,128)(2,1)S(1)}, u32[]{:S(2)}) copy-start(bf16[4,272,128]{2,1,0:T(8,128)(2,1)S(1)} %pad_maximum_fusion.mine_ref) | copy-start | bytes 835588
  36.9 6.4 %collective-permute-start.3 = (bf16[4,272,128]{2,1,0:T(8,128)(2,1)S(1)}, bf16[4,272,128]{2,1,0:T(8,128)(2,1)S(1)}, u32[]{:S(2)}, u32[]{:S(2)}) collective-permute-start(bf16[4,272,128]{2,1,0:T(8,128)(2,1)S(1)} %pad_maximum_fusion.mine_ref), channel_id=1, source_target_pairs={{0,32},{32,0},{1,33},{33,1},{2,34},{34,2},{3,35},{35,3},{4,36},{36... | collective-permute-start | bytes 835592 | tf_op jit(solution)/shard_map/ppermute | solution.py:130
  45.9 5.1 %copy-start = (bf16[4,528,128]{2,1,0:T(8,128)(2,1)S(1)}, bf16[4,528,128]{2,1,0:T(8,128)(2,1)}, u32[]{:S(2)}) copy-start(bf16[4,528,128]{2,1,0:T(8,128)(2,1)} %join.1.refs_3_) | copy-start | bytes 1622020
  47.2 26.9 %all-to-all-start.1 = ((bf16[16,128,256]{2,1,0:T(8,128)(2,1)}), bf16[16,128,256]{2,1,0:T(8,128)(2,1)S(1)}, u32[]{:S(2)}, u32[]{:S(2)}) async-start(bf16[16,128,256]{2,1,0:T(8,128)(2,1)} %bitcast.12), calls=%async_computation.1 | async-start | bytes 2097152 | tf_op jit(solution)/shard_map/all_to_all | solution.py:217
  51.0 15.9 %collective-permute-start.5 = (bf16[4,528,128]{2,1,0:T(8,128)(2,1)S(1)}, bf16[4,528,128]{2,1,0:T(8,128)(2,1)}, u32[]{:S(2)}, u32[]{:S(2)}) collective-permute-start(bf16[4,528,128]{2,1,0:T(8,128)(2,1)S(1)} %copy-done), channel_id=1, source_target_pairs={{0,4},{4,8},{8,12},{12,16},{16,20},{20,24},{24,28},{28,0},{32,60},... | collective-permute-start | bytes 1622024 | tf_op jit(solution)/shard_map/ppermute | solution.py:211
  66.9 18.3 %collective-permute-start.7 = (bf16[4,528,128]{2,1,0:T(8,128)(2,1)}, bf16[4,528,128]{2,1,0:T(8,128)(2,1)}, u32[]{:S(2)}, u32[]{:S(2)}) collective-permute-start(bf16[4,528,128]{2,1,0:T(8,128)(2,1)} %collective-permute-done.5.refs_3_), channel_id=1, source_target_pairs={{0,32},{32,0},{1,33},{33,1},{2,34},{34,2},{3,35},{35,3},{4,36},{36... | collective-permute-start | bytes 1622024 | tf_op jit(solution)/shard_map/ppermute | solution.py:130
  70.5 14.7 %collective-permute-start.6 = (bf16[4,528,128]{2,1,0:T(8,128)(2,1)}, bf16[4,528,128]{2,1,0:T(8,128)(2,1)}, u32[]{:S(2)}, u32[]{:S(2)}) collective-permute-start(bf16[4,528,128]{2,1,0:T(8,128)(2,1)} %collective-permute-done.5.refs_3_), channel_id=1, source_target_pairs={{0,4},{4,8},{8,12},{12,16},{16,20},{20,24},{24,28},{28,0},{32,60},... | collective-permute-start | bytes 1622024 | tf_op jit(solution)/shard_map/ppermute | solution.py:211
  74.2 5.4 %collective-permute-start.4 = (bf16[128,256]{1,0:T(8,128)(2,1)S(1)}, bf16[128,256]{1,0:T(8,128)(2,1)S(1)}, u32[]{:S(2)}, u32[]{:S(2)}) collective-permute-start(bf16[128,256]{1,0:T(8,128)(2,1)S(1)} %dynamic-slice_bitcast_fusion.1), channel_id=1, source_target_pairs={{0,64},{64,0},{1,65},{65,1},{2,66},{66,2},{3,67},{67,3},{4,68},{68... | collective-permute-start | bytes 196616 | tf_op jit(solution)/shard_map/ppermute | solution.py:130
  79.7 1.0 copy-start.1
  85.2 13.7 %collective-permute-start.9 = (bf16[4,528,128]{2,1,0:T(8,128)(2,1)}, bf16[4,528,128]{2,1,0:T(8,128)(2,1)S(1)}, u32[]{:S(2)}, u32[]{:S(2)}) collective-permute-start(bf16[4,528,128]{2,1,0:T(8,128)(2,1)} %collective-permute-done.6.refs_3_), channel_id=1, source_target_pairs={{0,32},{32,0},{1,33},{33,1},{2,34},{34,2},{3,35},{35,3},{4,36},{36... | collective-permute-start | bytes 1622024 | tf_op jit(solution)/shard_map/ppermute | solution.py:130
  87.1 12.6 %collective-permute-start.8 = (bf16[4,528,128]{2,1,0:T(8,128)(2,1)}, bf16[4,528,128]{2,1,0:T(8,128)(2,1)}, u32[]{:S(2)}, u32[]{:S(2)}) collective-permute-start(bf16[4,528,128]{2,1,0:T(8,128)(2,1)} %collective-permute-done.6.refs_3_), channel_id=1, source_target_pairs={{0,4},{4,8},{8,12},{12,16},{16,20},{20,24},{24,28},{28,0},{32,60},... | collective-permute-start | bytes 1622024 | tf_op jit(solution)/shard_map/ppermute | solution.py:211
  98.9 0.8 copy-start.2
  99.7 15.0 %collective-permute-start.11 = (bf16[4,528,128]{2,1,0:T(8,128)(2,1)}, bf16[4,528,128]{2,1,0:T(8,128)(2,1)}, u32[]{:S(2)}, u32[]{:S(2)}) collective-permute-start(bf16[4,528,128]{2,1,0:T(8,128)(2,1)} %collective-permute-done.8.refs_3_), channel_id=1, source_target_pairs={{0,32},{32,0},{1,33},{33,1},{2,34},{34,2},{3,35},{35,3},{4,36},{36... | collective-permute-start | bytes 1622024 | tf_op jit(solution)/shard_map/ppermute | solution.py:130
  103.3 11.4 %collective-permute-start.10 = (bf16[2,528,128]{2,1,0:T(8,128)(2,1)S(1)}, bf16[2,528,128]{2,1,0:T(8,128)(2,1)S(1)}, u32[]{:S(2)}, u32[]{:S(2)}) collective-permute-start(bf16[2,528,128]{2,1,0:T(8,128)(2,1)S(1)} %constant_dynamic-slice_fusion), channel_id=1, source_target_pairs={{0,4},{4,8},{8,12},{12,16},{16,20},{20,24},{24,28},{28,0},{32,60},... | collective-permute-start | bytes 811016 | tf_op jit(solution)/shard_map/ppermute | solution.py:211
  106.0 1.1 copy-start.3
  114.7 10.0 %collective-permute-start.12 = (bf16[2,528,128]{2,1,0:T(8,128)(2,1)S(1)}, bf16[2,528,128]{2,1,0:T(8,128)(2,1)S(1)}, u32[]{:S(2)}, u32[]{:S(2)}) collective-permute-start(bf16[2,528,128]{2,1,0:T(8,128)(2,1)S(1)} %collective-permute-done.10.refs_3_), channel_id=1, source_target_pairs={{0,32},{32,0},{1,33},{33,1},{2,34},{34,2},{3,35},{35,3},{4,36},{36... | collective-permute-start | bytes 811016 | tf_op jit(solution)/shard_map/ppermute | solution.py:130
  129.4 5.0 %collective-permute-start.13 = (bf16[128,256]{1,0:T(8,128)(2,1)S(1)}, bf16[128,256]{1,0:T(8,128)(2,1)S(1)}, u32[]{:S(2)}, u32[]{:S(2)}) collective-permute-start(bf16[128,256]{1,0:T(8,128)(2,1)S(1)} %dynamic-slice_bitcast_fusion), channel_id=1, source_target_pairs={{0,64},{64,0},{1,65},{65,1},{2,66},{66,2},{3,67},{67,3},{4,68},{68... | collective-permute-start | bytes 196616 | tf_op jit(solution)/shard_map/ppermute | solution.py:130
  (1 other events, 0.7 us)

commit v9 on v8

--- a/solution.py
+++ b/solution.py
@@ -196,14 +196,18 @@
     warm, other_warm = pick(holder, yl), pick(holder, 1 - yl)
     pieces = packed(key_values[0].reshape(ROWS, 2 * KVH * HD))
     pieces = lax.all_to_all(pieces, SECTION, 0, 0)
+    q = queries[0].reshape(ROWS, LAYERS, WIDE).transpose(1, 0, 2)
+    q, pieces = lax.optimization_barrier((q, pieces))
+    q = lax.all_to_all(q, SECTION, 0, 0)
+    q = swap(q, other_warm)
+    use_warm = ((ids == warm) | (ids == other_warm)).astype(jnp.int32)
+    pos = token_pos.astype(jnp.float32)[None, :]
     block_ids = jnp.broadcast_to((token_pos // BLOCK).astype(jnp.bfloat16)[None, :], (POS_ROWS, ROWS))
     wanted = [holder[LAYERS - 1], warm]
     shard = jnp.concatenate([pick(pieces, index) for index in wanted] + [block_ids], axis=0)
     mine = jnp.stack([shard] + [turn(shard, "yh", nyh, shift) for shift in range(1, nyh)])
     theirs = turn(mine, "core", 2, 1)
     line = joined(core, mine, theirs)
-    q, line = lax.optimization_barrier((queries[0], line))
-    q = q.reshape(ROWS, LAYERS, WIDE).transpose(1, 0, 2)
 
     pairs = [(z, (z + 1) % nz) for z in range(nz)] + [(nz + z, nz + (z - 1) % nz) for z in range(nz)]
 
@@ -214,28 +218,21 @@
         return turn(value, "core", 2, 1)
 
     arrived = onward(line)
-    q = lax.all_to_all(q, SECTION, 0, 0)
-    q = swap(q, other_warm)
-    use_warm = ((ids == warm) | (ids == other_warm)).astype(jnp.int32)
-    pos = token_pos.astype(jnp.float32)[None, :]
 
     def part(blocks, state, last=False):
         return attend(use_warm, q, pos, blocks, state, last)
 
-    held, state = [line], None
+    state = part([line], None)
+    arrived, state = lax.optimization_barrier((arrived, state))
     half = nyh // 2
     for step in range(nz // 2 - 1):
         if step < nz // 2 - 2:
             coming = onward(arrived)
         else:
             coming = onward(lax.dynamic_slice_in_dim(arrived, core * half, half, axis=0))
-        passed = handed(arrived)
-        state = part(held, state)
-        held = [arrived, passed]
-        arrived, held, state = lax.optimization_barrier((coming, held, state))
-    passed = handed(arrived)
-    state = part(held, state)
-    out = swap(part([arrived, passed], state, True), other_warm)
+        state = part([arrived, handed(arrived)], state)
+        arrived, state = lax.optimization_barrier((coming, state))
+    out = swap(part([arrived, handed(arrived)], state, True), other_warm)
     out = lax.all_to_all(out, SECTION, 0, 0)
     return out.transpose(1, 0, 2).reshape(1, ROWS, H * HD)
 

time: 160 us -> 156 us (0.975)
  waiting for transfers between devices: 15.2 us -> 23.7 us
  starting transfers between devices: 66.5 us -> 58.9 us
  local copies, waits for them, and re-layouts: 11 us -> 9.18 us
  blocking collectives: 22.3 us -> 20.6 us
    ppermute x10, waiting for transfers between devices: 5.48 us -> 14.2 us  [turn(): lax.ppermute(value, axis, [(i, (i + shift) % size) for i in range(size)])]
    ppermute x4, starting transfers between devices: 19.8 us -> 15.2 us  [onward(): return lax.ppermute(value, ('core', 'z'), pairs)]
    ppermute x10, starting transfers between devices: 32.6 us -> 28.9 us  [turn(): lax.ppermute(value, axis, [(i, (i + shift) % size) for i in range(size)])]
    ppermute x4, waiting for transfers between devices: 4.4 us -> 1.66 us  [onward(): return lax.ppermute(value, ('core', 'z'), pairs)]
    all_to_all x1, waiting for transfers between devices: 5.29 us -> 7.87 us  [per_device(): pieces = lax.all_to_all(pieces, SECTION, 0, 0)]
    unnamed x20 -> x14, local copies, waits for them, and re-layouts: 6.02 us -> 4.21 us
    all_to_all x1, blocking collectives: 22.3 us -> 20.6 us  [per_device(): out = lax.all_to_all(out, SECTION, 0, 0)]
    pallas_call x5, Pallas kernels: 32.5 us -> 30.9 us  [attend(): pl.pallas_call(functools.partial(attend_body, shards, state is None, last...]
  transfers between devices with their start and end apart: 16 -> 16, of which waited for: 7 -> 7; matrix products, arithmetic and copies ran while one was open for 2% -> 3% of each run, Pallas kernels for 18% -> 18%
where the time goes in v9:
time: 156 us; the launch traced here: 155 us
  starting transfers between devices  58.9 us (38%)
  Pallas kernels  34.7 us (22%)
  waiting for transfers between devices  23.7 us (15%)
  blocking collectives  20.6 us (13%)
  local copies, waits for them, and re-layouts  9.18 us (6%)
  between operations  6.08 us (4%)
    pallas_call x5, Pallas kernels, attend(): pl.pallas_call(functools.partial(attend_body, shards, state is None, last...  30.9 us
    ppermute x10, starting transfers between devices, turn(): lax.ppermute(value, axis, [(i, (i + shift) % size) for i in range(size)])  28.9 us
    all_to_all x1, blocking collectives, per_device(): out = lax.all_to_all(out, SECTION, 0, 0)  20.6 us
    ppermute x4, starting transfers between devices, onward(): return lax.ppermute(value, ('core', 'z'), pairs)  15.2 us
    ppermute x10, waiting for transfers between devices, turn(): lax.ppermute(value, axis, [(i, (i + shift) % size) for i in range(size)])  14.2 us
    all_to_all x1, starting transfers between devices, per_device(): pieces = lax.all_to_all(pieces, SECTION, 0, 0)  10.2 us
    all_to_all x1, waiting for transfers between devices, per_device(): pieces = lax.all_to_all(pieces, SECTION, 0, 0)  7.87 us
    all_to_all x1, starting transfers between devices, per_device(): q = lax.all_to_all(q, SECTION, 0, 0)  4.61 us
  transfers between devices with their start and end apart: 16, of which 7 were waited for; matrix products, arithmetic and copies ran while one was open for 3% of the time, Pallas kernels for 18%

profile of v9, /device:TPU:1, one launch (start us, length us, event | category | flops | bytes accessed | tf_op | source)
XLA Modules:
  0.0 154.6 jit_solution(14078102134455949546)
XLA Ops:
  3.6 10.2 %all-to-all-start = ((bf16[16,128,128]{2,1,0:T(8,128)(2,1)}), bf16[16,128,128]{2,1,0:T(8,128)(2,1)S(1)}, u32[]{:S(2)}, u32[]{:S(2)}) async-start(bf16[16,128,128]{2,1,0:T(8,128)(2,1)} %pack.1), calls=%async_computation | async-start | bytes 1048576 | tf_op jit(solution)/shard_map/all_to_all | solution.py:198
  15.9 7.9 %all-to-all-done = bf16[16,128,128]{2,1,0:T(8,128)(2,1)S(1)} async-done(((bf16[16,128,128]{2,1,0:T(8,128)(2,1)}), bf16[16,128,128]{2,1,0:T(8,128)(2,1)S(1)}, u32[]{:S(2)}, u32[]{:S(2)}) %all-to-all-start) | async-done | bytes 524320 | tf_op jit(solution)/shard_map/all_to_all | solution.py:198
  23.8 4.6 %all-to-all-start.1 = ((bf16[16,128,256]{2,1,0:T(8,128)(2,1)}), bf16[16,128,256]{2,1,0:T(8,128)(2,1)S(1)}, u32[]{:S(2)}, u32[]{:S(2)}) async-start(bf16[16,128,256]{2,1,0:T(8,128)(2,1)} %bitcast.3), calls=%async_computation.1 | async-start | bytes 2097152 | tf_op jit(solution)/shard_map/all_to_all | solution.py:201
  34.9 3.6 %collective-permute-start.2 = (bf16[272,128]{1,0:T(8,128)(2,1)S(1)}, bf16[272,128]{1,0:T(8,128)(2,1)S(1)}, u32[]{:S(2)}, u32[]{:S(2)}) collective-permute-start(bf16[272,128]{1,0:T(8,128)(2,1)S(1)} %get-tuple-element.68), channel_id=1, source_target_pairs={{0,2},{1,3},{2,0},{3,1},{4,6},{5,7},{6,4},{7,5},{8,10},{9,11},{10,... | collective-permute-start | bytes 208904 | tf_op jit(solution)/shard_map/ppermute | solution.py:130
  38.5 5.0 %collective-permute-start.3 = (bf16[272,128]{1,0:T(8,128)(2,1)S(1)}, bf16[272,128]{1,0:T(8,128)(2,1)S(1)}, u32[]{:S(2)}, u32[]{:S(2)}) collective-permute-start(bf16[272,128]{1,0:T(8,128)(2,1)S(1)} %get-tuple-element.68), channel_id=1, source_target_pairs={{0,3},{1,0},{2,1},{3,2},{4,7},{5,4},{6,5},{7,6},{8,11},{9,8},{10,9... | collective-permute-start | bytes 208904 | tf_op jit(solution)/shard_map/ppermute | solution.py:130
  43.5 3.0 %collective-permute-done.2 = bf16[272,128]{1,0:T(8,128)(2,1)S(1)} collective-permute-done((bf16[272,128]{1,0:T(8,128)(2,1)S(1)}, bf16[272,128]{1,0:T(8,128)(2,1)S(1)}, u32[]{:S(2)}, u32[]{:S(2)}) %collective-permute-start.2) | collective-permute-done | bytes 69664 | tf_op jit(solution)/shard_map/ppermute | solution.py:130
  46.5 4.0 %collective-permute-done.3 = bf16[272,128]{1,0:T(8,128)(2,1)S(1)} collective-permute-done((bf16[272,128]{1,0:T(8,128)(2,1)S(1)}, bf16[272,128]{1,0:T(8,128)(2,1)S(1)}, u32[]{:S(2)}, u32[]{:S(2)}) %collective-permute-start.3) | collective-permute-done | bytes 69664 | tf_op jit(solution)/shard_map/ppermute | solution.py:130
  50.5 2.4 %collective-permute-start.4 = (bf16[4,272,128]{2,1,0:T(8,128)(2,1)S(1)}, bf16[4,272,128]{2,1,0:T(8,128)(2,1)S(1)}, u32[]{:S(2)}, u32[]{:S(2)}) collective-permute-start(bf16[4,272,128]{2,1,0:T(8,128)(2,1)S(1)} %pad_maximum_fusion.mine_ref), channel_id=1, source_target_pairs={{0,32},{32,0},{1,33},{33,1},{2,34},{34,2},{3,35},{35,3},{4,36},{36... | collective-permute-start | bytes 835592 | tf_op jit(solution)/shard_map/ppermute | solution.py:130
  57.4 8.0 %collective-permute-start.5 = (bf16[4,528,128]{2,1,0:T(8,128)(2,1)}, bf16[4,528,128]{2,1,0:T(8,128)(2,1)}, u32[]{:S(2)}, u32[]{:S(2)}) collective-permute-start(bf16[4,528,128]{2,1,0:T(8,128)(2,1)} %join.1.refs_3_), channel_id=1, source_target_pairs={{0,4},{4,8},{8,12},{12,16},{16,20},{20,24},{24,28},{28,0},{32,60},... | collective-permute-start | bytes 1622024 | tf_op jit(solution)/shard_map/ppermute | solution.py:215
  65.5 1.9 %collective-permute-start = (bf16[128,256]{1,0:T(8,128)(2,1)S(1)}, bf16[128,256]{1,0:T(8,128)(2,1)S(1)}, u32[]{:S(2)}, u32[]{:S(2)}) collective-permute-start(bf16[128,256]{1,0:T(8,128)(2,1)S(1)} %dynamic-slice_bitcast_fusion.1), channel_id=1, source_target_pairs={{0,64},{64,0},{1,65},{65,1},{2,66},{66,2},{3,67},{67,3},{4,68},{68... | collective-permute-start | bytes 196616 | tf_op jit(solution)/shard_map/ppermute | solution.py:130
  68.7 2.2 %collective-permute-done = bf16[128,256]{1,0:T(8,128)(2,1)S(1)} collective-permute-done((bf16[128,256]{1,0:T(8,128)(2,1)S(1)}, bf16[128,256]{1,0:T(8,128)(2,1)S(1)}, u32[]{:S(2)}, u32[]{:S(2)}) %collective-permute-start) | collective-permute-done | bytes 65568 | tf_op jit(solution)/shard_map/ppermute | solution.py:130
  71.9 4.4 %attend.5 = (f32[16,8,256]{2,1,0:T(8,128)S(1)}, f32[16,8,256]{2,1,0:T(8,128)S(1)}, f32[16,128,256]{2,1,0:T(8,128)S(1)}) custom-call(s32[16]{0:T(128)S(1)} %or_convert_fusion.refs_0_, bf16[16,128,256]{2,1,0:T(8,128)(2,1)S(1)} %bitcast_dynamic-update-slice_fusion.1.refs_1_, f32[1,128]{1,0:T(1,128)S(1)} %get-tuple-element.73.refs_2_, ...), custom_call_target="tpu_custom_call" | custom-call | flops 1073741824 | bytes 8388608 | tf_op jit(solution)/shard_map/attend/pallas_call | solution.py:108
  78.3 3.2 %collective-permute-start.6 = (bf16[4,528,128]{2,1,0:T(8,128)(2,1)}, bf16[4,528,128]{2,1,0:T(8,128)(2,1)S(1)}, u32[]{:S(2)}, u32[]{:S(2)}) collective-permute-start(bf16[4,528,128]{2,1,0:T(8,128)(2,1)} %collective-permute-done.5.refs_3_), channel_id=1, source_target_pairs={{0,4},{4,8},{8,12},{12,16},{16,20},{20,24},{24,28},{28,0},{32,60},... | collective-permute-start | bytes 1622024 | tf_op jit(solution)/shard_map/ppermute | solution.py:215
  81.5 7.5 %attend.6 = (f32[16,8,256]{2,1,0:T(8,128)S(1)}, f32[16,8,256]{2,1,0:T(8,128)S(1)}, f32[16,128,256]{2,1,0:T(8,128)S(1)}) custom-call(s32[16]{0:T(128)S(1)} %or_convert_fusion.refs_0_, bf16[16,128,256]{2,1,0:T(8,128)(2,1)S(1)} %bitcast_dynamic-update-slice_fusion.1.refs_1_, ...), custom_call_target="tpu_custom_call", output_to_operand_aliasing={{0}: (5, {}), {1}: (6, {}), {2}: (7, {})} | custom-call | flops 2147483648 | bytes 8388608 | tf_op jit(solution)/shard_map/attend/pallas_call | solution.py:108
  88.9 4.4 %collective-permute-start.9 = (bf16[4,528,128]{2,1,0:T(8,128)(2,1)S(1)}, bf16[4,528,128]{2,1,0:T(8,128)(2,1)S(1)}, u32[]{:S(2)}, u32[]{:S(2)}) collective-permute-start(bf16[4,528,128]{2,1,0:T(8,128)(2,1)S(1)} %collective-permute-done.6.refs_3_), channel_id=1, source_target_pairs={{0,32},{32,0},{1,33},{33,1},{2,34},{34,2},{3,35},{35,3},{4,36},{36... | collective-permute-start | bytes 1622024 | tf_op jit(solution)/shard_map/ppermute | solution.py:130
  93.3 1.9 %collective-permute-start.8 = (bf16[4,528,128]{2,1,0:T(8,128)(2,1)S(1)}, bf16[4,528,128]{2,1,0:T(8,128)(2,1)}, u32[]{:S(2)}, u32[]{:S(2)}) collective-permute-start(bf16[4,528,128]{2,1,0:T(8,128)(2,1)S(1)} %collective-permute-done.6.refs_3_), channel_id=1, source_target_pairs={{0,4},{4,8},{8,12},{12,16},{16,20},{20,24},{24,28},{28,0},{32,60},... | collective-permute-start | bytes 1622024 | tf_op jit(solution)/shard_map/ppermute | solution.py:215
  95.3 6.9 %attend.7 = (f32[16,8,256]{2,1,0:T(8,128)S(1)}, f32[16,8,256]{2,1,0:T(8,128)S(1)}, f32[16,128,256]{2,1,0:T(8,128)S(1)}) custom-call(s32[16]{0:T(128)S(1)} %or_convert_fusion.refs_0_, bf16[16,128,256]{2,1,0:T(8,128)(2,1)S(1)} %bitcast_dynamic-update-slice_fusion.1.refs_1_, ...), custom_call_target="tpu_custom_call", output_to_operand_aliasing={{0}: (5, {}), {1}: (6, {}), {2}: (7, {})} | custom-call | flops 2147483648 | bytes 8388608 | tf_op jit(solution)/shard_map/attend/pallas_call | solution.py:108
  103.9 4.0 %collective-permute-start.11 = (bf16[4,528,128]{2,1,0:T(8,128)(2,1)}, bf16[4,528,128]{2,1,0:T(8,128)(2,1)}, u32[]{:S(2)}, u32[]{:S(2)}) collective-permute-start(bf16[4,528,128]{2,1,0:T(8,128)(2,1)} %collective-permute-done.8.refs_3_), channel_id=1, source_target_pairs={{0,32},{32,0},{1,33},{33,1},{2,34},{34,2},{3,35},{35,3},{4,36},{36... | collective-permute-start | bytes 1622024 | tf_op jit(solution)/shard_map/ppermute | solution.py:130
  108.8 2.1 %collective-permute-start.10 = (bf16[2,528,128]{2,1,0:T(8,128)(2,1)S(1)}, bf16[2,528,128]{2,1,0:T(8,128)(2,1)S(1)}, u32[]{:S(2)}, u32[]{:S(2)}) collective-permute-start(bf16[2,528,128]{2,1,0:T(8,128)(2,1)S(1)} %constant_dynamic-slice_fusion), channel_id=1, source_target_pairs={{0,4},{4,8},{8,12},{12,16},{16,20},{20,24},{24,28},{28,0},{32,60},... | collective-permute-start | bytes 811016 | tf_op jit(solution)/shard_map/ppermute | solution.py:215
  110.9 7.6 %attend.8 = (f32[16,8,256]{2,1,0:T(8,128)S(1)}, f32[16,8,256]{2,1,0:T(8,128)S(1)}, f32[16,128,256]{2,1,0:T(8,128)S(1)}) custom-call(s32[16]{0:T(128)S(1)} %or_convert_fusion.refs_0_, bf16[16,128,256]{2,1,0:T(8,128)(2,1)S(1)} %bitcast_dynamic-update-slice_fusion.1.refs_1_, ...), custom_call_target="tpu_custom_call", output_to_operand_aliasing={{0}: (5, {}), {1}: (6, {}), {2}: (7, {})} | custom-call | flops 2147483648 | bytes 8388608 | tf_op jit(solution)/shard_map/attend/pallas_call | solution.py:108
  118.5 1.9 %collective-permute-start.12 = (bf16[2,528,128]{2,1,0:T(8,128)(2,1)S(1)}, bf16[2,528,128]{2,1,0:T(8,128)(2,1)S(1)}, u32[]{:S(2)}, u32[]{:S(2)}) collective-permute-start(bf16[2,528,128]{2,1,0:T(8,128)(2,1)S(1)} %collective-permute-done.10.refs_3_), channel_id=1, source_target_pairs={{0,32},{32,0},{1,33},{33,1},{2,34},{34,2},{3,35},{35,3},{4,36},{36... | collective-permute-start | bytes 811016 | tf_op jit(solution)/shard_map/ppermute | solution.py:130
  122.0 4.6 %attend.9 = bf16[16,128,256]{2,1,0:T(8,128)(2,1)S(1)} custom-call(s32[16]{0:T(128)S(1)} %or_convert_fusion.refs_0_, bf16[16,128,256]{2,1,0:T(8,128)(2,1)S(1)} %bitcast_dynamic-update-slice_fusion.1.refs_1_, f32[1,128]{1,0:T(1,128)S(1)} %get-tuple-element.73.refs_2_, bf16[2,528,128]{2,1,0:T(8,128)(2,1)S(1)} %collective-permute-done.10.refs_3_, ...), custom_call_target="tpu_custom_call" | custom-call | flops 1073741824 | bytes 8388608 | tf_op jit(solution)/shard_map/attend/pallas_call | solution.py:108
  128.5 3.5 %collective-permute-done.13 = bf16[128,256]{1,0:T(8,128)(2,1)S(1)} collective-permute-done((bf16[128,256]{1,0:T(8,128)(2,1)S(1)}, bf16[128,256]{1,0:T(8,128)(2,1)S(1)}, u32[]{:S(2)}, u32[]{:S(2)}) %collective-permute-start.13) | collective-permute-done | bytes 65568 | tf_op jit(solution)/shard_map/ppermute | solution.py:130
  132.0 20.6 %all_to_all.15 = bf16[16,128,256]{2,1,0:T(8,128)(2,1)S(1)} all-to-all(bf16[16,128,256]{2,1,0:T(8,128)(2,1)S(1)} %bitcast_dynamic-update-slice_fusion), channel_id=1, replica_groups=mesh['x'=4,'yl'=2,'core'=2,'z'=8,'yh'=4] {'x','yl','core'}, dimensions={0} | all-to-all | bytes 2097152 | tf_op jit(solution)/shard_map/all_to_all | solution.py:236
  (46 shorter events, 23.3 us)
Async XLA Ops:
  0.0 13.9 %copy-start.2 = (bf16[1,128,4096]{2,1,0:T(8,128)(2,1)S(1)}, bf16[1,128,4096]{2,1,0:T(8,128)(2,1)}, u32[]{:S(2)}) copy-start(bf16[1,128,4096]{2,1,0:T(8,128)(2,1)} %param.4) | copy-start | bytes 3145732
  3.6 20.1 %all-to-all-start = ((bf16[16,128,128]{2,1,0:T(8,128)(2,1)}), bf16[16,128,128]{2,1,0:T(8,128)(2,1)S(1)}, u32[]{:S(2)}, u32[]{:S(2)}) async-start(bf16[16,128,128]{2,1,0:T(8,128)(2,1)} %pack.1), calls=%async_computation | async-start | bytes 1048576 | tf_op jit(solution)/shard_map/all_to_all | solution.py:198
  14.5 13.8 %copy-start.4 = (s32[16]{0:T(128)S(1)}, s32[16]{0:T(128)}, u32[]{:S(2)}) copy-start(s32[16]{0:T(128)} %param.7) | copy-start | bytes 196
  14.6 18.4 %copy-start.5 = (s32[128]{0:T(128)S(1)}, s32[128]{0:T(128)}, u32[]{:S(2)}) copy-start(s32[128]{0:T(128)} %param.6) | copy-start | bytes 1540
  23.8 41.7 %all-to-all-start.1 = ((bf16[16,128,256]{2,1,0:T(8,128)(2,1)}), bf16[16,128,256]{2,1,0:T(8,128)(2,1)S(1)}, u32[]{:S(2)}, u32[]{:S(2)}) async-start(bf16[16,128,256]{2,1,0:T(8,128)(2,1)} %bitcast.3), calls=%async_computation.1 | async-start | bytes 2097152 | tf_op jit(solution)/shard_map/all_to_all | solution.py:201
  33.0 10.5 %collective-permute-start.1 = (bf16[272,128]{1,0:T(8,128)(2,1)S(1)}, bf16[272,128]{1,0:T(8,128)(2,1)S(1)}, u32[]{:S(2)}, u32[]{:S(2)}) collective-permute-start(bf16[272,128]{1,0:T(8,128)(2,1)S(1)} %get-tuple-element.68), channel_id=1, source_target_pairs={{0,1},{1,2},{2,3},{3,0},{4,5},{5,6},{6,7},{7,4},{8,9},{9,10},{10,1... | collective-permute-start | bytes 208904 | tf_op jit(solution)/shard_map/ppermute | solution.py:130
  34.9 11.5 %collective-permute-start.2 = (bf16[272,128]{1,0:T(8,128)(2,1)S(1)}, bf16[272,128]{1,0:T(8,128)(2,1)S(1)}, u32[]{:S(2)}, u32[]{:S(2)}) collective-permute-start(bf16[272,128]{1,0:T(8,128)(2,1)S(1)} %get-tuple-element.68), channel_id=1, source_target_pairs={{0,2},{1,3},{2,0},{3,1},{4,6},{5,7},{6,4},{7,5},{8,10},{9,11},{10,... | collective-permute-start | bytes 208904 | tf_op jit(solution)/shard_map/ppermute | solution.py:130
  38.5 11.9 %collective-permute-start.3 = (bf16[272,128]{1,0:T(8,128)(2,1)S(1)}, bf16[272,128]{1,0:T(8,128)(2,1)S(1)}, u32[]{:S(2)}, u32[]{:S(2)}) collective-permute-start(bf16[272,128]{1,0:T(8,128)(2,1)S(1)} %get-tuple-element.68), channel_id=1, source_target_pairs={{0,3},{1,0},{2,1},{3,2},{4,7},{5,4},{6,5},{7,6},{8,11},{9,8},{10,9... | collective-permute-start | bytes 208904 | tf_op jit(solution)/shard_map/ppermute | solution.py:130
  50.5 4.3 %copy-start.1 = (bf16[4,272,128]{2,1,0:T(8,128)(2,1)}, bf16[4,272,128]{2,1,0:T(8,128)(2,1)S(1)}, u32[]{:S(2)}) copy-start(bf16[4,272,128]{2,1,0:T(8,128)(2,1)S(1)} %pad_maximum_fusion.mine_ref) | copy-start | bytes 835588
  50.5 4.3 %collective-permute-start.4 = (bf16[4,272,128]{2,1,0:T(8,128)(2,1)S(1)}, bf16[4,272,128]{2,1,0:T(8,128)(2,1)S(1)}, u32[]{:S(2)}, u32[]{:S(2)}) collective-permute-start(bf16[4,272,128]{2,1,0:T(8,128)(2,1)S(1)} %pad_maximum_fusion.mine_ref), channel_id=1, source_target_pairs={{0,32},{32,0},{1,33},{33,1},{2,34},{34,2},{3,35},{35,3},{4,36},{36... | collective-permute-start | bytes 835592 | tf_op jit(solution)/shard_map/ppermute | solution.py:130
  54.8 0.7 copy-start.3
  57.4 18.9 %collective-permute-start.5 = (bf16[4,528,128]{2,1,0:T(8,128)(2,1)}, bf16[4,528,128]{2,1,0:T(8,128)(2,1)}, u32[]{:S(2)}, u32[]{:S(2)}) collective-permute-start(bf16[4,528,128]{2,1,0:T(8,128)(2,1)} %join.1.refs_3_), channel_id=1, source_target_pairs={{0,4},{4,8},{8,12},{12,16},{16,20},{20,24},{24,28},{28,0},{32,60},... | collective-permute-start | bytes 1622024 | tf_op jit(solution)/shard_map/ppermute | solution.py:215
  65.5 5.4 %collective-permute-start = (bf16[128,256]{1,0:T(8,128)(2,1)S(1)}, bf16[128,256]{1,0:T(8,128)(2,1)S(1)}, u32[]{:S(2)}, u32[]{:S(2)}) collective-permute-start(bf16[128,256]{1,0:T(8,128)(2,1)S(1)} %dynamic-slice_bitcast_fusion.1), channel_id=1, source_target_pairs={{0,64},{64,0},{1,65},{65,1},{2,66},{66,2},{3,67},{67,3},{4,68},{68... | collective-permute-start | bytes 196616 | tf_op jit(solution)/shard_map/ppermute | solution.py:130
  70.9 1.0 copy-start
  76.3 5.1 %collective-permute-start.7 = (bf16[4,528,128]{2,1,0:T(8,128)(2,1)}, bf16[4,528,128]{2,1,0:T(8,128)(2,1)S(1)}, u32[]{:S(2)}, u32[]{:S(2)}) collective-permute-start(bf16[4,528,128]{2,1,0:T(8,128)(2,1)} %collective-permute-done.5.refs_3_), channel_id=1, source_target_pairs={{0,32},{32,0},{1,33},{33,1},{2,34},{34,2},{3,35},{35,3},{4,36},{36... | collective-permute-start | bytes 1622024 | tf_op jit(solution)/shard_map/ppermute | solution.py:130
  78.3 10.6 %collective-permute-start.6 = (bf16[4,528,128]{2,1,0:T(8,128)(2,1)}, bf16[4,528,128]{2,1,0:T(8,128)(2,1)S(1)}, u32[]{:S(2)}, u32[]{:S(2)}) collective-permute-start(bf16[4,528,128]{2,1,0:T(8,128)(2,1)} %collective-permute-done.5.refs_3_), channel_id=1, source_target_pairs={{0,4},{4,8},{8,12},{12,16},{16,20},{20,24},{24,28},{28,0},{32,60},... | collective-permute-start | bytes 1622024 | tf_op jit(solution)/shard_map/ppermute | solution.py:215
  88.9 6.4 %collective-permute-start.9 = (bf16[4,528,128]{2,1,0:T(8,128)(2,1)S(1)}, bf16[4,528,128]{2,1,0:T(8,128)(2,1)S(1)}, u32[]{:S(2)}, u32[]{:S(2)}) collective-permute-start(bf16[4,528,128]{2,1,0:T(8,128)(2,1)S(1)} %collective-permute-done.6.refs_3_), channel_id=1, source_target_pairs={{0,32},{32,0},{1,33},{33,1},{2,34},{34,2},{3,35},{35,3},{4,36},{36... | collective-permute-start | bytes 1622024 | tf_op jit(solution)/shard_map/ppermute | solution.py:130
  93.3 10.5 %collective-permute-start.8 = (bf16[4,528,128]{2,1,0:T(8,128)(2,1)S(1)}, bf16[4,528,128]{2,1,0:T(8,128)(2,1)}, u32[]{:S(2)}, u32[]{:S(2)}) collective-permute-start(bf16[4,528,128]{2,1,0:T(8,128)(2,1)S(1)} %collective-permute-done.6.refs_3_), channel_id=1, source_target_pairs={{0,4},{4,8},{8,12},{12,16},{16,20},{20,24},{24,28},{28,0},{32,60},... | collective-permute-start | bytes 1622024 | tf_op jit(solution)/shard_map/ppermute | solution.py:215
  103.9 7.1 %collective-permute-start.11 = (bf16[4,528,128]{2,1,0:T(8,128)(2,1)}, bf16[4,528,128]{2,1,0:T(8,128)(2,1)}, u32[]{:S(2)}, u32[]{:S(2)}) collective-permute-start(bf16[4,528,128]{2,1,0:T(8,128)(2,1)} %collective-permute-done.8.refs_3_), channel_id=1, source_target_pairs={{0,32},{32,0},{1,33},{33,1},{2,34},{34,2},{3,35},{35,3},{4,36},{36... | collective-permute-start | bytes 1622024 | tf_op jit(solution)/shard_map/ppermute | solution.py:130
  108.8 9.7 %collective-permute-start.10 = (bf16[2,528,128]{2,1,0:T(8,128)(2,1)S(1)}, bf16[2,528,128]{2,1,0:T(8,128)(2,1)S(1)}, u32[]{:S(2)}, u32[]{:S(2)}) collective-permute-start(bf16[2,528,128]{2,1,0:T(8,128)(2,1)S(1)} %constant_dynamic-slice_fusion), channel_id=1, source_target_pairs={{0,4},{4,8},{8,12},{12,16},{16,20},{20,24},{24,28},{28,0},{32,60},... | collective-permute-start | bytes 811016 | tf_op jit(solution)/shard_map/ppermute | solution.py:215
  118.5 3.4 %collective-permute-start.12 = (bf16[2,528,128]{2,1,0:T(8,128)(2,1)S(1)}, bf16[2,528,128]{2,1,0:T(8,128)(2,1)S(1)}, u32[]{:S(2)}, u32[]{:S(2)}) collective-permute-start(bf16[2,528,128]{2,1,0:T(8,128)(2,1)S(1)} %collective-permute-done.10.refs_3_), channel_id=1, source_target_pairs={{0,32},{32,0},{1,33},{33,1},{2,34},{34,2},{3,35},{35,3},{4,36},{36... | collective-permute-start | bytes 811016 | tf_op jit(solution)/shard_map/ppermute | solution.py:130
  126.6 5.5 %collective-permute-start.13 = (bf16[128,256]{1,0:T(8,128)(2,1)S(1)}, bf16[128,256]{1,0:T(8,128)(2,1)S(1)}, u32[]{:S(2)}, u32[]{:S(2)}) collective-permute-start(bf16[128,256]{1,0:T(8,128)(2,1)S(1)} %dynamic-slice_bitcast_fusion), channel_id=1, source_target_pairs={{0,64},{64,0},{1,65},{65,1},{2,66},{66,2},{3,67},{67,3},{4,68},{68... | collective-permute-start | bytes 196616 | tf_op jit(solution)/shard_map/ppermute | solution.py:130

commit v10 on v9

--- a/solution.py
+++ b/solution.py
@@ -18,8 +18,7 @@
 WIDE = HEADS * HD
 SLABS = 8
 POS_ROWS = 16
-PART = 2 * ROWS
-LINE_ROWS = 2 * PART + POS_ROWS
+HALF_ROWS = 2 * ROWS + POS_ROWS
 MASKED = -1e30
 SCALE = 1.4426950408889634 / HD**0.5
 SECTION = ("x", "yl", "core")
@@ -39,10 +38,10 @@
     for n, ref in zip(shards, blocks):
         for i in range(n):
             for source in range(2):
-                base = source * 2 * ROWS
+                base = source * ROWS
                 k[source, at : at + ROWS, :] = ref[i, base : base + ROWS]
-                v[source, :HD, at : at + ROWS] = ref[i, base + ROWS : base + 2 * ROWS]
-            ids = ref[i, 4 * ROWS : 4 * ROWS + POS_ROWS].astype(jnp.float32)
+                v[source, :HD, at : at + ROWS] = ref[i, HALF_ROWS + base : HALF_ROWS + base + ROWS]
+            ids = ref[i, 2 * ROWS : HALF_ROWS].astype(jnp.float32)
             for part in range(ROWS // BLOCK):
                 key_pos = ids[0:1, part * BLOCK : part * BLOCK + 1] * BLOCK + row
                 rows = slice(at + part * BLOCK, at + (part + 1) * BLOCK)
@@ -82,12 +81,14 @@
             outs[1][j] = den
             outs[2][j] = acc
 
-    @pl.loop(0, LAYERS // SLABS)
+    slabs = min(SLABS, q_ref.shape[0])
+
+    @pl.loop(0, q_ref.shape[0] // slabs)
     def _(step):
-        base = step * SLABS
+        base = step * slabs
         s = scores(base)
-        for j in range(SLABS):
-            ahead = scores(base + j + 1) if j + 1 < SLABS else None
+        for j in range(slabs):
+            ahead = scores(base + j + 1) if j + 1 < slabs else None
             absorb(base + j, s)
             s = ahead
 
@@ -95,6 +96,7 @@
 def attend(warm, q, pos, blocks, state, last):
     shards = tuple(b.shape[0] for b in blocks)
     count = sum(shards) * ROWS
+    layers = q.shape[0]
     args = [warm, q, pos, *blocks]
     aliases = {}
     if state is not None:
@@ -102,9 +104,9 @@
             aliases = {len(args) + i: i for i in range(len(state))}
         args += list(state)
     whole = pl.BlockSpec(memory_space=pltpu.VMEM)
-    one = jax.ShapeDtypeStruct((LAYERS, 8, WIDE), jnp.float32)
-    acc = jax.ShapeDtypeStruct((LAYERS, HD, WIDE), jnp.float32)
-    done = jax.ShapeDtypeStruct((LAYERS, ROWS, WIDE), jnp.bfloat16)
+    one = jax.ShapeDtypeStruct((layers, 8, WIDE), jnp.float32)
+    acc = jax.ShapeDtypeStruct((layers, HD, WIDE), jnp.float32)
+    done = jax.ShapeDtypeStruct((layers, ROWS, WIDE), jnp.bfloat16)
     return pl.pallas_call(
         functools.partial(attend_body, shards, state is None, last),
         in_specs=[pl.BlockSpec(memory_space=pltpu.SMEM)] + [whole] * (len(args) - 1),
@@ -118,9 +120,9 @@
         input_output_aliases=aliases,
         compiler_params=pltpu.CompilerParams(vmem_limit_bytes=24 << 20),
         cost_estimate=pl.CostEstimate(
-            flops=4 * ROWS * H * count * HD,
+            flops=4 * ROWS * layers * HEADS * count * HD,
             bytes_accessed=8 << 20,
-            transcendentals=ROWS * H * count,
+            transcendentals=ROWS * layers * HEADS * count,
         ),
         name="attend",
     )(*args)
@@ -148,44 +150,29 @@
     )(kv)
 
 
-def joined(core, mine, theirs):
-    def body(core_ref, mine_ref, theirs_ref, out_ref):
-        def fill(k_ref, v_ref):
-            for i in range(mine.shape[0]):
-                for s in range(2):
-                    rows = slice(s * ROWS, (s + 1) * ROWS)
-                    at = s * PART
-                    out_ref[i, at : at + ROWS] = k_ref[i, rows]
-                    out_ref[i, at + ROWS : at + PART] = v_ref[i, rows]
-
-        for i in range(mine.shape[0]):
-            out_ref[i, 2 * PART :] = mine_ref[i, 2 * ROWS :]
-
-        @pl.when(core_ref[0] == 0)
-        def _():
-            fill(mine_ref, theirs_ref)
-
-        @pl.when(core_ref[0] != 0)
-        def _():
-            fill(theirs_ref, mine_ref)
-
-    whole = pl.BlockSpec(memory_space=pltpu.VMEM)
+def spread_columns(slabs):
+    group = 4
+
+    def body(in_ref, out_ref):
+        for i in range(group):
+            out_ref[:, i * WIDE : (i + 1) * WIDE] = in_ref[pl.program_id(0) * group + i]
+
     return pl.pallas_call(
         body,
-        in_specs=[pl.BlockSpec(memory_space=pltpu.SMEM), whole, whole],
-        out_specs=whole,
-        out_shape=jax.ShapeDtypeStruct((mine.shape[0], LINE_ROWS, HD), jnp.bfloat16),
-        name="join",
-    )(core.astype(jnp.int32).reshape(1), mine, theirs)
+        grid=(LAYERS // group,),
+        in_specs=[pl.BlockSpec(memory_space=pltpu.VMEM)],
+        out_specs=pl.BlockSpec((ROWS, group * WIDE), lambda i: (0, i)),
+        out_shape=jax.ShapeDtypeStruct((ROWS, LAYERS * WIDE), slabs.dtype),
+        name="columns",
+    )(slabs)
 
 
 def pick(slabs, index):
-    return lax.dynamic_index_in_dim(slabs, index, 0, keepdims=False)
-
-
-def swap(slabs, index):
-    other = turn(pick(slabs, index), "yl", 2, 1)
-    return lax.dynamic_update_index_in_dim(slabs, other, index, 0)
+    return lax.dynamic_index_in_dim(slabs, index.astype(jnp.uint32), 0, keepdims=False)
+
+
+def put(slabs, slab, index):
+    return lax.dynamic_update_index_in_dim(slabs, slab, index.astype(jnp.uint32), 0)
 
 
 def per_device(sizes, queries, key_values, token_pos, layer_of_section):
@@ -193,21 +180,25 @@
     core, yl = lax.axis_index("core"), lax.axis_index("yl")
     ids = jnp.arange(LAYERS, dtype=jnp.int32)
     holder = jnp.sum(jnp.where(layer_of_section[None, :] == ids[:, None], ids[None, :], 0), axis=1)
-    warm, other_warm = pick(holder, yl), pick(holder, 1 - yl)
+    top_holder = holder[LAYERS - 1]
+    warm, other_warm = jnp.where(yl == 0, holder[0], holder[1]), jnp.where(yl == 0, holder[1], holder[0])
+    use_warm = ((ids == warm) | (ids == other_warm)).astype(jnp.int32)
+    pos = token_pos.astype(jnp.float32)[None, :]
+    block_ids = jnp.broadcast_to((token_pos // BLOCK).astype(jnp.bfloat16)[None, :], (POS_ROWS, ROWS))
     pieces = packed(key_values[0].reshape(ROWS, 2 * KVH * HD))
     pieces = lax.all_to_all(pieces, SECTION, 0, 0)
     q = queries[0].reshape(ROWS, LAYERS, WIDE).transpose(1, 0, 2)
-    q, pieces = lax.optimization_barrier((q, pieces))
+    q, pieces, top_holder, warm, other_warm, use_warm, pos, block_ids = lax.optimization_barrier(
+        (q, pieces, top_holder, warm, other_warm, use_warm, pos, block_ids)
+    )
     q = lax.all_to_all(q, SECTION, 0, 0)
-    q = swap(q, other_warm)
-    use_warm = ((ids == warm) | (ids == other_warm)).astype(jnp.int32)
-    pos = token_pos.astype(jnp.float32)[None, :]
-    block_ids = jnp.broadcast_to((token_pos // BLOCK).astype(jnp.bfloat16)[None, :], (POS_ROWS, ROWS))
-    wanted = [holder[LAYERS - 1], warm]
-    shard = jnp.concatenate([pick(pieces, index) for index in wanted] + [block_ids], axis=0)
+    q_other = turn(pick(q, other_warm), "yl", 2, 1)
+    q = put(q, q_other, other_warm)
+    shard = jnp.concatenate([pick(pieces, top_holder), pick(pieces, warm), block_ids], axis=0)
     mine = jnp.stack([shard] + [turn(shard, "yh", nyh, shift) for shift in range(1, nyh)])
     theirs = turn(mine, "core", 2, 1)
-    line = joined(core, mine, theirs)
+    keys, values = jnp.where(core == 0, mine, theirs), jnp.where(core == 0, theirs, mine)
+    line = jnp.concatenate([keys, values], axis=1)
 
     pairs = [(z, (z + 1) % nz) for z in range(nz)] + [(nz + z, nz + (z - 1) % nz) for z in range(nz)]
 
@@ -229,12 +220,17 @@
         if step < nz // 2 - 2:
             coming = onward(arrived)
         else:
-            coming = onward(lax.dynamic_slice_in_dim(arrived, core * half, half, axis=0))
+            coming = onward(lax.dynamic_slice_in_dim(arrived, (core * half).astype(jnp.uint32), half, axis=0))
         state = part([arrived, handed(arrived)], state)
         arrived, state = lax.optimization_barrier((coming, state))
-    out = swap(part([arrived, handed(arrived)], state, True), other_warm)
+    held = [arrived, handed(arrived)]
+    slab_state = [pick(value, other_warm)[None] for value in state]
+    slab = attend(jnp.ones(1, jnp.int32), q_other[None], pos, held, slab_state, True)
+    slab, state = lax.optimization_barrier((slab, state))
+    back = turn(slab[0], "yl", 2, 1)
+    out = put(part(held, state, True), back, other_warm)
     out = lax.all_to_all(out, SECTION, 0, 0)
-    return out.transpose(1, 0, 2).reshape(1, ROWS, H * HD)
+    return spread_columns(out)[None]
 
 
 def solution(mesh):

time: 156 us -> 151 us (0.968)
  starting transfers between devices: 58.9 us -> 63.5 us
  waiting for transfers between devices: 23.7 us -> 19.5 us
  local copies, waits for them, and re-layouts: 9.18 us -> 5.4 us
  Pallas kernels: 34.7 us -> 37.6 us
  between operations: 6.08 us -> 3.29 us
    ppermute x10, starting transfers between devices: 28.9 us -> 32.2 us  [turn(): lax.ppermute(value, axis, [(i, (i + shift) % size) for i in range(size)])]
    all_to_all x1, waiting for transfers between devices: 7.87 us -> 4.74 us  [per_device(): pieces = lax.all_to_all(pieces, SECTION, 0, 0)]
    pallas_call x5 -> x6, Pallas kernels: 30.9 us -> 33 us  [attend(): pl.pallas_call(functools.partial(attend_body, shards, state is None, last...]
    unnamed x14 -> x8, local copies, waits for them, and re-layouts: 4.21 us -> 2.45 us
  transfers between devices with their start and end apart: 16 -> 16, of which waited for: 7 -> 7; matrix products, arithmetic and copies ran while one was open for 3% -> 3% of each run, Pallas kernels for 18% -> 21%
where the time goes in v10:
time: 151 us; the launch traced here: 150 us
  starting transfers between devices  63.5 us (42%)
  Pallas kernels  37.6 us (25%)
  blocking collectives  20.1 us (13%)
  waiting for transfers between devices  19.5 us (13%)
  local copies, waits for them, and re-layouts  5.4 us (4%)
  between operations  3.29 us (2%)
    pallas_call x6, Pallas kernels, attend(): pl.pallas_call(functools.partial(attend_body, shards, state is None, last...  33 us
    ppermute x10, starting transfers between devices, turn(): lax.ppermute(value, axis, [(i, (i + shift) % size) for i in range(size)])  32.2 us
    all_to_all x1, blocking collectives, per_device(): out = lax.all_to_all(out, SECTION, 0, 0)  20.1 us
    ppermute x4, starting transfers between devices, onward(): return lax.ppermute(value, ('core', 'z'), pairs)  16.4 us
    ppermute x10, waiting for transfers between devices, turn(): lax.ppermute(value, axis, [(i, (i + shift) % size) for i in range(size)])  13.2 us
    all_to_all x1, starting transfers between devices, per_device(): pieces = lax.all_to_all(pieces, SECTION, 0, 0)  10.2 us
    all_to_all x1, waiting for transfers between devices, per_device(): pieces = lax.all_to_all(pieces, SECTION, 0, 0)  4.74 us
    all_to_all x1, starting transfers between devices, per_device(): q = lax.all_to_all(q, SECTION, 0, 0)  4.61 us
  transfers between devices with their start and end apart: 16, of which 7 were waited for; matrix products, arithmetic and copies ran while one was open for 3% of the time, Pallas kernels for 21%

profile of v10, /device:TPU:1, one launch (start us, length us, event | category | flops | bytes accessed | tf_op | source)
XLA Modules:
  0.0 150.5 jit_solution(1669765108513332204)
XLA Ops:
  3.6 10.2 %all-to-all-start = ((bf16[16,128,128]{2,1,0:T(8,128)(2,1)}), bf16[16,128,128]{2,1,0:T(8,128)(2,1)S(1)}, u32[]{:S(2)}, u32[]{:S(2)}) async-start(bf16[16,128,128]{2,1,0:T(8,128)(2,1)} %pack.1), calls=%async_computation | async-start | bytes 1048576 | tf_op jit(solution)/shard_map/all_to_all | solution.py:189
  19.0 4.7 %all-to-all-done = bf16[16,128,128]{2,1,0:T(8,128)(2,1)S(1)} async-done(((bf16[16,128,128]{2,1,0:T(8,128)(2,1)}), bf16[16,128,128]{2,1,0:T(8,128)(2,1)S(1)}, u32[]{:S(2)}, u32[]{:S(2)}) %all-to-all-start) | async-done | bytes 524320 | tf_op jit(solution)/shard_map/all_to_all | solution.py:189
  23.8 4.6 %all-to-all-start.1 = ((bf16[16,128,256]{2,1,0:T(8,128)(2,1)}), bf16[16,128,256]{2,1,0:T(8,128)(2,1)S(1)}, u32[]{:S(2)}, u32[]{:S(2)}) async-start(bf16[16,128,256]{2,1,0:T(8,128)(2,1)} %bitcast.1), calls=%async_computation.1 | async-start | bytes 2097152 | tf_op jit(solution)/shard_map/all_to_all | solution.py:194
  30.9 3.6 %collective-permute-start.2 = (bf16[272,128]{1,0:T(8,128)(2,1)S(1)}, bf16[272,128]{1,0:T(8,128)(2,1)S(1)}, u32[]{:S(2)}, u32[]{:S(2)}) collective-permute-start(bf16[272,128]{1,0:T(8,128)(2,1)S(1)} %get-tuple-element.90), channel_id=1, source_target_pairs={{0,2},{1,3},{2,0},{3,1},{4,6},{5,7},{6,4},{7,5},{8,10},{9,11},{10,... | collective-permute-start | bytes 208904 | tf_op jit(solution)/shard_map/ppermute | solution.py:132
  34.5 5.0 %collective-permute-start.3 = (bf16[272,128]{1,0:T(8,128)(2,1)S(1)}, bf16[272,128]{1,0:T(8,128)(2,1)S(1)}, u32[]{:S(2)}, u32[]{:S(2)}) collective-permute-start(bf16[272,128]{1,0:T(8,128)(2,1)S(1)} %get-tuple-element.90), channel_id=1, source_target_pairs={{0,3},{1,0},{2,1},{3,2},{4,7},{5,4},{6,5},{7,6},{8,11},{9,8},{10,9... | collective-permute-start | bytes 208904 | tf_op jit(solution)/shard_map/ppermute | solution.py:132
  39.4 4.0 %collective-permute-done.1 = bf16[272,128]{1,0:T(8,128)(2,1)S(1)} collective-permute-done((bf16[272,128]{1,0:T(8,128)(2,1)S(1)}, bf16[272,128]{1,0:T(8,128)(2,1)S(1)}, u32[]{:S(2)}, u32[]{:S(2)}) %collective-permute-start.1) | collective-permute-done | bytes 69664 | tf_op jit(solution)/shard_map/ppermute | solution.py:132
  43.4 4.6 %collective-permute-done.2 = bf16[272,128]{1,0:T(8,128)(2,1)S(1)} collective-permute-done((bf16[272,128]{1,0:T(8,128)(2,1)S(1)}, bf16[272,128]{1,0:T(8,128)(2,1)S(1)}, u32[]{:S(2)}, u32[]{:S(2)}) %collective-permute-start.2) | collective-permute-done | bytes 69664 | tf_op jit(solution)/shard_map/ppermute | solution.py:132
  48.0 2.6 %collective-permute-start.4 = (bf16[4,272,128]{2,1,0:T(8,128)(2,1)S(1)}, bf16[4,272,128]{2,1,0:T(8,128)(2,1)S(1)}, u32[]{:S(2)}, u32[]{:S(2)}) collective-permute-start(bf16[4,272,128]{2,1,0:T(8,128)(2,1)S(1)} %pad_maximum_fusion.1), channel_id=1, source_target_pairs={{0,32},{32,0},{1,33},{33,1},{2,34},{34,2},{3,35},{35,3},{4,36},{36... | collective-permute-start | bytes 835592 | tf_op jit(solution)/shard_map/ppermute | solution.py:132
  52.7 9.3 %collective-permute-start.5 = (bf16[4,544,128]{2,1,0:T(8,128)(2,1)}, bf16[4,544,128]{2,1,0:T(8,128)(2,1)}, u32[]{:S(2)}, u32[]{:S(2)}) collective-permute-start(bf16[4,544,128]{2,1,0:T(8,128)(2,1)} %pad_maximum_fusion.refs_3_), channel_id=1, source_target_pairs={{0,4},{4,8},{8,12},{12,16},{16,20},{20,24},{24,28},{28,0},{32,60},... | collective-permute-start | bytes 1671176 | tf_op jit(solution)/shard_map/ppermute | solution.py:206
  62.0 3.6 %collective-permute-start = (bf16[128,256]{1,0:T(8,128)(2,1)S(1)}, bf16[128,256]{1,0:T(8,128)(2,1)S(1)}, u32[]{:S(2)}, u32[]{:S(2)}) collective-permute-start(bf16[128,256]{1,0:T(8,128)(2,1)S(1)} %dynamic-slice_bitcast_fusion), channel_id=1, source_target_pairs={{0,64},{64,0},{1,65},{65,1},{2,66},{66,2},{3,67},{67,3},{4,68},{68... | collective-permute-start | bytes 196616 | tf_op jit(solution)/shard_map/ppermute | solution.py:132
  65.7 2.0 %collective-permute-done = bf16[128,256]{1,0:T(8,128)(2,1)S(1)} collective-permute-done((bf16[128,256]{1,0:T(8,128)(2,1)S(1)}, bf16[128,256]{1,0:T(8,128)(2,1)S(1)}, u32[]{:S(2)}, u32[]{:S(2)}) %collective-permute-start) | collective-permute-done | bytes 65568 | tf_op jit(solution)/shard_map/ppermute | solution.py:132
  67.7 4.9 %attend.6 = (f32[16,8,256]{2,1,0:T(8,128)S(1)}, f32[16,8,256]{2,1,0:T(8,128)S(1)}, f32[16,128,256]{2,1,0:T(8,128)S(1)}) custom-call(s32[16]{0:T(128)S(1)} %or_convert_fusion.refs_0_, bf16[16,128,256]{2,1,0:T(8,128)(2,1)S(1)} %constant_dynamic-update-slice_fusion.refs_1_, f32[1,128]{1,0:T(1,128)S(1)} %get-tuple-element.48.refs_2_, ...), custom_call_target="tpu_custom_call" | custom-call | flops 1073741824 | bytes 8388608 | tf_op jit(solution)/shard_map/attend/pallas_call | solution.py:110
  74.6 3.2 %collective-permute-start.6 = (bf16[4,544,128]{2,1,0:T(8,128)(2,1)}, bf16[4,544,128]{2,1,0:T(8,128)(2,1)S(1)}, u32[]{:S(2)}, u32[]{:S(2)}) collective-permute-start(bf16[4,544,128]{2,1,0:T(8,128)(2,1)} %collective-permute-done.5.refs_3_), channel_id=1, source_target_pairs={{0,4},{4,8},{8,12},{12,16},{16,20},{20,24},{24,28},{28,0},{32,60},... | collective-permute-start | bytes 1671176 | tf_op jit(solution)/shard_map/ppermute | solution.py:206
  77.8 7.7 %attend.7 = (f32[16,8,256]{2,1,0:T(8,128)S(1)}, f32[16,8,256]{2,1,0:T(8,128)S(1)}, f32[16,128,256]{2,1,0:T(8,128)S(1)}) custom-call(s32[16]{0:T(128)S(1)} %or_convert_fusion.refs_0_, bf16[16,128,256]{2,1,0:T(8,128)(2,1)S(1)} %constant_dynamic-update-slice_fusion.refs_1_, ...), custom_call_target="tpu_custom_call", output_to_operand_aliasing={{0}: (5, {}), {1}: (6, {}), {2}: (7, {})} | custom-call | flops 2147483648 | bytes 8388608 | tf_op jit(solution)/shard_map/attend/pallas_call | solution.py:110
  85.5 4.3 %collective-permute-start.9 = (bf16[4,544,128]{2,1,0:T(8,128)(2,1)S(1)}, bf16[4,544,128]{2,1,0:T(8,128)(2,1)S(1)}, u32[]{:S(2)}, u32[]{:S(2)}) collective-permute-start(bf16[4,544,128]{2,1,0:T(8,128)(2,1)S(1)} %collective-permute-done.6.refs_3_), channel_id=1, source_target_pairs={{0,32},{32,0},{1,33},{33,1},{2,34},{34,2},{3,35},{35,3},{4,36},{36... | collective-permute-start | bytes 1671176 | tf_op jit(solution)/shard_map/ppermute | solution.py:132
  89.9 1.9 %collective-permute-start.8 = (bf16[4,544,128]{2,1,0:T(8,128)(2,1)S(1)}, bf16[4,544,128]{2,1,0:T(8,128)(2,1)}, u32[]{:S(2)}, u32[]{:S(2)}) collective-permute-start(bf16[4,544,128]{2,1,0:T(8,128)(2,1)S(1)} %collective-permute-done.6.refs_3_), channel_id=1, source_target_pairs={{0,4},{4,8},{8,12},{12,16},{16,20},{20,24},{24,28},{28,0},{32,60},... | collective-permute-start | bytes 1671176 | tf_op jit(solution)/shard_map/ppermute | solution.py:206
  91.8 7.2 %attend.8 = (f32[16,8,256]{2,1,0:T(8,128)S(1)}, f32[16,8,256]{2,1,0:T(8,128)S(1)}, f32[16,128,256]{2,1,0:T(8,128)S(1)}) custom-call(s32[16]{0:T(128)S(1)} %or_convert_fusion.refs_0_, bf16[16,128,256]{2,1,0:T(8,128)(2,1)S(1)} %constant_dynamic-update-slice_fusion.refs_1_, ...), custom_call_target="tpu_custom_call", output_to_operand_aliasing={{0}: (5, {}), {1}: (6, {}), {2}: (7, {})} | custom-call | flops 2147483648 | bytes 8388608 | tf_op jit(solution)/shard_map/attend/pallas_call | solution.py:110
  100.5 4.0 %collective-permute-start.11 = (bf16[4,544,128]{2,1,0:T(8,128)(2,1)}, bf16[4,544,128]{2,1,0:T(8,128)(2,1)}, u32[]{:S(2)}, u32[]{:S(2)}) collective-permute-start(bf16[4,544,128]{2,1,0:T(8,128)(2,1)} %collective-permute-done.8.refs_3_), channel_id=1, source_target_pairs={{0,32},{32,0},{1,33},{33,1},{2,34},{34,2},{3,35},{35,3},{4,36},{36... | collective-permute-start | bytes 1671176 | tf_op jit(solution)/shard_map/ppermute | solution.py:132
  105.5 2.1 %collective-permute-start.10 = (bf16[2,544,128]{2,1,0:T(8,128)(2,1)S(1)}, bf16[2,544,128]{2,1,0:T(8,128)(2,1)S(1)}, u32[]{:S(2)}, u32[]{:S(2)}) collective-permute-start(bf16[2,544,128]{2,1,0:T(8,128)(2,1)S(1)} %constant_dynamic-slice_fusion.3), channel_id=1, source_target_pairs={{0,4},{4,8},{8,12},{12,16},{16,20},{20,24},{24,28},{28,0},{32,60},... | collective-permute-start | bytes 835592 | tf_op jit(solution)/shard_map/ppermute | solution.py:206
  107.6 7.9 %attend.9 = (f32[16,8,256]{2,1,0:T(8,128)S(1)}, f32[16,8,256]{2,1,0:T(8,128)S(1)}, f32[16,128,256]{2,1,0:T(8,128)S(1)}) custom-call(s32[16]{0:T(128)S(1)} %or_convert_fusion.refs_0_, bf16[16,128,256]{2,1,0:T(8,128)(2,1)S(1)} %constant_dynamic-update-slice_fusion.refs_1_, ...), custom_call_target="tpu_custom_call", output_to_operand_aliasing={{0}: (5, {}), {1}: (6, {}), {2}: (7, {})} | custom-call | flops 2147483648 | bytes 8388608 | tf_op jit(solution)/shard_map/attend/pallas_call | solution.py:110
  119.6 3.4 %collective-permute-start.13 = (bf16[128,256]{1,0:T(8,128)(2,1)S(1)}, bf16[128,256]{1,0:T(8,128)(2,1)S(1)}, u32[]{:S(2)}, u32[]{:S(2)}) collective-permute-start(bf16[128,256]{1,0:T(8,128)(2,1)S(1)} %bitcast.28), channel_id=1, source_target_pairs={{0,64},{64,0},{1,65},{65,1},{2,66},{66,2},{3,67},{67,3},{4,68},{68... | collective-permute-start | bytes 196616 | tf_op jit(solution)/shard_map/ppermute | solution.py:132
  123.0 4.6 %attend.11 = bf16[16,128,256]{2,1,0:T(8,128)(2,1)S(1)} custom-call(s32[16]{0:T(128)S(1)} %or_convert_fusion.refs_0_, bf16[16,128,256]{2,1,0:T(8,128)(2,1)S(1)} %constant_dynamic-update-slice_fusion.refs_1_, f32[1,128]{1,0:T(1,128)S(1)} %get-tuple-element.48.refs_2_, bf16[2,544,128]{2,1,0:T(8,128)(2,1)S(1)} %collective-permute-done.10.refs_3_, ...), custom_call_target="tpu_custom_call" | custom-call | flops 1073741824 | bytes 8388608 | tf_op jit(solution)/shard_map/attend/pallas_call | solution.py:110
  127.6 20.1 %all_to_all.15.in_ref = bf16[16,128,256]{2,1,0:T(8,128)(2,1)} all-to-all(bf16[16,128,256]{2,1,0:T(8,128)(2,1)S(1)} %bitcast_dynamic-update-slice_fusion), channel_id=1, replica_groups=mesh['x'=4,'yl'=2,'core'=2,'z'=8,'yh'=4] {'x','yl','core'}, dimensions={0} | all-to-all | bytes 2097152 | tf_op jit(solution)/shard_map/all_to_all | solution.py:232
  147.7 2.8 %columns.1 = bf16[128,4096]{1,0:T(8,128)(2,1)} custom-call(bf16[16,128,256]{2,1,0:T(8,128)(2,1)} %all_to_all.15.in_ref), custom_call_target="tpu_custom_call" | custom-call | tf_op jit(solution)/shard_map/columns/pallas_call | solution.py:160
  (42 shorter events, 19.1 us)
Async XLA Ops:
  0.0 13.9 %copy-start.1 = (s32[16]{0:T(128)S(1)}, s32[16]{0:T(128)}, u32[]{:S(2)}) copy-start(s32[16]{0:T(128)} %param.7) | copy-start | bytes 196
  0.0 17.0 %copy-start = (bf16[1,128,4096]{2,1,0:T(8,128)(2,1)S(1)}, bf16[1,128,4096]{2,1,0:T(8,128)(2,1)}, u32[]{:S(2)}) copy-start(bf16[1,128,4096]{2,1,0:T(8,128)(2,1)} %param.4) | copy-start | bytes 3145732
  3.6 20.1 %all-to-all-start = ((bf16[16,128,128]{2,1,0:T(8,128)(2,1)}), bf16[16,128,128]{2,1,0:T(8,128)(2,1)S(1)}, u32[]{:S(2)}, u32[]{:S(2)}) async-start(bf16[16,128,128]{2,1,0:T(8,128)(2,1)} %pack.1), calls=%async_computation | async-start | bytes 1048576 | tf_op jit(solution)/shard_map/all_to_all | solution.py:189
  17.0 2.0 %copy-start.2 = (s32[128]{0:T(128)S(1)}, s32[128]{0:T(128)}, u32[]{:S(2)}) copy-start(s32[128]{0:T(128)} %param.6) | copy-start | bytes 1540
  23.8 38.2 %all-to-all-start.1 = ((bf16[16,128,256]{2,1,0:T(8,128)(2,1)}), bf16[16,128,256]{2,1,0:T(8,128)(2,1)S(1)}, u32[]{:S(2)}, u32[]{:S(2)}) async-start(bf16[16,128,256]{2,1,0:T(8,128)(2,1)} %bitcast.1), calls=%async_computation.1 | async-start | bytes 2097152 | tf_op jit(solution)/shard_map/all_to_all | solution.py:194
  29.0 14.4 %collective-permute-start.1 = (bf16[272,128]{1,0:T(8,128)(2,1)S(1)}, bf16[272,128]{1,0:T(8,128)(2,1)S(1)}, u32[]{:S(2)}, u32[]{:S(2)}) collective-permute-start(bf16[272,128]{1,0:T(8,128)(2,1)S(1)} %get-tuple-element.90), channel_id=1, source_target_pairs={{0,1},{1,2},{2,3},{3,0},{4,5},{5,6},{6,7},{7,4},{8,9},{9,10},{10,1... | collective-permute-start | bytes 208904 | tf_op jit(solution)/shard_map/ppermute | solution.py:132
  30.9 17.1 %collective-permute-start.2 = (bf16[272,128]{1,0:T(8,128)(2,1)S(1)}, bf16[272,128]{1,0:T(8,128)(2,1)S(1)}, u32[]{:S(2)}, u32[]{:S(2)}) collective-permute-start(bf16[272,128]{1,0:T(8,128)(2,1)S(1)} %get-tuple-element.90), channel_id=1, source_target_pairs={{0,2},{1,3},{2,0},{3,1},{4,6},{5,7},{6,4},{7,5},{8,10},{9,11},{10,... | collective-permute-start | bytes 208904 | tf_op jit(solution)/shard_map/ppermute | solution.py:132
  34.5 13.5 %collective-permute-start.3 = (bf16[272,128]{1,0:T(8,128)(2,1)S(1)}, bf16[272,128]{1,0:T(8,128)(2,1)S(1)}, u32[]{:S(2)}, u32[]{:S(2)}) collective-permute-start(bf16[272,128]{1,0:T(8,128)(2,1)S(1)} %get-tuple-element.90), channel_id=1, source_target_pairs={{0,3},{1,0},{2,1},{3,2},{4,7},{5,4},{6,5},{7,6},{8,11},{9,8},{10,9... | collective-permute-start | bytes 208904 | tf_op jit(solution)/shard_map/ppermute | solution.py:132
  48.0 3.8 %collective-permute-start.4 = (bf16[4,272,128]{2,1,0:T(8,128)(2,1)S(1)}, bf16[4,272,128]{2,1,0:T(8,128)(2,1)S(1)}, u32[]{:S(2)}, u32[]{:S(2)}) collective-permute-start(bf16[4,272,128]{2,1,0:T(8,128)(2,1)S(1)} %pad_maximum_fusion.1), channel_id=1, source_target_pairs={{0,32},{32,0},{1,33},{33,1},{2,34},{34,2},{3,35},{35,3},{4,36},{36... | collective-permute-start | bytes 835592 | tf_op jit(solution)/shard_map/ppermute | solution.py:132
  52.7 19.9 %collective-permute-start.5 = (bf16[4,544,128]{2,1,0:T(8,128)(2,1)}, bf16[4,544,128]{2,1,0:T(8,128)(2,1)}, u32[]{:S(2)}, u32[]{:S(2)}) collective-permute-start(bf16[4,544,128]{2,1,0:T(8,128)(2,1)} %pad_maximum_fusion.refs_3_), channel_id=1, source_target_pairs={{0,4},{4,8},{8,12},{12,16},{16,20},{20,24},{24,28},{28,0},{32,60},... | collective-permute-start | bytes 1671176 | tf_op jit(solution)/shard_map/ppermute | solution.py:206
  62.0 5.7 %collective-permute-start = (bf16[128,256]{1,0:T(8,128)(2,1)S(1)}, bf16[128,256]{1,0:T(8,128)(2,1)S(1)}, u32[]{:S(2)}, u32[]{:S(2)}) collective-permute-start(bf16[128,256]{1,0:T(8,128)(2,1)S(1)} %dynamic-slice_bitcast_fusion), channel_id=1, source_target_pairs={{0,64},{64,0},{1,65},{65,1},{2,66},{66,2},{3,67},{67,3},{4,68},{68... | collective-permute-start | bytes 196616 | tf_op jit(solution)/shard_map/ppermute | solution.py:132
  72.7 5.1 %collective-permute-start.7 = (bf16[4,544,128]{2,1,0:T(8,128)(2,1)}, bf16[4,544,128]{2,1,0:T(8,128)(2,1)S(1)}, u32[]{:S(2)}, u32[]{:S(2)}) collective-permute-start(bf16[4,544,128]{2,1,0:T(8,128)(2,1)} %collective-permute-done.5.refs_3_), channel_id=1, source_target_pairs={{0,32},{32,0},{1,33},{33,1},{2,34},{34,2},{3,35},{35,3},{4,36},{36... | collective-permute-start | bytes 1671176 | tf_op jit(solution)/shard_map/ppermute | solution.py:132
  74.6 10.9 %collective-permute-start.6 = (bf16[4,544,128]{2,1,0:T(8,128)(2,1)}, bf16[4,544,128]{2,1,0:T(8,128)(2,1)S(1)}, u32[]{:S(2)}, u32[]{:S(2)}) collective-permute-start(bf16[4,544,128]{2,1,0:T(8,128)(2,1)} %collective-permute-done.5.refs_3_), channel_id=1, source_target_pairs={{0,4},{4,8},{8,12},{12,16},{16,20},{20,24},{24,28},{28,0},{32,60},... | collective-permute-start | bytes 1671176 | tf_op jit(solution)/shard_map/ppermute | solution.py:206
  85.5 6.3 %collective-permute-start.9 = (bf16[4,544,128]{2,1,0:T(8,128)(2,1)S(1)}, bf16[4,544,128]{2,1,0:T(8,128)(2,1)S(1)}, u32[]{:S(2)}, u32[]{:S(2)}) collective-permute-start(bf16[4,544,128]{2,1,0:T(8,128)(2,1)S(1)} %collective-permute-done.6.refs_3_), channel_id=1, source_target_pairs={{0,32},{32,0},{1,33},{33,1},{2,34},{34,2},{3,35},{35,3},{4,36},{36... | collective-permute-start | bytes 1671176 | tf_op jit(solution)/shard_map/ppermute | solution.py:132
  89.9 10.7 %collective-permute-start.8 = (bf16[4,544,128]{2,1,0:T(8,128)(2,1)S(1)}, bf16[4,544,128]{2,1,0:T(8,128)(2,1)}, u32[]{:S(2)}, u32[]{:S(2)}) collective-permute-start(bf16[4,544,128]{2,1,0:T(8,128)(2,1)S(1)} %collective-permute-done.6.refs_3_), channel_id=1, source_target_pairs={{0,4},{4,8},{8,12},{12,16},{16,20},{20,24},{24,28},{28,0},{32,60},... | collective-permute-start | bytes 1671176 | tf_op jit(solution)/shard_map/ppermute | solution.py:206
  100.5 7.1 %collective-permute-start.11 = (bf16[4,544,128]{2,1,0:T(8,128)(2,1)}, bf16[4,544,128]{2,1,0:T(8,128)(2,1)}, u32[]{:S(2)}, u32[]{:S(2)}) collective-permute-start(bf16[4,544,128]{2,1,0:T(8,128)(2,1)} %collective-permute-done.8.refs_3_), channel_id=1, source_target_pairs={{0,32},{32,0},{1,33},{33,1},{2,34},{34,2},{3,35},{35,3},{4,36},{36... | collective-permute-start | bytes 1671176 | tf_op jit(solution)/shard_map/ppermute | solution.py:132
  105.5 10.0 %collective-permute-start.10 = (bf16[2,544,128]{2,1,0:T(8,128)(2,1)S(1)}, bf16[2,544,128]{2,1,0:T(8,128)(2,1)S(1)}, u32[]{:S(2)}, u32[]{:S(2)}) collective-permute-start(bf16[2,544,128]{2,1,0:T(8,128)(2,1)S(1)} %constant_dynamic-slice_fusion.3), channel_id=1, source_target_pairs={{0,4},{4,8},{8,12},{12,16},{16,20},{20,24},{24,28},{28,0},{32,60},... | collective-permute-start | bytes 835592 | tf_op jit(solution)/shard_map/ppermute | solution.py:206
  115.5 3.5 %collective-permute-start.12 = (bf16[2,544,128]{2,1,0:T(8,128)(2,1)S(1)}, bf16[2,544,128]{2,1,0:T(8,128)(2,1)S(1)}, u32[]{:S(2)}, u32[]{:S(2)}) collective-permute-start(bf16[2,544,128]{2,1,0:T(8,128)(2,1)S(1)} %collective-permute-done.10.refs_3_), channel_id=1, source_target_pairs={{0,32},{32,0},{1,33},{33,1},{2,34},{34,2},{3,35},{35,3},{4,36},{36... | collective-permute-start | bytes 835592 | tf_op jit(solution)/shard_map/ppermute | solution.py:132
  119.6 8.0 %collective-permute-start.13 = (bf16[128,256]{1,0:T(8,128)(2,1)S(1)}, bf16[128,256]{1,0:T(8,128)(2,1)S(1)}, u32[]{:S(2)}, u32[]{:S(2)}) collective-permute-start(bf16[128,256]{1,0:T(8,128)(2,1)S(1)} %bitcast.28), channel_id=1, source_target_pairs={{0,64},{64,0},{1,65},{65,1},{2,66},{66,2},{3,67},{67,3},{4,68},{68... | collective-permute-start | bytes 196616 | tf_op jit(solution)/shard_map/ppermute | solution.py:132

commit v11 on v10

--- a/solution.py
+++ b/solution.py
@@ -150,23 +150,6 @@
     )(kv)
 
 
-def spread_columns(slabs):
-    group = 4
-
-    def body(in_ref, out_ref):
-        for i in range(group):
-            out_ref[:, i * WIDE : (i + 1) * WIDE] = in_ref[pl.program_id(0) * group + i]
-
-    return pl.pallas_call(
-        body,
-        grid=(LAYERS // group,),
-        in_specs=[pl.BlockSpec(memory_space=pltpu.VMEM)],
-        out_specs=pl.BlockSpec((ROWS, group * WIDE), lambda i: (0, i)),
-        out_shape=jax.ShapeDtypeStruct((ROWS, LAYERS * WIDE), slabs.dtype),
-        name="columns",
-    )(slabs)
-
-
 def pick(slabs, index):
     return lax.dynamic_index_in_dim(slabs, index.astype(jnp.uint32), 0, keepdims=False)
 
@@ -191,11 +174,12 @@
     q, pieces, top_holder, warm, other_warm, use_warm, pos, block_ids = lax.optimization_barrier(
         (q, pieces, top_holder, warm, other_warm, use_warm, pos, block_ids)
     )
+    shard = jnp.concatenate([pick(pieces, top_holder), pick(pieces, warm), block_ids], axis=0)
+    mine = jnp.stack([shard] + [turn(shard, "yh", nyh, shift) for shift in range(1, nyh)])
+    q, mine = lax.optimization_barrier((q, mine))
     q = lax.all_to_all(q, SECTION, 0, 0)
     q_other = turn(pick(q, other_warm), "yl", 2, 1)
     q = put(q, q_other, other_warm)
-    shard = jnp.concatenate([pick(pieces, top_holder), pick(pieces, warm), block_ids], axis=0)
-    mine = jnp.stack([shard] + [turn(shard, "yh", nyh, shift) for shift in range(1, nyh)])
     theirs = turn(mine, "core", 2, 1)
     keys, values = jnp.where(core == 0, mine, theirs), jnp.where(core == 0, theirs, mine)
     line = jnp.concatenate([keys, values], axis=1)
@@ -213,16 +197,16 @@
     def part(blocks, state, last=False):
         return attend(use_warm, q, pos, blocks, state, last)
 
-    state = part([line], None)
-    arrived, state = lax.optimization_barrier((arrived, state))
+    held, state = [line], None
     half = nyh // 2
     for step in range(nz // 2 - 1):
         if step < nz // 2 - 2:
             coming = onward(arrived)
         else:
             coming = onward(lax.dynamic_slice_in_dim(arrived, (core * half).astype(jnp.uint32), half, axis=0))
-        state = part([arrived, handed(arrived)], state)
+        state = part([*held, arrived, handed(arrived)], state)
         arrived, state = lax.optimization_barrier((coming, state))
+        held = []
     held = [arrived, handed(arrived)]
     slab_state = [pick(value, other_warm)[None] for value in state]
     slab = attend(jnp.ones(1, jnp.int32), q_other[None], pos, held, slab_state, True)
@@ -230,7 +214,7 @@
     back = turn(slab[0], "yl", 2, 1)
     out = put(part(held, state, True), back, other_warm)
     out = lax.all_to_all(out, SECTION, 0, 0)
-    return spread_columns(out)[None]
+    return out.transpose(1, 0, 2).reshape(1, ROWS, H * HD)
 
 
 def solution(mesh):

time: 151 us -> 151 us (level)
  local copies, waits for them, and re-layouts: 5.4 us -> 11.2 us
  Pallas kernels: 37.6 us -> 32.2 us
  starting transfers between devices: 63.5 us -> 66.1 us
  waiting for transfers between devices: 19.5 us -> 17.1 us
    ppermute x10, waiting for transfers between devices: 13.2 us -> 6.68 us  [turn(): lax.ppermute(value, axis, [(i, (i + shift) % size) for i in range(size)])]
    ppermute x4, waiting for transfers between devices: 1.58 us -> 5.72 us  [onward(): return lax.ppermute(value, ('core', 'z'), pairs)]
    unnamed x8 -> x16, local copies, waits for them, and re-layouts: 2.45 us -> 6.17 us
    all_to_all x1, starting transfers between devices: 4.61 us -> 7.75 us  [per_device(): q = lax.all_to_all(q, SECTION, 0, 0)]
    pallas_call x1 -> x0, Pallas kernels: 2.77 us -> none  [spread_columns(): pl.pallas_call(body, grid=(LAYERS // group,), in_specs=[pl.BlockSpec(memo...]
    pallas_call x6 -> x5, Pallas kernels: 33 us -> 30.3 us  [attend(): pl.pallas_call(functools.partial(attend_body, shards, state is None, last...]
    ppermute x10, starting transfers between devices: 32.2 us -> 29.6 us  [turn(): lax.ppermute(value, axis, [(i, (i + shift) % size) for i in range(size)])]
    ppermute x4, starting transfers between devices: 16.4 us -> 18.5 us  [onward(): return lax.ppermute(value, ('core', 'z'), pairs)]
  transfers between devices with their start and end apart: 16 -> 16, of which waited for: 7 -> 6; matrix products, arithmetic and copies ran while one was open for 3% -> 3% of each run, Pallas kernels for 21% -> 20%
where the time goes in v11:
time: 151 us; the launch traced here: 150 us
  starting transfers between devices  66.1 us (44%)
  Pallas kernels  32.2 us (21%)
  blocking collectives  20.1 us (13%)
  waiting for transfers between devices  17.1 us (11%)
  local copies, waits for them, and re-layouts  11.2 us (7%)
  between operations  3.49 us (2%)
    pallas_call x5, Pallas kernels, attend(): pl.pallas_call(functools.partial(attend_body, shards, state is None, last...  30.3 us
    ppermute x10, starting transfers between devices, turn(): lax.ppermute(value, axis, [(i, (i + shift) % size) for i in range(size)])  29.6 us
    all_to_all x1, blocking collectives, per_device(): out = lax.all_to_all(out, SECTION, 0, 0)  20.1 us
    ppermute x4, starting transfers between devices, onward(): return lax.ppermute(value, ('core', 'z'), pairs)  18.5 us
    all_to_all x1, starting transfers between devices, per_device(): pieces = lax.all_to_all(pieces, SECTION, 0, 0)  10.2 us
    all_to_all x1, starting transfers between devices, per_device(): q = lax.all_to_all(q, SECTION, 0, 0)  7.75 us
    ppermute x10, waiting for transfers between devices, turn(): lax.ppermute(value, axis, [(i, (i + shift) % size) for i in range(size)])  6.68 us
    unnamed x16, local copies, waits for them, and re-layouts  6.17 us
  transfers between devices with their start and end apart: 16, of which 6 were waited for; matrix products, arithmetic and copies ran while one was open for 3% of the time, Pallas kernels for 20%

profile of v11, /device:TPU:1, one launch (start us, length us, event | category | flops | bytes accessed | tf_op | source)
XLA Modules:
  0.0 150.3 jit_solution(6361579652146203293)
XLA Ops:
  3.6 10.2 %all-to-all-start = ((bf16[16,128,128]{2,1,0:T(8,128)(2,1)}), bf16[16,128,128]{2,1,0:T(8,128)(2,1)S(1)}, u32[]{:S(2)}, u32[]{:S(2)}) async-start(bf16[16,128,128]{2,1,0:T(8,128)(2,1)} %pack.1), calls=%async_computation | async-start | bytes 1048576 | tf_op jit(solution)/shard_map/all_to_all | solution.py:172
  19.1 4.7 %all-to-all-done = bf16[16,128,128]{2,1,0:T(8,128)(2,1)S(1)} async-done(((bf16[16,128,128]{2,1,0:T(8,128)(2,1)}), bf16[16,128,128]{2,1,0:T(8,128)(2,1)S(1)}, u32[]{:S(2)}, u32[]{:S(2)}) %all-to-all-start) | async-done | bytes 524320 | tf_op jit(solution)/shard_map/all_to_all | solution.py:172
  24.5 3.1 %collective-permute-start.1 = (bf16[272,128]{1,0:T(8,128)(2,1)S(1)}, bf16[272,128]{1,0:T(8,128)(2,1)S(1)}, u32[]{:S(2)}, u32[]{:S(2)}) collective-permute-start(bf16[272,128]{1,0:T(8,128)(2,1)S(1)} %get-tuple-element.80), channel_id=1, source_target_pairs={{0,2},{1,3},{2,0},{3,1},{4,6},{5,7},{6,4},{7,5},{8,10},{9,11},{10,... | collective-permute-start | bytes 208904 | tf_op jit(solution)/shard_map/ppermute | solution.py:132
  27.6 2.9 %collective-permute-start.2 = (bf16[272,128]{1,0:T(8,128)(2,1)S(1)}, bf16[272,128]{1,0:T(8,128)(2,1)S(1)}, u32[]{:S(2)}, u32[]{:S(2)}) collective-permute-start(bf16[272,128]{1,0:T(8,128)(2,1)S(1)} %get-tuple-element.80), channel_id=1, source_target_pairs={{0,3},{1,0},{2,1},{3,2},{4,7},{5,4},{6,5},{7,6},{8,11},{9,8},{10,9... | collective-permute-start | bytes 208904 | tf_op jit(solution)/shard_map/ppermute | solution.py:132
  30.4 3.3 %collective-permute-start = (bf16[272,128]{1,0:T(8,128)(2,1)S(1)}, bf16[272,128]{1,0:T(8,128)(2,1)S(1)}, u32[]{:S(2)}, u32[]{:S(2)}) collective-permute-start(bf16[272,128]{1,0:T(8,128)(2,1)S(1)} %get-tuple-element.80), channel_id=1, source_target_pairs={{0,1},{1,2},{2,3},{3,0},{4,5},{5,6},{6,7},{7,4},{8,9},{9,10},{10,1... | collective-permute-start | bytes 208904 | tf_op jit(solution)/shard_map/ppermute | solution.py:132
  33.8 3.9 %collective-permute-done = bf16[272,128]{1,0:T(8,128)(2,1)S(1)} collective-permute-done((bf16[272,128]{1,0:T(8,128)(2,1)S(1)}, bf16[272,128]{1,0:T(8,128)(2,1)S(1)}, u32[]{:S(2)}, u32[]{:S(2)}) %collective-permute-start) | collective-permute-done | bytes 69664 | tf_op jit(solution)/shard_map/ppermute | solution.py:132
  37.7 7.8 %all-to-all-start.1 = ((bf16[16,128,256]{2,1,0:T(8,128)(2,1)}), bf16[16,128,256]{2,1,0:T(8,128)(2,1)S(1)}, u32[]{:S(2)}, u32[]{:S(2)}) async-start(bf16[16,128,256]{2,1,0:T(8,128)(2,1)} %bitcast.1), calls=%async_computation.1 | async-start | bytes 2097152 | tf_op jit(solution)/shard_map/all_to_all | solution.py:180
  45.5 2.1 %collective-permute-start.4 = (bf16[4,272,128]{2,1,0:T(8,128)(2,1)S(1)}, bf16[4,272,128]{2,1,0:T(8,128)(2,1)S(1)}, u32[]{:S(2)}, u32[]{:S(2)}) collective-permute-start(bf16[4,272,128]{2,1,0:T(8,128)(2,1)S(1)} %pad_maximum_fusion.1), channel_id=1, source_target_pairs={{0,32},{32,0},{1,33},{33,1},{2,34},{34,2},{3,35},{35,3},{4,36},{36... | collective-permute-start | bytes 835592 | tf_op jit(solution)/shard_map/ppermute | solution.py:132
  49.0 9.3 %collective-permute-start.5 = (bf16[4,544,128]{2,1,0:T(8,128)(2,1)S(1)}, bf16[4,544,128]{2,1,0:T(8,128)(2,1)}, u32[]{:S(2)}, u32[]{:S(2)}) collective-permute-start(bf16[4,544,128]{2,1,0:T(8,128)(2,1)S(1)} %pad_maximum_fusion.refs_3_), channel_id=1, source_target_pairs={{0,4},{4,8},{8,12},{12,16},{16,20},{20,24},{24,28},{28,0},{32,60},... | collective-permute-start | bytes 1671176 | tf_op jit(solution)/shard_map/ppermute | solution.py:190
  59.1 5.6 %collective-permute-done.5.refs_4_ = bf16[4,544,128]{2,1,0:T(8,128)(2,1)} collective-permute-done((bf16[4,544,128]{2,1,0:T(8,128)(2,1)S(1)}, bf16[4,544,128]{2,1,0:T(8,128)(2,1)}, u32[]{:S(2)}, u32[]{:S(2)}) %collective-permute-start.5) | collective-permute-done | bytes 557088 | tf_op jit(solution)/shard_map/ppermute | solution.py:190
  64.8 3.6 %collective-permute-start.7 = (bf16[4,544,128]{2,1,0:T(8,128)(2,1)}, bf16[4,544,128]{2,1,0:T(8,128)(2,1)S(1)}, u32[]{:S(2)}, u32[]{:S(2)}) collective-permute-start(bf16[4,544,128]{2,1,0:T(8,128)(2,1)} %collective-permute-done.5.refs_4_), channel_id=1, source_target_pairs={{0,32},{32,0},{1,33},{33,1},{2,34},{34,2},{3,35},{35,3},{4,36},{36... | collective-permute-start | bytes 1671176 | tf_op jit(solution)/shard_map/ppermute | solution.py:132
  68.4 3.4 %collective-permute-start.3 = (bf16[128,256]{1,0:T(8,128)(2,1)S(1)}, bf16[128,256]{1,0:T(8,128)(2,1)S(1)}, u32[]{:S(2)}, u32[]{:S(2)}) collective-permute-start(bf16[128,256]{1,0:T(8,128)(2,1)S(1)} %dynamic-slice_bitcast_fusion), channel_id=1, source_target_pairs={{0,64},{64,0},{1,65},{65,1},{2,66},{66,2},{3,67},{67,3},{4,68},{68... | collective-permute-start | bytes 196616 | tf_op jit(solution)/shard_map/ppermute | solution.py:132
  71.8 3.6 %collective-permute-start.6 = (bf16[4,544,128]{2,1,0:T(8,128)(2,1)}, bf16[4,544,128]{2,1,0:T(8,128)(2,1)S(1)}, u32[]{:S(2)}, u32[]{:S(2)}) collective-permute-start(bf16[4,544,128]{2,1,0:T(8,128)(2,1)} %collective-permute-done.5.refs_4_), channel_id=1, source_target_pairs={{0,4},{4,8},{8,12},{12,16},{16,20},{20,24},{24,28},{28,0},{32,60},... | collective-permute-start | bytes 1671176 | tf_op jit(solution)/shard_map/ppermute | solution.py:190
  78.4 10.0 %attend.5 = (f32[16,8,256]{2,1,0:T(8,128)S(1)}, f32[16,8,256]{2,1,0:T(8,128)S(1)}, f32[16,128,256]{2,1,0:T(8,128)S(1)}) custom-call(s32[16]{0:T(128)S(1)} %or_convert_fusion.refs_0_, bf16[16,128,256]{2,1,0:T(8,128)(2,1)S(1)} %constant_dynamic-update-slice_fusion.refs_1_, f32[1,128]{1,0:T(1,128)S(1)} %get-tuple-element.48.refs_2_, ...), custom_call_target="tpu_custom_call" | custom-call | flops 3221225472 | bytes 8388608 | tf_op jit(solution)/shard_map/attend/pallas_call | solution.py:110
  88.4 1.9 %collective-permute-start.9 = (bf16[4,544,128]{2,1,0:T(8,128)(2,1)S(1)}, bf16[4,544,128]{2,1,0:T(8,128)(2,1)S(1)}, u32[]{:S(2)}, u32[]{:S(2)}) collective-permute-start(bf16[4,544,128]{2,1,0:T(8,128)(2,1)S(1)} %collective-permute-done.6.refs_3_), channel_id=1, source_target_pairs={{0,32},{32,0},{1,33},{33,1},{2,34},{34,2},{3,35},{35,3},{4,36},{36... | collective-permute-start | bytes 1671176 | tf_op jit(solution)/shard_map/ppermute | solution.py:132
  90.3 3.4 %collective-permute-start.8 = (bf16[4,544,128]{2,1,0:T(8,128)(2,1)S(1)}, bf16[4,544,128]{2,1,0:T(8,128)(2,1)}, u32[]{:S(2)}, u32[]{:S(2)}) collective-permute-start(bf16[4,544,128]{2,1,0:T(8,128)(2,1)S(1)} %collective-permute-done.6.refs_3_), channel_id=1, source_target_pairs={{0,4},{4,8},{8,12},{12,16},{16,20},{20,24},{24,28},{28,0},{32,60},... | collective-permute-start | bytes 1671176 | tf_op jit(solution)/shard_map/ppermute | solution.py:190
  93.8 7.2 %attend.6 = (f32[16,8,256]{2,1,0:T(8,128)S(1)}, f32[16,8,256]{2,1,0:T(8,128)S(1)}, f32[16,128,256]{2,1,0:T(8,128)S(1)}) custom-call(s32[16]{0:T(128)S(1)} %or_convert_fusion.refs_0_, bf16[16,128,256]{2,1,0:T(8,128)(2,1)S(1)} %constant_dynamic-update-slice_fusion.refs_1_, ...), custom_call_target="tpu_custom_call", output_to_operand_aliasing={{0}: (5, {}), {1}: (6, {}), {2}: (7, {})} | custom-call | flops 2147483648 | bytes 8388608 | tf_op jit(solution)/shard_map/attend/pallas_call | solution.py:110
  101.0 4.5 %collective-permute-start.11 = (bf16[4,544,128]{2,1,0:T(8,128)(2,1)}, bf16[4,544,128]{2,1,0:T(8,128)(2,1)}, u32[]{:S(2)}, u32[]{:S(2)}) collective-permute-start(bf16[4,544,128]{2,1,0:T(8,128)(2,1)} %collective-permute-done.8.refs_3_), channel_id=1, source_target_pairs={{0,32},{32,0},{1,33},{33,1},{2,34},{34,2},{3,35},{35,3},{4,36},{36... | collective-permute-start | bytes 1671176 | tf_op jit(solution)/shard_map/ppermute | solution.py:132
  106.5 2.1 %collective-permute-start.10 = (bf16[2,544,128]{2,1,0:T(8,128)(2,1)S(1)}, bf16[2,544,128]{2,1,0:T(8,128)(2,1)S(1)}, u32[]{:S(2)}, u32[]{:S(2)}) collective-permute-start(bf16[2,544,128]{2,1,0:T(8,128)(2,1)S(1)} %constant_dynamic-slice_fusion.3), channel_id=1, source_target_pairs={{0,4},{4,8},{8,12},{12,16},{16,20},{20,24},{24,28},{28,0},{32,60},... | collective-permute-start | bytes 835592 | tf_op jit(solution)/shard_map/ppermute | solution.py:190
  108.6 7.9 %attend.7 = (f32[16,8,256]{2,1,0:T(8,128)S(1)}, f32[16,8,256]{2,1,0:T(8,128)S(1)}, f32[16,128,256]{2,1,0:T(8,128)S(1)}) custom-call(s32[16]{0:T(128)S(1)} %or_convert_fusion.refs_0_, bf16[16,128,256]{2,1,0:T(8,128)(2,1)S(1)} %constant_dynamic-update-slice_fusion.refs_1_, ...), custom_call_target="tpu_custom_call", output_to_operand_aliasing={{0}: (5, {}), {1}: (6, {}), {2}: (7, {})} | custom-call | flops 2147483648 | bytes 8388608 | tf_op jit(solution)/shard_map/attend/pallas_call | solution.py:110
  116.5 1.9 %collective-permute-start.12 = (bf16[2,544,128]{2,1,0:T(8,128)(2,1)S(1)}, bf16[2,544,128]{2,1,0:T(8,128)(2,1)S(1)}, u32[]{:S(2)}, u32[]{:S(2)}) collective-permute-start(bf16[2,544,128]{2,1,0:T(8,128)(2,1)S(1)} %collective-permute-done.10.refs_3_), channel_id=1, source_target_pairs={{0,32},{32,0},{1,33},{33,1},{2,34},{34,2},{3,35},{35,3},{4,36},{36... | collective-permute-start | bytes 835592 | tf_op jit(solution)/shard_map/ppermute | solution.py:132
  120.6 2.9 %collective-permute-start.13 = (bf16[128,256]{1,0:T(8,128)(2,1)S(1)}, bf16[128,256]{1,0:T(8,128)(2,1)S(1)}, u32[]{:S(2)}, u32[]{:S(2)}) collective-permute-start(bf16[128,256]{1,0:T(8,128)(2,1)S(1)} %bitcast.29), channel_id=1, source_target_pairs={{0,64},{64,0},{1,65},{65,1},{2,66},{66,2},{3,67},{67,3},{4,68},{68... | collective-permute-start | bytes 196616 | tf_op jit(solution)/shard_map/ppermute | solution.py:132
  123.6 4.6 %attend.9 = bf16[16,128,256]{2,1,0:T(8,128)(2,1)S(1)} custom-call(s32[16]{0:T(128)S(1)} %or_convert_fusion.refs_0_, bf16[16,128,256]{2,1,0:T(8,128)(2,1)S(1)} %constant_dynamic-update-slice_fusion.refs_1_, f32[1,128]{1,0:T(1,128)S(1)} %get-tuple-element.48.refs_2_, bf16[2,544,128]{2,1,0:T(8,128)(2,1)S(1)} %collective-permute-done.10.refs_3_, ...), custom_call_target="tpu_custom_call" | custom-call | flops 1073741824 | bytes 8388608 | tf_op jit(solution)/shard_map/attend/pallas_call | solution.py:110
  128.2 20.1 %all_to_all.15 = bf16[16,128,256]{2,1,0:T(8,128)(2,1)S(1)} all-to-all(bf16[16,128,256]{2,1,0:T(8,128)(2,1)S(1)} %bitcast_dynamic-update-slice_fusion), channel_id=1, replica_groups=mesh['x'=4,'yl'=2,'core'=2,'z'=8,'yh'=4] {'x','yl','core'}, dimensions={0} | all-to-all | bytes 2097152 | tf_op jit(solution)/shard_map/all_to_all | solution.py:216
  (50 shorter events, 16.8 us)
Async XLA Ops:
  0.0 13.9 %copy-start.5 = (s32[16]{0:T(128)S(1)}, s32[16]{0:T(128)}, u32[]{:S(2)}) copy-start(s32[16]{0:T(128)} %param.7) | copy-start | bytes 196
  0.0 17.1 %copy-start.4 = (bf16[1,128,4096]{2,1,0:T(8,128)(2,1)S(1)}, bf16[1,128,4096]{2,1,0:T(8,128)(2,1)}, u32[]{:S(2)}) copy-start(bf16[1,128,4096]{2,1,0:T(8,128)(2,1)} %param.4) | copy-start | bytes 3145732
  3.6 20.1 %all-to-all-start = ((bf16[16,128,128]{2,1,0:T(8,128)(2,1)}), bf16[16,128,128]{2,1,0:T(8,128)(2,1)S(1)}, u32[]{:S(2)}, u32[]{:S(2)}) async-start(bf16[16,128,128]{2,1,0:T(8,128)(2,1)} %pack.1), calls=%async_computation | async-start | bytes 1048576 | tf_op jit(solution)/shard_map/all_to_all | solution.py:172
  17.1 2.0 %copy-start.6 = (s32[128]{0:T(128)S(1)}, s32[128]{0:T(128)}, u32[]{:S(2)}) copy-start(s32[128]{0:T(128)} %param.6) | copy-start | bytes 1540
  24.5 9.3 %collective-permute-start.1 = (bf16[272,128]{1,0:T(8,128)(2,1)S(1)}, bf16[272,128]{1,0:T(8,128)(2,1)S(1)}, u32[]{:S(2)}, u32[]{:S(2)}) collective-permute-start(bf16[272,128]{1,0:T(8,128)(2,1)S(1)} %get-tuple-element.80), channel_id=1, source_target_pairs={{0,2},{1,3},{2,0},{3,1},{4,6},{5,7},{6,4},{7,5},{8,10},{9,11},{10,... | collective-permute-start | bytes 208904 | tf_op jit(solution)/shard_map/ppermute | solution.py:132
  27.6 6.2 %collective-permute-start.2 = (bf16[272,128]{1,0:T(8,128)(2,1)S(1)}, bf16[272,128]{1,0:T(8,128)(2,1)S(1)}, u32[]{:S(2)}, u32[]{:S(2)}) collective-permute-start(bf16[272,128]{1,0:T(8,128)(2,1)S(1)} %get-tuple-element.80), channel_id=1, source_target_pairs={{0,3},{1,0},{2,1},{3,2},{4,7},{5,4},{6,5},{7,6},{8,11},{9,8},{10,9... | collective-permute-start | bytes 208904 | tf_op jit(solution)/shard_map/ppermute | solution.py:132
  30.4 7.2 %collective-permute-start = (bf16[272,128]{1,0:T(8,128)(2,1)S(1)}, bf16[272,128]{1,0:T(8,128)(2,1)S(1)}, u32[]{:S(2)}, u32[]{:S(2)}) collective-permute-start(bf16[272,128]{1,0:T(8,128)(2,1)S(1)} %get-tuple-element.80), channel_id=1, source_target_pairs={{0,1},{1,2},{2,3},{3,0},{4,5},{5,6},{6,7},{7,4},{8,9},{9,10},{10,1... | collective-permute-start | bytes 208904 | tf_op jit(solution)/shard_map/ppermute | solution.py:132
  37.7 30.6 %all-to-all-start.1 = ((bf16[16,128,256]{2,1,0:T(8,128)(2,1)}), bf16[16,128,256]{2,1,0:T(8,128)(2,1)S(1)}, u32[]{:S(2)}, u32[]{:S(2)}) async-start(bf16[16,128,256]{2,1,0:T(8,128)(2,1)} %bitcast.1), calls=%async_computation.1 | async-start | bytes 2097152 | tf_op jit(solution)/shard_map/all_to_all | solution.py:180
  45.5 3.4 %collective-permute-start.4 = (bf16[4,272,128]{2,1,0:T(8,128)(2,1)S(1)}, bf16[4,272,128]{2,1,0:T(8,128)(2,1)S(1)}, u32[]{:S(2)}, u32[]{:S(2)}) collective-permute-start(bf16[4,272,128]{2,1,0:T(8,128)(2,1)S(1)} %pad_maximum_fusion.1), channel_id=1, source_target_pairs={{0,32},{32,0},{1,33},{33,1},{2,34},{34,2},{3,35},{35,3},{4,36},{36... | collective-permute-start | bytes 835592 | tf_op jit(solution)/shard_map/ppermute | solution.py:132
  49.0 15.8 %collective-permute-start.5 = (bf16[4,544,128]{2,1,0:T(8,128)(2,1)S(1)}, bf16[4,544,128]{2,1,0:T(8,128)(2,1)}, u32[]{:S(2)}, u32[]{:S(2)}) collective-permute-start(bf16[4,544,128]{2,1,0:T(8,128)(2,1)S(1)} %pad_maximum_fusion.refs_3_), channel_id=1, source_target_pairs={{0,4},{4,8},{8,12},{12,16},{16,20},{20,24},{24,28},{28,0},{32,60},... | collective-permute-start | bytes 1671176 | tf_op jit(solution)/shard_map/ppermute | solution.py:190
  58.3 0.8 copy-start
  64.8 10.7 %collective-permute-start.7 = (bf16[4,544,128]{2,1,0:T(8,128)(2,1)}, bf16[4,544,128]{2,1,0:T(8,128)(2,1)S(1)}, u32[]{:S(2)}, u32[]{:S(2)}) collective-permute-start(bf16[4,544,128]{2,1,0:T(8,128)(2,1)} %collective-permute-done.5.refs_4_), channel_id=1, source_target_pairs={{0,32},{32,0},{1,33},{33,1},{2,34},{34,2},{3,35},{35,3},{4,36},{36... | collective-permute-start | bytes 1671176 | tf_op jit(solution)/shard_map/ppermute | solution.py:132
  68.4 7.1 %collective-permute-start.3 = (bf16[128,256]{1,0:T(8,128)(2,1)S(1)}, bf16[128,256]{1,0:T(8,128)(2,1)S(1)}, u32[]{:S(2)}, u32[]{:S(2)}) collective-permute-start(bf16[128,256]{1,0:T(8,128)(2,1)S(1)} %dynamic-slice_bitcast_fusion), channel_id=1, source_target_pairs={{0,64},{64,0},{1,65},{65,1},{2,66},{66,2},{3,67},{67,3},{4,68},{68... | collective-permute-start | bytes 196616 | tf_op jit(solution)/shard_map/ppermute | solution.py:132
  71.8 16.6 %collective-permute-start.6 = (bf16[4,544,128]{2,1,0:T(8,128)(2,1)}, bf16[4,544,128]{2,1,0:T(8,128)(2,1)S(1)}, u32[]{:S(2)}, u32[]{:S(2)}) collective-permute-start(bf16[4,544,128]{2,1,0:T(8,128)(2,1)} %collective-permute-done.5.refs_4_), channel_id=1, source_target_pairs={{0,4},{4,8},{8,12},{12,16},{16,20},{20,24},{24,28},{28,0},{32,60},... | collective-permute-start | bytes 1671176 | tf_op jit(solution)/shard_map/ppermute | solution.py:190
  75.5 0.8 copy-start.2
  76.3 1.1 copy-start.1
  77.3 1.1 copy-start.3
  88.4 5.4 %collective-permute-start.9 = (bf16[4,544,128]{2,1,0:T(8,128)(2,1)S(1)}, bf16[4,544,128]{2,1,0:T(8,128)(2,1)S(1)}, u32[]{:S(2)}, u32[]{:S(2)}) collective-permute-start(bf16[4,544,128]{2,1,0:T(8,128)(2,1)S(1)} %collective-permute-done.6.refs_3_), channel_id=1, source_target_pairs={{0,32},{32,0},{1,33},{33,1},{2,34},{34,2},{3,35},{35,3},{4,36},{36... | collective-permute-start | bytes 1671176 | tf_op jit(solution)/shard_map/ppermute | solution.py:132
  90.3 10.7 %collective-permute-start.8 = (bf16[4,544,128]{2,1,0:T(8,128)(2,1)S(1)}, bf16[4,544,128]{2,1,0:T(8,128)(2,1)}, u32[]{:S(2)}, u32[]{:S(2)}) collective-permute-start(bf16[4,544,128]{2,1,0:T(8,128)(2,1)S(1)} %collective-permute-done.6.refs_3_), channel_id=1, source_target_pairs={{0,4},{4,8},{8,12},{12,16},{16,20},{20,24},{24,28},{28,0},{32,60},... | collective-permute-start | bytes 1671176 | tf_op jit(solution)/shard_map/ppermute | solution.py:190
  101.0 7.6 %collective-permute-start.11 = (bf16[4,544,128]{2,1,0:T(8,128)(2,1)}, bf16[4,544,128]{2,1,0:T(8,128)(2,1)}, u32[]{:S(2)}, u32[]{:S(2)}) collective-permute-start(bf16[4,544,128]{2,1,0:T(8,128)(2,1)} %collective-permute-done.8.refs_3_), channel_id=1, source_target_pairs={{0,32},{32,0},{1,33},{33,1},{2,34},{34,2},{3,35},{35,3},{4,36},{36... | collective-permute-start | bytes 1671176 | tf_op jit(solution)/shard_map/ppermute | solution.py:132
  106.5 10.0 %collective-permute-start.10 = (bf16[2,544,128]{2,1,0:T(8,128)(2,1)S(1)}, bf16[2,544,128]{2,1,0:T(8,128)(2,1)S(1)}, u32[]{:S(2)}, u32[]{:S(2)}) collective-permute-start(bf16[2,544,128]{2,1,0:T(8,128)(2,1)S(1)} %constant_dynamic-slice_fusion.3), channel_id=1, source_target_pairs={{0,4},{4,8},{8,12},{12,16},{16,20},{20,24},{24,28},{28,0},{32,60},... | collective-permute-start | bytes 835592 | tf_op jit(solution)/shard_map/ppermute | solution.py:190
  116.5 3.5 %collective-permute-start.12 = (bf16[2,544,128]{2,1,0:T(8,128)(2,1)S(1)}, bf16[2,544,128]{2,1,0:T(8,128)(2,1)S(1)}, u32[]{:S(2)}, u32[]{:S(2)}) collective-permute-start(bf16[2,544,128]{2,1,0:T(8,128)(2,1)S(1)} %collective-permute-done.10.refs_3_), channel_id=1, source_target_pairs={{0,32},{32,0},{1,33},{33,1},{2,34},{34,2},{3,35},{35,3},{4,36},{36... | collective-permute-start | bytes 835592 | tf_op jit(solution)/shard_map/ppermute | solution.py:132
  120.6 7.6 %collective-permute-start.13 = (bf16[128,256]{1,0:T(8,128)(2,1)S(1)}, bf16[128,256]{1,0:T(8,128)(2,1)S(1)}, u32[]{:S(2)}, u32[]{:S(2)}) collective-permute-start(bf16[128,256]{1,0:T(8,128)(2,1)S(1)} %bitcast.29), channel_id=1, source_target_pairs={{0,64},{64,0},{1,65},{65,1},{2,66},{66,2},{3,67},{67,3},{4,68},{68... | collective-permute-start | bytes 196616 | tf_op jit(solution)/shard_map/ppermute | solution.py:132

commit v12 on v11

--- a/solution.py
+++ b/solution.py
@@ -135,8 +135,8 @@
 def packed(kv):
     def body(kv_ref, out_ref):
         for h in range(KVH):
-            k = kv_ref[:, h * HD : (h + 1) * HD]
-            v = kv_ref[:, (KVH + h) * HD : (KVH + h + 1) * HD].T
+            k = kv_ref[:, 0, h * HD : (h + 1) * HD]
+            v = kv_ref[:, 1, h * HD : (h + 1) * HD].T
             for yl in range(LAYERS // KVH // 2):
                 out_ref[h * 4 + yl * 2] = k
                 out_ref[h * 4 + yl * 2 + 1] = v
@@ -168,7 +168,7 @@
     use_warm = ((ids == warm) | (ids == other_warm)).astype(jnp.int32)
     pos = token_pos.astype(jnp.float32)[None, :]
     block_ids = jnp.broadcast_to((token_pos // BLOCK).astype(jnp.bfloat16)[None, :], (POS_ROWS, ROWS))
-    pieces = packed(key_values[0].reshape(ROWS, 2 * KVH * HD))
+    pieces = packed(key_values[0])
     pieces = lax.all_to_all(pieces, SECTION, 0, 0)
     q = queries[0].reshape(ROWS, LAYERS, WIDE).transpose(1, 0, 2)
     q, pieces, top_holder, warm, other_warm, use_warm, pos, block_ids = lax.optimization_barrier(
@@ -193,6 +193,7 @@
         return turn(value, "core", 2, 1)
 
     arrived = onward(line)
+    arrived, q, q_other = lax.optimization_barrier((arrived, q, q_other))
 
     def part(blocks, state, last=False):
         return attend(use_warm, q, pos, blocks, state, last)

time: 151 us -> 149 us (0.987)
  local copies, waits for them, and re-layouts: 11.2 us -> 7.44 us
  waiting for transfers between devices: 17.1 us -> 20.7 us
  blocking collectives: 20.1 us -> 18.5 us
  starting transfers between devices: 66.1 us -> 64.5 us
    ppermute x10, waiting for transfers between devices: 6.68 us -> 11.8 us  [turn(): lax.ppermute(value, axis, [(i, (i + shift) % size) for i in range(size)])]
    ppermute x4, waiting for transfers between devices: 5.72 us -> 1.32 us  [onward(): return lax.ppermute(value, ('core', 'z'), pairs)]
    all_to_all x1, starting transfers between devices: 7.75 us -> 3.95 us  [per_device(): q = lax.all_to_all(q, SECTION, 0, 0)]
    unnamed x16 -> x9, local copies, waits for them, and re-layouts: 6.17 us -> 2.53 us
    all_to_all x1, waiting for transfers between devices: 0.01 us -> 3.46 us  [per_device(): q = lax.all_to_all(q, SECTION, 0, 0)]
    ppermute x4, starting transfers between devices: 18.5 us -> 20.5 us  [onward(): return lax.ppermute(value, ('core', 'z'), pairs)]
    all_to_all x1, blocking collectives: 20.1 us -> 18.5 us  [per_device(): out = lax.all_to_all(out, SECTION, 0, 0)]
  transfers between devices with their start and end apart: 16 -> 16, of which waited for: 6 -> 8; matrix products, arithmetic and copies ran while one was open for 3% -> 3% of each run, Pallas kernels for 20% -> 20%
where the time goes in v12:
time: 149 us; the launch traced here: 148 us
  starting transfers between devices  64.5 us (43%)
  Pallas kernels  32.8 us (22%)
  waiting for transfers between devices  20.7 us (14%)
  blocking collectives  18.5 us (12%)
  local copies, waits for them, and re-layouts  7.44 us (5%)
  between operations  3.3 us (2%)
    pallas_call x5, Pallas kernels, attend(): pl.pallas_call(functools.partial(attend_body, shards, state is None, last...  30.3 us
    ppermute x10, starting transfers between devices, turn(): lax.ppermute(value, axis, [(i, (i + shift) % size) for i in range(size)])  29.8 us
    ppermute x4, starting transfers between devices, onward(): return lax.ppermute(value, ('core', 'z'), pairs)  20.5 us
    all_to_all x1, blocking collectives, per_device(): out = lax.all_to_all(out, SECTION, 0, 0)  18.5 us
    ppermute x10, waiting for transfers between devices, turn(): lax.ppermute(value, axis, [(i, (i + shift) % size) for i in range(size)])  11.8 us
    all_to_all x1, starting transfers between devices, per_device(): pieces = lax.all_to_all(pieces, SECTION, 0, 0)  10.2 us
    all_to_all x1, waiting for transfers between devices, per_device(): pieces = lax.all_to_all(pieces, SECTION, 0, 0)  4.09 us
    all_to_all x1, starting transfers between devices, per_device(): q = lax.all_to_all(q, SECTION, 0, 0)  3.95 us
  transfers between devices with their start and end apart: 16, of which 8 were waited for; matrix products, arithmetic and copies ran while one was open for 3% of the time, Pallas kernels for 20%

profile of v12, /device:TPU:1, one launch (start us, length us, event | category | flops | bytes accessed | tf_op | source)
XLA Modules:
  0.0 148.1 jit_solution(542710916278025194)
XLA Ops:
  0.0 2.5 %pack.1 = bf16[16,128,128]{2,1,0:T(8,128)(2,1)} custom-call(bf16[128,2,512]{2,1,0:T(2,128)(2,1)} %bitcast.32), custom_call_target="tpu_custom_call" | custom-call | tf_op jit(solution)/shard_map/pack/pallas_call | solution.py:144
  2.5 10.2 %all-to-all-start = ((bf16[16,128,128]{2,1,0:T(8,128)(2,1)}), bf16[16,128,128]{2,1,0:T(8,128)(2,1)S(1)}, u32[]{:S(2)}, u32[]{:S(2)}) async-start(bf16[16,128,128]{2,1,0:T(8,128)(2,1)} %pack.1), calls=%async_computation | async-start | bytes 1048576 | tf_op jit(solution)/shard_map/all_to_all | solution.py:172
  18.5 4.1 %all-to-all-done = bf16[16,128,128]{2,1,0:T(8,128)(2,1)S(1)} async-done(((bf16[16,128,128]{2,1,0:T(8,128)(2,1)}), bf16[16,128,128]{2,1,0:T(8,128)(2,1)S(1)}, u32[]{:S(2)}, u32[]{:S(2)}) %all-to-all-start) | async-done | bytes 524320 | tf_op jit(solution)/shard_map/all_to_all | solution.py:172
  23.2 1.9 %collective-permute-start = (bf16[272,128]{1,0:T(8,128)(2,1)S(1)}, bf16[272,128]{1,0:T(8,128)(2,1)S(1)}, u32[]{:S(2)}, u32[]{:S(2)}) collective-permute-start(bf16[272,128]{1,0:T(8,128)(2,1)S(1)} %get-tuple-element.86), channel_id=1, source_target_pairs={{0,1},{1,2},{2,3},{3,0},{4,5},{5,6},{6,7},{7,4},{8,9},{9,10},{10,1... | collective-permute-start | bytes 208904 | tf_op jit(solution)/shard_map/ppermute | solution.py:132
  25.1 3.6 %collective-permute-start.1 = (bf16[272,128]{1,0:T(8,128)(2,1)S(1)}, bf16[272,128]{1,0:T(8,128)(2,1)S(1)}, u32[]{:S(2)}, u32[]{:S(2)}) collective-permute-start(bf16[272,128]{1,0:T(8,128)(2,1)S(1)} %get-tuple-element.86), channel_id=1, source_target_pairs={{0,2},{1,3},{2,0},{3,1},{4,6},{5,7},{6,4},{7,5},{8,10},{9,11},{10,... | collective-permute-start | bytes 208904 | tf_op jit(solution)/shard_map/ppermute | solution.py:132
  28.7 5.0 %collective-permute-start.2 = (bf16[272,128]{1,0:T(8,128)(2,1)S(1)}, bf16[272,128]{1,0:T(8,128)(2,1)S(1)}, u32[]{:S(2)}, u32[]{:S(2)}) collective-permute-start(bf16[272,128]{1,0:T(8,128)(2,1)S(1)} %get-tuple-element.86), channel_id=1, source_target_pairs={{0,3},{1,0},{2,1},{3,2},{4,7},{5,4},{6,5},{7,6},{8,11},{9,8},{10,9... | collective-permute-start | bytes 208904 | tf_op jit(solution)/shard_map/ppermute | solution.py:132
  34.2 6.3 %collective-permute-done.2 = bf16[272,128]{1,0:T(8,128)(2,1)S(1)} collective-permute-done((bf16[272,128]{1,0:T(8,128)(2,1)S(1)}, bf16[272,128]{1,0:T(8,128)(2,1)S(1)}, u32[]{:S(2)}, u32[]{:S(2)}) %collective-permute-start.2) | collective-permute-done | bytes 69664 | tf_op jit(solution)/shard_map/ppermute | solution.py:132
  40.5 3.9 %all-to-all-start.1 = ((bf16[16,128,256]{2,1,0:T(8,128)(2,1)}), bf16[16,128,256]{2,1,0:T(8,128)(2,1)S(1)}, u32[]{:S(2)}, u32[]{:S(2)}) async-start(bf16[16,128,256]{2,1,0:T(8,128)(2,1)} %bitcast.1), calls=%async_computation.1 | async-start | bytes 2097152 | tf_op jit(solution)/shard_map/all_to_all | solution.py:180
  44.5 2.1 %collective-permute-start.3 = (bf16[4,272,128]{2,1,0:T(8,128)(2,1)S(1)}, bf16[4,272,128]{2,1,0:T(8,128)(2,1)S(1)}, u32[]{:S(2)}, u32[]{:S(2)}) collective-permute-start(bf16[4,272,128]{2,1,0:T(8,128)(2,1)S(1)} %pad_maximum_fusion.1), channel_id=1, source_target_pairs={{0,32},{32,0},{1,33},{33,1},{2,34},{34,2},{3,35},{35,3},{4,36},{36... | collective-permute-start | bytes 835592 | tf_op jit(solution)/shard_map/ppermute | solution.py:132
  48.0 8.1 %collective-permute-start.4 = (bf16[4,544,128]{2,1,0:T(8,128)(2,1)S(1)}, bf16[4,544,128]{2,1,0:T(8,128)(2,1)}, u32[]{:S(2)}, u32[]{:S(2)}) collective-permute-start(bf16[4,544,128]{2,1,0:T(8,128)(2,1)S(1)} %pad_maximum_fusion.refs_3_), channel_id=1, source_target_pairs={{0,4},{4,8},{8,12},{12,16},{16,20},{20,24},{24,28},{28,0},{32,60},... | collective-permute-start | bytes 1671176 | tf_op jit(solution)/shard_map/ppermute | solution.py:190
  56.9 3.5 %all-to-all-done.1 = bf16[16,128,256]{2,1,0:T(8,128)(2,1)S(1)} async-done(((bf16[16,128,256]{2,1,0:T(8,128)(2,1)}), bf16[16,128,256]{2,1,0:T(8,128)(2,1)S(1)}, u32[]{:S(2)}, u32[]{:S(2)}) %all-to-all-start.1) | async-done | bytes 1048608 | tf_op jit(solution)/shard_map/all_to_all | solution.py:180
  60.4 2.7 %collective-permute-start.5 = (bf16[128,256]{1,0:T(8,128)(2,1)S(1)}, bf16[128,256]{1,0:T(8,128)(2,1)S(1)}, u32[]{:S(2)}, u32[]{:S(2)}) collective-permute-start(bf16[128,256]{1,0:T(8,128)(2,1)S(1)} %dynamic-slice_bitcast_fusion), channel_id=1, source_target_pairs={{0,64},{64,0},{1,65},{65,1},{2,66},{66,2},{3,67},{67,3},{4,68},{68... | collective-permute-start | bytes 196616 | tf_op jit(solution)/shard_map/ppermute | solution.py:132
  63.1 2.3 %collective-permute-done.5 = bf16[128,256]{1,0:T(8,128)(2,1)S(1)} collective-permute-done((bf16[128,256]{1,0:T(8,128)(2,1)S(1)}, bf16[128,256]{1,0:T(8,128)(2,1)S(1)}, u32[]{:S(2)}, u32[]{:S(2)}) %collective-permute-start.5) | collective-permute-done | bytes 65568 | tf_op jit(solution)/shard_map/ppermute | solution.py:132
  65.4 3.9 %collective-permute-start.7 = (bf16[4,544,128]{2,1,0:T(8,128)(2,1)}, bf16[4,544,128]{2,1,0:T(8,128)(2,1)S(1)}, u32[]{:S(2)}, u32[]{:S(2)}) collective-permute-start(bf16[4,544,128]{2,1,0:T(8,128)(2,1)} %collective-permute-done.4.refs_4_), channel_id=1, source_target_pairs={{0,32},{32,0},{1,33},{33,1},{2,34},{34,2},{3,35},{35,3},{4,36},{36... | collective-permute-start | bytes 1671176 | tf_op jit(solution)/shard_map/ppermute | solution.py:132
  69.3 8.1 %collective-permute-start.6 = (bf16[4,544,128]{2,1,0:T(8,128)(2,1)}, bf16[4,544,128]{2,1,0:T(8,128)(2,1)S(1)}, u32[]{:S(2)}, u32[]{:S(2)}) collective-permute-start(bf16[4,544,128]{2,1,0:T(8,128)(2,1)} %collective-permute-done.4.refs_4_), channel_id=1, source_target_pairs={{0,4},{4,8},{8,12},{12,16},{16,20},{20,24},{24,28},{28,0},{32,60},... | collective-permute-start | bytes 1671176 | tf_op jit(solution)/shard_map/ppermute | solution.py:190
  78.5 10.0 %attend.5 = (f32[16,8,256]{2,1,0:T(8,128)S(1)}, f32[16,8,256]{2,1,0:T(8,128)S(1)}, f32[16,128,256]{2,1,0:T(8,128)S(1)}) custom-call(s32[16]{0:T(128)S(1)} %or_convert_fusion.refs_0_, bf16[16,128,256]{2,1,0:T(8,128)(2,1)S(1)} %bitcast_dynamic-update-slice_fusion.1.refs_1_, f32[1,128]{1,0:T(1,128)S(1)} %get-tuple-element.53.refs_2_, ...), custom_call_target="tpu_custom_call" | custom-call | flops 3221225472 | bytes 8388608 | tf_op jit(solution)/shard_map/attend/pallas_call | solution.py:110
  90.4 2.2 %collective-permute-start.8 = (bf16[4,544,128]{2,1,0:T(8,128)(2,1)S(1)}, bf16[4,544,128]{2,1,0:T(8,128)(2,1)}, u32[]{:S(2)}, u32[]{:S(2)}) collective-permute-start(bf16[4,544,128]{2,1,0:T(8,128)(2,1)S(1)} %collective-permute-done.6.refs_3_), channel_id=1, source_target_pairs={{0,4},{4,8},{8,12},{12,16},{16,20},{20,24},{24,28},{28,0},{32,60},... | collective-permute-start | bytes 1671176 | tf_op jit(solution)/shard_map/ppermute | solution.py:190
  92.6 7.2 %attend.6 = (f32[16,8,256]{2,1,0:T(8,128)S(1)}, f32[16,8,256]{2,1,0:T(8,128)S(1)}, f32[16,128,256]{2,1,0:T(8,128)S(1)}) custom-call(s32[16]{0:T(128)S(1)} %or_convert_fusion.refs_0_, bf16[16,128,256]{2,1,0:T(8,128)(2,1)S(1)} %bitcast_dynamic-update-slice_fusion.1.refs_1_, ...), custom_call_target="tpu_custom_call", output_to_operand_aliasing={{0}: (5, {}), {1}: (6, {}), {2}: (7, {})} | custom-call | flops 2147483648 | bytes 8388608 | tf_op jit(solution)/shard_map/attend/pallas_call | solution.py:110
  101.1 4.5 %collective-permute-start.11 = (bf16[4,544,128]{2,1,0:T(8,128)(2,1)}, bf16[4,544,128]{2,1,0:T(8,128)(2,1)}, u32[]{:S(2)}, u32[]{:S(2)}) collective-permute-start(bf16[4,544,128]{2,1,0:T(8,128)(2,1)} %collective-permute-done.8.refs_3_), channel_id=1, source_target_pairs={{0,32},{32,0},{1,33},{33,1},{2,34},{34,2},{3,35},{35,3},{4,36},{36... | collective-permute-start | bytes 1671176 | tf_op jit(solution)/shard_map/ppermute | solution.py:132
  106.6 2.1 %collective-permute-start.10 = (bf16[2,544,128]{2,1,0:T(8,128)(2,1)S(1)}, bf16[2,544,128]{2,1,0:T(8,128)(2,1)S(1)}, u32[]{:S(2)}, u32[]{:S(2)}) collective-permute-start(bf16[2,544,128]{2,1,0:T(8,128)(2,1)S(1)} %constant_dynamic-slice_fusion.3), channel_id=1, source_target_pairs={{0,4},{4,8},{8,12},{12,16},{16,20},{20,24},{24,28},{28,0},{32,60},... | collective-permute-start | bytes 835592 | tf_op jit(solution)/shard_map/ppermute | solution.py:190
  108.7 7.9 %attend.7 = (f32[16,8,256]{2,1,0:T(8,128)S(1)}, f32[16,8,256]{2,1,0:T(8,128)S(1)}, f32[16,128,256]{2,1,0:T(8,128)S(1)}) custom-call(s32[16]{0:T(128)S(1)} %or_convert_fusion.refs_0_, bf16[16,128,256]{2,1,0:T(8,128)(2,1)S(1)} %bitcast_dynamic-update-slice_fusion.1.refs_1_, ...), custom_call_target="tpu_custom_call", output_to_operand_aliasing={{0}: (5, {}), {1}: (6, {}), {2}: (7, {})} | custom-call | flops 2147483648 | bytes 8388608 | tf_op jit(solution)/shard_map/attend/pallas_call | solution.py:110
  120.7 2.3 %collective-permute-start.13 = (bf16[128,256]{1,0:T(8,128)(2,1)S(1)}, bf16[128,256]{1,0:T(8,128)(2,1)S(1)}, u32[]{:S(2)}, u32[]{:S(2)}) collective-permute-start(bf16[128,256]{1,0:T(8,128)(2,1)S(1)} %bitcast.28), channel_id=1, source_target_pairs={{0,64},{64,0},{1,65},{65,1},{2,66},{66,2},{3,67},{67,3},{4,68},{68... | collective-permute-start | bytes 196616 | tf_op jit(solution)/shard_map/ppermute | solution.py:132
  123.0 4.6 %attend.9 = bf16[16,128,256]{2,1,0:T(8,128)(2,1)S(1)} custom-call(s32[16]{0:T(128)S(1)} %or_convert_fusion.refs_0_, bf16[16,128,256]{2,1,0:T(8,128)(2,1)S(1)} %bitcast_dynamic-update-slice_fusion.1.refs_1_, f32[1,128]{1,0:T(1,128)S(1)} %get-tuple-element.53.refs_2_, bf16[2,544,128]{2,1,0:T(8,128)(2,1)S(1)} %collective-permute-done.10.refs_3_, ...), custom_call_target="tpu_custom_call" | custom-call | flops 1073741824 | bytes 8388608 | tf_op jit(solution)/shard_map/attend/pallas_call | solution.py:110
  127.6 18.5 %all_to_all.15 = bf16[16,128,256]{2,1,0:T(8,128)(2,1)S(1)} all-to-all(bf16[16,128,256]{2,1,0:T(8,128)(2,1)S(1)} %bitcast_dynamic-update-slice_fusion), channel_id=1, replica_groups=mesh['x'=4,'yl'=2,'core'=2,'z'=8,'yh'=4] {'x','yl','core'}, dimensions={0} | all-to-all | bytes 2097152 | tf_op jit(solution)/shard_map/all_to_all | solution.py:217
  (43 shorter events, 17.5 us)
Async XLA Ops:
  0.0 16.5 %copy-start.2 = (bf16[1,128,4096]{2,1,0:T(8,128)(2,1)S(1)}, bf16[1,128,4096]{2,1,0:T(8,128)(2,1)}, u32[]{:S(2)}) copy-start(bf16[1,128,4096]{2,1,0:T(8,128)(2,1)} %param.4) | copy-start | bytes 3145732
  2.5 20.1 %all-to-all-start = ((bf16[16,128,128]{2,1,0:T(8,128)(2,1)}), bf16[16,128,128]{2,1,0:T(8,128)(2,1)S(1)}, u32[]{:S(2)}, u32[]{:S(2)}) async-start(bf16[16,128,128]{2,1,0:T(8,128)(2,1)} %pack.1), calls=%async_computation | async-start | bytes 1048576 | tf_op jit(solution)/shard_map/all_to_all | solution.py:172
  16.5 2.0 %copy-start.3 = (s32[128]{0:T(128)S(1)}, s32[128]{0:T(128)}, u32[]{:S(2)}) copy-start(s32[128]{0:T(128)} %param.6) | copy-start | bytes 1540
  23.2 10.5 %collective-permute-start = (bf16[272,128]{1,0:T(8,128)(2,1)S(1)}, bf16[272,128]{1,0:T(8,128)(2,1)S(1)}, u32[]{:S(2)}, u32[]{:S(2)}) collective-permute-start(bf16[272,128]{1,0:T(8,128)(2,1)S(1)} %get-tuple-element.86), channel_id=1, source_target_pairs={{0,1},{1,2},{2,3},{3,0},{4,5},{5,6},{6,7},{7,4},{8,9},{9,10},{10,1... | collective-permute-start | bytes 208904 | tf_op jit(solution)/shard_map/ppermute | solution.py:132
  25.1 9.1 %collective-permute-start.1 = (bf16[272,128]{1,0:T(8,128)(2,1)S(1)}, bf16[272,128]{1,0:T(8,128)(2,1)S(1)}, u32[]{:S(2)}, u32[]{:S(2)}) collective-permute-start(bf16[272,128]{1,0:T(8,128)(2,1)S(1)} %get-tuple-element.86), channel_id=1, source_target_pairs={{0,2},{1,3},{2,0},{3,1},{4,6},{5,7},{6,4},{7,5},{8,10},{9,11},{10,... | collective-permute-start | bytes 208904 | tf_op jit(solution)/shard_map/ppermute | solution.py:132
  28.7 11.8 %collective-permute-start.2 = (bf16[272,128]{1,0:T(8,128)(2,1)S(1)}, bf16[272,128]{1,0:T(8,128)(2,1)S(1)}, u32[]{:S(2)}, u32[]{:S(2)}) collective-permute-start(bf16[272,128]{1,0:T(8,128)(2,1)S(1)} %get-tuple-element.86), channel_id=1, source_target_pairs={{0,3},{1,0},{2,1},{3,2},{4,7},{5,4},{6,5},{7,6},{8,11},{9,8},{10,9... | collective-permute-start | bytes 208904 | tf_op jit(solution)/shard_map/ppermute | solution.py:132
  40.5 19.9 %all-to-all-start.1 = ((bf16[16,128,256]{2,1,0:T(8,128)(2,1)}), bf16[16,128,256]{2,1,0:T(8,128)(2,1)S(1)}, u32[]{:S(2)}, u32[]{:S(2)}) async-start(bf16[16,128,256]{2,1,0:T(8,128)(2,1)} %bitcast.1), calls=%async_computation.1 | async-start | bytes 2097152 | tf_op jit(solution)/shard_map/all_to_all | solution.py:180
  44.5 3.4 %collective-permute-start.3 = (bf16[4,272,128]{2,1,0:T(8,128)(2,1)S(1)}, bf16[4,272,128]{2,1,0:T(8,128)(2,1)S(1)}, u32[]{:S(2)}, u32[]{:S(2)}) collective-permute-start(bf16[4,272,128]{2,1,0:T(8,128)(2,1)S(1)} %pad_maximum_fusion.1), channel_id=1, source_target_pairs={{0,32},{32,0},{1,33},{33,1},{2,34},{34,2},{3,35},{35,3},{4,36},{36... | collective-permute-start | bytes 835592 | tf_op jit(solution)/shard_map/ppermute | solution.py:132
  48.0 17.4 %collective-permute-start.4 = (bf16[4,544,128]{2,1,0:T(8,128)(2,1)S(1)}, bf16[4,544,128]{2,1,0:T(8,128)(2,1)}, u32[]{:S(2)}, u32[]{:S(2)}) collective-permute-start(bf16[4,544,128]{2,1,0:T(8,128)(2,1)S(1)} %pad_maximum_fusion.refs_3_), channel_id=1, source_target_pairs={{0,4},{4,8},{8,12},{12,16},{16,20},{20,24},{24,28},{28,0},{32,60},... | collective-permute-start | bytes 1671176 | tf_op jit(solution)/shard_map/ppermute | solution.py:190
  56.1 0.8 copy-start
  60.4 5.0 %collective-permute-start.5 = (bf16[128,256]{1,0:T(8,128)(2,1)S(1)}, bf16[128,256]{1,0:T(8,128)(2,1)S(1)}, u32[]{:S(2)}, u32[]{:S(2)}) collective-permute-start(bf16[128,256]{1,0:T(8,128)(2,1)S(1)} %dynamic-slice_bitcast_fusion), channel_id=1, source_target_pairs={{0,64},{64,0},{1,65},{65,1},{2,66},{66,2},{3,67},{67,3},{4,68},{68... | collective-permute-start | bytes 196616 | tf_op jit(solution)/shard_map/ppermute | solution.py:132
  65.4 12.0 %collective-permute-start.7 = (bf16[4,544,128]{2,1,0:T(8,128)(2,1)}, bf16[4,544,128]{2,1,0:T(8,128)(2,1)S(1)}, u32[]{:S(2)}, u32[]{:S(2)}) collective-permute-start(bf16[4,544,128]{2,1,0:T(8,128)(2,1)} %collective-permute-done.4.refs_4_), channel_id=1, source_target_pairs={{0,32},{32,0},{1,33},{33,1},{2,34},{34,2},{3,35},{35,3},{4,36},{36... | collective-permute-start | bytes 1671176 | tf_op jit(solution)/shard_map/ppermute | solution.py:132
  69.3 19.2 %collective-permute-start.6 = (bf16[4,544,128]{2,1,0:T(8,128)(2,1)}, bf16[4,544,128]{2,1,0:T(8,128)(2,1)S(1)}, u32[]{:S(2)}, u32[]{:S(2)}) collective-permute-start(bf16[4,544,128]{2,1,0:T(8,128)(2,1)} %collective-permute-done.4.refs_4_), channel_id=1, source_target_pairs={{0,4},{4,8},{8,12},{12,16},{16,20},{20,24},{24,28},{28,0},{32,60},... | collective-permute-start | bytes 1671176 | tf_op jit(solution)/shard_map/ppermute | solution.py:190
  77.4 1.1 copy-start.1
  88.5 4.1 %collective-permute-start.9 = (bf16[4,544,128]{2,1,0:T(8,128)(2,1)S(1)}, bf16[4,544,128]{2,1,0:T(8,128)(2,1)S(1)}, u32[]{:S(2)}, u32[]{:S(2)}) collective-permute-start(bf16[4,544,128]{2,1,0:T(8,128)(2,1)S(1)} %collective-permute-done.6.refs_3_), channel_id=1, source_target_pairs={{0,32},{32,0},{1,33},{33,1},{2,34},{34,2},{3,35},{35,3},{4,36},{36... | collective-permute-start | bytes 1671176 | tf_op jit(solution)/shard_map/ppermute | solution.py:132
  90.4 10.7 %collective-permute-start.8 = (bf16[4,544,128]{2,1,0:T(8,128)(2,1)S(1)}, bf16[4,544,128]{2,1,0:T(8,128)(2,1)}, u32[]{:S(2)}, u32[]{:S(2)}) collective-permute-start(bf16[4,544,128]{2,1,0:T(8,128)(2,1)S(1)} %collective-permute-done.6.refs_3_), channel_id=1, source_target_pairs={{0,4},{4,8},{8,12},{12,16},{16,20},{20,24},{24,28},{28,0},{32,60},... | collective-permute-start | bytes 1671176 | tf_op jit(solution)/shard_map/ppermute | solution.py:190
  101.1 7.6 %collective-permute-start.11 = (bf16[4,544,128]{2,1,0:T(8,128)(2,1)}, bf16[4,544,128]{2,1,0:T(8,128)(2,1)}, u32[]{:S(2)}, u32[]{:S(2)}) collective-permute-start(bf16[4,544,128]{2,1,0:T(8,128)(2,1)} %collective-permute-done.8.refs_3_), channel_id=1, source_target_pairs={{0,32},{32,0},{1,33},{33,1},{2,34},{34,2},{3,35},{35,3},{4,36},{36... | collective-permute-start | bytes 1671176 | tf_op jit(solution)/shard_map/ppermute | solution.py:132
  106.6 10.0 %collective-permute-start.10 = (bf16[2,544,128]{2,1,0:T(8,128)(2,1)S(1)}, bf16[2,544,128]{2,1,0:T(8,128)(2,1)S(1)}, u32[]{:S(2)}, u32[]{:S(2)}) collective-permute-start(bf16[2,544,128]{2,1,0:T(8,128)(2,1)S(1)} %constant_dynamic-slice_fusion.3), channel_id=1, source_target_pairs={{0,4},{4,8},{8,12},{12,16},{16,20},{20,24},{24,28},{28,0},{32,60},... | collective-permute-start | bytes 835592 | tf_op jit(solution)/shard_map/ppermute | solution.py:190
  116.6 3.5 %collective-permute-start.12 = (bf16[2,544,128]{2,1,0:T(8,128)(2,1)S(1)}, bf16[2,544,128]{2,1,0:T(8,128)(2,1)S(1)}, u32[]{:S(2)}, u32[]{:S(2)}) collective-permute-start(bf16[2,544,128]{2,1,0:T(8,128)(2,1)S(1)} %collective-permute-done.10.refs_3_), channel_id=1, source_target_pairs={{0,32},{32,0},{1,33},{33,1},{2,34},{34,2},{3,35},{35,3},{4,36},{36... | collective-permute-start | bytes 835592 | tf_op jit(solution)/shard_map/ppermute | solution.py:132
  120.7 6.9 %collective-permute-start.13 = (bf16[128,256]{1,0:T(8,128)(2,1)S(1)}, bf16[128,256]{1,0:T(8,128)(2,1)S(1)}, u32[]{:S(2)}, u32[]{:S(2)}) collective-permute-start(bf16[128,256]{1,0:T(8,128)(2,1)S(1)} %bitcast.28), channel_id=1, source_target_pairs={{0,64},{64,0},{1,65},{65,1},{2,66},{66,2},{3,67},{67,3},{4,68},{68... | collective-permute-start | bytes 196616 | tf_op jit(solution)/shard_map/ppermute | solution.py:132

commit v13 on v12

--- a/solution.py
+++ b/solution.py
@@ -175,8 +175,9 @@
         (q, pieces, top_holder, warm, other_warm, use_warm, pos, block_ids)
     )
     shard = jnp.concatenate([pick(pieces, top_holder), pick(pieces, warm), block_ids], axis=0)
-    mine = jnp.stack([shard] + [turn(shard, "yh", nyh, shift) for shift in range(1, nyh)])
-    q, mine = lax.optimization_barrier((q, mine))
+    others = [turn(shard, "yh", nyh, shift) for shift in range(1, nyh)]
+    q, others[0] = lax.optimization_barrier((q, others[0]))
+    mine = jnp.stack([shard, *others])
     q = lax.all_to_all(q, SECTION, 0, 0)
     q_other = turn(pick(q, other_warm), "yl", 2, 1)
     q = put(q, q_other, other_warm)

time: 149 us -> 158 us (1.060)
  waiting for transfers between devices: 20.7 us -> 25.3 us
  starting transfers between devices: 64.5 us -> 67.1 us
    ppermute x10, waiting for transfers between devices: 11.8 us -> 21 us  [turn(): lax.ppermute(value, axis, [(i, (i + shift) % size) for i in range(size)])]
    all_to_all x1, waiting for transfers between devices: 3.46 us -> 0.01 us  [per_device(): q = lax.all_to_all(q, SECTION, 0, 0)]
    all_to_all x1, starting transfers between devices: 3.95 us -> 5.64 us  [per_device(): q = lax.all_to_all(q, SECTION, 0, 0)]
    ppermute x10, starting transfers between devices: 29.8 us -> 31.5 us  [turn(): lax.ppermute(value, axis, [(i, (i + shift) % size) for i in range(size)])]
  transfers between devices with their start and end apart: 16 -> 16, of which waited for: 8 -> 7; matrix products, arithmetic and copies ran while one was open for 3% -> 3% of each run, Pallas kernels for 20% -> 19%
where the time goes in v13:
time: 158 us; the launch traced here: 157 us
  starting transfers between devices  67.1 us (42%)
  Pallas kernels  32.8 us (21%)
  waiting for transfers between devices  25.3 us (16%)
  blocking collectives  19.9 us (13%)
  local copies, waits for them, and re-layouts  7.44 us (5%)
  between operations  3.3 us (2%)
    ppermute x10, starting transfers between devices, turn(): lax.ppermute(value, axis, [(i, (i + shift) % size) for i in range(size)])  31.5 us
    pallas_call x5, Pallas kernels, attend(): pl.pallas_call(functools.partial(attend_body, shards, state is None, last...  30.3 us
    ppermute x10, waiting for transfers between devices, turn(): lax.ppermute(value, axis, [(i, (i + shift) % size) for i in range(size)])  21 us
    all_to_all x1, blocking collectives, per_device(): out = lax.all_to_all(out, SECTION, 0, 0)  19.9 us
    ppermute x4, starting transfers between devices, onward(): return lax.ppermute(value, ('core', 'z'), pairs)  19.8 us
    all_to_all x1, starting transfers between devices, per_device(): pieces = lax.all_to_all(pieces, SECTION, 0, 0)  10.2 us
    all_to_all x1, starting transfers between devices, per_device(): q = lax.all_to_all(q, SECTION, 0, 0)  5.64 us
    all_to_all x1, waiting for transfers between devices, per_device(): pieces = lax.all_to_all(pieces, SECTION, 0, 0)  4.09 us
  transfers between devices with their start and end apart: 16, of which 7 were waited for; matrix products, arithmetic and copies ran while one was open for 3% of the time, Pallas kernels for 19%

profile of v13, /device:TPU:1, one launch (start us, length us, event | category | flops | bytes accessed | tf_op | source)
XLA Modules:
  0.0 156.7 jit_solution(858518878324819274)
XLA Ops:
  0.0 2.5 %pack.1 = bf16[16,128,128]{2,1,0:T(8,128)(2,1)} custom-call(bf16[128,2,512]{2,1,0:T(2,128)(2,1)} %bitcast.38), custom_call_target="tpu_custom_call" | custom-call | tf_op jit(solution)/shard_map/pack/pallas_call | solution.py:144
  2.5 10.2 %all-to-all-start = ((bf16[16,128,128]{2,1,0:T(8,128)(2,1)}), bf16[16,128,128]{2,1,0:T(8,128)(2,1)S(1)}, u32[]{:S(2)}, u32[]{:S(2)}) async-start(bf16[16,128,128]{2,1,0:T(8,128)(2,1)} %pack.1), calls=%async_computation | async-start | bytes 1048576 | tf_op jit(solution)/shard_map/all_to_all | solution.py:172
  18.5 4.1 %all-to-all-done = bf16[16,128,128]{2,1,0:T(8,128)(2,1)S(1)} async-done(((bf16[16,128,128]{2,1,0:T(8,128)(2,1)}), bf16[16,128,128]{2,1,0:T(8,128)(2,1)S(1)}, u32[]{:S(2)}, u32[]{:S(2)}) %all-to-all-start) | async-done | bytes 524320 | tf_op jit(solution)/shard_map/all_to_all | solution.py:172
  23.2 1.9 %collective-permute-start = (bf16[272,128]{1,0:T(8,128)(2,1)S(1)}, bf16[272,128]{1,0:T(8,128)(2,1)S(1)}, u32[]{:S(2)}, u32[]{:S(2)}) collective-permute-start(bf16[272,128]{1,0:T(8,128)(2,1)S(1)} %get-tuple-element.86), channel_id=1, source_target_pairs={{0,1},{1,2},{2,3},{3,0},{4,5},{5,6},{6,7},{7,4},{8,9},{9,10},{10,1... | collective-permute-start | bytes 208904 | tf_op jit(solution)/shard_map/ppermute | solution.py:132
  25.1 5.7 %collective-permute-done = bf16[272,128]{1,0:T(8,128)(2,1)S(1)} collective-permute-done((bf16[272,128]{1,0:T(8,128)(2,1)S(1)}, bf16[272,128]{1,0:T(8,128)(2,1)S(1)}, u32[]{:S(2)}, u32[]{:S(2)}) %collective-permute-start) | collective-permute-done | bytes 69664 | tf_op jit(solution)/shard_map/ppermute | solution.py:132
  30.9 5.6 %all-to-all-start.1 = ((bf16[16,128,256]{2,1,0:T(8,128)(2,1)}), bf16[16,128,256]{2,1,0:T(8,128)(2,1)S(1)}, u32[]{:S(2)}, u32[]{:S(2)}) async-start(bf16[16,128,256]{2,1,0:T(8,128)(2,1)} %bitcast.1), calls=%async_computation.1 | async-start | bytes 2097152 | tf_op jit(solution)/shard_map/all_to_all | solution.py:181
  36.5 3.1 %collective-permute-start.1 = (bf16[272,128]{1,0:T(8,128)(2,1)S(1)}, bf16[272,128]{1,0:T(8,128)(2,1)S(1)}, u32[]{:S(2)}, u32[]{:S(2)}) collective-permute-start(bf16[272,128]{1,0:T(8,128)(2,1)S(1)} %get-tuple-element.86), channel_id=1, source_target_pairs={{0,2},{1,3},{2,0},{3,1},{4,6},{5,7},{6,4},{7,5},{8,10},{9,11},{10,... | collective-permute-start | bytes 208904 | tf_op jit(solution)/shard_map/ppermute | solution.py:132
  39.7 2.8 %collective-permute-start.2 = (bf16[272,128]{1,0:T(8,128)(2,1)S(1)}, bf16[272,128]{1,0:T(8,128)(2,1)S(1)}, u32[]{:S(2)}, u32[]{:S(2)}) collective-permute-start(bf16[272,128]{1,0:T(8,128)(2,1)S(1)} %get-tuple-element.86), channel_id=1, source_target_pairs={{0,3},{1,0},{2,1},{3,2},{4,7},{5,4},{6,5},{7,6},{8,11},{9,8},{10,9... | collective-permute-start | bytes 208904 | tf_op jit(solution)/shard_map/ppermute | solution.py:132
  42.4 10.8 %collective-permute-done.1 = bf16[272,128]{1,0:T(8,128)(2,1)S(1)} collective-permute-done((bf16[272,128]{1,0:T(8,128)(2,1)S(1)}, bf16[272,128]{1,0:T(8,128)(2,1)S(1)}, u32[]{:S(2)}, u32[]{:S(2)}) %collective-permute-start.1) | collective-permute-done | bytes 69664 | tf_op jit(solution)/shard_map/ppermute | solution.py:132
  53.3 2.6 %collective-permute-start.3 = (bf16[4,272,128]{2,1,0:T(8,128)(2,1)S(1)}, bf16[4,272,128]{2,1,0:T(8,128)(2,1)S(1)}, u32[]{:S(2)}, u32[]{:S(2)}) collective-permute-start(bf16[4,272,128]{2,1,0:T(8,128)(2,1)S(1)} %pad_maximum_fusion.1), channel_id=1, source_target_pairs={{0,32},{32,0},{1,33},{33,1},{2,34},{34,2},{3,35},{35,3},{4,36},{36... | collective-permute-start | bytes 835592 | tf_op jit(solution)/shard_map/ppermute | solution.py:132
  57.1 10.8 %collective-permute-start.4 = (bf16[4,544,128]{2,1,0:T(8,128)(2,1)S(1)}, bf16[4,544,128]{2,1,0:T(8,128)(2,1)}, u32[]{:S(2)}, u32[]{:S(2)}) collective-permute-start(bf16[4,544,128]{2,1,0:T(8,128)(2,1)S(1)} %pad_maximum_fusion.refs_3_), channel_id=1, source_target_pairs={{0,4},{4,8},{8,12},{12,16},{16,20},{20,24},{24,28},{28,0},{32,60},... | collective-permute-start | bytes 1671176 | tf_op jit(solution)/shard_map/ppermute | solution.py:191
  68.7 5.2 %collective-permute-start.5 = (bf16[128,256]{1,0:T(8,128)(2,1)S(1)}, bf16[128,256]{1,0:T(8,128)(2,1)S(1)}, u32[]{:S(2)}, u32[]{:S(2)}) collective-permute-start(bf16[128,256]{1,0:T(8,128)(2,1)S(1)} %dynamic-slice_bitcast_fusion), channel_id=1, source_target_pairs={{0,64},{64,0},{1,65},{65,1},{2,66},{66,2},{3,67},{67,3},{4,68},{68... | collective-permute-start | bytes 196616 | tf_op jit(solution)/shard_map/ppermute | solution.py:132
  75.8 2.3 %collective-permute-start.7 = (bf16[4,544,128]{2,1,0:T(8,128)(2,1)}, bf16[4,544,128]{2,1,0:T(8,128)(2,1)S(1)}, u32[]{:S(2)}, u32[]{:S(2)}) collective-permute-start(bf16[4,544,128]{2,1,0:T(8,128)(2,1)} %collective-permute-done.4.refs_4_), channel_id=1, source_target_pairs={{0,32},{32,0},{1,33},{33,1},{2,34},{34,2},{3,35},{35,3},{4,36},{36... | collective-permute-start | bytes 1671176 | tf_op jit(solution)/shard_map/ppermute | solution.py:132
  78.1 3.6 %collective-permute-start.6 = (bf16[4,544,128]{2,1,0:T(8,128)(2,1)}, bf16[4,544,128]{2,1,0:T(8,128)(2,1)S(1)}, u32[]{:S(2)}, u32[]{:S(2)}) collective-permute-start(bf16[4,544,128]{2,1,0:T(8,128)(2,1)} %collective-permute-done.4.refs_4_), channel_id=1, source_target_pairs={{0,4},{4,8},{8,12},{12,16},{16,20},{20,24},{24,28},{28,0},{32,60},... | collective-permute-start | bytes 1671176 | tf_op jit(solution)/shard_map/ppermute | solution.py:191
  82.8 10.0 %attend.5 = (f32[16,8,256]{2,1,0:T(8,128)S(1)}, f32[16,8,256]{2,1,0:T(8,128)S(1)}, f32[16,128,256]{2,1,0:T(8,128)S(1)}) custom-call(s32[16]{0:T(128)S(1)} %or_convert_fusion.refs_0_, bf16[16,128,256]{2,1,0:T(8,128)(2,1)S(1)} %bitcast_dynamic-update-slice_fusion.1.refs_1_, f32[1,128]{1,0:T(1,128)S(1)} %get-tuple-element.53.refs_2_, ...), custom_call_target="tpu_custom_call" | custom-call | flops 3221225472 | bytes 8388608 | tf_op jit(solution)/shard_map/attend/pallas_call | solution.py:110
  92.8 1.9 %collective-permute-start.9 = (bf16[4,544,128]{2,1,0:T(8,128)(2,1)S(1)}, bf16[4,544,128]{2,1,0:T(8,128)(2,1)S(1)}, u32[]{:S(2)}, u32[]{:S(2)}) collective-permute-start(bf16[4,544,128]{2,1,0:T(8,128)(2,1)S(1)} %collective-permute-done.6.refs_3_), channel_id=1, source_target_pairs={{0,32},{32,0},{1,33},{33,1},{2,34},{34,2},{3,35},{35,3},{4,36},{36... | collective-permute-start | bytes 1671176 | tf_op jit(solution)/shard_map/ppermute | solution.py:132
  94.7 3.3 %collective-permute-start.8 = (bf16[4,544,128]{2,1,0:T(8,128)(2,1)S(1)}, bf16[4,544,128]{2,1,0:T(8,128)(2,1)}, u32[]{:S(2)}, u32[]{:S(2)}) collective-permute-start(bf16[4,544,128]{2,1,0:T(8,128)(2,1)S(1)} %collective-permute-done.6.refs_3_), channel_id=1, source_target_pairs={{0,4},{4,8},{8,12},{12,16},{16,20},{20,24},{24,28},{28,0},{32,60},... | collective-permute-start | bytes 1671176 | tf_op jit(solution)/shard_map/ppermute | solution.py:191
  98.0 7.2 %attend.6 = (f32[16,8,256]{2,1,0:T(8,128)S(1)}, f32[16,8,256]{2,1,0:T(8,128)S(1)}, f32[16,128,256]{2,1,0:T(8,128)S(1)}) custom-call(s32[16]{0:T(128)S(1)} %or_convert_fusion.refs_0_, bf16[16,128,256]{2,1,0:T(8,128)(2,1)S(1)} %bitcast_dynamic-update-slice_fusion.1.refs_1_, ...), custom_call_target="tpu_custom_call", output_to_operand_aliasing={{0}: (5, {}), {1}: (6, {}), {2}: (7, {})} | custom-call | flops 2147483648 | bytes 8388608 | tf_op jit(solution)/shard_map/attend/pallas_call | solution.py:110
  105.4 4.5 %collective-permute-start.11 = (bf16[4,544,128]{2,1,0:T(8,128)(2,1)}, bf16[4,544,128]{2,1,0:T(8,128)(2,1)}, u32[]{:S(2)}, u32[]{:S(2)}) collective-permute-start(bf16[4,544,128]{2,1,0:T(8,128)(2,1)} %collective-permute-done.8.refs_3_), channel_id=1, source_target_pairs={{0,32},{32,0},{1,33},{33,1},{2,34},{34,2},{3,35},{35,3},{4,36},{36... | collective-permute-start | bytes 1671176 | tf_op jit(solution)/shard_map/ppermute | solution.py:132
  110.9 2.1 %collective-permute-start.10 = (bf16[2,544,128]{2,1,0:T(8,128)(2,1)S(1)}, bf16[2,544,128]{2,1,0:T(8,128)(2,1)S(1)}, u32[]{:S(2)}, u32[]{:S(2)}) collective-permute-start(bf16[2,544,128]{2,1,0:T(8,128)(2,1)S(1)} %constant_dynamic-slice_fusion.3), channel_id=1, source_target_pairs={{0,4},{4,8},{8,12},{12,16},{16,20},{20,24},{24,28},{28,0},{32,60},... | collective-permute-start | bytes 835592 | tf_op jit(solution)/shard_map/ppermute | solution.py:191
  113.0 7.9 %attend.7 = (f32[16,8,256]{2,1,0:T(8,128)S(1)}, f32[16,8,256]{2,1,0:T(8,128)S(1)}, f32[16,128,256]{2,1,0:T(8,128)S(1)}) custom-call(s32[16]{0:T(128)S(1)} %or_convert_fusion.refs_0_, bf16[16,128,256]{2,1,0:T(8,128)(2,1)S(1)} %bitcast_dynamic-update-slice_fusion.1.refs_1_, ...), custom_call_target="tpu_custom_call", output_to_operand_aliasing={{0}: (5, {}), {1}: (6, {}), {2}: (7, {})} | custom-call | flops 2147483648 | bytes 8388608 | tf_op jit(solution)/shard_map/attend/pallas_call | solution.py:110
  125.0 5.2 %collective-permute-start.13 = (bf16[128,256]{1,0:T(8,128)(2,1)S(1)}, bf16[128,256]{1,0:T(8,128)(2,1)S(1)}, u32[]{:S(2)}, u32[]{:S(2)}) collective-permute-start(bf16[128,256]{1,0:T(8,128)(2,1)S(1)} %bitcast.28), channel_id=1, source_target_pairs={{0,64},{64,0},{1,65},{65,1},{2,66},{66,2},{3,67},{67,3},{4,68},{68... | collective-permute-start | bytes 196616 | tf_op jit(solution)/shard_map/ppermute | solution.py:132
  130.2 4.6 %attend.9 = bf16[16,128,256]{2,1,0:T(8,128)(2,1)S(1)} custom-call(s32[16]{0:T(128)S(1)} %or_convert_fusion.refs_0_, bf16[16,128,256]{2,1,0:T(8,128)(2,1)S(1)} %bitcast_dynamic-update-slice_fusion.1.refs_1_, f32[1,128]{1,0:T(1,128)S(1)} %get-tuple-element.53.refs_2_, bf16[2,544,128]{2,1,0:T(8,128)(2,1)S(1)} %collective-permute-done.10.refs_3_, ...), custom_call_target="tpu_custom_call" | custom-call | flops 1073741824 | bytes 8388608 | tf_op jit(solution)/shard_map/attend/pallas_call | solution.py:110
  134.9 19.9 %all_to_all.15 = bf16[16,128,256]{2,1,0:T(8,128)(2,1)S(1)} all-to-all(bf16[16,128,256]{2,1,0:T(8,128)(2,1)S(1)} %bitcast_dynamic-update-slice_fusion), channel_id=1, replica_groups=mesh['x'=4,'yl'=2,'core'=2,'z'=8,'yh'=4] {'x','yl','core'}, dimensions={0} | all-to-all | bytes 2097152 | tf_op jit(solution)/shard_map/all_to_all | solution.py:218
  (43 shorter events, 15.7 us)
Async XLA Ops:
  0.0 16.5 %copy-start.2 = (bf16[1,128,4096]{2,1,0:T(8,128)(2,1)S(1)}, bf16[1,128,4096]{2,1,0:T(8,128)(2,1)}, u32[]{:S(2)}) copy-start(bf16[1,128,4096]{2,1,0:T(8,128)(2,1)} %param.4) | copy-start | bytes 3145732
  2.5 20.1 %all-to-all-start = ((bf16[16,128,128]{2,1,0:T(8,128)(2,1)}), bf16[16,128,128]{2,1,0:T(8,128)(2,1)S(1)}, u32[]{:S(2)}, u32[]{:S(2)}) async-start(bf16[16,128,128]{2,1,0:T(8,128)(2,1)} %pack.1), calls=%async_computation | async-start | bytes 1048576 | tf_op jit(solution)/shard_map/all_to_all | solution.py:172
  16.5 2.0 %copy-start.3 = (s32[128]{0:T(128)S(1)}, s32[128]{0:T(128)}, u32[]{:S(2)}) copy-start(s32[128]{0:T(128)} %param.6) | copy-start | bytes 1540
  23.2 7.7 %collective-permute-start = (bf16[272,128]{1,0:T(8,128)(2,1)S(1)}, bf16[272,128]{1,0:T(8,128)(2,1)S(1)}, u32[]{:S(2)}, u32[]{:S(2)}) collective-permute-start(bf16[272,128]{1,0:T(8,128)(2,1)S(1)} %get-tuple-element.86), channel_id=1, source_target_pairs={{0,1},{1,2},{2,3},{3,0},{4,5},{5,6},{6,7},{7,4},{8,9},{9,10},{10,1... | collective-permute-start | bytes 208904 | tf_op jit(solution)/shard_map/ppermute | solution.py:132
  30.9 37.9 %all-to-all-start.1 = ((bf16[16,128,256]{2,1,0:T(8,128)(2,1)}), bf16[16,128,256]{2,1,0:T(8,128)(2,1)S(1)}, u32[]{:S(2)}, u32[]{:S(2)}) async-start(bf16[16,128,256]{2,1,0:T(8,128)(2,1)} %bitcast.1), calls=%async_computation.1 | async-start | bytes 2097152 | tf_op jit(solution)/shard_map/all_to_all | solution.py:181
  36.5 16.7 %collective-permute-start.1 = (bf16[272,128]{1,0:T(8,128)(2,1)S(1)}, bf16[272,128]{1,0:T(8,128)(2,1)S(1)}, u32[]{:S(2)}, u32[]{:S(2)}) collective-permute-start(bf16[272,128]{1,0:T(8,128)(2,1)S(1)} %get-tuple-element.86), channel_id=1, source_target_pairs={{0,2},{1,3},{2,0},{3,1},{4,6},{5,7},{6,4},{7,5},{8,10},{9,11},{10,... | collective-permute-start | bytes 208904 | tf_op jit(solution)/shard_map/ppermute | solution.py:132
  39.7 13.6 %collective-permute-start.2 = (bf16[272,128]{1,0:T(8,128)(2,1)S(1)}, bf16[272,128]{1,0:T(8,128)(2,1)S(1)}, u32[]{:S(2)}, u32[]{:S(2)}) collective-permute-start(bf16[272,128]{1,0:T(8,128)(2,1)S(1)} %get-tuple-element.86), channel_id=1, source_target_pairs={{0,3},{1,0},{2,1},{3,2},{4,7},{5,4},{6,5},{7,6},{8,11},{9,8},{10,9... | collective-permute-start | bytes 208904 | tf_op jit(solution)/shard_map/ppermute | solution.py:132
  53.3 3.8 %collective-permute-start.3 = (bf16[4,272,128]{2,1,0:T(8,128)(2,1)S(1)}, bf16[4,272,128]{2,1,0:T(8,128)(2,1)S(1)}, u32[]{:S(2)}, u32[]{:S(2)}) collective-permute-start(bf16[4,272,128]{2,1,0:T(8,128)(2,1)S(1)} %pad_maximum_fusion.1), channel_id=1, source_target_pairs={{0,32},{32,0},{1,33},{33,1},{2,34},{34,2},{3,35},{35,3},{4,36},{36... | collective-permute-start | bytes 835592 | tf_op jit(solution)/shard_map/ppermute | solution.py:132
  57.1 18.6 %collective-permute-start.4 = (bf16[4,544,128]{2,1,0:T(8,128)(2,1)S(1)}, bf16[4,544,128]{2,1,0:T(8,128)(2,1)}, u32[]{:S(2)}, u32[]{:S(2)}) collective-permute-start(bf16[4,544,128]{2,1,0:T(8,128)(2,1)S(1)} %pad_maximum_fusion.refs_3_), channel_id=1, source_target_pairs={{0,4},{4,8},{8,12},{12,16},{16,20},{20,24},{24,28},{28,0},{32,60},... | collective-permute-start | bytes 1671176 | tf_op jit(solution)/shard_map/ppermute | solution.py:191
  67.9 0.8 copy-start
  68.7 7.0 %collective-permute-start.5 = (bf16[128,256]{1,0:T(8,128)(2,1)S(1)}, bf16[128,256]{1,0:T(8,128)(2,1)S(1)}, u32[]{:S(2)}, u32[]{:S(2)}) collective-permute-start(bf16[128,256]{1,0:T(8,128)(2,1)S(1)} %dynamic-slice_bitcast_fusion), channel_id=1, source_target_pairs={{0,64},{64,0},{1,65},{65,1},{2,66},{66,2},{3,67},{67,3},{4,68},{68... | collective-permute-start | bytes 196616 | tf_op jit(solution)/shard_map/ppermute | solution.py:132
  75.8 5.9 %collective-permute-start.7 = (bf16[4,544,128]{2,1,0:T(8,128)(2,1)}, bf16[4,544,128]{2,1,0:T(8,128)(2,1)S(1)}, u32[]{:S(2)}, u32[]{:S(2)}) collective-permute-start(bf16[4,544,128]{2,1,0:T(8,128)(2,1)} %collective-permute-done.4.refs_4_), channel_id=1, source_target_pairs={{0,32},{32,0},{1,33},{33,1},{2,34},{34,2},{3,35},{35,3},{4,36},{36... | collective-permute-start | bytes 1671176 | tf_op jit(solution)/shard_map/ppermute | solution.py:132
  78.1 14.7 %collective-permute-start.6 = (bf16[4,544,128]{2,1,0:T(8,128)(2,1)}, bf16[4,544,128]{2,1,0:T(8,128)(2,1)S(1)}, u32[]{:S(2)}, u32[]{:S(2)}) collective-permute-start(bf16[4,544,128]{2,1,0:T(8,128)(2,1)} %collective-permute-done.4.refs_4_), channel_id=1, source_target_pairs={{0,4},{4,8},{8,12},{12,16},{16,20},{20,24},{24,28},{28,0},{32,60},... | collective-permute-start | bytes 1671176 | tf_op jit(solution)/shard_map/ppermute | solution.py:191
  81.7 1.1 copy-start.1
  92.8 5.2 %collective-permute-start.9 = (bf16[4,544,128]{2,1,0:T(8,128)(2,1)S(1)}, bf16[4,544,128]{2,1,0:T(8,128)(2,1)S(1)}, u32[]{:S(2)}, u32[]{:S(2)}) collective-permute-start(bf16[4,544,128]{2,1,0:T(8,128)(2,1)S(1)} %collective-permute-done.6.refs_3_), channel_id=1, source_target_pairs={{0,32},{32,0},{1,33},{33,1},{2,34},{34,2},{3,35},{35,3},{4,36},{36... | collective-permute-start | bytes 1671176 | tf_op jit(solution)/shard_map/ppermute | solution.py:132
  94.7 10.7 %collective-permute-start.8 = (bf16[4,544,128]{2,1,0:T(8,128)(2,1)S(1)}, bf16[4,544,128]{2,1,0:T(8,128)(2,1)}, u32[]{:S(2)}, u32[]{:S(2)}) collective-permute-start(bf16[4,544,128]{2,1,0:T(8,128)(2,1)S(1)} %collective-permute-done.6.refs_3_), channel_id=1, source_target_pairs={{0,4},{4,8},{8,12},{12,16},{16,20},{20,24},{24,28},{28,0},{32,60},... | collective-permute-start | bytes 1671176 | tf_op jit(solution)/shard_map/ppermute | solution.py:191
  105.4 7.6 %collective-permute-start.11 = (bf16[4,544,128]{2,1,0:T(8,128)(2,1)}, bf16[4,544,128]{2,1,0:T(8,128)(2,1)}, u32[]{:S(2)}, u32[]{:S(2)}) collective-permute-start(bf16[4,544,128]{2,1,0:T(8,128)(2,1)} %collective-permute-done.8.refs_3_), channel_id=1, source_target_pairs={{0,32},{32,0},{1,33},{33,1},{2,34},{34,2},{3,35},{35,3},{4,36},{36... | collective-permute-start | bytes 1671176 | tf_op jit(solution)/shard_map/ppermute | solution.py:132
  110.9 10.0 %collective-permute-start.10 = (bf16[2,544,128]{2,1,0:T(8,128)(2,1)S(1)}, bf16[2,544,128]{2,1,0:T(8,128)(2,1)S(1)}, u32[]{:S(2)}, u32[]{:S(2)}) collective-permute-start(bf16[2,544,128]{2,1,0:T(8,128)(2,1)S(1)} %constant_dynamic-slice_fusion.3), channel_id=1, source_target_pairs={{0,4},{4,8},{8,12},{12,16},{16,20},{20,24},{24,28},{28,0},{32,60},... | collective-permute-start | bytes 835592 | tf_op jit(solution)/shard_map/ppermute | solution.py:191
  120.9 3.5 %collective-permute-start.12 = (bf16[2,544,128]{2,1,0:T(8,128)(2,1)S(1)}, bf16[2,544,128]{2,1,0:T(8,128)(2,1)S(1)}, u32[]{:S(2)}, u32[]{:S(2)}) collective-permute-start(bf16[2,544,128]{2,1,0:T(8,128)(2,1)S(1)} %collective-permute-done.10.refs_3_), channel_id=1, source_target_pairs={{0,32},{32,0},{1,33},{33,1},{2,34},{34,2},{3,35},{35,3},{4,36},{36... | collective-permute-start | bytes 835592 | tf_op jit(solution)/shard_map/ppermute | solution.py:132
  125.0 9.8 %collective-permute-start.13 = (bf16[128,256]{1,0:T(8,128)(2,1)S(1)}, bf16[128,256]{1,0:T(8,128)(2,1)S(1)}, u32[]{:S(2)}, u32[]{:S(2)}) collective-permute-start(bf16[128,256]{1,0:T(8,128)(2,1)S(1)} %bitcast.28), channel_id=1, source_target_pairs={{0,64},{64,0},{1,65},{65,1},{2,66},{66,2},{3,67},{67,3},{4,68},{68... | collective-permute-start | bytes 196616 | tf_op jit(solution)/shard_map/ppermute | solution.py:132
